TPU v7x, 32 devices: a whole 2x2x4 slice. The times are simulated.
32 devices in a mesh: gx: 4 (over z), gy: 4 (over x, core), gz: 2 (over y).
Axes of the slice: x: 2, y: 2, z: 4, core: 2. Of those that a mesh axis runs over, the one named last changes fastest.
Arguments:
- phase_mask: int32 [64, 128, 256], P('gx', 'gy', 'gz'), may hold values from 0 to 2
- pressure: float32 [64, 128, 256], P('gx', 'gy', 'gz'), may hold values from -6 to 6
- velocity_cot: float32 [3, 64, 128, 256], P(None, 'gx', 'gy', 'gz'), may hold values from -30 to 30
Outputs:
- ustar_cot: float32 [3, 64, 128, 256], P(None, 'gx', 'gy', 'gz')
- coef_cot: float32 [64, 128, 256], P('gx', 'gy', 'gz')
Inputs may be any that keep to these rules, and one draw needn't show every extreme that they name: `phase_mask`: 0 air, 1 water, 2 interface band.
All inputs are finite; a program needn't handle non-finite values.
Results may differ from a plain program's by a relative error of at most 0.0001.
Values sent between devices are 32-bit elements; how exact they have to be, the bound alone decides.
No kernel may reach another device: no remote copies, remote signals or barrier semaphores. Data moves between devices by JAX's collectives and lax.ppermute only.
A program may use at most 64 MiB of HBM per device.

v0:
```python
import jax
import jax.numpy as jnp
from jax import lax
from jax.sharding import PartitionSpec as P

ITERS = 3


def extended(cells, sides, width):
    for axis, dim in sides:
        count = lax.axis_size(axis)
        ends = count - 1
        head = lax.slice_in_dim(cells, 0, width, axis=dim)
        tail = lax.slice_in_dim(cells, cells.shape[dim] - width, cells.shape[dim], axis=dim)
        cells = jnp.concatenate(
            [
                lax.ppermute(tail, axis, [(i, (i + 1) % count) for i in range(ends)]),
                cells,
                lax.ppermute(head, axis, [((i + 1) % count, i) for i in range(ends)]),
            ],
            axis=dim,
        )
    return cells


def coefficient(phase_mask):
    return jnp.where(phase_mask == 0, 8.0, jnp.where(phase_mask == 1, 1.0, 2.0)).astype(jnp.float32)


def face_pair(padded, dim_idx):
    count = padded.shape[dim_idx]
    lower = lax.slice_in_dim(padded, 0, count - 1, axis=dim_idx)
    upper = lax.slice_in_dim(padded, 1, count, axis=dim_idx)
    for other in range(3):
        if other != dim_idx:
            width = padded.shape[other]
            lower = lax.slice_in_dim(lower, 1, width - 1, axis=other)
            upper = lax.slice_in_dim(upper, 1, width - 1, axis=other)
    return (upper, lower)


def face_grads(padded):
    result = []
    for dim_idx in range(3):
        upper, lower = face_pair(padded, dim_idx)
        result.append(upper - lower)
    return tuple(result)


def face_weights(coef_padded):
    result = []
    for dim_idx in range(3):
        upper, lower = face_pair(coef_padded, dim_idx)
        result.append(0.5 * (upper + lower))
    return tuple(result)


def diverge(fluxes):
    total = None
    for dim_idx in range(3):
        flux = fluxes[dim_idx]
        count = flux.shape[dim_idx]
        term = lax.slice_in_dim(flux, 0, count - 1, axis=dim_idx) - lax.slice_in_dim(
            flux, 1, count, axis=dim_idx
        )
        total = term if total is None else total + term
    return total


def spread(fluxes):
    total = None
    for dim_idx in range(3):
        flux = fluxes[dim_idx]
        count = flux.shape[dim_idx]
        term = lax.slice_in_dim(flux, 0, count - 1, axis=dim_idx) + lax.slice_in_dim(
            flux, 1, count, axis=dim_idx
        )
        total = term if total is None else total + term
    return total


def extend(field):
    return extended(field, (("gx", 0), ("gy", 1), ("gz", 2)), 1)


def operate(field, weights):
    grads = face_grads(extend(field))
    return diverge(tuple((weights[dim_idx] * grads[dim_idx] for dim_idx in range(3))))


def paired_sums(resid, precd, image):
    return lax.psum((jnp.sum(resid * precd), jnp.sum(precd * image)), ("gx", "gy", "gz"))


def on_device(phase_mask, pressure, velocity_cot):
    coef_cells = coefficient(phase_mask)
    stacked = jnp.concatenate([coef_cells[None], pressure[None], velocity_cot], 0)
    padded = extended(stacked, (("gx", 1), ("gy", 2), ("gz", 3)), 1)
    coef_padded = padded[0]
    press_padded = padded[1]
    vel_faces = tuple((face_pair(padded[2 + dim_idx], dim_idx)[1] for dim_idx in range(3)))
    weights = face_weights(coef_padded)
    precond = 1.0 / spread(weights)
    rhs = -diverge(tuple((weights[dim_idx] * vel_faces[dim_idx] for dim_idx in range(3))))
    press_grads = face_grads(press_padded)
    solution = jnp.zeros_like(rhs)
    resid = rhs
    precd = precond * resid
    image = operate(precd, weights)
    rz_now, curve = paired_sums(resid, precd, image)
    step_len = rz_now / curve
    direction = precd
    along = image
    for iteration in range(ITERS):
        solution = solution + step_len * direction
        resid = resid - step_len * along
        if iteration + 1 < ITERS:
            precd = precond * resid
            image = operate(precd, weights)
            rz_next, curve = paired_sums(resid, precd, image)
            ratio = rz_next / rz_now
            step_len = rz_next / (curve - ratio * rz_next / step_len)
            direction = precd + ratio * direction
            along = image + ratio * along
            rz_now = rz_next
    lam_grads = face_grads(extend(solution))
    columns = []
    for dim_idx in range(3):
        count = lam_grads[dim_idx].shape[dim_idx]
        columns.append(
            velocity_cot[dim_idx] + lax.slice_in_dim(lam_grads[dim_idx], 1, count, axis=dim_idx)
        )
    ustar_cot = jnp.stack(columns, 0)
    wbar = tuple(
        (-press_grads[dim_idx] * (vel_faces[dim_idx] + lam_grads[dim_idx]) for dim_idx in range(3))
    )
    coef_cot = 0.5 * spread(wbar)
    return (ustar_cot, coef_cot)


def solution(mesh):
    in_specs = (P("gx", "gy", "gz"), P("gx", "gy", "gz"), P(None, "gx", "gy", "gz"))
    out_specs = (P(None, "gx", "gy", "gz"), P("gx", "gy", "gz"))
    return jax.shard_map(
        on_device, mesh=mesh, in_specs=in_specs, out_specs=out_specs, check_vma=False
    )
```

profile of v0, /device:TPU:0, one launch (start us, length us, event | category | flops | bytes accessed | tf_op | source)
XLA Modules:
  0.0 304.1 jit_solution(9295342261873549775)
XLA Ops:
  2.6 4.9 %collective-permute-start = (f32[5,1,32,128]{3,2,1,0:T(8,128)S(1)}, f32[5,1,32,128]{3,2,1,0:T(8,128)S(1)}, u32[]{:S(2)}, u32[]{:S(2)}) collective-permute-start(f32[5,1,32,128]{3,2,1,0:T(8,128)S(1)} %get-tuple-element.46), channel_id=1, source_target_pairs={{0,8},{8,16},{16,24},{1,9},{9,17},{17,25},{2,10},{10,18},{18,26},{... | collective-permute-start | bytes 245768 | tf_op jit(solution)/shard_map/ppermute | solution.py:17
  9.6 4.3 %collective-permute-done.1 = f32[5,1,32,128]{3,2,1,0:T(8,128)S(1)} collective-permute-done((f32[5,1,32,128]{3,2,1,0:T(8,128)S(1)}, f32[5,1,32,128]{3,2,1,0:T(8,128)S(1)}, u32[]{:S(2)}, u32[]{:S(2)}) %collective-permute-start.1) | collective-permute-done | bytes 81952 | tf_op jit(solution)/shard_map/ppermute | solution.py:19
  16.5 3.5 %collective-permute-done.3 = f32[5,18,1,128]{3,2,1,0:T(1,128)S(1)} collective-permute-done((f32[5,18,1,128]{3,2,1,0:T(1,128)S(1)}, f32[5,18,1,128]{3,2,1,0:T(1,128)S(1)}, u32[]{:S(2)}, u32[]{:S(2)}) %collective-permute-start.3) | collective-permute-done | bytes 46112 | tf_op jit(solution)/shard_map/ppermute | solution.py:19
  24.4 3.4 %collective-permute-start.4 = (f32[5,18,34,1]{2,3,1,0:T(1,128)S(1)}, f32[5,18,34,1]{2,3,1,0:T(1,128)S(1)}, u32[]{:S(2)}, u32[]{:S(2)}) collective-permute-start(f32[5,18,34,1]{2,3,1,0:T(1,128)S(1)} %copy.18), channel_id=1, source_target_pairs={{0,1},{2,3},{4,5},{6,7},{8,9},{10,11},{12,13},{14,15},{16,17},{18,... | collective-permute-start | bytes 36728 | tf_op jit(solution)/shard_map/ppermute | solution.py:17
  31.3 4.2 %collective-permute-done.5 = f32[5,18,34,1]{2,3,1,0:T(1,128)} collective-permute-done((f32[5,18,34,1]{2,3,1,0:T(1,128)}, f32[5,18,34,1]{2,3,1,0:T(1,128)}, u32[]{:S(2)}, u32[]{:S(2)}) %collective-permute-start.5) | collective-permute-done | bytes 12272 | tf_op jit(solution)/shard_map/ppermute | solution.py:19
  38.2 5.5 %pad_maximum_fusion = f32[5,18,34,130]{3,2,1,0:T(8,128)S(1)} fusion(f32[5,18,34,1]{3,2,1,0:T(8,128)} %copy.17, f32[5,18,1,128]{3,2,1,0:T(1,128)S(1)} %collective-permute-done.3, f32[5,1,32,128]{3,2,1,0:T(8,128)S(1)} %collective-permute-done.1, f32[3,16,32,128]{3,2,1,0:T(8,128)S(1)} %copy-done, f32[1,16,32,128]{3,2,1,0:T(8,128)S(1)} %bitcast.36, ...), kind=kLoop, calls=%fused_computation | loop fusion | flops 3182400 | bytes 3182400 | tf_op jit(solution)/shard_map/concatenate | solution.py:15
  49.0 4.5 %collective-permute-start.7 = (f32[1,32,128]{2,1,0:T(8,128)S(1)}, f32[1,32,128]{2,1,0:T(8,128)S(1)}, u32[]{:S(2)}, u32[]{:S(2)}) collective-permute-start(f32[1,32,128]{2,1,0:T(8,128)S(1)} %get-tuple-element.75), channel_id=1, source_target_pairs={{0,8},{8,16},{16,24},{1,9},{9,17},{17,25},{2,10},{10,18},{18,26},{... | collective-permute-start | bytes 49160 | tf_op jit(solution)/shard_map/ppermute | solution.py:17
  56.3 3.0 collective-permute-start.9
  61.7 4.6 %collective-permute-start.11 = (f32[18,34,1]{2,1,0:T(8,128)S(1)}, f32[18,34,1]{2,1,0:T(8,128)S(1)}, u32[]{:S(2)}, u32[]{:S(2)}) collective-permute-start(f32[18,34,1]{2,1,0:T(8,128)S(1)} %get-tuple-element.58), channel_id=1, source_target_pairs={{0,1},{2,3},{4,5},{6,7},{8,9},{10,11},{12,13},{14,15},{16,17},{18,... | collective-permute-start | bytes 7352 | tf_op jit(solution)/shard_map/ppermute | solution.py:17
  66.3 6.1 %collective-permute-done.10 = f32[18,34,1]{2,1,0:T(8,128)S(1)} collective-permute-done((f32[18,34,1]{2,1,0:T(8,128)S(1)}, f32[18,34,1]{2,1,0:T(8,128)S(1)}, u32[]{:S(2)}, u32[]{:S(2)}) %collective-permute-start.10) | collective-permute-done | bytes 2480 | tf_op jit(solution)/shard_map/ppermute | solution.py:19
  76.0 43.6 %all-reduce.2 = (f32[]{:T(128)}, f32[]{:T(128)}) all-reduce(f32[]{:T(128)} %get-tuple-element.9, f32[]{:T(128)} %get-tuple-element.8), channel_id=1, replica_groups=mesh['gx'=4,'gy'=4,'gz'=2] {'gx','gy','gz'}, use_global_device_ids=true, to_apply=%region_1.2 | all-reduce | flops 2 | bytes 16 | tf_op jit(solution)/shard_map/psum | solution.py:92
  123.3 4.5 %collective-permute-start.13 = (f32[1,32,128]{2,1,0:T(8,128)S(1)}, f32[1,32,128]{2,1,0:T(8,128)S(1)}, u32[]{:S(2)}, u32[]{:S(2)}) collective-permute-start(f32[1,32,128]{2,1,0:T(8,128)S(1)} %get-tuple-element.73), channel_id=1, source_target_pairs={{0,8},{8,16},{16,24},{1,9},{9,17},{17,25},{2,10},{10,18},{18,26},{... | collective-permute-start | bytes 49160 | tf_op jit(solution)/shard_map/ppermute | solution.py:17
  130.6 3.0 collective-permute-start.15
  136.2 4.6 %collective-permute-start.17 = (f32[18,34,1]{2,1,0:T(8,128)S(1)}, f32[18,34,1]{2,1,0:T(8,128)S(1)}, u32[]{:S(2)}, u32[]{:S(2)}) collective-permute-start(f32[18,34,1]{2,1,0:T(8,128)S(1)} %get-tuple-element.56), channel_id=1, source_target_pairs={{0,1},{2,3},{4,5},{6,7},{8,9},{10,11},{12,13},{14,15},{16,17},{18,... | collective-permute-start | bytes 7352 | tf_op jit(solution)/shard_map/ppermute | solution.py:17
  140.8 6.5 %collective-permute-done.16 = f32[18,34,1]{2,1,0:T(8,128)S(1)} collective-permute-done((f32[18,34,1]{2,1,0:T(8,128)S(1)}, f32[18,34,1]{2,1,0:T(8,128)S(1)}, u32[]{:S(2)}, u32[]{:S(2)}) %collective-permute-start.16) | collective-permute-done | bytes 2480 | tf_op jit(solution)/shard_map/ppermute | solution.py:19
  150.9 42.8 %all-reduce.1 = (f32[]{:T(128)}, f32[]{:T(128)}) all-reduce(f32[]{:T(128)} %get-tuple-element.7, f32[]{:T(128)} %get-tuple-element.6), channel_id=1, replica_groups=mesh['gx'=4,'gy'=4,'gz'=2] {'gx','gy','gz'}, use_global_device_ids=true, to_apply=%region_5.6 | all-reduce | flops 2 | bytes 16 | tf_op jit(solution)/shard_map/psum | solution.py:92
  200.7 4.5 %collective-permute-start.19 = (f32[1,32,128]{2,1,0:T(8,128)S(1)}, f32[1,32,128]{2,1,0:T(8,128)S(1)}, u32[]{:S(2)}, u32[]{:S(2)}) collective-permute-start(f32[1,32,128]{2,1,0:T(8,128)S(1)} %get-tuple-element.71), channel_id=1, source_target_pairs={{0,8},{8,16},{16,24},{1,9},{9,17},{17,25},{2,10},{10,18},{18,26},{... | collective-permute-start | bytes 49160 | tf_op jit(solution)/shard_map/ppermute | solution.py:17
  208.0 3.0 collective-permute-start.21
  213.3 4.8 %collective-permute-start.23 = (f32[18,34,1]{2,1,0:T(8,128)S(1)}, f32[18,34,1]{2,1,0:T(8,128)S(1)}, u32[]{:S(2)}, u32[]{:S(2)}) collective-permute-start(f32[18,34,1]{2,1,0:T(8,128)S(1)} %get-tuple-element.54), channel_id=1, source_target_pairs={{0,1},{2,3},{4,5},{6,7},{8,9},{10,11},{12,13},{14,15},{16,17},{18,... | collective-permute-start | bytes 7352 | tf_op jit(solution)/shard_map/ppermute | solution.py:17
  218.2 6.3 %collective-permute-done.22 = f32[18,34,1]{2,1,0:T(8,128)S(1)} collective-permute-done((f32[18,34,1]{2,1,0:T(8,128)S(1)}, f32[18,34,1]{2,1,0:T(8,128)S(1)}, u32[]{:S(2)}, u32[]{:S(2)}) %collective-permute-start.22) | collective-permute-done | bytes 2480 | tf_op jit(solution)/shard_map/ppermute | solution.py:19
  227.4 42.6 %all-reduce = (f32[]{:T(128)}, f32[]{:T(128)}) all-reduce(f32[]{:T(128)} %get-tuple-element.5, f32[]{:T(128)} %get-tuple-element.4), channel_id=1, replica_groups=mesh['gx'=4,'gy'=4,'gz'=2] {'gx','gy','gz'}, use_global_device_ids=true, to_apply=%region_9.10 | all-reduce | flops 2 | bytes 16 | tf_op jit(solution)/shard_map/psum | solution.py:92
  274.9 4.5 %collective-permute-start.25 = (f32[1,32,128]{2,1,0:T(8,128)S(1)}, f32[1,32,128]{2,1,0:T(8,128)S(1)}, u32[]{:S(2)}, u32[]{:S(2)}) collective-permute-start(f32[1,32,128]{2,1,0:T(8,128)S(1)} %get-tuple-element.69), channel_id=1, source_target_pairs={{0,8},{8,16},{16,24},{1,9},{9,17},{17,25},{2,10},{10,18},{18,26},{... | collective-permute-start | bytes 49160 | tf_op jit(solution)/shard_map/ppermute | solution.py:17
  288.7 4.6 %collective-permute-start.29 = (f32[18,34,1]{2,1,0:T(8,128)S(1)}, f32[18,34,1]{2,1,0:T(8,128)S(1)}, u32[]{:S(2)}, u32[]{:S(2)}) collective-permute-start(f32[18,34,1]{2,1,0:T(8,128)S(1)} %get-tuple-element.52), channel_id=1, source_target_pairs={{0,1},{2,3},{4,5},{6,7},{8,9},{10,11},{12,13},{14,15},{16,17},{18,... | collective-permute-start | bytes 7352 | tf_op jit(solution)/shard_map/ppermute | solution.py:17
  294.8 5.1 %collective-permute-done.28 = f32[18,34,1]{2,1,0:T(8,128)S(1)} collective-permute-done((f32[18,34,1]{2,1,0:T(8,128)S(1)}, f32[18,34,1]{2,1,0:T(8,128)S(1)}, u32[]{:S(2)}, u32[]{:S(2)}) %collective-permute-start.28) | collective-permute-done | bytes 2480 | tf_op jit(solution)/shard_map/ppermute | solution.py:19
  (108 shorter events, 68.9 us)
Async XLA Ops:
  2.6 7.0 %collective-permute-start = (f32[5,1,32,128]{3,2,1,0:T(8,128)S(1)}, f32[5,1,32,128]{3,2,1,0:T(8,128)S(1)}, u32[]{:S(2)}, u32[]{:S(2)}) collective-permute-start(f32[5,1,32,128]{3,2,1,0:T(8,128)S(1)} %get-tuple-element.46), channel_id=1, source_target_pairs={{0,8},{8,16},{16,24},{1,9},{9,17},{17,25},{2,10},{10,18},{18,26},{... | collective-permute-start | bytes 245768 | tf_op jit(solution)/shard_map/ppermute | solution.py:17
  7.5 6.3 %collective-permute-start.1 = (f32[5,1,32,128]{3,2,1,0:T(8,128)S(1)}, f32[5,1,32,128]{3,2,1,0:T(8,128)S(1)}, u32[]{:S(2)}, u32[]{:S(2)}) collective-permute-start(f32[5,1,32,128]{3,2,1,0:T(8,128)S(1)} %get-tuple-element.47), channel_id=1, source_target_pairs={{8,0},{16,8},{24,16},{9,1},{17,9},{25,17},{10,2},{18,10},{26,18},{... | collective-permute-start | bytes 245768 | tf_op jit(solution)/shard_map/ppermute | solution.py:19
  15.2 4.8 %collective-permute-start.3 = (f32[5,18,1,128]{3,2,1,0:T(1,128)S(1)}, f32[5,18,1,128]{3,2,1,0:T(1,128)S(1)}, u32[]{:S(2)}, u32[]{:S(2)}) collective-permute-start(f32[5,18,1,128]{3,2,1,0:T(1,128)S(1)} %get-tuple-element.45), channel_id=1, source_target_pairs={{2,0},{4,2},{6,4},{3,1},{5,3},{7,5},{10,8},{12,10},{14,12},{11,9},... | collective-permute-start | bytes 138248 | tf_op jit(solution)/shard_map/ppermute | solution.py:19
  24.4 6.1 %collective-permute-start.4 = (f32[5,18,34,1]{2,3,1,0:T(1,128)S(1)}, f32[5,18,34,1]{2,3,1,0:T(1,128)S(1)}, u32[]{:S(2)}, u32[]{:S(2)}) collective-permute-start(f32[5,18,34,1]{2,3,1,0:T(1,128)S(1)} %copy.18), channel_id=1, source_target_pairs={{0,1},{2,3},{4,5},{6,7},{8,9},{10,11},{12,13},{14,15},{16,17},{18,... | collective-permute-start | bytes 36728 | tf_op jit(solution)/shard_map/ppermute | solution.py:17
  29.2 6.3 %collective-permute-start.5 = (f32[5,18,34,1]{2,3,1,0:T(1,128)}, f32[5,18,34,1]{2,3,1,0:T(1,128)}, u32[]{:S(2)}, u32[]{:S(2)}) collective-permute-start(f32[5,18,34,1]{2,3,1,0:T(1,128)} %copy.19), channel_id=1, source_target_pairs={{1,0},{3,2},{5,4},{7,6},{9,8},{11,10},{13,12},{15,14},{17,16},{19,... | collective-permute-start | bytes 36728 | tf_op jit(solution)/shard_map/ppermute | solution.py:19
  47.7 5.8 %collective-permute-start.6 = (f32[1,32,128]{2,1,0:T(8,128)S(1)}, f32[1,32,128]{2,1,0:T(8,128)S(1)}, u32[]{:S(2)}, u32[]{:S(2)}) collective-permute-start(f32[1,32,128]{2,1,0:T(8,128)S(1)} %get-tuple-element.76), channel_id=1, source_target_pairs={{8,0},{16,8},{24,16},{9,1},{17,9},{25,17},{10,2},{18,10},{26,18},{... | collective-permute-start | bytes 49160 | tf_op jit(solution)/shard_map/ppermute | solution.py:19
  49.0 6.0 %collective-permute-start.7 = (f32[1,32,128]{2,1,0:T(8,128)S(1)}, f32[1,32,128]{2,1,0:T(8,128)S(1)}, u32[]{:S(2)}, u32[]{:S(2)}) collective-permute-start(f32[1,32,128]{2,1,0:T(8,128)S(1)} %get-tuple-element.75), channel_id=1, source_target_pairs={{0,8},{8,16},{16,24},{1,9},{9,17},{17,25},{2,10},{10,18},{18,26},{... | collective-permute-start | bytes 49160 | tf_op jit(solution)/shard_map/ppermute | solution.py:17
  55.0 4.4 %collective-permute-start.8 = (f32[18,1,128]{2,1,0:T(1,128)S(1)}, f32[18,1,128]{2,1,0:T(1,128)S(1)}, u32[]{:S(2)}, u32[]{:S(2)}) collective-permute-start(f32[18,1,128]{2,1,0:T(1,128)S(1)} %get-tuple-element.68), channel_id=1, source_target_pairs={{2,0},{4,2},{6,4},{3,1},{5,3},{7,5},{10,8},{12,10},{14,12},{11,9},... | collective-permute-start | bytes 27656 | tf_op jit(solution)/shard_map/ppermute | solution.py:19
  60.4 12.1 %collective-permute-start.10 = (f32[18,34,1]{2,1,0:T(8,128)S(1)}, f32[18,34,1]{2,1,0:T(8,128)S(1)}, u32[]{:S(2)}, u32[]{:S(2)}) collective-permute-start(f32[18,34,1]{2,1,0:T(8,128)S(1)} %get-tuple-element.57), channel_id=1, source_target_pairs={{1,0},{3,2},{5,4},{7,6},{9,8},{11,10},{13,12},{15,14},{17,16},{19,... | collective-permute-start | bytes 7352 | tf_op jit(solution)/shard_map/ppermute | solution.py:19
  61.7 12.6 %collective-permute-start.11 = (f32[18,34,1]{2,1,0:T(8,128)S(1)}, f32[18,34,1]{2,1,0:T(8,128)S(1)}, u32[]{:S(2)}, u32[]{:S(2)}) collective-permute-start(f32[18,34,1]{2,1,0:T(8,128)S(1)} %get-tuple-element.58), channel_id=1, source_target_pairs={{0,1},{2,3},{4,5},{6,7},{8,9},{10,11},{12,13},{14,15},{16,17},{18,... | collective-permute-start | bytes 7352 | tf_op jit(solution)/shard_map/ppermute | solution.py:17
  122.0 5.9 %collective-permute-start.12 = (f32[1,32,128]{2,1,0:T(8,128)S(1)}, f32[1,32,128]{2,1,0:T(8,128)S(1)}, u32[]{:S(2)}, u32[]{:S(2)}) collective-permute-start(f32[1,32,128]{2,1,0:T(8,128)S(1)} %get-tuple-element.74), channel_id=1, source_target_pairs={{8,0},{16,8},{24,16},{9,1},{17,9},{25,17},{10,2},{18,10},{26,18},{... | collective-permute-start | bytes 49160 | tf_op jit(solution)/shard_map/ppermute | solution.py:19
  123.3 6.0 %collective-permute-start.13 = (f32[1,32,128]{2,1,0:T(8,128)S(1)}, f32[1,32,128]{2,1,0:T(8,128)S(1)}, u32[]{:S(2)}, u32[]{:S(2)}) collective-permute-start(f32[1,32,128]{2,1,0:T(8,128)S(1)} %get-tuple-element.73), channel_id=1, source_target_pairs={{0,8},{8,16},{16,24},{1,9},{9,17},{17,25},{2,10},{10,18},{18,26},{... | collective-permute-start | bytes 49160 | tf_op jit(solution)/shard_map/ppermute | solution.py:17
  134.7 12.6 %collective-permute-start.16 = (f32[18,34,1]{2,1,0:T(8,128)S(1)}, f32[18,34,1]{2,1,0:T(8,128)S(1)}, u32[]{:S(2)}, u32[]{:S(2)}) collective-permute-start(f32[18,34,1]{2,1,0:T(8,128)S(1)} %get-tuple-element.55), channel_id=1, source_target_pairs={{1,0},{3,2},{5,4},{7,6},{9,8},{11,10},{13,12},{15,14},{17,16},{19,... | collective-permute-start | bytes 7352 | tf_op jit(solution)/shard_map/ppermute | solution.py:19
  136.2 13.0 %collective-permute-start.17 = (f32[18,34,1]{2,1,0:T(8,128)S(1)}, f32[18,34,1]{2,1,0:T(8,128)S(1)}, u32[]{:S(2)}, u32[]{:S(2)}) collective-permute-start(f32[18,34,1]{2,1,0:T(8,128)S(1)} %get-tuple-element.56), channel_id=1, source_target_pairs={{0,1},{2,3},{4,5},{6,7},{8,9},{10,11},{12,13},{14,15},{16,17},{18,... | collective-permute-start | bytes 7352 | tf_op jit(solution)/shard_map/ppermute | solution.py:17
  199.4 5.9 %collective-permute-start.18 = (f32[1,32,128]{2,1,0:T(8,128)S(1)}, f32[1,32,128]{2,1,0:T(8,128)S(1)}, u32[]{:S(2)}, u32[]{:S(2)}) collective-permute-start(f32[1,32,128]{2,1,0:T(8,128)S(1)} %get-tuple-element.72), channel_id=1, source_target_pairs={{8,0},{16,8},{24,16},{9,1},{17,9},{25,17},{10,2},{18,10},{26,18},{... | collective-permute-start | bytes 49160 | tf_op jit(solution)/shard_map/ppermute | solution.py:19
  200.7 6.0 %collective-permute-start.19 = (f32[1,32,128]{2,1,0:T(8,128)S(1)}, f32[1,32,128]{2,1,0:T(8,128)S(1)}, u32[]{:S(2)}, u32[]{:S(2)}) collective-permute-start(f32[1,32,128]{2,1,0:T(8,128)S(1)} %get-tuple-element.71), channel_id=1, source_target_pairs={{0,8},{8,16},{16,24},{1,9},{9,17},{17,25},{2,10},{10,18},{18,26},{... | collective-permute-start | bytes 49160 | tf_op jit(solution)/shard_map/ppermute | solution.py:17
  212.0 12.5 %collective-permute-start.22 = (f32[18,34,1]{2,1,0:T(8,128)S(1)}, f32[18,34,1]{2,1,0:T(8,128)S(1)}, u32[]{:S(2)}, u32[]{:S(2)}) collective-permute-start(f32[18,34,1]{2,1,0:T(8,128)S(1)} %get-tuple-element.53), channel_id=1, source_target_pairs={{1,0},{3,2},{5,4},{7,6},{9,8},{11,10},{13,12},{15,14},{17,16},{19,... | collective-permute-start | bytes 7352 | tf_op jit(solution)/shard_map/ppermute | solution.py:19
  213.3 13.0 %collective-permute-start.23 = (f32[18,34,1]{2,1,0:T(8,128)S(1)}, f32[18,34,1]{2,1,0:T(8,128)S(1)}, u32[]{:S(2)}, u32[]{:S(2)}) collective-permute-start(f32[18,34,1]{2,1,0:T(8,128)S(1)} %get-tuple-element.54), channel_id=1, source_target_pairs={{0,1},{2,3},{4,5},{6,7},{8,9},{10,11},{12,13},{14,15},{16,17},{18,... | collective-permute-start | bytes 7352 | tf_op jit(solution)/shard_map/ppermute | solution.py:17
  273.6 5.9 %collective-permute-start.24 = (f32[1,32,128]{2,1,0:T(8,128)S(1)}, f32[1,32,128]{2,1,0:T(8,128)S(1)}, u32[]{:S(2)}, u32[]{:S(2)}) collective-permute-start(f32[1,32,128]{2,1,0:T(8,128)S(1)} %get-tuple-element.70), channel_id=1, source_target_pairs={{8,0},{16,8},{24,16},{9,1},{17,9},{25,17},{10,2},{18,10},{26,18},{... | collective-permute-start | bytes 49160 | tf_op jit(solution)/shard_map/ppermute | solution.py:19
  274.9 6.0 %collective-permute-start.25 = (f32[1,32,128]{2,1,0:T(8,128)S(1)}, f32[1,32,128]{2,1,0:T(8,128)S(1)}, u32[]{:S(2)}, u32[]{:S(2)}) collective-permute-start(f32[1,32,128]{2,1,0:T(8,128)S(1)} %get-tuple-element.69), channel_id=1, source_target_pairs={{0,8},{8,16},{16,24},{1,9},{9,17},{17,25},{2,10},{10,18},{18,26},{... | collective-permute-start | bytes 49160 | tf_op jit(solution)/shard_map/ppermute | solution.py:17
  280.9 6.2 %collective-permute-start.26 = (f32[18,1,128]{2,1,0:T(1,128)S(1)}, f32[18,1,128]{2,1,0:T(1,128)S(1)}, u32[]{:S(2)}, u32[]{:S(2)}) collective-permute-start(f32[18,1,128]{2,1,0:T(1,128)S(1)} %get-tuple-element.62), channel_id=1, source_target_pairs={{2,0},{4,2},{6,4},{3,1},{5,3},{7,5},{10,8},{12,10},{14,12},{11,9},... | collective-permute-start | bytes 27656 | tf_op jit(solution)/shard_map/ppermute | solution.py:19
  282.2 4.9 %collective-permute-start.27 = (f32[18,1,128]{2,1,0:T(1,128)S(1)}, f32[18,1,128]{2,1,0:T(1,128)S(1)}, u32[]{:S(2)}, u32[]{:S(2)}) collective-permute-start(f32[18,1,128]{2,1,0:T(1,128)S(1)} %get-tuple-element.61), channel_id=1, source_target_pairs={{0,2},{2,4},{4,6},{1,3},{3,5},{5,7},{8,10},{10,12},{12,14},{9,11},... | collective-permute-start | bytes 27656 | tf_op jit(solution)/shard_map/ppermute | solution.py:17
  287.3 12.6 %collective-permute-start.28 = (f32[18,34,1]{2,1,0:T(8,128)S(1)}, f32[18,34,1]{2,1,0:T(8,128)S(1)}, u32[]{:S(2)}, u32[]{:S(2)}) collective-permute-start(f32[18,34,1]{2,1,0:T(8,128)S(1)} %get-tuple-element.51), channel_id=1, source_target_pairs={{1,0},{3,2},{5,4},{7,6},{9,8},{11,10},{13,12},{15,14},{17,16},{19,... | collective-permute-start | bytes 7352 | tf_op jit(solution)/shard_map/ppermute | solution.py:19
  288.7 12.9 %collective-permute-start.29 = (f32[18,34,1]{2,1,0:T(8,128)S(1)}, f32[18,34,1]{2,1,0:T(8,128)S(1)}, u32[]{:S(2)}, u32[]{:S(2)}) collective-permute-start(f32[18,34,1]{2,1,0:T(8,128)S(1)} %get-tuple-element.52), channel_id=1, source_target_pairs={{0,1},{2,3},{4,5},{6,7},{8,9},{10,11},{12,13},{14,15},{16,17},{18,... | collective-permute-start | bytes 7352 | tf_op jit(solution)/shard_map/ppermute | solution.py:17
  (14 other events, 183.7 us)
where the time goes:
time: 306 us; the launch traced here: 304 us
  blocking collectives  129 us (42%)
  starting transfers between devices  78.1 us (26%)
  waiting for transfers between devices  52 us (17%)
  other arithmetic  22.8 us (7%)
  local copies, waits for them, and re-layouts  11.8 us (4%)
  between operations  10.4 us (3%)
    psum x3, blocking collectives, paired_sums(): lax.psum((jnp.sum(resid * precd), jnp.sum(precd * image)), ('gx', 'gy', '...  129 us
    ppermute x15, starting transfers between devices, extended(): lax.ppermute(tail, axis, [(i, (i + 1) % count) for i in range(ends)])  58.5 us
    ppermute x15, waiting for transfers between devices, extended(): lax.ppermute(head, axis, [((i + 1) % count, i) for i in range(ends)])  36.1 us
    ppermute x15, starting transfers between devices, extended(): lax.ppermute(head, axis, [((i + 1) % count, i) for i in range(ends)])  19.6 us
    ppermute x15, waiting for transfers between devices, extended(): lax.ppermute(tail, axis, [(i, (i + 1) % count) for i in range(ends)])  15.8 us
  transfers between devices with their start and end apart: 30, of which 19 were waited for; matrix products, arithmetic and copies ran while one was open for 2% of the time, Pallas kernels for 0%

commit v1 on v0

v1 whole, which is shorter than its diff:
```python
import functools

import jax
import jax.numpy as jnp
from jax import lax
from jax.experimental import pallas as pl
from jax.experimental.pallas import tpu as pltpu
from jax.sharding import PartitionSpec as P

AXES = ("gx", "gy", "gz")
DEPTH = 4
GROUP = 4 * DEPTH
LANES = 128
ROWS = 8
VMEM = pl.BlockSpec(memory_space=pltpu.VMEM)
SMEM = pl.BlockSpec(memory_space=pltpu.SMEM)
ANY = pl.BlockSpec(memory_space=pl.ANY)
PARAMS = pltpu.CompilerParams(vmem_limit_bytes=48 * 1024 * 1024)


def swaps(count, first):
    pairs = []
    for i in range(first, count - 1, 2):
        pairs += [(i, i + 1), (i + 1, i)]
    return pairs


def exchange(sends, axis):
    count = lax.axis_size(axis)
    return [lax.ppermute(send, axis, swaps(count, turn)) for turn, send in enumerate(sends)]


def turns(axis):
    return min(2, lax.axis_size(axis) - 1)


def coefficient(phase):
    return jnp.where(phase == 0, 8.0, jnp.where(phase == 1, 1.0, 2.0)).astype(jnp.float32)


def sides(even, got, load):
    one = load(got[0])
    two = load(got[1]) if len(got) > 1 else jnp.zeros_like(one)
    return jnp.where(even, two, one), jnp.where(even, one, two)


def lane_index(shape):
    return lax.broadcasted_iota(jnp.int32, shape, len(shape) - 1)


def row_index(shape):
    return lax.broadcasted_iota(jnp.int32, shape, len(shape) - 2)


def roll_rows(plane, shift):
    return pltpu.roll(plane, shift % plane.shape[0], 0)


def roll_lanes(plane, shift):
    return pltpu.roll(plane, shift % plane.shape[1], 1)


def pack_x(nx, parity, phase, press, vel, *refs):
    count = (len(refs) - 2) // 1
    outs, held, sem = refs[:count], refs[count], refs[count + 1]
    copies = []
    for turn, out in enumerate(outs):
        top = parity[0] == turn
        deep = jnp.where(top, nx - DEPTH, 0)
        less = jnp.where(top, nx - DEPTH + 1, 0)
        last = jnp.where(top, nx - 1, 0)
        parts = [
            (phase.at[pl.ds(deep, DEPTH)], held.at[turn]),
            (vel.at[0, pl.ds(deep, DEPTH)], out.at[pl.ds(DEPTH, DEPTH)]),
            (vel.at[1, pl.ds(less, DEPTH - 1)], out.at[pl.ds(2 * DEPTH, DEPTH - 1)]),
            (vel.at[2, pl.ds(less, DEPTH - 1)], out.at[pl.ds(3 * DEPTH - 1, DEPTH - 1)]),
            (press.at[pl.ds(last, 1)], out.at[pl.ds(4 * DEPTH - 2, 1)]),
        ]
        for which, (src, dst) in enumerate(parts):
            copy = pltpu.make_async_copy(src, dst, sem.at[turn, which])
            copy.start()
            copies.append(copy)
    for copy in copies:
        copy.wait()
    for turn, out in enumerate(outs):
        out[:DEPTH] = coefficient(held[turn])


def halo_planes(nx, even_x, got_x, row, height):
    def load(field, plane):
        above = plane < nx + DEPTH
        layer = plane - nx if above else plane - nx - DEPTH
        if field >= 2:
            layer = layer if above else layer - 1
            if layer < 0 or layer >= DEPTH - 1:
                return jnp.zeros((height, LANES), jnp.float32)
        base = (0, DEPTH, 2 * DEPTH, 3 * DEPTH - 1)[field]
        low, high = sides(even_x, got_x, lambda ref: ref[base + layer, pl.ds(row, height), :])
        return high if above else low

    return load


def pack_y(nx, ny, n_x, parity, phase, press, vel, *refs):
    got_x, outs = refs[:n_x], refs[n_x:]
    even_x = parity[0] == 0
    rows = row_index((ROWS, LANES))
    for turn, out in enumerate(outs):
        top = parity[1] == turn
        row = pl.multiple_of(jnp.where(top, ny - ROWS, 0), ROWS)
        halo = halo_planes(nx, even_x, got_x, row, ROWS)
        for plane in range(nx + 2 * DEPTH):
            if plane < nx:
                fields = [coefficient(phase[plane, pl.ds(row, ROWS), :])]
                fields += [vel[k, plane, pl.ds(row, ROWS), :] for k in range(3)]
            else:
                fields = [halo(f, plane) for f in range(4)]
            for half in range(2):
                one, two = fields[2 * half], fields[2 * half + 1]
                one = jnp.where(top, roll_rows(one, DEPTH), one)
                two = jnp.where(top, two, roll_rows(two, DEPTH))
                out[plane, half * ROWS : (half + 1) * ROWS, :] = jnp.where(rows < DEPTH, one, two)
        for plane in range(nx):
            tile = press[plane, pl.ds(row, ROWS), :]
            edge = jnp.where(top, tile[ROWS - 1 : ROWS], tile[0:1])
            at = nx + 2 * DEPTH + plane // GROUP
            out[at, plane % GROUP : plane % GROUP + 1, :] = edge


def pack_z(nx, ny, n_x, n_y, n_z, parity, phase, press, vel, *refs):
    got_x, got_y = refs[:n_x], refs[n_x : n_x + n_y]
    full, ends, *sends = refs[n_x + n_y :]
    even_x, even_y = parity[0] == 0, parity[1] == 0
    total, height = nx + 2 * DEPTH, ny + 2 * DEPTH
    groups = total // ROWS
    rows = row_index((ROWS, LANES))
    lanes = lane_index((height, LANES))
    halo = halo_planes(nx, even_x, got_x, 0, ny)
    for group in range(groups):
        tops = bottoms = jnp.zeros((height, LANES), jnp.float32)
        for seat in range(ROWS):
            plane = seat * groups + group
            for f in range(4):
                if plane >= nx:
                    own = halo(f, plane)
                elif f == 0:
                    own = coefficient(phase[plane])
                else:
                    own = vel[f - 1, plane]
                half = slice(f // 2 * ROWS, f // 2 * ROWS + ROWS)
                low, high = sides(even_y, got_y, lambda ref: ref[plane, half, :])
                if f % 2 == 0:
                    low = roll_rows(low, DEPTH)
                else:
                    high = roll_rows(high, DEPTH)
                cells = jnp.concatenate([own, jnp.where(rows < DEPTH, high, low)], 0)
                full[f, plane] = cells
                at = GROUP * seat + DEPTH * f
                here = (lanes >= at) & (lanes < at + DEPTH)
                tops = jnp.where(here, roll_lanes(cells, at + DEPTH), tops)
                bottoms = jnp.where(here, roll_lanes(cells, at), bottoms)
        ends[0, group] = tops
        ends[1, group] = bottoms
    tops = bottoms = jnp.zeros((ny, LANES), jnp.float32)
    lanes = lane_index((ny, LANES))
    for plane in range(nx):
        here = lanes == 2 * plane
        tops = jnp.where(here, roll_lanes(press[plane], 2 * plane + 1), tops)
        bottoms = jnp.where(here, roll_lanes(press[plane], 2 * plane), bottoms)
    pad = jnp.zeros((2 * DEPTH, LANES), jnp.float32)
    for turn, send in enumerate(sends):
        top = parity[2] == turn
        send[:groups] = jnp.where(top, ends[0], ends[1])
        send[groups] = jnp.concatenate([jnp.where(top, tops, bottoms), pad], 0)


def tree_sum(parts):
    while len(parts) > 1:
        parts = [parts[i] + parts[i + 1] if i + 1 < len(parts) else parts[i] for i in range(0, len(parts), 2)]
    return parts[0]


class Totals:
    def __init__(self):
        self.stack = []

    def add(self, tile):
        level = 0
        while self.stack and self.stack[-1][0] == level:
            tile = self.stack.pop()[1] + tile
            level += 1
        self.stack.append((level, tile))

    def value(self):
        tiles = [tile for _, tile in self.stack]
        total = tiles.pop()
        while tiles:
            total = tiles.pop() + total
        return total


def krylov(nx, ny, n_z, parity, full, ends, *refs):
    got_z = refs[:n_z]
    basis, basis_z, sums = refs[n_z : n_z + 3]
    wx, wy, wz, inverse, pw, pinv, pv, spill = refs[n_z + 3 :]
    even_z = parity[2] == 0
    total, height = nx + 2 * DEPTH, ny + 2 * DEPTH
    groups = total // ROWS
    lanes = lane_index((height, LANES))
    seat_lane = lanes % GROUP
    at_low, at_high = lanes == 0, lanes == LANES - 1
    edge = at_low | at_high

    def px(planes, group, step):
        if 0 <= group + step < groups:
            return planes[group + step]
        return roll_lanes(planes[(group + step) % groups], -GROUP * step)

    def spilled(which, group, up, down):
        spill[which, group] = jnp.where(seat_lane == 10, roll_lanes(up, 7), down)

    packed = []
    for f in range(4):
        planes = []
        for group in range(groups):
            low, high = sides(even_z, got_z, lambda ref: ref[group])
            parts = (ends[0, group], high, low, ends[1, group])
            cells = parts[3]
            cells = roll_lanes(cells, 3 * DEPTH - DEPTH * f)
            for seat in range(3):
                moved = roll_lanes(parts[seat], DEPTH * (seat - f))
                here = (seat_lane >= DEPTH * seat) & (seat_lane < DEPTH * (seat + 1))
                cells = jnp.where(here, moved, cells)
            planes.append(cells)
        packed.append(planes)
    coef, vx, vy, vz = packed
    for g in range(groups):
        pw[0, g] = 0.5 * (coef[g] + px(coef, g, 1))
        pw[1, g] = 0.5 * (coef[g] + roll_rows(coef[g], -1))
        pw[2, g] = 0.5 * (coef[g] + roll_lanes(coef[g], -1))
    flux = [pw[0, g] * vx[g] for g in range(groups)]
    weight = [pw[0, g] for g in range(groups)]
    for g in range(groups):
        wy_, wz_ = pw[1, g], pw[2, g]
        fy, fz = wy_ * vy[g], wz_ * vz[g]
        spilled(0, g, wz_, wz_)
        spilled(1, g, fz, -fz)
        diag = weight[g] + px(weight, g, -1) + wy_ + roll_rows(wy_, 1) + wz_ + roll_lanes(wz_, 1)
        rhs = flux[g] - px(flux, g, -1) + fy - roll_rows(fy, 1) + fz - roll_lanes(fz, 1)
        scale = jnp.where(coef[g] > 0, 1.0 / jnp.where(coef[g] > 0, diag, 1.0), 0.0)
        pinv[g] = scale
        basis_z[0, g] = scale * rhs
    for n in range(3):
        field = [basis_z[n, g] for g in range(groups)]
        flux = [pw[0, g] * (px(field, g, 1) - field[g]) for g in range(groups)]
        for g in range(groups):
            fy = pw[1, g] * (roll_rows(field[g], -1) - field[g])
            fz = pw[2, g] * (roll_lanes(field[g], -1) - field[g])
            spilled(2 + n, g, -fz, fz)
            if n < 2:
                image = px(flux, g, -1) - flux[g] + roll_rows(fy, 1) - fy + roll_lanes(fz, 1) - fz
                basis_z[n + 1, g] = pinv[g] * image
    for g in range(groups):
        basis_z[3, g] = vz[g]

    def inject(which, plane):
        group, seat = plane % groups, plane // groups
        return jnp.where(edge, roll_lanes(spill[which, group], LANES - 1 - 10 - GROUP * seat), 0.0)

    totals = [Totals() for _ in range(6)]

    def count(which, left, right):
        product = left[:ny] * right[:ny]
        totals[which].add(tree_sum([product[i : i + ROWS] for i in range(0, ny, ROWS)]))

    old_weight = old_flux = None
    for x in range(-DEPTH, nx + DEPTH - 1):
        e = x % total
        here, above = full[0, e], full[0, (e + 1) % total]
        weight = 0.5 * (here + above)
        wx[e] = weight
        flux = weight * full[1, e]
        if x > -DEPTH:
            wy_ = 0.5 * (here + roll_rows(here, -1))
            wz_ = jnp.where(at_high, 0.0, 0.5 * (here + roll_lanes(here, -1)))
            wy[e], wz[e] = wy_, wz_
            fy, fz = wy_ * full[2, e], wz_ * full[3, e]
            diag = weight + old_weight + wy_ + roll_rows(wy_, 1) + wz_ + roll_lanes(wz_, 1) + inject(0, e)
            rhs = flux - old_flux + fy - roll_rows(fy, 1) + fz - roll_lanes(fz, 1) + inject(1, e)
            inside = here > 0
            scale = jnp.where(inside, 1.0 / jnp.where(inside, diag, 1.0), 0.0)
            inverse[e] = scale
            field = scale * rhs
            basis[0, e] = field
            if 0 <= x < nx:
                count(0, field, rhs)
        old_weight, old_flux = weight, flux
    for n in range(3):
        reach = 2 - n
        old_flux = None
        here = basis[n, (-reach - 1) % total]
        for x in range(-reach - 1, nx + reach):
            e = x % total
            above = basis[n, (e + 1) % total]
            flux = wx[e] * (above - here)
            if x >= -reach:
                fy = wy[e] * (roll_rows(here, -1) - here)
                fz = wz[e] * (roll_lanes(here, -1) - here)
                image = old_flux - flux + roll_rows(fy, 1) - fy + roll_lanes(fz, 1) - fz + inject(2 + n, e)
                own = 0 <= x < nx
                if own:
                    count(2 * n + 1, here, image)
                if n < 2:
                    following = inverse[e] * image
                    basis[n + 1, e] = following
                    if own:
                        count(2 * n + 2, following, image)
            old_flux, here = flux, above
    lane = lane_index((1, LANES))
    row = jnp.zeros((1, LANES), jnp.float32)
    for which, total_ in enumerate(totals):
        value = jnp.sum(jnp.sum(total_.value(), 0, keepdims=True), 1, keepdims=True)
        row = jnp.where(lane == which, value, row)
    sums[...] = row


def finish(nx, ny, n_x, n_y, n_z, parity, gathered, press, vel, basis, basis_z, *refs):
    got_x, got_y, got_z = refs[:n_x], refs[n_x : n_x + n_y], refs[n_x + n_y : n_x + n_y + n_z]
    ustar, coef_cot = refs[n_x + n_y + n_z :]
    even_x, even_y, even_z = parity[0] == 0, parity[1] == 0, parity[2] == 0
    total, height = nx + 2 * DEPTH, ny + 2 * DEPTH
    groups = total // ROWS
    parts = gathered[...]
    while parts.shape[0] > ROWS:
        half = parts.shape[0] // 2
        parts = parts[:half] + parts[half:]
    sums = jnp.sum(parts, 0, keepdims=True)
    lane = lane_index((1, LANES))
    m0, m1, m2, m3, m4, m5 = [
        jnp.sum(jnp.where(lane == which, sums, 0.0), 1, keepdims=True) for which in range(6)
    ]
    l1, l2 = m2 / m1, m3 / m1
    d1, cross, d2 = m3 - l1 * m2, m4 - l1 * m3, m5 - l2 * m3
    l21 = cross / d1
    d2 = d2 - l21 * cross
    y1 = -l1 * m0 + m1
    y2 = m2 - l2 * m0 - l21 * y1
    c2 = y2 / d2
    c1 = y1 / d1 - l21 * c2
    c0 = m0 / m1 - l1 * c1 - l2 * c2

    lanes = lane_index((height, LANES))
    seat_lane = lanes % GROUP
    spill = []
    for g in range(groups):
        cells = c0 * basis_z[0, g] + c1 * basis_z[1, g] + c2 * basis_z[2, g]
        spill.append(jnp.where(seat_lane == 10, roll_lanes(cells, 6), cells))
    lanes = lane_index((ny, LANES))
    at_low, at_high = lanes == 0, lanes == LANES - 1
    low_z, high_z = sides(even_z, got_z, lambda ref: ref[groups, :ny, :])
    press_z = jnp.where(lanes % 2 == 0, high_z, roll_lanes(low_z, 1))
    p_base, layer = 4 * DEPTH - 2, 2 * DEPTH - 1
    p_low, p_high = sides(even_x, got_x, lambda ref: ref[p_base])
    u_low, _ = sides(even_x, got_x, lambda ref: ref[layer])

    def solved(x):
        e = x % total
        return c0 * basis[0, e] + c1 * basis[1, e] + c2 * basis[2, e]

    rows = row_index((ROWS, LANES))
    below, here = solved(-1), solved(0)
    face_low = (p_low - press[0]) * (u_low + here[:ny] - below[:ny])
    for x in range(nx):
        above = solved(x + 1)
        group, seat = x % groups, x // groups
        own, p = here[:ny], press[x]
        out = vel[0, x] + (above[:ny] - own)
        ustar[0, x] = out
        face = (p - (press[x + 1] if x + 1 < nx else p_high)) * out
        answer = face_low + face
        face_low = face
        low, high = sides(even_y, got_y, lambda ref: ref[nx + 2 * DEPTH + x // GROUP, x % GROUP : x % GROUP + 1, :])
        shape = (ROWS, LANES)
        p_tile = jnp.where(rows == 0, jnp.broadcast_to(high, shape), jnp.broadcast_to(low, shape))
        p_tall = jnp.concatenate([p, p_tile], 0)
        u_row, _ = sides(even_y, got_y, lambda ref: ref[x, 3 * DEPTH - 1 : 3 * DEPTH, :])
        u_tall = jnp.concatenate([vel[1, x], jnp.broadcast_to(u_row, shape)], 0)
        out = u_tall + (roll_rows(here, -1) - here)
        ustar[1, x] = out[:ny]
        face = (p_tall - roll_rows(p_tall, -1)) * out
        answer = answer + (face + roll_rows(face, 1))[:ny]
        shift = LANES - 1 - 10 - GROUP * seat
        lam_end = roll_lanes(spill[group][:ny], shift)
        u_end = roll_lanes(basis_z[3, group, :ny, :], shift)
        p_end = roll_lanes(press_z, LANES - 1 - 2 * x)
        out = vel[2, x] + (jnp.where(at_high, lam_end, roll_lanes(own, -1)) - own)
        ustar[2, x] = out
        face = (p - jnp.where(at_high, p_end, roll_lanes(p, -1))) * out
        first = (p_end - p) * (u_end + own - lam_end)
        answer = answer + face + jnp.where(at_low, first, roll_lanes(face, 1))
        coef_cot[x] = 0.5 * answer
        here = above


def on_device(phase, press, vel):
    nx, ny, nz = phase.shape
    total, height = nx + 2 * DEPTH, ny + 2 * DEPTH
    groups = total // ROWS
    devices = lax.axis_size(AXES)
    n_x, n_y, n_z = (turns(axis) for axis in AXES)
    f32 = lambda *shape: jax.ShapeDtypeStruct(shape, jnp.float32)
    parity = jnp.stack([lax.axis_index(axis) % 2 for axis in AXES]).astype(jnp.int32)
    scratch = lambda *shape: pltpu.VMEM(shape, jnp.float32)

    send = pl.pallas_call(
        functools.partial(pack_x, nx),
        out_shape=[f32(4 * DEPTH - 1, ny, nz)] * n_x,
        in_specs=[SMEM, ANY, ANY, ANY],
        out_specs=[VMEM] * n_x,
        scratch_shapes=[pltpu.VMEM((n_x, DEPTH, ny, nz), jnp.int32), pltpu.SemaphoreType.DMA((n_x, 5))],
        compiler_params=PARAMS,
        name="pack_x",
    )(parity, phase, press, vel)
    got_x = exchange(send, "gx")
    send = pl.pallas_call(
        functools.partial(pack_y, nx, ny, n_x),
        out_shape=[f32(total + -(-nx // GROUP), GROUP, nz)] * n_y,
        in_specs=[SMEM] + [VMEM] * (3 + n_x),
        out_specs=[VMEM] * n_y,
        compiler_params=PARAMS,
        name="pack_y",
    )(parity, phase, press, vel, *got_x)
    got_y = exchange(send, "gy")
    full, ends, *send = pl.pallas_call(
        functools.partial(pack_z, nx, ny, n_x, n_y, n_z),
        out_shape=[f32(4, total, height, nz), f32(2, groups, height, LANES)] + [f32(groups + 1, height, LANES)] * n_z,
        in_specs=[SMEM] + [VMEM] * (3 + n_x + n_y),
        out_specs=[VMEM] * (2 + n_z),
        compiler_params=PARAMS,
        name="pack_z",
    )(parity, phase, press, vel, *got_x, *got_y)
    got_z = exchange(send, "gz")
    basis, basis_z, sums = pl.pallas_call(
        functools.partial(krylov, nx, ny, n_z),
        out_shape=[f32(3, total, height, nz), f32(4, groups, height, LANES), f32(1, LANES)],
        in_specs=[SMEM] + [VMEM] * (2 + n_z),
        out_specs=[VMEM] * 3,
        scratch_shapes=[scratch(total, height, nz)] * 4
        + [scratch(3, groups, height, LANES), scratch(groups, height, LANES), scratch(groups, height, LANES)]
        + [scratch(5, groups, height, LANES)],
        compiler_params=PARAMS,
        name="krylov",
    )(parity, full, ends, *got_z)
    spread = jnp.broadcast_to(sums[None], (devices, 1, LANES))
    gathered = lax.all_to_all(spread, AXES, 0, 0).reshape(devices, LANES)
    return pl.pallas_call(
        functools.partial(finish, nx, ny, n_x, n_y, n_z),
        out_shape=[f32(*vel.shape), f32(nx, ny, nz)],
        in_specs=[SMEM] + [VMEM] * (5 + n_x + n_y + n_z),
        out_specs=[VMEM] * 2,
        compiler_params=PARAMS,
        name="finish",
    )(parity, gathered, press, vel, basis, basis_z, *got_x, *got_y, *got_z)


def solution(mesh):
    cells, faces = P(*AXES), P(None, *AXES)
    return jax.shard_map(
        on_device, mesh=mesh, in_specs=(cells, cells, faces), out_specs=(faces, cells), check_vma=False
    )
```

time: 306 us -> 53.4 us (0.17)
  blocking collectives: 129 us -> 21 us
  starting transfers between devices: 78.1 us -> 6.38 us
  waiting for transfers between devices: 52 us -> 8.65 us
  other arithmetic: 22.8 us -> 0.08 us
  Pallas kernels: 0 us -> 13.3 us
  between operations: 10.4 us -> 0.73 us
  local copies, waits for them, and re-layouts: 11.8 us -> 3.06 us
    psum x3 -> x0, blocking collectives: 129 us -> none  [paired_sums(): lax.psum((jnp.sum(resid * precd), jnp.sum(precd * image)), ('gx', 'gy', '...]
    ppermute x30 -> x5, starting transfers between devices: 78.1 us -> 6.38 us  [exchange(): lax.ppermute(send, axis, swaps(count, turn))]
    ppermute x30 -> x5, waiting for transfers between devices: 52 us -> 8.65 us  [exchange(): lax.ppermute(send, axis, swaps(count, turn))]
    all_to_all x0 -> x1, blocking collectives: none -> 21 us  [on_device(): gathered = lax.all_to_all(spread, AXES, 0, 0).reshape(devices, LANES)]
    pallas_call x0 -> x5, Pallas kernels: none -> 13.3 us  [the longest x1 7.2 us: on_device(): pl.pallas_call(functools.partial(krylov, nx, ny, n_z), out_shape=[f32(3,...]
    mul x19 -> x0, other arithmetic: 9.8 us -> none  [the longest x3 3.71 us: on_device(): -press_grads[dim_idx] * (vel_faces[dim_idx] + lam_grads[dim_idx])]
    concatenate x10 -> x0, other arithmetic: 6.03 us -> none  [extended(): jnp.concatenate([lax.ppermute(tail, axis, [(i, (i + 1) % count) for i in...]
    slice x10 -> x0, local copies, waits for them, and re-layouts: 3.87 us -> none  [the longest x5 1.85 us: extended(): lax.slice_in_dim(cells, cells.shape[dim] - width, cells.shape[dim], axis=...]
  transfers between devices with their start and end apart: 30 -> 5, of which waited for: 19 -> 3; matrix products, arithmetic and copies ran while one was open for 2% -> 0% of each run, Pallas kernels for 0% -> 0%
where the time goes in v1:
time: 53.4 us; the launch traced here: 53.1 us
  blocking collectives  21 us (39%)
  Pallas kernels  13.3 us (25%)
  waiting for transfers between devices  8.65 us (16%)
  starting transfers between devices  6.38 us (12%)
  local copies, waits for them, and re-layouts  3.06 us (6%)
  between operations  0.73 us (1%)
    all_to_all x1, blocking collectives, on_device(): gathered = lax.all_to_all(spread, AXES, 0, 0).reshape(devices, LANES)  21 us
    ppermute x5, waiting for transfers between devices, exchange(): lax.ppermute(send, axis, swaps(count, turn))  8.65 us
    pallas_call x1, Pallas kernels, on_device(): pl.pallas_call(functools.partial(krylov, nx, ny, n_z), out_shape=[f32(3,...  7.2 us
    ppermute x5, starting transfers between devices, exchange(): lax.ppermute(send, axis, swaps(count, turn))  6.38 us
    unnamed x10, local copies, waits for them, and re-layouts  3.05 us
    pallas_call x1, Pallas kernels, on_device(): pl.pallas_call(functools.partial(finish, nx, ny, n_x, n_y, n_z), out_shap...  2.42 us
    pallas_call x1, Pallas kernels, on_device(): pl.pallas_call(functools.partial(pack_z, nx, ny, n_x, n_y, n_z), out_shap...  1.68 us
    pallas_call x1, Pallas kernels, on_device(): pl.pallas_call(functools.partial(pack_x, nx), out_shape=[f32(4 * DEPTH -...  1.31 us
  transfers between devices with their start and end apart: 5, of which 3 were waited for; matrix products, arithmetic and copies ran while one was open for 0% of the time, Pallas kernels for 0%

profile of v1, /device:TPU:0, one launch (start us, length us, event | category | flops | bytes accessed | tf_op | source)
XLA Modules:
  0.0 53.1 jit_solution(6418467324316474994)
XLA Ops:
  0.7 0.1 pad_add_fusion.parity
  0.7 1.1 %copy-done = f32[3,16,32,128]{3,2,1,0:T(8,128)S(1)} copy-done((f32[3,16,32,128]{3,2,1,0:T(8,128)S(1)}, f32[3,16,32,128]{3,2,1,0:T(8,128)}, u32[]{:S(2)}) %copy-start) | copy-done | bytes 786456
  1.9 0.9 %copy-done.2 = f32[16,32,128]{2,1,0:T(8,128)S(1)} copy-done((f32[16,32,128]{2,1,0:T(8,128)S(1)}, f32[16,32,128]{2,1,0:T(8,128)}, u32[]{:S(2)}) %copy-start.2) | copy-done | bytes 262168
  2.8 0.9 %copy-done.4 = s32[16,32,128]{2,1,0:T(8,128)S(1)} copy-done((s32[16,32,128]{2,1,0:T(8,128)S(1)}, s32[16,32,128]{2,1,0:T(8,128)}, u32[]{:S(2)}) %copy-start.4) | copy-done | bytes 262168
  3.8 1.3 %pack_x.1 = (f32[15,32,128]{2,1,0:T(8,128)S(1)}, f32[15,32,128]{2,1,0:T(8,128)S(1)}) custom-call(s32[3]{0:T(128)S(1)} %pad_add_fusion.parity, s32[16,32,128]{2,1,0:T(8,128)S(1)} %copy-done.4, f32[16,32,128]{2,1,0:T(8,128)S(1)} %copy-done.2, f32[3,16,32,128]{3,2,1,0:T(8,128)S(1)} %copy-done), custom_call_target="tpu_custom_call" | custom-call | tf_op jit(solution)/shard_map/pack_x/pallas_call | solution.py:415
  5.1 3.1 %collective-permute-start = (f32[15,32,128]{2,1,0:T(8,128)S(1)}, f32[15,32,128]{2,1,0:T(8,128)S(1)}, u32[]{:S(2)}, u32[]{:S(2)}) collective-permute-start(f32[15,32,128]{2,1,0:T(8,128)S(1)} %get-tuple-element.12), channel_id=1, source_target_pairs={{0,8},{8,0},{16,24},{24,16},{1,9},{9,1},{17,25},{25,17},{2,10},{10... | collective-permute-start | bytes 737288 | tf_op jit(solution)/shard_map/ppermute | solution.py:30
  8.2 0.7 %collective-permute-start.1 = (f32[15,32,128]{2,1,0:T(8,128)S(1)}, f32[15,32,128]{2,1,0:T(8,128)S(1)}, u32[]{:S(2)}, u32[]{:S(2)}) collective-permute-start(f32[15,32,128]{2,1,0:T(8,128)S(1)} %get-tuple-element.13), channel_id=1, source_target_pairs={{8,16},{16,8},{9,17},{17,9},{10,18},{18,10},{11,19},{19,11},{12,20... | collective-permute-start | bytes 737288 | tf_op jit(solution)/shard_map/ppermute | solution.py:30
  8.8 5.3 %collective-permute-done.refs_0_ = f32[15,32,128]{2,1,0:T(8,128)S(1)} collective-permute-done((f32[15,32,128]{2,1,0:T(8,128)S(1)}, f32[15,32,128]{2,1,0:T(8,128)S(1)}, u32[]{:S(2)}, u32[]{:S(2)}) %collective-permute-start) | collective-permute-done | bytes 245792 | tf_op jit(solution)/shard_map/ppermute | solution.py:30
  14.1 0.0 collective-permute-done.1.refs_1_
  14.1 0.7 %pack_y.1 = (f32[25,16,128]{2,1,0:T(8,128)S(1)}, f32[25,16,128]{2,1,0:T(8,128)S(1)}) custom-call(s32[3]{0:T(128)S(1)} %pad_add_fusion.parity, s32[16,32,128]{2,1,0:T(8,128)S(1)} %copy-done.4, f32[16,32,128]{2,1,0:T(8,128)S(1)} %copy-done.2, f32[3,16,32,128]{3,2,1,0:T(8,128)S(1)} %copy-done, f32[15,32,128]{2,1,0:T(8,128)S(1)} %collective-permute-done.refs_0_, ...), custom_call_target="tpu_custom_call" | custom-call | tf_op jit(solution)/shard_map/pack_y/pallas_call | solution.py:425
  14.8 0.1 collective-permute-start.2
  14.9 0.0 copy-start.1
  14.9 0.0 copy-start.3
  14.9 0.8 %collective-permute-start.3 = (f32[25,16,128]{2,1,0:T(8,128)S(1)}, f32[25,16,128]{2,1,0:T(8,128)S(1)}, u32[]{:S(2)}, u32[]{:S(2)}) collective-permute-start(f32[25,16,128]{2,1,0:T(8,128)S(1)} %get-tuple-element.15), channel_id=1, source_target_pairs={{2,4},{4,2},{3,5},{5,3},{10,12},{12,10},{11,13},{13,11},{18,20},{2... | collective-permute-start | bytes 614408 | tf_op jit(solution)/shard_map/ppermute | solution.py:30
  15.7 0.6 %collective-permute-done.2.refs_2_ = f32[25,16,128]{2,1,0:T(8,128)S(1)} collective-permute-done((f32[25,16,128]{2,1,0:T(8,128)S(1)}, f32[25,16,128]{2,1,0:T(8,128)S(1)}, u32[]{:S(2)}, u32[]{:S(2)}) %collective-permute-start.2) | collective-permute-done | bytes 204832 | tf_op jit(solution)/shard_map/ppermute | solution.py:30
  16.3 0.0 collective-permute-done.3.refs_3_
  16.3 1.7 %pack_z.1 = (f32[4,24,40,128]{3,2,1,0:T(8,128)S(1)}, f32[2,3,40,128]{3,2,1,0:T(8,128)S(1)}, f32[4,40,128]{2,1,0:T(8,128)S(1)}) custom-call(s32[3]{0:T(128)S(1)} %pad_add_fusion.parity, s32[16,32,128]{2,1,0:T(8,128)S(1)} %copy-done.4, f32[16,32,128]{2,1,0:T(8,128)S(1)} %copy-done.2, f32[3,16,32,128]{3,2,1,0:T(8,128)S(1)} %copy-done, ...), custom_call_target="tpu_custom_call" | custom-call | tf_op jit(solution)/shard_map/pack_z/pallas_call | solution.py:434
  18.0 1.7 %collective-permute-start.4 = (f32[4,40,128]{2,1,0:T(8,128)S(1)}, f32[4,40,128]{2,1,0:T(8,128)S(1)}, u32[]{:S(2)}, u32[]{:S(2)}) collective-permute-start(f32[4,40,128]{2,1,0:T(8,128)S(1)} %get-tuple-element.18), channel_id=1, source_target_pairs={{0,1},{1,0},{2,3},{3,2},{4,5},{5,4},{6,7},{7,6},{8,9},{9,8},{10,11... | collective-permute-start | bytes 245768 | tf_op jit(solution)/shard_map/ppermute | solution.py:30
  19.8 2.8 %collective-permute-done.4.refs_0_.refs_4_ = f32[4,40,128]{2,1,0:T(8,128)S(1)} collective-permute-done((f32[4,40,128]{2,1,0:T(8,128)S(1)}, f32[4,40,128]{2,1,0:T(8,128)S(1)}, u32[]{:S(2)}, u32[]{:S(2)}) %collective-permute-start.4) | collective-permute-done | bytes 81952 | tf_op jit(solution)/shard_map/ppermute | solution.py:30
  22.5 7.2 %krylov.1 = (f32[3,24,40,128]{3,2,1,0:T(8,128)S(1)}, f32[4,3,40,128]{3,2,1,0:T(8,128)S(1)}, f32[1,128]{1,0:T(1,128)S(1)}) custom-call(s32[3]{0:T(128)S(1)} %pad_add_fusion.parity, f32[4,24,40,128]{3,2,1,0:T(8,128)S(1)} %get-tuple-element.16.full, f32[2,3,40,128]{3,2,1,0:T(8,128)S(1)} %get-tuple-element.17.ends, ...), custom_call_target="tpu_custom_call" | custom-call | tf_op jit(solution)/shard_map/krylov/pallas_call | solution.py:443
  29.7 21.0 %all_to_all.5 = f32[32,1,128]{2,1,0:T(1,128)S(1)} all-to-all(f32[32,1,128]{2,1,0:T(1,128)S(1)} %broadcast_in_dim.9), channel_id=1, replica_groups=mesh['gx'=4,'gy'=4,'gz'=2] {'gx','gy','gz'}, dimensions={0} | all-to-all | bytes 32768 | tf_op jit(solution)/shard_map/all_to_all | solution.py:455
  50.7 0.0 copy-done.1
  50.7 0.0 copy-done.3
  50.7 2.4 %finish.1 = (f32[3,16,32,128]{3,2,1,0:T(8,128)}, f32[16,32,128]{2,1,0:T(8,128)}) custom-call(s32[3]{0:T(128)S(1)} %pad_add_fusion.parity, f32[32,128]{1,0:T(8,128)S(1)} %bitcast.5, f32[16,32,128]{2,1,0:T(8,128)S(1)} %copy-done.3, f32[3,16,32,128]{3,2,1,0:T(8,128)S(1)} %copy-done.1, f32[3,24,40,128]{3,2,1,0:T(8,128)S(1)} %get-tuple-element.20.basis, ...), custom_call_target="tpu_custom_call" | custom-call | tf_op jit(solution)/shard_map/finish/pallas_call | solution.py:456
  (4 shorter events, 0.0 us)
Async XLA Ops:
  0.7 1.1 %copy-start = (f32[3,16,32,128]{3,2,1,0:T(8,128)S(1)}, f32[3,16,32,128]{3,2,1,0:T(8,128)}, u32[]{:S(2)}) copy-start(f32[3,16,32,128]{3,2,1,0:T(8,128)} %vel.7) | copy-start | bytes 2359300
  1.9 0.9 %copy-start.2 = (f32[16,32,128]{2,1,0:T(8,128)S(1)}, f32[16,32,128]{2,1,0:T(8,128)}, u32[]{:S(2)}) copy-start(f32[16,32,128]{2,1,0:T(8,128)} %press.7) | copy-start | bytes 786436
  2.8 0.9 %copy-start.4 = (s32[16,32,128]{2,1,0:T(8,128)S(1)}, s32[16,32,128]{2,1,0:T(8,128)}, u32[]{:S(2)}) copy-start(s32[16,32,128]{2,1,0:T(8,128)} %phase.5) | copy-start | bytes 786436
  5.1 9.0 %collective-permute-start = (f32[15,32,128]{2,1,0:T(8,128)S(1)}, f32[15,32,128]{2,1,0:T(8,128)S(1)}, u32[]{:S(2)}, u32[]{:S(2)}) collective-permute-start(f32[15,32,128]{2,1,0:T(8,128)S(1)} %get-tuple-element.12), channel_id=1, source_target_pairs={{0,8},{8,0},{16,24},{24,16},{1,9},{9,1},{17,25},{25,17},{2,10},{10... | collective-permute-start | bytes 737288 | tf_op jit(solution)/shard_map/ppermute | solution.py:30
  8.2 6.0 %collective-permute-start.1 = (f32[15,32,128]{2,1,0:T(8,128)S(1)}, f32[15,32,128]{2,1,0:T(8,128)S(1)}, u32[]{:S(2)}, u32[]{:S(2)}) collective-permute-start(f32[15,32,128]{2,1,0:T(8,128)S(1)} %get-tuple-element.13), channel_id=1, source_target_pairs={{8,16},{16,8},{9,17},{17,9},{10,18},{18,10},{11,19},{19,11},{12,20... | collective-permute-start | bytes 737288 | tf_op jit(solution)/shard_map/ppermute | solution.py:30
  14.8 1.5 %collective-permute-start.2 = (f32[25,16,128]{2,1,0:T(8,128)S(1)}, f32[25,16,128]{2,1,0:T(8,128)S(1)}, u32[]{:S(2)}, u32[]{:S(2)}) collective-permute-start(f32[25,16,128]{2,1,0:T(8,128)S(1)} %get-tuple-element.14), channel_id=1, source_target_pairs={{0,2},{2,0},{4,6},{6,4},{1,3},{3,1},{5,7},{7,5},{8,10},{10,8},{12,... | collective-permute-start | bytes 614408 | tf_op jit(solution)/shard_map/ppermute | solution.py:30
  14.9 35.8 %copy-start.1 = (f32[3,16,32,128]{3,2,1,0:T(8,128)S(1)}, f32[3,16,32,128]{3,2,1,0:T(8,128)}, u32[]{:S(2)}) copy-start(f32[3,16,32,128]{3,2,1,0:T(8,128)} %vel.7) | copy-start | bytes 2359300
  14.9 35.8 %copy-start.3 = (f32[16,32,128]{2,1,0:T(8,128)S(1)}, f32[16,32,128]{2,1,0:T(8,128)}, u32[]{:S(2)}) copy-start(f32[16,32,128]{2,1,0:T(8,128)} %press.7) | copy-start | bytes 786436
  14.9 1.4 %collective-permute-start.3 = (f32[25,16,128]{2,1,0:T(8,128)S(1)}, f32[25,16,128]{2,1,0:T(8,128)S(1)}, u32[]{:S(2)}, u32[]{:S(2)}) collective-permute-start(f32[25,16,128]{2,1,0:T(8,128)S(1)} %get-tuple-element.15), channel_id=1, source_target_pairs={{2,4},{4,2},{3,5},{5,3},{10,12},{12,10},{11,13},{13,11},{18,20},{2... | collective-permute-start | bytes 614408 | tf_op jit(solution)/shard_map/ppermute | solution.py:30
  18.0 4.5 %collective-permute-start.4 = (f32[4,40,128]{2,1,0:T(8,128)S(1)}, f32[4,40,128]{2,1,0:T(8,128)S(1)}, u32[]{:S(2)}, u32[]{:S(2)}) collective-permute-start(f32[4,40,128]{2,1,0:T(8,128)S(1)} %get-tuple-element.18), channel_id=1, source_target_pairs={{0,1},{1,0},{2,3},{3,2},{4,5},{5,4},{6,7},{7,6},{8,9},{9,8},{10,11... | collective-permute-start | bytes 245768 | tf_op jit(solution)/shard_map/ppermute | solution.py:30

commit v2 on v1

v2 whole, which is shorter than its diff:
```python
import functools

import jax
import jax.numpy as jnp
from jax import lax
from jax.experimental import pallas as pl
from jax.experimental.pallas import tpu as pltpu
from jax.sharding import PartitionSpec as P

AXES = ("gx", "gy", "gz")
DEPTH = 4
GROUP = 4 * DEPTH
LANES = 128
ROWS = 8
VMEM = pl.BlockSpec(memory_space=pltpu.VMEM)
SMEM = pl.BlockSpec(memory_space=pltpu.SMEM)
HBM = pl.BlockSpec(memory_space=pltpu.HBM)
ANY = pl.BlockSpec(memory_space=pl.ANY)
PARAMS = pltpu.CompilerParams(vmem_limit_bytes=40 * 1024 * 1024)


def swaps(count, first):
    pairs = []
    for i in range(first, count - 1, 2):
        pairs += [(i, i + 1), (i + 1, i)]
    return pairs


def exchange(sends, axis):
    count = lax.axis_size(axis)
    return [lax.ppermute(send, axis, swaps(count, turn)) for turn, send in enumerate(sends)]


def turns(axis):
    return min(2, lax.axis_size(axis) - 1)


def coefficient(phase):
    return jnp.where(phase == 0, 8.0, jnp.where(phase == 1, 1.0, 2.0)).astype(jnp.float32)


def sides(even, got, load):
    one = load(got[0])
    two = load(got[1]) if len(got) > 1 else jnp.zeros_like(one)
    return jnp.where(even, two, one), jnp.where(even, one, two)


def lane_index(shape):
    return lax.broadcasted_iota(jnp.int32, shape, len(shape) - 1)


def row_index(shape):
    return lax.broadcasted_iota(jnp.int32, shape, len(shape) - 2)


def roll_rows(plane, shift):
    return pltpu.roll(plane, shift % plane.shape[0], 0)


def roll_lanes(plane, shift):
    return pltpu.roll(plane, shift % plane.shape[1], 1)


def pack_x(nx, parity, phase, press, vel, *refs):
    count = (len(refs) - 2) // 1
    outs, held, sem = refs[:count], refs[count], refs[count + 1]
    copies = []
    for turn, out in enumerate(outs):
        top = parity[0] == turn
        deep = jnp.where(top, nx - DEPTH, 0)
        less = jnp.where(top, nx - DEPTH + 1, 0)
        last = jnp.where(top, nx - 1, 0)
        parts = [
            (phase.at[pl.ds(deep, DEPTH)], held.at[turn]),
            (vel.at[0, pl.ds(deep, DEPTH)], out.at[pl.ds(DEPTH, DEPTH)]),
            (vel.at[1, pl.ds(less, DEPTH - 1)], out.at[pl.ds(2 * DEPTH, DEPTH - 1)]),
            (vel.at[2, pl.ds(less, DEPTH - 1)], out.at[pl.ds(3 * DEPTH - 1, DEPTH - 1)]),
            (press.at[pl.ds(last, 1)], out.at[pl.ds(4 * DEPTH - 2, 1)]),
        ]
        for which, (src, dst) in enumerate(parts):
            copy = pltpu.make_async_copy(src, dst, sem.at[turn, which])
            copy.start()
            copies.append(copy)
    for copy in copies:
        copy.wait()
    for turn, out in enumerate(outs):
        out[:DEPTH] = coefficient(held[turn])


def load(phase, press, vel, after, coef, press_out, vel_out, held, sem):
    del after
    copies = []
    for which, (src, dst) in enumerate(((phase, held), (press, press_out), (vel, vel_out))):
        copies.append(pltpu.make_async_copy(src, dst, sem.at[which]))
        copies[-1].start()
    copies[0].wait()
    for plane in range(coef.shape[0]):
        coef[plane] = coefficient(held[plane])
    copies[1].wait()
    copies[2].wait()


def halo_planes(nx, even_x, got_x, row, height):
    def load(field, plane):
        above = plane < nx + DEPTH
        layer = plane - nx if above else plane - nx - DEPTH
        if field >= 2:
            layer = layer if above else layer - 1
            if layer < 0 or layer >= DEPTH - 1:
                return jnp.zeros((height, LANES), jnp.float32)
        base = (0, DEPTH, 2 * DEPTH, 3 * DEPTH - 1)[field]
        low, high = sides(even_x, got_x, lambda ref: ref[base + layer, pl.ds(row, height), :])
        return high if above else low

    return load


def pack_y(nx, ny, n_x, parity, coef, press, vel, *refs):
    got_x, outs = refs[:n_x], refs[n_x:]
    even_x = parity[0] == 0
    rows = row_index((ROWS, LANES))
    for turn, out in enumerate(outs):
        top = parity[1] == turn
        row = pl.multiple_of(jnp.where(top, ny - ROWS, 0), ROWS)
        halo = halo_planes(nx, even_x, got_x, row, ROWS)
        for plane in range(nx + 2 * DEPTH):
            if plane < nx:
                fields = [coef[plane, pl.ds(row, ROWS), :]]
                fields += [vel[k, plane, pl.ds(row, ROWS), :] for k in range(3)]
            else:
                fields = [halo(f, plane) for f in range(4)]
            for half in range(2):
                one, two = fields[2 * half], fields[2 * half + 1]
                one = jnp.where(top, roll_rows(one, DEPTH), one)
                two = jnp.where(top, two, roll_rows(two, DEPTH))
                out[plane, half * ROWS : (half + 1) * ROWS, :] = jnp.where(rows < DEPTH, one, two)
        for plane in range(nx):
            tile = press[plane, pl.ds(row, ROWS), :]
            edge = jnp.where(top, tile[ROWS - 1 : ROWS], tile[0:1])
            at = nx + 2 * DEPTH + plane // GROUP
            out[at, plane % GROUP : plane % GROUP + 1, :] = edge


def tall_planes(nx, ny, parity, coef, vel, got_x, got_y):
    even_x, even_y = parity[0] == 0, parity[1] == 0
    rows = row_index((ROWS, LANES))
    halo = halo_planes(nx, even_x, got_x, 0, ny)

    def cells(field, plane):
        if plane >= nx:
            own = halo(field, plane)
        elif field == 0:
            own = coef[plane]
        else:
            own = vel[field - 1, plane]
        half = slice(field // 2 * ROWS, field // 2 * ROWS + ROWS)
        low, high = sides(even_y, got_y, lambda ref: ref[plane, half, :])
        if field % 2 == 0:
            low = roll_rows(low, DEPTH)
        else:
            high = roll_rows(high, DEPTH)
        return jnp.concatenate([own, jnp.where(rows < DEPTH, high, low)], 0)

    return cells


def pack_z(nx, ny, n_x, n_y, parity, coef, press, vel, *refs):
    got_x, got_y, sends = refs[:n_x], refs[n_x : n_x + n_y], refs[n_x + n_y :]
    groups = (nx + 2 * DEPTH) // ROWS
    lanes = lane_index((ny + 2 * DEPTH, LANES))
    cells = tall_planes(nx, ny, parity, coef, vel, got_x, got_y)
    low_lanes = lane_index((ny, LANES))
    pad = jnp.zeros((2 * DEPTH, LANES), jnp.float32)
    for turn, send in enumerate(sends):
        top = parity[2] == turn
        for group in range(groups):
            parts = jnp.zeros((ny + 2 * DEPTH, LANES), jnp.float32)
            for seat in range(ROWS):
                for f in range(4):
                    at = GROUP * seat + DEPTH * f
                    here = (lanes >= at) & (lanes < at + DEPTH)
                    shift = jnp.where(top, (at + DEPTH) % LANES, at)
                    parts = jnp.where(here, pltpu.roll(cells(f, seat * groups + group), shift, 1), parts)
            send[group] = parts
        parts = jnp.zeros((ny, LANES), jnp.float32)
        for plane in range(nx):
            shift = jnp.where(top, 2 * plane + 1, 2 * plane)
            parts = jnp.where(low_lanes == 2 * plane, pltpu.roll(press[plane], shift, 1), parts)
        send[groups] = jnp.concatenate([parts, pad], 0)


def prepare(nx, ny, n_x, n_y, parity, coef, vel, after, *refs):
    del after
    got_x, got_y = refs[:n_x], refs[n_x : n_x + n_y]
    wx, wy, wz, diag_out, rhs_out, ends = refs[n_x + n_y :]
    total, height = nx + 2 * DEPTH, ny + 2 * DEPTH
    groups = total // ROWS
    lanes = lane_index((height, LANES))
    cells = tall_planes(nx, ny, parity, coef, vel, got_x, got_y)
    for group in range(groups):
        tops = bottoms = jnp.zeros((height, LANES), jnp.float32)
        for seat in range(ROWS):
            for f in range(4):
                plane = cells(f, seat * groups + group)
                at = GROUP * seat + DEPTH * f
                here = (lanes >= at) & (lanes < at + DEPTH)
                tops = jnp.where(here, roll_lanes(plane, at + DEPTH), tops)
                bottoms = jnp.where(here, roll_lanes(plane, at), bottoms)
        ends[0, group] = tops
        ends[1, group] = bottoms
    old_weight = old_flux = None
    here = cells(0, nx + DEPTH)
    for x in range(-DEPTH, nx + DEPTH - 1):
        e = x % total
        above = cells(0, (e + 1) % total)
        weight = 0.5 * (here + above)
        wx[e] = weight
        flux = weight * cells(1, e)
        if x > -DEPTH:
            vy, vz = cells(2, e), cells(3, e)
            up, down = 0.5 * (here + roll_rows(here, -1)), 0.5 * (here + roll_rows(here, 1))
            right = jnp.where(lanes == LANES - 1, 0.0, 0.5 * (here + roll_lanes(here, -1)))
            left = jnp.where(lanes == 0, 0.0, 0.5 * (here + roll_lanes(here, 1)))
            wy[0, e], wy[1, e], wz[0, e], wz[1, e] = up, down, right, left
            diag = (weight + old_weight) + (up + down) + (right + left)
            diag_out[e] = jnp.where(here > 0, diag, 0.0)
            rhs_out[e] = (
                (flux - old_flux) + (up * vy - down * roll_rows(vy, 1)) + (right * vz - left * roll_lanes(vz, 1))
            )
        old_weight, old_flux, here = weight, flux, above


def tree_sum(parts):
    while len(parts) > 1:
        parts = [parts[i] + parts[i + 1] if i + 1 < len(parts) else parts[i] for i in range(0, len(parts), 2)]
    return parts[0]


class Totals:
    def __init__(self):
        self.stack = []

    def add(self, tile):
        level = 0
        while self.stack and self.stack[-1][0] == level:
            tile = self.stack.pop()[1] + tile
            level += 1
        self.stack.append((level, tile))

    def value(self):
        tiles = [tile for _, tile in self.stack]
        total = tiles.pop()
        while tiles:
            total = tiles.pop() + total
        return total


def krylov(nx, ny, n_z, parity, wx, wy, wz, diag_in, rhs_in, ends, *refs):
    got_z = refs[:n_z]
    basis, basis_z, sums = refs[n_z : n_z + 3]
    inverse, pw, pinv, spill = refs[n_z + 3 :]
    even_z = parity[2] == 0
    total, height = nx + 2 * DEPTH, ny + 2 * DEPTH
    groups = total // ROWS
    lanes = lane_index((height, LANES))
    seat_lane = lanes % GROUP
    edge = (lanes == 0) | (lanes == LANES - 1)

    def along(planes, group, step):
        if 0 <= group + step < groups:
            return planes[group + step]
        return roll_lanes(planes[(group + step) % groups], -GROUP * step)

    def spilled(which, group, up, down):
        spill[which, group] = jnp.where(seat_lane == 10, roll_lanes(up, 7), down)

    packed = []
    for f in range(4):
        planes = []
        for group in range(groups):
            low, high = sides(even_z, got_z, lambda ref: ref[group])
            parts = (ends[0, group], high, low, ends[1, group])
            plane = roll_lanes(parts[3], 3 * DEPTH - DEPTH * f)
            for seat in range(3):
                moved = roll_lanes(parts[seat], DEPTH * (seat - f))
                here = (seat_lane >= DEPTH * seat) & (seat_lane < DEPTH * (seat + 1))
                plane = jnp.where(here, moved, plane)
            planes.append(plane)
        packed.append(planes)
    coef, vx, vy, vz = packed
    for g in range(groups):
        here = coef[g]
        neighbours = (along(coef, g, 1), along(coef, g, -1), roll_rows(here, -1), roll_rows(here, 1))
        neighbours += (roll_lanes(here, -1), roll_lanes(here, 1))
        weights = [0.5 * (here + other) for other in neighbours]
        for which, weight in enumerate(weights):
            pw[which, g] = weight
        diag = (weights[0] + weights[1]) + (weights[2] + weights[3]) + (weights[4] + weights[5])
        fz = weights[4] * vz[g]
        spilled(0, g, weights[4], weights[4])
        spilled(1, g, fz, -fz)
        rhs = weights[0] * vx[g] - weights[1] * along(vx, g, -1)
        rhs = rhs + (weights[2] * vy[g] - weights[3] * roll_rows(vy[g], 1))
        rhs = rhs + (fz - weights[5] * roll_lanes(vz[g], 1))
        inside = here > 0
        scale = jnp.where(inside, 1.0 / jnp.where(inside, diag, 1.0), 0.0)
        pinv[g] = scale
        basis_z[0, g] = scale * rhs
        basis_z[3, g] = vz[g]
    for n in range(3):
        field = [basis_z[n, g] for g in range(groups)]
        for g in range(groups):
            here = field[g]
            fz = pw[4, g] * (roll_lanes(here, -1) - here)
            spilled(2 + n, g, -fz, fz)
            if n < 2:
                image = pw[0, g] * (here - along(field, g, 1)) + pw[1, g] * (here - along(field, g, -1))
                image = image + (pw[2, g] * (here - roll_rows(here, -1)) + pw[3, g] * (here - roll_rows(here, 1)))
                image = image + (pw[5, g] * (here - roll_lanes(here, 1)) - fz)
                basis_z[n + 1, g] = pinv[g] * image

    def inject(which, plane):
        group, seat = plane % groups, plane // groups
        return jnp.where(edge, roll_lanes(spill[which, group], LANES - 1 - 10 - GROUP * seat), 0.0)

    totals = [Totals() for _ in range(6)]

    def count(which, left, right):
        product = left[:ny] * right[:ny]
        totals[which].add(tree_sum([product[i : i + ROWS] for i in range(0, ny, ROWS)]))

    for x in range(-DEPTH + 1, nx + DEPTH - 1):
        e = x % total
        diag, rhs = diag_in[e], rhs_in[e] + inject(1, e)
        inside = diag > 0
        scale = jnp.where(inside, 1.0 / jnp.where(inside, diag + inject(0, e), 1.0), 0.0)
        inverse[e] = scale
        field = scale * rhs
        basis[0, e] = field
        if 0 <= x < nx:
            count(0, field, rhs)
    for n in range(3):
        reach = 2 - n
        old_flux = None
        here = basis[n, (-reach - 1) % total]
        for x in range(-reach - 1, nx + reach):
            e = x % total
            above = basis[n, (e + 1) % total]
            flux = wx[e] * (above - here)
            if x >= -reach:
                image = (old_flux - flux) + inject(2 + n, e)
                image = image + (
                    wy[0, e] * (here - roll_rows(here, -1)) + wy[1, e] * (here - roll_rows(here, 1))
                )
                image = image + (
                    wz[0, e] * (here - roll_lanes(here, -1)) + wz[1, e] * (here - roll_lanes(here, 1))
                )
                own = 0 <= x < nx
                if own:
                    count(2 * n + 1, here, image)
                if n < 2:
                    following = inverse[e] * image
                    basis[n + 1, e] = following
                    if own:
                        count(2 * n + 2, following, image)
            old_flux, here = flux, above
    lane = lane_index((1, LANES))
    row = jnp.zeros((1, LANES), jnp.float32)
    for which, total_ in enumerate(totals):
        value = jnp.sum(jnp.sum(total_.value(), 0, keepdims=True), 1, keepdims=True)
        row = jnp.where(lane == which, value, row)
    sums[...] = row


def finish(nx, ny, n_x, n_y, n_z, parity, gathered, press, vel, basis, basis_z, *refs):
    got_x, got_y, got_z = refs[:n_x], refs[n_x : n_x + n_y], refs[n_x + n_y : n_x + n_y + n_z]
    ustar, coef_cot = refs[n_x + n_y + n_z :]
    even_x, even_y, even_z = parity[0] == 0, parity[1] == 0, parity[2] == 0
    total, height = nx + 2 * DEPTH, ny + 2 * DEPTH
    groups = total // ROWS
    parts = gathered[...]
    while parts.shape[0] > ROWS:
        half = parts.shape[0] // 2
        parts = parts[:half] + parts[half:]
    sums = jnp.sum(parts, 0, keepdims=True)
    lane = lane_index((1, LANES))
    m0, m1, m2, m3, m4, m5 = [
        jnp.sum(jnp.where(lane == which, sums, 0.0), 1, keepdims=True) for which in range(6)
    ]
    l1, l2 = m2 / m1, m3 / m1
    d1, cross, d2 = m3 - l1 * m2, m4 - l1 * m3, m5 - l2 * m3
    l21 = cross / d1
    d2 = d2 - l21 * cross
    y1 = -l1 * m0 + m1
    y2 = m2 - l2 * m0 - l21 * y1
    c2 = y2 / d2
    c1 = y1 / d1 - l21 * c2
    c0 = (m0 / m1 - l1 * c1 - l2 * c2)[0, 0]
    c1, c2 = c1[0, 0], c2[0, 0]

    lanes = lane_index((height, LANES))
    seat_lane = lanes % GROUP
    spill = []
    for g in range(groups):
        cells = c0 * basis_z[0, g] + c1 * basis_z[1, g] + c2 * basis_z[2, g]
        spill.append(jnp.where(seat_lane == 10, roll_lanes(cells, 6), cells))
    lanes = lane_index((ny, LANES))
    at_low, at_high = lanes == 0, lanes == LANES - 1
    low_z, high_z = sides(even_z, got_z, lambda ref: ref[groups, :ny, :])
    press_z = jnp.where(lanes % 2 == 0, high_z, roll_lanes(low_z, 1))
    p_base, layer = 4 * DEPTH - 2, 2 * DEPTH - 1
    p_low, p_high = sides(even_x, got_x, lambda ref: ref[p_base])
    u_low, _ = sides(even_x, got_x, lambda ref: ref[layer])

    def solved(x):
        e = x % total
        return c0 * basis[0, e] + c1 * basis[1, e] + c2 * basis[2, e]

    rows = row_index((ROWS, LANES))
    below, here = solved(-1), solved(0)
    face_low = (p_low - press[0]) * (u_low + here[:ny] - below[:ny])
    for x in range(nx):
        above = solved(x + 1)
        group, seat = x % groups, x // groups
        own, p = here[:ny], press[x]
        out = vel[0, x] + (above[:ny] - own)
        ustar[0, x] = out
        face = (p - (press[x + 1] if x + 1 < nx else p_high)) * out
        answer = face_low + face
        face_low = face
        low, high = sides(even_y, got_y, lambda ref: ref[nx + 2 * DEPTH + x // GROUP, x % GROUP : x % GROUP + 1, :])
        shape = (ROWS, LANES)
        p_tile = jnp.where(rows == 0, jnp.broadcast_to(high, shape), jnp.broadcast_to(low, shape))
        p_tall = jnp.concatenate([p, p_tile], 0)
        u_row, _ = sides(even_y, got_y, lambda ref: ref[x, 3 * DEPTH - 1 : 3 * DEPTH, :])
        u_tall = jnp.concatenate([vel[1, x], jnp.broadcast_to(u_row, shape)], 0)
        out = vel[1, x] + (roll_rows(here, -1)[:ny] - own)
        ustar[1, x] = out
        back = roll_rows(u_tall, 1)[:ny] + (own - roll_rows(here, 1)[:ny])
        answer = answer + ((p - roll_rows(p_tall, -1)[:ny]) * out + (roll_rows(p_tall, 1)[:ny] - p) * back)
        shift = LANES - 1 - 10 - GROUP * seat
        lam_end = roll_lanes(spill[group][:ny], shift)
        u_end = roll_lanes(basis_z[3, group, :ny, :], shift)
        p_end = roll_lanes(press_z, LANES - 1 - 2 * x)
        out = vel[2, x] + (jnp.where(at_high, lam_end, roll_lanes(own, -1)) - own)
        ustar[2, x] = out
        answer = answer + (p - jnp.where(at_high, p_end, roll_lanes(p, -1))) * out
        back = jnp.where(at_low, u_end, roll_lanes(vel[2, x], 1))
        back = back + (own - jnp.where(at_low, lam_end, roll_lanes(own, 1)))
        answer = answer + (jnp.where(at_low, p_end, roll_lanes(p, 1)) - p) * back
        coef_cot[x] = 0.5 * answer
        here = above


def on_device(phase, press, vel):
    nx, ny, nz = phase.shape
    total, height = nx + 2 * DEPTH, ny + 2 * DEPTH
    groups = total // ROWS
    devices = lax.axis_size(AXES)
    n_x, n_y, n_z = (turns(axis) for axis in AXES)
    f32 = lambda *shape: jax.ShapeDtypeStruct(shape, jnp.float32)
    scratch = lambda *shape: pltpu.VMEM(shape, jnp.float32)
    parity = jnp.stack([lax.axis_index(axis) % 2 for axis in AXES]).astype(jnp.int32)
    inputs = [pltpu.with_memory_space_constraint(array, pltpu.HBM) for array in (phase, press, vel)]

    def call(kernel, args, in_specs, shapes, name, scratch_shapes=()):
        return pl.pallas_call(
            kernel,
            out_shape=shapes,
            in_specs=in_specs,
            out_specs=[VMEM] * len(shapes),
            scratch_shapes=list(scratch_shapes),
            compiler_params=PARAMS,
            cost_estimate=pl.CostEstimate(flops=3_000_000, bytes_accessed=3_000_000, transcendentals=0),
            name=name,
        )(*args)

    to_x = call(
        functools.partial(pack_x, nx),
        [parity] + inputs,
        [SMEM] + [HBM] * 3,
        [f32(4 * DEPTH - 1, ny, nz)] * n_x,
        "pack_x",
        [pltpu.VMEM((n_x, DEPTH, ny, nz), jnp.int32), pltpu.SemaphoreType.DMA((n_x, 5))],
    )
    got_x = exchange(to_x, "gx")
    coef, press, vel = call(
        load,
        inputs + [to_x[0]],
        [HBM] * 3 + [ANY],
        [f32(*press.shape), f32(*press.shape), f32(*vel.shape)],
        "load",
        [pltpu.VMEM(phase.shape, jnp.int32), pltpu.SemaphoreType.DMA((3,))],
    )
    to_y = call(
        functools.partial(pack_y, nx, ny, n_x),
        [parity, coef, press, vel, *got_x],
        [SMEM] + [VMEM] * (3 + n_x),
        [f32(total + -(-nx // GROUP), GROUP, nz)] * n_y,
        "pack_y",
    )
    got_y = exchange(to_y, "gy")
    to_z = call(
        functools.partial(pack_z, nx, ny, n_x, n_y),
        [parity, coef, press, vel, *got_x, *got_y],
        [SMEM] + [VMEM] * (3 + n_x + n_y),
        [f32(groups + 1, height, LANES)] * n_z,
        "pack_z",
    )
    got_z = exchange(to_z, "gz")
    cube = (total, height, nz)
    ready = call(
        functools.partial(prepare, nx, ny, n_x, n_y),
        [parity, coef, vel, to_z[0], *got_x, *got_y],
        [SMEM] + [VMEM] * 2 + [ANY] + [VMEM] * (n_x + n_y),
        [f32(*cube), f32(2, *cube), f32(2, *cube), f32(*cube), f32(*cube), f32(2, groups, height, LANES)],
        "prepare",
    )
    basis, basis_z, sums = call(
        functools.partial(krylov, nx, ny, n_z),
        [parity, *ready, *got_z],
        [SMEM] + [VMEM] * (6 + n_z),
        [f32(3, *cube), f32(4, groups, height, LANES), f32(1, LANES)],
        "krylov",
        [scratch(*cube)] + [scratch(n, groups, height, LANES) for n in (6,)] + [scratch(groups, height, LANES)]
        + [scratch(5, groups, height, LANES)],
    )
    spread = jnp.broadcast_to(sums[None], (devices, 1, LANES))
    gathered = lax.all_to_all(spread, AXES, 0, 0).reshape(devices, LANES)
    return call(
        functools.partial(finish, nx, ny, n_x, n_y, n_z),
        [parity, gathered, press, vel, basis, basis_z, *got_x, *got_y, *got_z],
        [SMEM] + [VMEM] * (5 + n_x + n_y + n_z),
        [f32(*vel.shape), f32(nx, ny, nz)],
        "finish",
    )


def solution(mesh):
    cells, faces = P(*AXES), P(None, *AXES)
    return jax.shard_map(
        on_device, mesh=mesh, in_specs=(cells, cells, faces), out_specs=(faces, cells), check_vma=False
    )
```

time: 53.4 us -> 44.8 us (0.84)
  blocking collectives: 21 us -> 16.6 us
  local copies, waits for them, and re-layouts: 3.06 us -> 0.01 us
  waiting for transfers between devices: 8.65 us -> 5.83 us
  starting transfers between devices: 6.38 us -> 8.9 us
  Pallas kernels: 13.3 us -> 12.4 us
    all_to_all x1, blocking collectives: 21 us -> 16.6 us  [on_device(): gathered = lax.all_to_all(spread, AXES, 0, 0).reshape(devices, LANES)]
    unnamed x10 -> x0, local copies, waits for them, and re-layouts: 3.05 us -> none
    ppermute x5, waiting for transfers between devices: 8.65 us -> 5.83 us  [exchange(): lax.ppermute(send, axis, swaps(count, turn))]
    ppermute x5, starting transfers between devices: 6.38 us -> 8.9 us  [exchange(): lax.ppermute(send, axis, swaps(count, turn))]
    pallas_call x5 -> x7, Pallas kernels: 13.3 us -> 12.4 us  [call(): pl.pallas_call(kernel, out_shape=shapes, in_specs=in_specs, out_specs=[VM...]
  transfers between devices with their start and end apart: 5 -> 5, of which waited for: 3 -> 3; matrix products, arithmetic and copies ran while one was open for 0% -> 0% of each run, Pallas kernels for 0% -> 8%
where the time goes in v2:
time: 44.8 us; the launch traced here: 44.6 us
  blocking collectives  16.6 us (37%)
  Pallas kernels  12.4 us (28%)
  starting transfers between devices  8.9 us (20%)
  waiting for transfers between devices  5.83 us (13%)
  between operations  0.73 us (2%)
    all_to_all x1, blocking collectives, on_device(): gathered = lax.all_to_all(spread, AXES, 0, 0).reshape(devices, LANES)  16.6 us
    pallas_call x7, Pallas kernels, call(): pl.pallas_call(kernel, out_shape=shapes, in_specs=in_specs, out_specs=[VM...  12.4 us
    ppermute x5, starting transfers between devices, exchange(): lax.ppermute(send, axis, swaps(count, turn))  8.9 us
    ppermute x5, waiting for transfers between devices, exchange(): lax.ppermute(send, axis, swaps(count, turn))  5.83 us
  transfers between devices with their start and end apart: 5, of which 3 were waited for; matrix products, arithmetic and copies ran while one was open for 0% of the time, Pallas kernels for 8%

profile of v2, /device:TPU:0, one launch (start us, length us, event | category | flops | bytes accessed | tf_op | source)
XLA Modules:
  0.0 44.6 jit_solution(4185116563168532020)
XLA Ops:
  0.7 0.1 pad_add_fusion.parity
  0.7 1.7 %pack_x.1 = (f32[15,32,128]{2,1,0:T(8,128)S(1)}, f32[15,32,128]{2,1,0:T(8,128)S(1)}) custom-call(s32[3]{0:T(128)S(1)} %pad_add_fusion.parity, s32[16,32,128]{2,1,0:T(8,128)} %phase.3, f32[16,32,128]{2,1,0:T(8,128)} %press.3, f32[3,16,32,128]{3,2,1,0:T(8,128)} %vel.3), custom_call_target="tpu_custom_call" | custom-call | flops 3000000 | bytes 3000000 | tf_op jit(solution)/shard_map/pack_x/pallas_call | solution.py:467
  2.4 0.7 %collective-permute-start.1 = (f32[15,32,128]{2,1,0:T(8,128)S(1)}, f32[15,32,128]{2,1,0:T(8,128)S(1)}, u32[]{:S(2)}, u32[]{:S(2)}) collective-permute-start(f32[15,32,128]{2,1,0:T(8,128)S(1)} %get-tuple-element.22), channel_id=1, source_target_pairs={{8,16},{16,8},{9,17},{17,9},{10,18},{18,10},{11,19},{19,11},{12,20... | collective-permute-start | bytes 737288 | tf_op jit(solution)/shard_map/ppermute | solution.py:31
  3.1 5.9 %collective-permute-start = (f32[15,32,128]{2,1,0:T(8,128)S(1)}, f32[15,32,128]{2,1,0:T(8,128)S(1)}, u32[]{:S(2)}, u32[]{:S(2)}) collective-permute-start(f32[15,32,128]{2,1,0:T(8,128)S(1)} %get-tuple-element.18.after), channel_id=1, source_target_pairs={{0,8},{8,0},{16,24},{24,16},{1,9},{9,1},{17,25},{25,17},{2,10},{10... | collective-permute-start | bytes 737288 | tf_op jit(solution)/shard_map/ppermute | solution.py:31
  9.0 1.3 %load.1 = (f32[16,32,128]{2,1,0:T(8,128)S(1)}, f32[16,32,128]{2,1,0:T(8,128)S(1)}, f32[3,16,32,128]{3,2,1,0:T(8,128)S(1)}) custom-call(s32[16,32,128]{2,1,0:T(8,128)} %phase.3, f32[16,32,128]{2,1,0:T(8,128)} %press.3, f32[3,16,32,128]{3,2,1,0:T(8,128)} %vel.3, f32[15,32,128]{2,1,0:T(8,128)S(1)} %get-tuple-element.18.after), custom_call_target="tpu_custom_call" | custom-call | flops 3000000 | bytes 3000000 | tf_op jit(solution)/shard_map/load/pallas_call | solution.py:467
  10.3 0.0 collective-permute-done.1.refs_1_
  10.3 4.3 %collective-permute-done.refs_0_ = f32[15,32,128]{2,1,0:T(8,128)S(1)} collective-permute-done((f32[15,32,128]{2,1,0:T(8,128)S(1)}, f32[15,32,128]{2,1,0:T(8,128)S(1)}, u32[]{:S(2)}, u32[]{:S(2)}) %collective-permute-start) | collective-permute-done | bytes 245792 | tf_op jit(solution)/shard_map/ppermute | solution.py:31
  14.7 0.7 %pack_y.1 = (f32[25,16,128]{2,1,0:T(8,128)S(1)}, f32[25,16,128]{2,1,0:T(8,128)S(1)}) custom-call(s32[3]{0:T(128)S(1)} %pad_add_fusion.parity, f32[16,32,128]{2,1,0:T(8,128)S(1)} %get-tuple-element.19.coef, f32[16,32,128]{2,1,0:T(8,128)S(1)} %get-tuple-element.21.press, f32[3,16,32,128]{3,2,1,0:T(8,128)S(1)} %get-tuple-element.20.vel, ...), custom_call_target="tpu_custom_call" | custom-call | flops 3000000 | bytes 3000000 | tf_op jit(solution)/shard_map/pack_y/pallas_call | solution.py:467
  15.3 0.1 collective-permute-start.2
  15.4 0.7 %collective-permute-start.3 = (f32[25,16,128]{2,1,0:T(8,128)S(1)}, f32[25,16,128]{2,1,0:T(8,128)S(1)}, u32[]{:S(2)}, u32[]{:S(2)}) collective-permute-start(f32[25,16,128]{2,1,0:T(8,128)S(1)} %get-tuple-element.24), channel_id=1, source_target_pairs={{2,4},{4,2},{3,5},{5,3},{10,12},{12,10},{11,13},{13,11},{18,20},{2... | collective-permute-start | bytes 614408 | tf_op jit(solution)/shard_map/ppermute | solution.py:31
  16.1 0.8 %collective-permute-done.2.refs_2_ = f32[25,16,128]{2,1,0:T(8,128)S(1)} collective-permute-done((f32[25,16,128]{2,1,0:T(8,128)S(1)}, f32[25,16,128]{2,1,0:T(8,128)S(1)}, u32[]{:S(2)}, u32[]{:S(2)}) %collective-permute-start.2) | collective-permute-done | bytes 204832 | tf_op jit(solution)/shard_map/ppermute | solution.py:31
  16.8 0.0 collective-permute-done.3.refs_3_
  16.9 1.2 %pack_z.1.after = f32[4,40,128]{2,1,0:T(8,128)S(1)} custom-call(s32[3]{0:T(128)S(1)} %pad_add_fusion.parity, f32[16,32,128]{2,1,0:T(8,128)S(1)} %get-tuple-element.19.coef, f32[16,32,128]{2,1,0:T(8,128)S(1)} %get-tuple-element.21.press, f32[3,16,32,128]{3,2,1,0:T(8,128)S(1)} %get-tuple-element.20.vel, f32[15,32,128]{2,1,0:T(8,128)S(1)} %collective-permute-done.refs_0_, ...), custom_call_target="tpu_custom_call" | custom-call | flops 3000000 | bytes 3000000 | tf_op jit(solution)/shard_map/pack_z/pallas_call | solution.py:467
  18.1 1.6 %collective-permute-start.4 = (f32[4,40,128]{2,1,0:T(8,128)S(1)}, f32[4,40,128]{2,1,0:T(8,128)S(1)}, u32[]{:S(2)}, u32[]{:S(2)}) collective-permute-start(f32[4,40,128]{2,1,0:T(8,128)S(1)} %pack_z.1.after), channel_id=1, source_target_pairs={{0,1},{1,0},{2,3},{3,2},{4,5},{5,4},{6,7},{7,6},{8,9},{9,8},{10,11... | collective-permute-start | bytes 245768 | tf_op jit(solution)/shard_map/ppermute | solution.py:31
  19.6 2.2 %prepare.1 = (f32[24,40,128]{2,1,0:T(8,128)S(1)}, f32[2,24,40,128]{3,2,1,0:T(8,128)S(1)}, f32[2,24,40,128]{3,2,1,0:T(8,128)S(1)}, f32[24,40,128]{2,1,0:T(8,128)S...) custom-call(s32[3]{0:T(128)S(1)} %pad_add_fusion.parity, f32[16,32,128]{2,1,0:T(8,128)S(1)} %get-tuple-element.19.coef, ...), custom_call_target="tpu_custom_call" | custom-call | flops 3000000 | bytes 3000000 | tf_op jit(solution)/shard_map/prepare/pallas_call | solution.py:467
  21.8 0.7 %collective-permute-done.4.refs_0_.refs_4_ = f32[4,40,128]{2,1,0:T(8,128)S(1)} collective-permute-done((f32[4,40,128]{2,1,0:T(8,128)S(1)}, f32[4,40,128]{2,1,0:T(8,128)S(1)}, u32[]{:S(2)}, u32[]{:S(2)}) %collective-permute-start.4) | collective-permute-done | bytes 81952 | tf_op jit(solution)/shard_map/ppermute | solution.py:31
  22.6 3.1 %krylov.1 = (f32[3,24,40,128]{3,2,1,0:T(8,128)S(1)}, f32[4,3,40,128]{3,2,1,0:T(8,128)S(1)}, f32[1,128]{1,0:T(1,128)S(1)}) custom-call(s32[3]{0:T(128)S(1)} %pad_add_fusion.parity, f32[24,40,128]{2,1,0:T(8,128)S(1)} %get-tuple-element.25.wx, f32[2,24,40,128]{3,2,1,0:T(8,128)S(1)} %get-tuple-element.26.wy, f32[2,24,40,128]{3,2,1,0:T(8,128)S(1)} %get-tuple-element.27.wz, ...), custom_call_target="tpu_custom_call" | custom-call | flops 3000000 | bytes 3000000 | tf_op jit(solution)/shard_map/krylov/pallas_call | solution.py:467
  25.7 16.6 %all_to_all.5 = f32[32,1,128]{2,1,0:T(1,128)S(1)} all-to-all(f32[32,1,128]{2,1,0:T(1,128)S(1)} %broadcast_in_dim.9), channel_id=1, replica_groups=mesh['gx'=4,'gy'=4,'gz'=2] {'gx','gy','gz'}, dimensions={0} | all-to-all | bytes 32768 | tf_op jit(solution)/shard_map/all_to_all | solution.py:529
  42.3 2.3 %finish.1 = (f32[3,16,32,128]{3,2,1,0:T(8,128)}, f32[16,32,128]{2,1,0:T(8,128)}) custom-call(s32[3]{0:T(128)S(1)} %pad_add_fusion.parity, f32[32,128]{1,0:T(8,128)S(1)} %bitcast.5, f32[16,32,128]{2,1,0:T(8,128)S(1)} %get-tuple-element.21.press, f32[3,16,32,128]{3,2,1,0:T(8,128)S(1)} %get-tuple-element.20.vel, ...), custom_call_target="tpu_custom_call" | custom-call | flops 3000000 | bytes 3000000 | tf_op jit(solution)/shard_map/finish/pallas_call | solution.py:467
  (1 shorter events, 0.0 us)
Async XLA Ops:
  2.4 7.9 %collective-permute-start.1 = (f32[15,32,128]{2,1,0:T(8,128)S(1)}, f32[15,32,128]{2,1,0:T(8,128)S(1)}, u32[]{:S(2)}, u32[]{:S(2)}) collective-permute-start(f32[15,32,128]{2,1,0:T(8,128)S(1)} %get-tuple-element.22), channel_id=1, source_target_pairs={{8,16},{16,8},{9,17},{17,9},{10,18},{18,10},{11,19},{19,11},{12,20... | collective-permute-start | bytes 737288 | tf_op jit(solution)/shard_map/ppermute | solution.py:31
  3.1 11.6 %collective-permute-start = (f32[15,32,128]{2,1,0:T(8,128)S(1)}, f32[15,32,128]{2,1,0:T(8,128)S(1)}, u32[]{:S(2)}, u32[]{:S(2)}) collective-permute-start(f32[15,32,128]{2,1,0:T(8,128)S(1)} %get-tuple-element.18.after), channel_id=1, source_target_pairs={{0,8},{8,0},{16,24},{24,16},{1,9},{9,1},{17,25},{25,17},{2,10},{10... | collective-permute-start | bytes 737288 | tf_op jit(solution)/shard_map/ppermute | solution.py:31
  15.3 1.5 %collective-permute-start.2 = (f32[25,16,128]{2,1,0:T(8,128)S(1)}, f32[25,16,128]{2,1,0:T(8,128)S(1)}, u32[]{:S(2)}, u32[]{:S(2)}) collective-permute-start(f32[25,16,128]{2,1,0:T(8,128)S(1)} %get-tuple-element.23), channel_id=1, source_target_pairs={{0,2},{2,0},{4,6},{6,4},{1,3},{3,1},{5,7},{7,5},{8,10},{10,8},{12,... | collective-permute-start | bytes 614408 | tf_op jit(solution)/shard_map/ppermute | solution.py:31
  15.4 1.4 %collective-permute-start.3 = (f32[25,16,128]{2,1,0:T(8,128)S(1)}, f32[25,16,128]{2,1,0:T(8,128)S(1)}, u32[]{:S(2)}, u32[]{:S(2)}) collective-permute-start(f32[25,16,128]{2,1,0:T(8,128)S(1)} %get-tuple-element.24), channel_id=1, source_target_pairs={{2,4},{4,2},{3,5},{5,3},{10,12},{12,10},{11,13},{13,11},{18,20},{2... | collective-permute-start | bytes 614408 | tf_op jit(solution)/shard_map/ppermute | solution.py:31
  18.1 4.5 %collective-permute-start.4 = (f32[4,40,128]{2,1,0:T(8,128)S(1)}, f32[4,40,128]{2,1,0:T(8,128)S(1)}, u32[]{:S(2)}, u32[]{:S(2)}) collective-permute-start(f32[4,40,128]{2,1,0:T(8,128)S(1)} %pack_z.1.after), channel_id=1, source_target_pairs={{0,1},{1,0},{2,3},{3,2},{4,5},{5,4},{6,7},{7,6},{8,9},{9,8},{10,11... | collective-permute-start | bytes 245768 | tf_op jit(solution)/shard_map/ppermute | solution.py:31

commit v3 on v2

--- a/solution.py
+++ b/solution.py
@@ -61,9 +61,22 @@
     return pltpu.roll(plane, shift % plane.shape[1], 1)
 
 
-def pack_x(nx, parity, phase, press, vel, *refs):
-    count = (len(refs) - 2) // 1
-    outs, held, sem = refs[:count], refs[count], refs[count + 1]
+def inner_rhs(coef, vy, vz):
+    rows, lanes = row_index(coef.shape), lane_index(coef.shape)
+    up = jnp.where(rows == coef.shape[0] - 1, 0.0, 0.5 * (coef + roll_rows(coef, -1)))
+    down = jnp.where(rows == 0, 0.0, 0.5 * (coef + roll_rows(coef, 1)))
+    right = jnp.where(lanes == LANES - 1, 0.0, 0.5 * (coef + roll_lanes(coef, -1)))
+    left = jnp.where(lanes == 0, 0.0, 0.5 * (coef + roll_lanes(coef, 1)))
+    return (up * vy - down * roll_rows(vy, 1)) + (right * vz - left * roll_lanes(vz, 1))
+
+
+RHS, VX, PRESS, VZ, VY = DEPTH, 2 * DEPTH - 1, 2 * DEPTH, 2 * DEPTH + 1, 2 * DEPTH + 2
+
+
+def pack_x(nx, ny, parity, phase, press, vel, *refs):
+    count = len(refs) - 5
+    outs = refs[:count]
+    held, held_x, held_y, held_z, sem = refs[count:]
     copies = []
     for turn, out in enumerate(outs):
         top = parity[0] == turn
@@ -72,10 +85,10 @@
         last = jnp.where(top, nx - 1, 0)
         parts = [
             (phase.at[pl.ds(deep, DEPTH)], held.at[turn]),
-            (vel.at[0, pl.ds(deep, DEPTH)], out.at[pl.ds(DEPTH, DEPTH)]),
-            (vel.at[1, pl.ds(less, DEPTH - 1)], out.at[pl.ds(2 * DEPTH, DEPTH - 1)]),
-            (vel.at[2, pl.ds(less, DEPTH - 1)], out.at[pl.ds(3 * DEPTH - 1, DEPTH - 1)]),
-            (press.at[pl.ds(last, 1)], out.at[pl.ds(4 * DEPTH - 2, 1)]),
+            (vel.at[0, pl.ds(deep, DEPTH)], held_x.at[turn]),
+            (vel.at[1, pl.ds(less, DEPTH - 1)], held_y.at[turn]),
+            (vel.at[2, pl.ds(less, DEPTH - 1)], held_z.at[turn]),
+            (press.at[last], out.at[pl.ds(PRESS * ny, ny)]),
         ]
         for which, (src, dst) in enumerate(parts):
             copy = pltpu.make_async_copy(src, dst, sem.at[turn, which])
@@ -83,151 +96,255 @@
             copies.append(copy)
     for copy in copies:
         copy.wait()
+    lanes = lane_index((ny, LANES))
+    rows = row_index((ROWS, LANES))
     for turn, out in enumerate(outs):
-        out[:DEPTH] = coefficient(held[turn])
-
-
-def load(phase, press, vel, after, coef, press_out, vel_out, held, sem):
+        top = parity[0] == turn
+        coefs = [coefficient(held[turn, j]) for j in range(DEPTH)]
+        flux = [0.5 * (coefs[j] + coefs[j + 1]) * held_x[turn, j] for j in range(DEPTH - 1)]
+        columns = jnp.zeros((ny, LANES), jnp.float32)
+        lines = jnp.zeros((ROWS, LANES), jnp.float32)
+        for j in range(DEPTH):
+            out[j * ny : (j + 1) * ny, :] = coefs[j]
+        for j in range(DEPTH - 1):
+            vy, vz = held_y[turn, j], held_z[turn, j]
+            upper = (flux[j + 1] - flux[j]) if j + 1 < DEPTH - 1 else -flux[j]
+            lower = (flux[j] - flux[j - 1]) if j else flux[j]
+            inner = inner_rhs(jnp.where(top, coefs[j + 1], coefs[j]), vy, vz)
+            out[(RHS + j) * ny : (RHS + j + 1) * ny, :] = jnp.where(top, upper, lower) + inner
+            columns = jnp.where(lanes == j, roll_lanes(vz, j + 1), columns)
+            lines = jnp.where(rows == j, roll_rows(vy[ny - ROWS :], j + 1), lines)
+        out[VX * ny : (VX + 1) * ny, :] = held_x[turn, DEPTH - 1]
+        out[VZ * ny : (VZ + 1) * ny, :] = columns
+        out[VY * ny :, :] = lines
+
+
+def load(phase, press, vel, after, coef, press_out, vel_out, rhs, held, sem):
     del after
     copies = []
     for which, (src, dst) in enumerate(((phase, held), (press, press_out), (vel, vel_out))):
         copies.append(pltpu.make_async_copy(src, dst, sem.at[which]))
         copies[-1].start()
     copies[0].wait()
-    for plane in range(coef.shape[0]):
-        coef[plane] = coefficient(held[plane])
     copies[1].wait()
     copies[2].wait()
-
-
-def halo_planes(nx, even_x, got_x, row, height):
-    def load(field, plane):
-        above = plane < nx + DEPTH
-        layer = plane - nx if above else plane - nx - DEPTH
-        if field >= 2:
-            layer = layer if above else layer - 1
+    nx = coef.shape[0]
+    here = coefficient(held[0])
+    old_flux = None
+    for x in range(nx):
+        coef[x] = here
+        answer = inner_rhs(here, vel_out[1, x], vel_out[2, x])
+        if old_flux is not None:
+            answer = answer - old_flux
+        if x + 1 < nx:
+            above = coefficient(held[x + 1])
+            old_flux = 0.5 * (here + above) * vel_out[0, x]
+            answer = answer + old_flux
+            here = above
+        rhs[x] = answer
+
+
+class Block:
+    def __init__(self, nx, ny, parity, coef, vel, rhs, got_x, row=0, height=None):
+        self.nx, self.ny = nx, ny
+        self.own_coef, self.vel, self.own_rhs, self.got_x = coef, vel, rhs, got_x
+        self.even = parity[0] == 0
+        self.row, self.height = row, height or ny
+        self.low_face = 0.5 * (self.coef(nx + 2 * DEPTH - 1) + self.coef(0)) * self.halo(VX)[0]
+        self.high_face = 0.5 * (self.coef(nx - 1) + self.coef(nx)) * self.take(vel, 0, nx - 1)
+
+    def take(self, ref, *index):
+        return ref[(*index, pl.ds(self.row, self.height), slice(None))]
+
+    def halo(self, part):
+        return sides(self.even, self.got_x, lambda ref: ref[pl.ds(part * self.ny + self.row, self.height), :])
+
+    def coef(self, plane):
+        if plane < self.nx:
+            return self.take(self.own_coef, plane)
+        above = plane < self.nx + DEPTH
+        return self.halo((plane - self.nx) % DEPTH)[1 if above else 0]
+
+    def rhs(self, plane):
+        nx = self.nx
+        if plane < nx:
+            answer = self.take(self.own_rhs, plane)
+        else:
+            above = plane < nx + DEPTH
+            layer = plane - nx if above else plane - nx - DEPTH - 1
             if layer < 0 or layer >= DEPTH - 1:
-                return jnp.zeros((height, LANES), jnp.float32)
-        base = (0, DEPTH, 2 * DEPTH, 3 * DEPTH - 1)[field]
-        low, high = sides(even_x, got_x, lambda ref: ref[base + layer, pl.ds(row, height), :])
-        return high if above else low
-
-    return load
-
-
-def pack_y(nx, ny, n_x, parity, coef, press, vel, *refs):
+                return jnp.zeros((self.height, LANES), jnp.float32)
+            answer = self.halo(RHS + layer)[1 if above else 0]
+        if plane == 0:
+            answer = answer - self.low_face
+        if plane == nx + 2 * DEPTH - 1:
+            answer = answer + self.low_face
+        if plane == nx - 1:
+            answer = answer + self.high_face
+        if plane == nx:
+            answer = answer - self.high_face
+        return answer
+
+    def layer(self, plane):
+        if plane < self.nx + DEPTH:
+            place = (1, plane - self.nx)
+        else:
+            place = (0, plane - self.nx - DEPTH - 1)
+        return place if 0 <= place[1] < DEPTH - 1 else None
+
+    def vz_end(self, plane):
+        if plane < self.nx:
+            return self.vel[2, plane], LANES - 1
+        place = self.layer(plane)
+        if place is None:
+            return jnp.zeros((self.ny, LANES), jnp.float32), 0
+        return self.halo(VZ)[place[0]], place[1]
+
+    def vy_end(self, plane):
+        if plane < self.nx:
+            return self.vel[1, plane, self.ny - 1 :, :]
+        place = self.layer(plane)
+        if place is None:
+            return jnp.zeros((1, LANES), jnp.float32)
+        at = VY * self.ny + place[1]
+        return sides(self.even, self.got_x, lambda ref: ref[at : at + 1, :])[place[0]]
+
+
+def pack_y(nx, ny, n_x, parity, coef, press, vel, rhs, *refs):
     got_x, outs = refs[:n_x], refs[n_x:]
-    even_x = parity[0] == 0
-    rows = row_index((ROWS, LANES))
+    total = nx + 2 * DEPTH
+    rows, lanes = row_index((ROWS, LANES)), lane_index((ROWS, LANES))
     for turn, out in enumerate(outs):
         top = parity[1] == turn
         row = pl.multiple_of(jnp.where(top, ny - ROWS, 0), ROWS)
-        halo = halo_planes(nx, even_x, got_x, row, ROWS)
-        for plane in range(nx + 2 * DEPTH):
+        block = Block(nx, ny, parity, coef, vel, rhs, got_x, row, ROWS)
+        columns = jnp.zeros((ROWS, LANES), jnp.float32)
+        low_end, high_end = block.halo(VZ)
+        for plane in range(total):
+            one, two = block.coef(plane), block.rhs(plane)
+            one = jnp.where(top, roll_rows(one, DEPTH), one)
+            two = jnp.where(top, roll_rows(two, -1), roll_rows(two, DEPTH))
+            tile = jnp.where(rows < DEPTH, one, two)
+            out[plane] = jnp.where(rows == ROWS - 1, block.vy_end(plane), tile)
             if plane < nx:
-                fields = [coef[plane, pl.ds(row, ROWS), :]]
-                fields += [vel[k, plane, pl.ds(row, ROWS), :] for k in range(3)]
+                source, lane = vel[2, plane, pl.ds(row, ROWS), :], LANES - 1
+            elif block.layer(plane) is None:
+                continue
             else:
-                fields = [halo(f, plane) for f in range(4)]
-            for half in range(2):
-                one, two = fields[2 * half], fields[2 * half + 1]
-                one = jnp.where(top, roll_rows(one, DEPTH), one)
-                two = jnp.where(top, two, roll_rows(two, DEPTH))
-                out[plane, half * ROWS : (half + 1) * ROWS, :] = jnp.where(rows < DEPTH, one, two)
+                side, lane = block.layer(plane)
+                source = (low_end, high_end)[side]
+            columns = jnp.where(lanes == plane, roll_lanes(source, plane - lane), columns)
+        out[total + nx // ROWS] = jnp.where(top, roll_rows(columns, DEPTH - 1), columns)
         for plane in range(nx):
             tile = press[plane, pl.ds(row, ROWS), :]
             edge = jnp.where(top, tile[ROWS - 1 : ROWS], tile[0:1])
-            at = nx + 2 * DEPTH + plane // GROUP
-            out[at, plane % GROUP : plane % GROUP + 1, :] = edge
-
-
-def tall_planes(nx, ny, parity, coef, vel, got_x, got_y):
-    even_x, even_y = parity[0] == 0, parity[1] == 0
+            out[total + plane // ROWS, plane % ROWS : plane % ROWS + 1, :] = edge
+
+
+def tall_end(block, tile_end, plane, lane):
+    source, at = block.vz_end(plane)
+    return jnp.concatenate([roll_lanes(source, lane - at), roll_lanes(tile_end, lane - plane)], 0)
+
+
+def tile_of_ends(nx, even_y, got_y):
     rows = row_index((ROWS, LANES))
-    halo = halo_planes(nx, even_x, got_x, 0, ny)
-
-    def cells(field, plane):
-        if plane >= nx:
-            own = halo(field, plane)
-        elif field == 0:
-            own = coef[plane]
+    low, high = sides(even_y, got_y, lambda ref: ref[nx + 2 * DEPTH + nx // ROWS])
+    return jnp.where(rows < DEPTH, high, roll_rows(low, DEPTH + 1))
+
+
+def press_lane(x):
+    return GROUP * (x % ROWS) + ROWS + 2 * (x // ROWS)
+
+
+def pack_z(nx, ny, n_x, n_y, n_z, parity, coef, press, vel, rhs, *refs):
+    got_x, got_y = refs[:n_x], refs[n_x : n_x + n_y]
+    full_coef, full_rhs, *sends = refs[n_x + n_y :]
+    total, height = nx + 2 * DEPTH, ny + 2 * DEPTH
+    groups = total // ROWS
+    even_y = parity[1] == 0
+    rows = row_index((ROWS, LANES))
+    lanes = lane_index((height, LANES))
+    block = Block(nx, ny, parity, coef, vel, rhs, got_x)
+    tile_end = tile_of_ends(nx, even_y, got_y)
+    parts = [jnp.zeros((height, LANES), jnp.float32) for _ in range(groups // 2 + 1)]
+    made = [list(parts) for _ in sends]
+    for plane in range(total):
+        low, high = sides(even_y, got_y, lambda ref: ref[plane])
+        c_own, c_tile = block.coef(plane), jnp.where(rows < DEPTH, high, roll_rows(low, DEPTH))
+        r_own, r_tile = block.rhs(plane), jnp.where(rows < DEPTH, roll_rows(high, -DEPTH), roll_rows(low, 1))
+        up = 0.5 * (c_own[ny - 1 :] + c_tile[:1]) * block.vy_end(plane)
+        down = 0.5 * (c_tile[ROWS - 1 :] + c_own[:1]) * low[ROWS - 1 :]
+        first, last = r_own[:ROWS], r_own[ny - ROWS :]
+        r_tile = jnp.where(rows == 0, r_tile - up, jnp.where(rows == ROWS - 1, r_tile + down, r_tile))
+        middle = [r_own[ROWS : ny - ROWS]] if ny > 2 * ROWS else []
+        if ny > ROWS:
+            first = jnp.where(rows == 0, first - down, first)
+            last = jnp.where(rows == ROWS - 1, last + up, last)
+            r_all = jnp.concatenate([first] + middle + [last, r_tile], 0)
         else:
-            own = vel[field - 1, plane]
-        half = slice(field // 2 * ROWS, field // 2 * ROWS + ROWS)
-        low, high = sides(even_y, got_y, lambda ref: ref[plane, half, :])
-        if field % 2 == 0:
-            low = roll_rows(low, DEPTH)
-        else:
-            high = roll_rows(high, DEPTH)
-        return jnp.concatenate([own, jnp.where(rows < DEPTH, high, low)], 0)
-
-    return cells
-
-
-def pack_z(nx, ny, n_x, n_y, parity, coef, press, vel, *refs):
-    got_x, got_y, sends = refs[:n_x], refs[n_x : n_x + n_y], refs[n_x + n_y :]
-    groups = (nx + 2 * DEPTH) // ROWS
-    lanes = lane_index((ny + 2 * DEPTH, LANES))
-    cells = tall_planes(nx, ny, parity, coef, vel, got_x, got_y)
-    low_lanes = lane_index((ny, LANES))
-    pad = jnp.zeros((2 * DEPTH, LANES), jnp.float32)
+            only = jnp.where(rows == 0, first - down, jnp.where(rows == ROWS - 1, first + up, first))
+            r_all = jnp.concatenate([only, r_tile], 0)
+        c_all = jnp.concatenate([c_own, c_tile], 0)
+        full_coef[plane], full_rhs[plane] = c_all, r_all
+        group, seat = plane % groups, plane // groups
+        at = GROUP * seat + ROWS * (group % 2)
+        end = tall_end(block, tile_end, plane, at + ROWS - 1)
+        for turn in range(len(sends)):
+            top = parity[2] == turn
+            c_move = pltpu.roll(c_all, jnp.where(top, (at + DEPTH) % LANES, at), 1)
+            r_move = pltpu.roll(r_all, jnp.where(top, (at + ROWS - 1) % LANES, at + DEPTH), 1)
+            value = made[turn][group // 2]
+            value = jnp.where((lanes >= at) & (lanes < at + DEPTH), c_move, value)
+            value = jnp.where((lanes >= at + DEPTH) & (lanes < at + ROWS - 1), r_move, value)
+            made[turn][group // 2] = jnp.where(lanes == at + ROWS - 1, end, value)
     for turn, send in enumerate(sends):
         top = parity[2] == turn
-        for group in range(groups):
-            parts = jnp.zeros((ny + 2 * DEPTH, LANES), jnp.float32)
-            for seat in range(ROWS):
-                for f in range(4):
-                    at = GROUP * seat + DEPTH * f
-                    here = (lanes >= at) & (lanes < at + DEPTH)
-                    shift = jnp.where(top, (at + DEPTH) % LANES, at)
-                    parts = jnp.where(here, pltpu.roll(cells(f, seat * groups + group), shift, 1), parts)
-            send[group] = parts
-        parts = jnp.zeros((ny, LANES), jnp.float32)
+        value = made[turn][groups // 2][:ny]
         for plane in range(nx):
-            shift = jnp.where(top, 2 * plane + 1, 2 * plane)
-            parts = jnp.where(low_lanes == 2 * plane, pltpu.roll(press[plane], shift, 1), parts)
-        send[groups] = jnp.concatenate([parts, pad], 0)
-
-
-def prepare(nx, ny, n_x, n_y, parity, coef, vel, after, *refs):
-    del after
+            at = press_lane(plane)
+            moved = pltpu.roll(press[plane], jnp.where(top, (at + 1) % LANES, at), 1)
+            value = jnp.where(lanes[:ny] == at, moved, value)
+        made[turn][groups // 2] = jnp.concatenate([value, made[turn][groups // 2][ny:]], 0)
+        for which, value in enumerate(made[turn]):
+            send[which] = value
+
+
+def prepare(nx, ny, n_x, n_y, parity, coef, vel, rhs, full_coef, full_rhs, *refs):
     got_x, got_y = refs[:n_x], refs[n_x : n_x + n_y]
-    wx, wy, wz, diag_out, rhs_out, ends = refs[n_x + n_y :]
+    wx, wy, wz, diag_out, ends = refs[n_x + n_y :]
     total, height = nx + 2 * DEPTH, ny + 2 * DEPTH
     groups = total // ROWS
     lanes = lane_index((height, LANES))
-    cells = tall_planes(nx, ny, parity, coef, vel, got_x, got_y)
+    block = Block(nx, ny, parity, coef, vel, rhs, got_x)
+    tile_end = tile_of_ends(nx, parity[1] == 0, got_y)
     for group in range(groups):
-        tops = bottoms = jnp.zeros((height, LANES), jnp.float32)
+        made = [jnp.zeros((height, LANES), jnp.float32) for _ in range(3)]
         for seat in range(ROWS):
-            for f in range(4):
-                plane = cells(f, seat * groups + group)
-                at = GROUP * seat + DEPTH * f
-                here = (lanes >= at) & (lanes < at + DEPTH)
-                tops = jnp.where(here, roll_lanes(plane, at + DEPTH), tops)
-                bottoms = jnp.where(here, roll_lanes(plane, at), bottoms)
-        ends[0, group] = tops
-        ends[1, group] = bottoms
-    old_weight = old_flux = None
-    here = cells(0, nx + DEPTH)
+            plane = seat * groups + group
+            at = GROUP * seat
+            upper = (lanes >= at) & (lanes < at + DEPTH)
+            lower = (lanes >= at + 3 * DEPTH) & (lanes < at + GROUP)
+            for which, source in enumerate((full_coef[plane], full_rhs[plane])):
+                value = jnp.where(upper, roll_lanes(source, at + DEPTH), made[which])
+                made[which] = jnp.where(lower, roll_lanes(source, at + 3 * DEPTH), value)
+            end = tall_end(block, tile_end, plane, at + DEPTH - 1)
+            made[2] = jnp.where(lanes == at + DEPTH - 1, end, made[2])
+        for which in range(3):
+            ends[which, group] = made[which]
+    old_weight = None
+    here = full_coef[nx + DEPTH]
     for x in range(-DEPTH, nx + DEPTH - 1):
         e = x % total
-        above = cells(0, (e + 1) % total)
+        above = full_coef[(e + 1) % total]
         weight = 0.5 * (here + above)
         wx[e] = weight
-        flux = weight * cells(1, e)
         if x > -DEPTH:
-            vy, vz = cells(2, e), cells(3, e)
             up, down = 0.5 * (here + roll_rows(here, -1)), 0.5 * (here + roll_rows(here, 1))
             right = jnp.where(lanes == LANES - 1, 0.0, 0.5 * (here + roll_lanes(here, -1)))
             left = jnp.where(lanes == 0, 0.0, 0.5 * (here + roll_lanes(here, 1)))
             wy[0, e], wy[1, e], wz[0, e], wz[1, e] = up, down, right, left
-            diag = (weight + old_weight) + (up + down) + (right + left)
-            diag_out[e] = jnp.where(here > 0, diag, 0.0)
-            rhs_out[e] = (
-                (flux - old_flux) + (up * vy - down * roll_rows(vy, 1)) + (right * vz - left * roll_lanes(vz, 1))
-            )
-        old_weight, old_flux, here = weight, flux, above
+            diag_out[e] = jnp.where(here > 0, (weight + old_weight) + (up + down) + (right + left), 0.0)
+        old_weight, here = weight, above
 
 
 def tree_sum(parts):
@@ -274,20 +391,17 @@
     def spilled(which, group, up, down):
         spill[which, group] = jnp.where(seat_lane == 10, roll_lanes(up, 7), down)
 
-    packed = []
-    for f in range(4):
-        planes = []
-        for group in range(groups):
-            low, high = sides(even_z, got_z, lambda ref: ref[group])
-            parts = (ends[0, group], high, low, ends[1, group])
-            plane = roll_lanes(parts[3], 3 * DEPTH - DEPTH * f)
-            for seat in range(3):
-                moved = roll_lanes(parts[seat], DEPTH * (seat - f))
-                here = (seat_lane >= DEPTH * seat) & (seat_lane < DEPTH * (seat + 1))
-                plane = jnp.where(here, moved, plane)
-            planes.append(plane)
-        packed.append(planes)
-    coef, vx, vy, vz = packed
+    coef, rhs_z, vz = [], [], []
+    for g in range(groups):
+        low, high = sides(even_z, got_z, lambda ref: ref[g // 2])
+        skip = ROWS * (g % 2)
+        above = (seat_lane >= DEPTH) & (seat_lane < 2 * DEPTH)
+        below = (seat_lane >= 2 * DEPTH) & (seat_lane < 3 * DEPTH)
+        value = jnp.where(above, roll_lanes(high, DEPTH - skip), ends[0, g])
+        coef.append(jnp.where(below, roll_lanes(low, 2 * DEPTH - skip), value))
+        value = jnp.where(above, roll_lanes(high, -skip), ends[1, g])
+        rhs_z.append(jnp.where(below, roll_lanes(low, DEPTH + 1 - skip), value))
+        vz.append(jnp.where(below, roll_lanes(low, DEPTH - skip), ends[2, g]))
     for g in range(groups):
         here = coef[g]
         neighbours = (along(coef, g, 1), along(coef, g, -1), roll_rows(here, -1), roll_rows(here, 1))
@@ -296,12 +410,13 @@
         for which, weight in enumerate(weights):
             pw[which, g] = weight
         diag = (weights[0] + weights[1]) + (weights[2] + weights[3]) + (weights[4] + weights[5])
+        face = (seat_lane == DEPTH - 1) | (seat_lane == 3 * DEPTH - 1)
+        next_face = (seat_lane == DEPTH) | (seat_lane == 3 * DEPTH)
         fz = weights[4] * vz[g]
         spilled(0, g, weights[4], weights[4])
         spilled(1, g, fz, -fz)
-        rhs = weights[0] * vx[g] - weights[1] * along(vx, g, -1)
-        rhs = rhs + (weights[2] * vy[g] - weights[3] * roll_rows(vy[g], 1))
-        rhs = rhs + (fz - weights[5] * roll_lanes(vz[g], 1))
+        rhs = rhs_z[g] + jnp.where(face, fz, 0.0)
+        rhs = rhs - jnp.where(next_face, weights[5] * roll_lanes(vz[g], 1), 0.0)
         inside = here > 0
         scale = jnp.where(inside, 1.0 / jnp.where(inside, diag, 1.0), 0.0)
         pinv[g] = scale
@@ -406,11 +521,10 @@
         spill.append(jnp.where(seat_lane == 10, roll_lanes(cells, 6), cells))
     lanes = lane_index((ny, LANES))
     at_low, at_high = lanes == 0, lanes == LANES - 1
-    low_z, high_z = sides(even_z, got_z, lambda ref: ref[groups, :ny, :])
+    low_z, high_z = sides(even_z, got_z, lambda ref: ref[groups // 2, :ny, :])
     press_z = jnp.where(lanes % 2 == 0, high_z, roll_lanes(low_z, 1))
-    p_base, layer = 4 * DEPTH - 2, 2 * DEPTH - 1
-    p_low, p_high = sides(even_x, got_x, lambda ref: ref[p_base])
-    u_low, _ = sides(even_x, got_x, lambda ref: ref[layer])
+    p_low, p_high = sides(even_x, got_x, lambda ref: ref[PRESS * ny : (PRESS + 1) * ny, :])
+    u_low, _ = sides(even_x, got_x, lambda ref: ref[VX * ny : (VX + 1) * ny, :])
 
     def solved(x):
         e = x % total
@@ -428,11 +542,11 @@
         face = (p - (press[x + 1] if x + 1 < nx else p_high)) * out
         answer = face_low + face
         face_low = face
-        low, high = sides(even_y, got_y, lambda ref: ref[nx + 2 * DEPTH + x // GROUP, x % GROUP : x % GROUP + 1, :])
+        low, high = sides(even_y, got_y, lambda ref: ref[total + x // ROWS, x % ROWS : x % ROWS + 1, :])
         shape = (ROWS, LANES)
         p_tile = jnp.where(rows == 0, jnp.broadcast_to(high, shape), jnp.broadcast_to(low, shape))
         p_tall = jnp.concatenate([p, p_tile], 0)
-        u_row, _ = sides(even_y, got_y, lambda ref: ref[x, 3 * DEPTH - 1 : 3 * DEPTH, :])
+        u_row, _ = sides(even_y, got_y, lambda ref: ref[x, ROWS - 1 :, :])
         u_tall = jnp.concatenate([vel[1, x], jnp.broadcast_to(u_row, shape)], 0)
         out = vel[1, x] + (roll_rows(here, -1)[:ny] - own)
         ustar[1, x] = out
@@ -441,7 +555,7 @@
         shift = LANES - 1 - 10 - GROUP * seat
         lam_end = roll_lanes(spill[group][:ny], shift)
         u_end = roll_lanes(basis_z[3, group, :ny, :], shift)
-        p_end = roll_lanes(press_z, LANES - 1 - 2 * x)
+        p_end = roll_lanes(press_z, LANES - 1 - press_lane(x))
         out = vel[2, x] + (jnp.where(at_high, lam_end, roll_lanes(own, -1)) - own)
         ustar[2, x] = out
         answer = answer + (p - jnp.where(at_high, p_end, roll_lanes(p, -1))) * out
@@ -476,53 +590,55 @@
         )(*args)
 
     to_x = call(
-        functools.partial(pack_x, nx),
+        functools.partial(pack_x, nx, ny),
         [parity] + inputs,
         [SMEM] + [HBM] * 3,
-        [f32(4 * DEPTH - 1, ny, nz)] * n_x,
+        [f32(VY * ny + ROWS, nz)] * n_x,
         "pack_x",
-        [pltpu.VMEM((n_x, DEPTH, ny, nz), jnp.int32), pltpu.SemaphoreType.DMA((n_x, 5))],
+        [pltpu.VMEM((n_x, DEPTH, ny, nz), jnp.int32), scratch(n_x, DEPTH, ny, nz)]
+        + [scratch(n_x, DEPTH - 1, ny, nz)] * 2
+        + [pltpu.SemaphoreType.DMA((n_x, 5))],
     )
     got_x = exchange(to_x, "gx")
-    coef, press, vel = call(
+    coef, press, vel, rhs = call(
         load,
         inputs + [to_x[0]],
         [HBM] * 3 + [ANY],
-        [f32(*press.shape), f32(*press.shape), f32(*vel.shape)],
+        [f32(*press.shape), f32(*press.shape), f32(*vel.shape), f32(*press.shape)],
         "load",
         [pltpu.VMEM(phase.shape, jnp.int32), pltpu.SemaphoreType.DMA((3,))],
     )
     to_y = call(
         functools.partial(pack_y, nx, ny, n_x),
-        [parity, coef, press, vel, *got_x],
-        [SMEM] + [VMEM] * (3 + n_x),
-        [f32(total + -(-nx // GROUP), GROUP, nz)] * n_y,
+        [parity, coef, press, vel, rhs, *got_x],
+        [SMEM] + [VMEM] * (4 + n_x),
+        [f32(total + nx // ROWS + 1, ROWS, nz)] * n_y,
         "pack_y",
     )
     got_y = exchange(to_y, "gy")
-    to_z = call(
-        functools.partial(pack_z, nx, ny, n_x, n_y),
-        [parity, coef, press, vel, *got_x, *got_y],
-        [SMEM] + [VMEM] * (3 + n_x + n_y),
-        [f32(groups + 1, height, LANES)] * n_z,
+    cube = (total, height, nz)
+    full_coef, full_rhs, *to_z = call(
+        functools.partial(pack_z, nx, ny, n_x, n_y, n_z),
+        [parity, coef, press, vel, rhs, *got_x, *got_y],
+        [SMEM] + [VMEM] * (4 + n_x + n_y),
+        [f32(*cube)] * 2 + [f32(groups // 2 + 1, height, LANES)] * n_z,
         "pack_z",
     )
     got_z = exchange(to_z, "gz")
-    cube = (total, height, nz)
-    ready = call(
+    wx, wy, wz, diag, ends = call(
         functools.partial(prepare, nx, ny, n_x, n_y),
-        [parity, coef, vel, to_z[0], *got_x, *got_y],
-        [SMEM] + [VMEM] * 2 + [ANY] + [VMEM] * (n_x + n_y),
-        [f32(*cube), f32(2, *cube), f32(2, *cube), f32(*cube), f32(*cube), f32(2, groups, height, LANES)],
+        [parity, coef, vel, rhs, full_coef, full_rhs, *got_x, *got_y],
+        [SMEM] + [VMEM] * (5 + n_x + n_y),
+        [f32(*cube), f32(2, *cube), f32(2, *cube), f32(*cube), f32(3, groups, height, LANES)],
         "prepare",
     )
     basis, basis_z, sums = call(
         functools.partial(krylov, nx, ny, n_z),
-        [parity, *ready, *got_z],
+        [parity, wx, wy, wz, diag, full_rhs, ends, *got_z],
         [SMEM] + [VMEM] * (6 + n_z),
         [f32(3, *cube), f32(4, groups, height, LANES), f32(1, LANES)],
         "krylov",
-        [scratch(*cube)] + [scratch(n, groups, height, LANES) for n in (6,)] + [scratch(groups, height, LANES)]
+        [scratch(*cube), scratch(6, groups, height, LANES), scratch(groups, height, LANES)]
         + [scratch(5, groups, height, LANES)],
     )
     spread = jnp.broadcast_to(sums[None], (devices, 1, LANES))

time: 44.8 us -> 41 us (0.915)
  waiting for transfers between devices: 5.83 us -> 3.93 us
  Pallas kernels: 12.4 us -> 11.4 us
  blocking collectives: 16.6 us -> 15.8 us
    ppermute x5, waiting for transfers between devices: 5.83 us -> 3.93 us  [exchange(): lax.ppermute(send, axis, swaps(count, turn))]
    pallas_call x7, Pallas kernels: 12.4 us -> 11.4 us  [call(): pl.pallas_call(kernel, out_shape=shapes, in_specs=in_specs, out_specs=[VM...]
    all_to_all x1, blocking collectives: 16.6 us -> 15.8 us  [on_device(): gathered = lax.all_to_all(spread, AXES, 0, 0).reshape(devices, LANES)]
where the time goes in v3:
time: 41 us; the launch traced here: 40.8 us
  blocking collectives  15.8 us (39%)
  Pallas kernels  11.4 us (28%)
  starting transfers between devices  8.89 us (22%)
  waiting for transfers between devices  3.93 us (10%)
  between operations  0.72 us (2%)
    all_to_all x1, blocking collectives, on_device(): gathered = lax.all_to_all(spread, AXES, 0, 0).reshape(devices, LANES)  15.8 us
    pallas_call x7, Pallas kernels, call(): pl.pallas_call(kernel, out_shape=shapes, in_specs=in_specs, out_specs=[VM...  11.4 us
    ppermute x5, starting transfers between devices, exchange(): lax.ppermute(send, axis, swaps(count, turn))  8.89 us
    ppermute x5, waiting for transfers between devices, exchange(): lax.ppermute(send, axis, swaps(count, turn))  3.93 us
  transfers between devices with their start and end apart: 5, of which 3 were waited for; matrix products, arithmetic and copies ran while one was open for 0% of the time, Pallas kernels for 8%

profile of v3, /device:TPU:0, one launch (start us, length us, event | category | flops | bytes accessed | tf_op | source)
XLA Modules:
  0.0 40.8 jit_solution(14905601229685759484)
XLA Ops:
  0.7 0.1 pad_add_fusion.parity
  0.7 1.8 %pack_x.1 = (f32[328,128]{1,0:T(8,128)S(1)}, f32[328,128]{1,0:T(8,128)S(1)}) custom-call(s32[3]{0:T(128)S(1)} %pad_add_fusion.parity, s32[16,32,128]{2,1,0:T(8,128)} %phase.3, f32[16,32,128]{2,1,0:T(8,128)} %press.3, f32[3,16,32,128]{3,2,1,0:T(8,128)} %vel.3), custom_call_target="tpu_custom_call" | custom-call | flops 3000000 | bytes 3000000 | tf_op jit(solution)/shard_map/pack_x/pallas_call | solution.py:581
  2.5 0.7 %collective-permute-start.1 = (f32[328,128]{1,0:T(8,128)S(1)}, f32[328,128]{1,0:T(8,128)S(1)}, u32[]{:S(2)}, u32[]{:S(2)}) collective-permute-start(f32[328,128]{1,0:T(8,128)S(1)} %get-tuple-element.26), channel_id=1, source_target_pairs={{8,16},{16,8},{9,17},{17,9},{10,18},{18,10},{11,19},{19,11},{12,20... | collective-permute-start | bytes 503816 | tf_op jit(solution)/shard_map/ppermute | solution.py:31
  3.2 5.9 %collective-permute-start = (f32[328,128]{1,0:T(8,128)S(1)}, f32[328,128]{1,0:T(8,128)S(1)}, u32[]{:S(2)}, u32[]{:S(2)}) collective-permute-start(f32[328,128]{1,0:T(8,128)S(1)} %get-tuple-element.21.after), channel_id=1, source_target_pairs={{0,8},{8,0},{16,24},{24,16},{1,9},{9,1},{17,25},{25,17},{2,10},{10... | collective-permute-start | bytes 503816 | tf_op jit(solution)/shard_map/ppermute | solution.py:31
  9.1 1.6 %load.1 = (f32[16,32,128]{2,1,0:T(8,128)S(1)}, f32[16,32,128]{2,1,0:T(8,128)S(1)}, f32[3,16,32,128]{3,2,1,0:T(8,128)S(1)}, f32[16,32,128]{2,1,0:T(8,128)S(1)}) custom-call(s32[16,32,128]{2,1,0:T(8,128)} %phase.3, f32[16,32,128]{2,1,0:T(8,128)} %press.3, f32[3,16,32,128]{3,2,1,0:T(8,128)} %vel.3, f32[328,128]{1,0:T(8,128)S(1)} %get-tuple-element.21.after), custom_call_target="tpu_custom_call" | custom-call | flops 3000000 | bytes 3000000 | tf_op jit(solution)/shard_map/load/pallas_call | solution.py:581
  10.7 0.0 collective-permute-done.1.refs_1_
  10.7 2.4 %collective-permute-done.refs_0_ = f32[328,128]{1,0:T(8,128)S(1)} collective-permute-done((f32[328,128]{1,0:T(8,128)S(1)}, f32[328,128]{1,0:T(8,128)S(1)}, u32[]{:S(2)}, u32[]{:S(2)}) %collective-permute-start) | collective-permute-done | bytes 167968 | tf_op jit(solution)/shard_map/ppermute | solution.py:31
  13.1 0.7 %pack_y.1 = (f32[27,8,128]{2,1,0:T(8,128)S(1)}, f32[27,8,128]{2,1,0:T(8,128)S(1)}) custom-call(s32[3]{0:T(128)S(1)} %pad_add_fusion.parity, f32[16,32,128]{2,1,0:T(8,128)S(1)} %get-tuple-element.22.coef, f32[16,32,128]{2,1,0:T(8,128)S(1)} %get-tuple-element.25.press, f32[3,16,32,128]{3,2,1,0:T(8,128)S(1)} %get-tuple-element.23.vel, ...), custom_call_target="tpu_custom_call" | custom-call | flops 3000000 | bytes 3000000 | tf_op jit(solution)/shard_map/pack_y/pallas_call | solution.py:581
  13.8 0.1 collective-permute-start.2
  13.9 0.7 %collective-permute-start.3 = (f32[27,8,128]{2,1,0:T(8,128)S(1)}, f32[27,8,128]{2,1,0:T(8,128)S(1)}, u32[]{:S(2)}, u32[]{:S(2)}) collective-permute-start(f32[27,8,128]{2,1,0:T(8,128)S(1)} %get-tuple-element.28), channel_id=1, source_target_pairs={{2,4},{4,2},{3,5},{5,3},{10,12},{12,10},{11,13},{13,11},{18,20},{2... | collective-permute-start | bytes 331784 | tf_op jit(solution)/shard_map/ppermute | solution.py:31
  14.6 0.6 %collective-permute-done.2.refs_2_ = f32[27,8,128]{2,1,0:T(8,128)S(1)} collective-permute-done((f32[27,8,128]{2,1,0:T(8,128)S(1)}, f32[27,8,128]{2,1,0:T(8,128)S(1)}, u32[]{:S(2)}, u32[]{:S(2)}) %collective-permute-start.2) | collective-permute-done | bytes 110624 | tf_op jit(solution)/shard_map/ppermute | solution.py:31
  15.2 0.0 collective-permute-done.3.refs_3_
  15.2 1.1 %pack_z.1 = (f32[24,40,128]{2,1,0:T(8,128)S(1)}, f32[24,40,128]{2,1,0:T(8,128)S(1)}, f32[2,40,128]{2,1,0:T(8,128)S(1)}) custom-call(s32[3]{0:T(128)S(1)} %pad_add_fusion.parity, f32[16,32,128]{2,1,0:T(8,128)S(1)} %get-tuple-element.22.coef, f32[16,32,128]{2,1,0:T(8,128)S(1)} %get-tuple-element.25.press, f32[3,16,32,128]{3,2,1,0:T(8,128)S(1)} %get-tuple-element.23.vel, ...), custom_call_target="tpu_custom_call" | custom-call | flops 3000000 | bytes 3000000 | tf_op jit(solution)/shard_map/pack_z/pallas_call | solution.py:581
  16.3 1.6 %collective-permute-start.4 = (f32[2,40,128]{2,1,0:T(8,128)S(1)}, f32[2,40,128]{2,1,0:T(8,128)S(1)}, u32[]{:S(2)}, u32[]{:S(2)}) collective-permute-start(f32[2,40,128]{2,1,0:T(8,128)S(1)} %get-tuple-element.36), channel_id=1, source_target_pairs={{0,1},{1,0},{2,3},{3,2},{4,5},{5,4},{6,7},{7,6},{8,9},{9,8},{10,11... | collective-permute-start | bytes 122888 | tf_op jit(solution)/shard_map/ppermute | solution.py:31
  17.9 1.5 %prepare.1 = (f32[24,40,128]{2,1,0:T(8,128)S(1)}, f32[2,24,40,128]{3,2,1,0:T(8,128)S(1)}, f32[2,24,40,128]{3,2,1,0:T(8,128)S(1)}, f32[24,40,128]{2,1,0:T(8,128)S(1)}, f32[3,3,40,128]{3,2,1,0:T(8,128)S(1)}) custom-call(s32[3]{0:T(128)S(1)} %pad_add_fusion.parity, f32[16,32,128]{2,1,0:T(8,128)S(1)} %get-tuple-element.22.coef, ...), custom_call_target="tpu_custom_call" | custom-call | flops 3000000 | bytes 3000000 | tf_op jit(solution)/shard_map/prepare/pallas_call | solution.py:581
  19.4 0.9 %collective-permute-done.4.refs_0_.refs_4_ = f32[2,40,128]{2,1,0:T(8,128)S(1)} collective-permute-done((f32[2,40,128]{2,1,0:T(8,128)S(1)}, f32[2,40,128]{2,1,0:T(8,128)S(1)}, u32[]{:S(2)}, u32[]{:S(2)}) %collective-permute-start.4) | collective-permute-done | bytes 40992 | tf_op jit(solution)/shard_map/ppermute | solution.py:31
  20.4 2.4 %krylov.1 = (f32[3,24,40,128]{3,2,1,0:T(8,128)S(1)}, f32[4,3,40,128]{3,2,1,0:T(8,128)S(1)}, f32[1,128]{1,0:T(1,128)S(1)}) custom-call(s32[3]{0:T(128)S(1)} %pad_add_fusion.parity, f32[24,40,128]{2,1,0:T(8,128)S(1)} %get-tuple-element.31.wx, f32[2,24,40,128]{3,2,1,0:T(8,128)S(1)} %get-tuple-element.32.wy, f32[2,24,40,128]{3,2,1,0:T(8,128)S(1)} %get-tuple-element.33.wz, ...), custom_call_target="tpu_custom_call" | custom-call | flops 3000000 | bytes 3000000 | tf_op jit(solution)/shard_map/krylov/pallas_call | solution.py:581
  22.8 15.8 %all_to_all.5 = f32[32,1,128]{2,1,0:T(1,128)S(1)} all-to-all(f32[32,1,128]{2,1,0:T(1,128)S(1)} %broadcast_in_dim.9), channel_id=1, replica_groups=mesh['gx'=4,'gy'=4,'gz'=2] {'gx','gy','gz'}, dimensions={0} | all-to-all | bytes 32768 | tf_op jit(solution)/shard_map/all_to_all | solution.py:645
  38.5 2.3 %finish.1 = (f32[3,16,32,128]{3,2,1,0:T(8,128)}, f32[16,32,128]{2,1,0:T(8,128)}) custom-call(s32[3]{0:T(128)S(1)} %pad_add_fusion.parity, f32[32,128]{1,0:T(8,128)S(1)} %bitcast.5, f32[16,32,128]{2,1,0:T(8,128)S(1)} %get-tuple-element.25.press, f32[3,16,32,128]{3,2,1,0:T(8,128)S(1)} %get-tuple-element.23.vel, ...), custom_call_target="tpu_custom_call" | custom-call | flops 3000000 | bytes 3000000 | tf_op jit(solution)/shard_map/finish/pallas_call | solution.py:581
  (1 shorter events, 0.0 us)
Async XLA Ops:
  2.5 8.2 %collective-permute-start.1 = (f32[328,128]{1,0:T(8,128)S(1)}, f32[328,128]{1,0:T(8,128)S(1)}, u32[]{:S(2)}, u32[]{:S(2)}) collective-permute-start(f32[328,128]{1,0:T(8,128)S(1)} %get-tuple-element.26), channel_id=1, source_target_pairs={{8,16},{16,8},{9,17},{17,9},{10,18},{18,10},{11,19},{19,11},{12,20... | collective-permute-start | bytes 503816 | tf_op jit(solution)/shard_map/ppermute | solution.py:31
  3.2 9.9 %collective-permute-start = (f32[328,128]{1,0:T(8,128)S(1)}, f32[328,128]{1,0:T(8,128)S(1)}, u32[]{:S(2)}, u32[]{:S(2)}) collective-permute-start(f32[328,128]{1,0:T(8,128)S(1)} %get-tuple-element.21.after), channel_id=1, source_target_pairs={{0,8},{8,0},{16,24},{24,16},{1,9},{9,1},{17,25},{25,17},{2,10},{10... | collective-permute-start | bytes 503816 | tf_op jit(solution)/shard_map/ppermute | solution.py:31
  13.8 1.4 %collective-permute-start.2 = (f32[27,8,128]{2,1,0:T(8,128)S(1)}, f32[27,8,128]{2,1,0:T(8,128)S(1)}, u32[]{:S(2)}, u32[]{:S(2)}) collective-permute-start(f32[27,8,128]{2,1,0:T(8,128)S(1)} %get-tuple-element.27), channel_id=1, source_target_pairs={{0,2},{2,0},{4,6},{6,4},{1,3},{3,1},{5,7},{7,5},{8,10},{10,8},{12,... | collective-permute-start | bytes 331784 | tf_op jit(solution)/shard_map/ppermute | solution.py:31
  13.9 1.3 %collective-permute-start.3 = (f32[27,8,128]{2,1,0:T(8,128)S(1)}, f32[27,8,128]{2,1,0:T(8,128)S(1)}, u32[]{:S(2)}, u32[]{:S(2)}) collective-permute-start(f32[27,8,128]{2,1,0:T(8,128)S(1)} %get-tuple-element.28), channel_id=1, source_target_pairs={{2,4},{4,2},{3,5},{5,3},{10,12},{12,10},{11,13},{13,11},{18,20},{2... | collective-permute-start | bytes 331784 | tf_op jit(solution)/shard_map/ppermute | solution.py:31
  16.3 4.1 %collective-permute-start.4 = (f32[2,40,128]{2,1,0:T(8,128)S(1)}, f32[2,40,128]{2,1,0:T(8,128)S(1)}, u32[]{:S(2)}, u32[]{:S(2)}) collective-permute-start(f32[2,40,128]{2,1,0:T(8,128)S(1)} %get-tuple-element.36), channel_id=1, source_target_pairs={{0,1},{1,0},{2,3},{3,2},{4,5},{5,4},{6,7},{7,6},{8,9},{9,8},{10,11... | collective-permute-start | bytes 122888 | tf_op jit(solution)/shard_map/ppermute | solution.py:31

commit v4 on v3

--- a/solution.py
+++ b/solution.py
@@ -11,9 +11,9 @@
 DEPTH = 4
 GROUP = 4 * DEPTH
 LANES = 128
+STRIDE = 4
 ROWS = 8
 VMEM = pl.BlockSpec(memory_space=pltpu.VMEM)
-SMEM = pl.BlockSpec(memory_space=pltpu.SMEM)
 HBM = pl.BlockSpec(memory_space=pltpu.HBM)
 ANY = pl.BlockSpec(memory_space=pl.ANY)
 PARAMS = pltpu.CompilerParams(vmem_limit_bytes=40 * 1024 * 1024)
@@ -31,6 +31,10 @@
     return [lax.ppermute(send, axis, swaps(count, turn)) for turn, send in enumerate(sends)]
 
 
+def even(axis):
+    return lax.axis_index(axis) % 2 == 0
+
+
 def turns(axis):
     return min(2, lax.axis_size(axis) - 1)
 
@@ -39,10 +43,10 @@
     return jnp.where(phase == 0, 8.0, jnp.where(phase == 1, 1.0, 2.0)).astype(jnp.float32)
 
 
-def sides(even, got, load):
+def sides(is_even, got, load):
     one = load(got[0])
     two = load(got[1]) if len(got) > 1 else jnp.zeros_like(one)
-    return jnp.where(even, two, one), jnp.where(even, one, two)
+    return jnp.where(is_even, two, one), jnp.where(is_even, one, two)
 
 
 def lane_index(shape):
@@ -73,21 +77,18 @@
 RHS, VX, PRESS, VZ, VY = DEPTH, 2 * DEPTH - 1, 2 * DEPTH, 2 * DEPTH + 1, 2 * DEPTH + 2
 
 
-def pack_x(nx, ny, parity, phase, press, vel, *refs):
-    count = len(refs) - 5
+def pack_x(nx, ny, phase, press, vel, *refs):
+    count = len(refs) - 3
     outs = refs[:count]
-    held, held_x, held_y, held_z, sem = refs[count:]
+    held, held_vel, sem = refs[count:]
     copies = []
     for turn, out in enumerate(outs):
-        top = parity[0] == turn
+        top = even("gx") == (turn == 0)
         deep = jnp.where(top, nx - DEPTH, 0)
-        less = jnp.where(top, nx - DEPTH + 1, 0)
         last = jnp.where(top, nx - 1, 0)
         parts = [
+            (vel.at[:, pl.ds(deep, DEPTH)], held_vel.at[turn]),
             (phase.at[pl.ds(deep, DEPTH)], held.at[turn]),
-            (vel.at[0, pl.ds(deep, DEPTH)], held_x.at[turn]),
-            (vel.at[1, pl.ds(less, DEPTH - 1)], held_y.at[turn]),
-            (vel.at[2, pl.ds(less, DEPTH - 1)], held_z.at[turn]),
             (press.at[last], out.at[pl.ds(PRESS * ny, ny)]),
         ]
         for which, (src, dst) in enumerate(parts):
@@ -99,22 +100,23 @@
     lanes = lane_index((ny, LANES))
     rows = row_index((ROWS, LANES))
     for turn, out in enumerate(outs):
-        top = parity[0] == turn
+        top = even("gx") == (turn == 0)
         coefs = [coefficient(held[turn, j]) for j in range(DEPTH)]
-        flux = [0.5 * (coefs[j] + coefs[j + 1]) * held_x[turn, j] for j in range(DEPTH - 1)]
+        flux = [0.5 * (coefs[j] + coefs[j + 1]) * held_vel[turn, 0, j] for j in range(DEPTH - 1)]
         columns = jnp.zeros((ny, LANES), jnp.float32)
         lines = jnp.zeros((ROWS, LANES), jnp.float32)
         for j in range(DEPTH):
             out[j * ny : (j + 1) * ny, :] = coefs[j]
         for j in range(DEPTH - 1):
-            vy, vz = held_y[turn, j], held_z[turn, j]
+            vy = jnp.where(top, held_vel[turn, 1, j + 1], held_vel[turn, 1, j])
+            vz = jnp.where(top, held_vel[turn, 2, j + 1], held_vel[turn, 2, j])
             upper = (flux[j + 1] - flux[j]) if j + 1 < DEPTH - 1 else -flux[j]
             lower = (flux[j] - flux[j - 1]) if j else flux[j]
             inner = inner_rhs(jnp.where(top, coefs[j + 1], coefs[j]), vy, vz)
             out[(RHS + j) * ny : (RHS + j + 1) * ny, :] = jnp.where(top, upper, lower) + inner
             columns = jnp.where(lanes == j, roll_lanes(vz, j + 1), columns)
             lines = jnp.where(rows == j, roll_rows(vy[ny - ROWS :], j + 1), lines)
-        out[VX * ny : (VX + 1) * ny, :] = held_x[turn, DEPTH - 1]
+        out[VX * ny : (VX + 1) * ny, :] = held_vel[turn, 0, DEPTH - 1]
         out[VZ * ny : (VZ + 1) * ny, :] = columns
         out[VY * ny :, :] = lines
 
@@ -145,10 +147,10 @@
 
 
 class Block:
-    def __init__(self, nx, ny, parity, coef, vel, rhs, got_x, row=0, height=None):
+    def __init__(self, nx, ny, coef, vel, rhs, got_x, row=0, height=None):
         self.nx, self.ny = nx, ny
         self.own_coef, self.vel, self.own_rhs, self.got_x = coef, vel, rhs, got_x
-        self.even = parity[0] == 0
+        self.even = even("gx")
         self.row, self.height = row, height or ny
         self.low_face = 0.5 * (self.coef(nx + 2 * DEPTH - 1) + self.coef(0)) * self.halo(VX)[0]
         self.high_face = 0.5 * (self.coef(nx - 1) + self.coef(nx)) * self.take(vel, 0, nx - 1)
@@ -210,14 +212,14 @@
         return sides(self.even, self.got_x, lambda ref: ref[at : at + 1, :])[place[0]]
 
 
-def pack_y(nx, ny, n_x, parity, coef, press, vel, rhs, *refs):
+def pack_y(nx, ny, n_x, coef, press, vel, rhs, *refs):
     got_x, outs = refs[:n_x], refs[n_x:]
     total = nx + 2 * DEPTH
     rows, lanes = row_index((ROWS, LANES)), lane_index((ROWS, LANES))
     for turn, out in enumerate(outs):
-        top = parity[1] == turn
+        top = even("gy") == (turn == 0)
         row = pl.multiple_of(jnp.where(top, ny - ROWS, 0), ROWS)
-        block = Block(nx, ny, parity, coef, vel, rhs, got_x, row, ROWS)
+        block = Block(nx, ny, coef, vel, rhs, got_x, row, ROWS)
         columns = jnp.zeros((ROWS, LANES), jnp.float32)
         low_end, high_end = block.halo(VZ)
         for plane in range(total):
@@ -256,15 +258,15 @@
     return GROUP * (x % ROWS) + ROWS + 2 * (x // ROWS)
 
 
-def pack_z(nx, ny, n_x, n_y, n_z, parity, coef, press, vel, rhs, *refs):
+def pack_z(nx, ny, n_x, n_y, n_z, coef, press, vel, rhs, *refs):
     got_x, got_y = refs[:n_x], refs[n_x : n_x + n_y]
     full_coef, full_rhs, *sends = refs[n_x + n_y :]
     total, height = nx + 2 * DEPTH, ny + 2 * DEPTH
     groups = total // ROWS
-    even_y = parity[1] == 0
+    even_y = even("gy")
     rows = row_index((ROWS, LANES))
     lanes = lane_index((height, LANES))
-    block = Block(nx, ny, parity, coef, vel, rhs, got_x)
+    block = Block(nx, ny, coef, vel, rhs, got_x)
     tile_end = tile_of_ends(nx, even_y, got_y)
     parts = [jnp.zeros((height, LANES), jnp.float32) for _ in range(groups // 2 + 1)]
     made = [list(parts) for _ in sends]
@@ -290,7 +292,7 @@
         at = GROUP * seat + ROWS * (group % 2)
         end = tall_end(block, tile_end, plane, at + ROWS - 1)
         for turn in range(len(sends)):
-            top = parity[2] == turn
+            top = even("gz") == (turn == 0)
             c_move = pltpu.roll(c_all, jnp.where(top, (at + DEPTH) % LANES, at), 1)
             r_move = pltpu.roll(r_all, jnp.where(top, (at + ROWS - 1) % LANES, at + DEPTH), 1)
             value = made[turn][group // 2]
@@ -298,7 +300,7 @@
             value = jnp.where((lanes >= at + DEPTH) & (lanes < at + ROWS - 1), r_move, value)
             made[turn][group // 2] = jnp.where(lanes == at + ROWS - 1, end, value)
     for turn, send in enumerate(sends):
-        top = parity[2] == turn
+        top = even("gz") == (turn == 0)
         value = made[turn][groups // 2][:ny]
         for plane in range(nx):
             at = press_lane(plane)
@@ -309,14 +311,14 @@
             send[which] = value
 
 
-def prepare(nx, ny, n_x, n_y, parity, coef, vel, rhs, full_coef, full_rhs, *refs):
+def prepare(nx, ny, n_x, n_y, coef, vel, rhs, full_coef, full_rhs, *refs):
     got_x, got_y = refs[:n_x], refs[n_x : n_x + n_y]
     wx, wy, wz, diag_out, ends = refs[n_x + n_y :]
     total, height = nx + 2 * DEPTH, ny + 2 * DEPTH
     groups = total // ROWS
     lanes = lane_index((height, LANES))
-    block = Block(nx, ny, parity, coef, vel, rhs, got_x)
-    tile_end = tile_of_ends(nx, parity[1] == 0, got_y)
+    block = Block(nx, ny, coef, vel, rhs, got_x)
+    tile_end = tile_of_ends(nx, even("gy"), got_y)
     for group in range(groups):
         made = [jnp.zeros((height, LANES), jnp.float32) for _ in range(3)]
         for seat in range(ROWS):
@@ -372,11 +374,11 @@
         return total
 
 
-def krylov(nx, ny, n_z, parity, wx, wy, wz, diag_in, rhs_in, ends, *refs):
+def krylov(nx, ny, n_z, wx, wy, wz, diag_in, rhs_in, ends, *refs):
     got_z = refs[:n_z]
     basis, basis_z, sums = refs[n_z : n_z + 3]
     inverse, pw, pinv, spill = refs[n_z + 3 :]
-    even_z = parity[2] == 0
+    even_z = even("gz")
     total, height = nx + 2 * DEPTH, ny + 2 * DEPTH
     groups = total // ROWS
     lanes = lane_index((height, LANES))
@@ -487,10 +489,10 @@
     sums[...] = row
 
 
-def finish(nx, ny, n_x, n_y, n_z, parity, gathered, press, vel, basis, basis_z, *refs):
+def finish(nx, ny, n_x, n_y, n_z, gathered, press, vel, basis, basis_z, *refs):
     got_x, got_y, got_z = refs[:n_x], refs[n_x : n_x + n_y], refs[n_x + n_y : n_x + n_y + n_z]
-    ustar, coef_cot = refs[n_x + n_y + n_z :]
-    even_x, even_y, even_z = parity[0] == 0, parity[1] == 0, parity[2] == 0
+    ustar_out, coef_out, ustar, coef_cot, sem = refs[n_x + n_y + n_z :]
+    even_x, even_y, even_z = even("gx"), even("gy"), even("gz")
     total, height = nx + 2 * DEPTH, ny + 2 * DEPTH
     groups = total // ROWS
     parts = gathered[...]
@@ -530,6 +532,7 @@
         e = x % total
         return c0 * basis[0, e] + c1 * basis[1, e] + c2 * basis[2, e]
 
+    copies = []
     rows = row_index((ROWS, LANES))
     below, here = solved(-1), solved(0)
     face_low = (p_low - press[0]) * (u_low + here[:ny] - below[:ny])
@@ -564,6 +567,15 @@
         answer = answer + (jnp.where(at_low, p_end, roll_lanes(p, 1)) - p) * back
         coef_cot[x] = 0.5 * answer
         here = above
+        if (x + 1) % STRIDE == 0:
+            part = pl.ds(x + 1 - STRIDE, STRIDE)
+            for which, (src, dst) in enumerate(
+                ((ustar.at[:, part], ustar_out.at[:, part]), (coef_cot.at[part], coef_out.at[part]))
+            ):
+                copies.append(pltpu.make_async_copy(src, dst, sem.at[which, x // STRIDE]))
+                copies[-1].start()
+    for copy in copies:
+        copy.wait()
 
 
 def on_device(phase, press, vel):
@@ -574,15 +586,14 @@
     n_x, n_y, n_z = (turns(axis) for axis in AXES)
     f32 = lambda *shape: jax.ShapeDtypeStruct(shape, jnp.float32)
     scratch = lambda *shape: pltpu.VMEM(shape, jnp.float32)
-    parity = jnp.stack([lax.axis_index(axis) % 2 for axis in AXES]).astype(jnp.int32)
     inputs = [pltpu.with_memory_space_constraint(array, pltpu.HBM) for array in (phase, press, vel)]
 
-    def call(kernel, args, in_specs, shapes, name, scratch_shapes=()):
+    def call(kernel, args, in_specs, shapes, name, scratch_shapes=(), out_spec=VMEM):
         return pl.pallas_call(
             kernel,
             out_shape=shapes,
             in_specs=in_specs,
-            out_specs=[VMEM] * len(shapes),
+            out_specs=[out_spec] * len(shapes),
             scratch_shapes=list(scratch_shapes),
             compiler_params=PARAMS,
             cost_estimate=pl.CostEstimate(flops=3_000_000, bytes_accessed=3_000_000, transcendentals=0),
@@ -591,13 +602,12 @@
 
     to_x = call(
         functools.partial(pack_x, nx, ny),
-        [parity] + inputs,
-        [SMEM] + [HBM] * 3,
+        inputs,
+        [HBM] * 3,
         [f32(VY * ny + ROWS, nz)] * n_x,
         "pack_x",
-        [pltpu.VMEM((n_x, DEPTH, ny, nz), jnp.int32), scratch(n_x, DEPTH, ny, nz)]
-        + [scratch(n_x, DEPTH - 1, ny, nz)] * 2
-        + [pltpu.SemaphoreType.DMA((n_x, 5))],
+        [pltpu.VMEM((n_x, DEPTH, ny, nz), jnp.int32), scratch(n_x, 3, DEPTH, ny, nz)]
+        + [pltpu.SemaphoreType.DMA((n_x, 3))],
     )
     got_x = exchange(to_x, "gx")
     coef, press, vel, rhs = call(
@@ -610,8 +620,8 @@
     )
     to_y = call(
         functools.partial(pack_y, nx, ny, n_x),
-        [parity, coef, press, vel, rhs, *got_x],
-        [SMEM] + [VMEM] * (4 + n_x),
+        [coef, press, vel, rhs, *got_x],
+        [VMEM] * (4 + n_x),
         [f32(total + nx // ROWS + 1, ROWS, nz)] * n_y,
         "pack_y",
     )
@@ -619,23 +629,23 @@
     cube = (total, height, nz)
     full_coef, full_rhs, *to_z = call(
         functools.partial(pack_z, nx, ny, n_x, n_y, n_z),
-        [parity, coef, press, vel, rhs, *got_x, *got_y],
-        [SMEM] + [VMEM] * (4 + n_x + n_y),
+        [coef, press, vel, rhs, *got_x, *got_y],
+        [VMEM] * (4 + n_x + n_y),
         [f32(*cube)] * 2 + [f32(groups // 2 + 1, height, LANES)] * n_z,
         "pack_z",
     )
     got_z = exchange(to_z, "gz")
     wx, wy, wz, diag, ends = call(
         functools.partial(prepare, nx, ny, n_x, n_y),
-        [parity, coef, vel, rhs, full_coef, full_rhs, *got_x, *got_y],
-        [SMEM] + [VMEM] * (5 + n_x + n_y),
+        [coef, vel, rhs, full_coef, full_rhs, *got_x, *got_y],
+        [VMEM] * (5 + n_x + n_y),
         [f32(*cube), f32(2, *cube), f32(2, *cube), f32(*cube), f32(3, groups, height, LANES)],
         "prepare",
     )
     basis, basis_z, sums = call(
         functools.partial(krylov, nx, ny, n_z),
-        [parity, wx, wy, wz, diag, full_rhs, ends, *got_z],
-        [SMEM] + [VMEM] * (6 + n_z),
+        [wx, wy, wz, diag, full_rhs, ends, *got_z],
+        [VMEM] * (6 + n_z),
         [f32(3, *cube), f32(4, groups, height, LANES), f32(1, LANES)],
         "krylov",
         [scratch(*cube), scratch(6, groups, height, LANES), scratch(groups, height, LANES)]
@@ -645,10 +655,12 @@
     gathered = lax.all_to_all(spread, AXES, 0, 0).reshape(devices, LANES)
     return call(
         functools.partial(finish, nx, ny, n_x, n_y, n_z),
-        [parity, gathered, press, vel, basis, basis_z, *got_x, *got_y, *got_z],
-        [SMEM] + [VMEM] * (5 + n_x + n_y + n_z),
+        [gathered, press, vel, basis, basis_z, *got_x, *got_y, *got_z],
+        [VMEM] * (5 + n_x + n_y + n_z),
         [f32(*vel.shape), f32(nx, ny, nz)],
         "finish",
+        [scratch(*vel.shape), scratch(nx, ny, nz), pltpu.SemaphoreType.DMA((2, nx // STRIDE))],
+        HBM,
     )
 
 

time: 41 us -> 38.1 us (0.929)
  Pallas kernels: 11.4 us -> 8.08 us
  waiting for transfers between devices: 3.93 us -> 4.48 us
    pallas_call x7, Pallas kernels: 11.4 us -> 8.08 us  [call(): pl.pallas_call(kernel, out_shape=shapes, in_specs=in_specs, out_specs=[ou...]
    ppermute x5, waiting for transfers between devices: 3.93 us -> 4.48 us  [exchange(): lax.ppermute(send, axis, swaps(count, turn))]
  transfers between devices with their start and end apart: 5 -> 5, of which waited for: 3 -> 3; matrix products, arithmetic and copies ran while one was open for 0% -> 0% of each run, Pallas kernels for 8% -> 7%
where the time goes in v4:
time: 38.1 us; the launch traced here: 37.9 us
  blocking collectives  15.8 us (41%)
  starting transfers between devices  8.89 us (23%)
  Pallas kernels  8.08 us (21%)
  waiting for transfers between devices  4.48 us (12%)
  between operations  0.7 us (2%)
    all_to_all x1, blocking collectives, on_device(): gathered = lax.all_to_all(spread, AXES, 0, 0).reshape(devices, LANES)  15.8 us
    ppermute x5, starting transfers between devices, exchange(): lax.ppermute(send, axis, swaps(count, turn))  8.89 us
    pallas_call x7, Pallas kernels, call(): pl.pallas_call(kernel, out_shape=shapes, in_specs=in_specs, out_specs=[ou...  8.08 us
    ppermute x5, waiting for transfers between devices, exchange(): lax.ppermute(send, axis, swaps(count, turn))  4.48 us
  transfers between devices with their start and end apart: 5, of which 3 were waited for; matrix products, arithmetic and copies ran while one was open for 0% of the time, Pallas kernels for 7%

profile of v4, /device:TPU:0, one launch (start us, length us, event | category | flops | bytes accessed | tf_op | source)
XLA Modules:
  0.0 37.9 jit_solution(7606672361957858425)
XLA Ops:
  0.6 1.3 %pack_x.1 = (f32[328,128]{1,0:T(8,128)S(1)}, f32[328,128]{1,0:T(8,128)S(1)}) custom-call(s32[16,32,128]{2,1,0:T(8,128)} %phase.3, f32[16,32,128]{2,1,0:T(8,128)} %press.3, f32[3,16,32,128]{3,2,1,0:T(8,128)} %vel.3), custom_call_target="tpu_custom_call" | custom-call | flops 3000000 | bytes 3000000 | tf_op jit(solution)/shard_map/pack_x/pallas_call | solution.py:592
  1.9 0.7 %collective-permute-start.1 = (f32[328,128]{1,0:T(8,128)S(1)}, f32[328,128]{1,0:T(8,128)S(1)}, u32[]{:S(2)}, u32[]{:S(2)}) collective-permute-start(f32[328,128]{1,0:T(8,128)S(1)} %get-tuple-element.26), channel_id=1, source_target_pairs={{8,16},{16,8},{9,17},{17,9},{10,18},{18,10},{11,19},{19,11},{12,20... | collective-permute-start | bytes 503816 | tf_op jit(solution)/shard_map/ppermute | solution.py:31
  2.6 5.9 %collective-permute-start = (f32[328,128]{1,0:T(8,128)S(1)}, f32[328,128]{1,0:T(8,128)S(1)}, u32[]{:S(2)}, u32[]{:S(2)}) collective-permute-start(f32[328,128]{1,0:T(8,128)S(1)} %get-tuple-element.21.after), channel_id=1, source_target_pairs={{0,8},{8,0},{16,24},{24,16},{1,9},{9,1},{17,25},{25,17},{2,10},{10... | collective-permute-start | bytes 503816 | tf_op jit(solution)/shard_map/ppermute | solution.py:31
  8.5 1.6 %load.1 = (f32[16,32,128]{2,1,0:T(8,128)S(1)}, f32[16,32,128]{2,1,0:T(8,128)S(1)}, f32[3,16,32,128]{3,2,1,0:T(8,128)S(1)}, f32[16,32,128]{2,1,0:T(8,128)S(1)}) custom-call(s32[16,32,128]{2,1,0:T(8,128)} %phase.3, f32[16,32,128]{2,1,0:T(8,128)} %press.3, f32[3,16,32,128]{3,2,1,0:T(8,128)} %vel.3, f32[328,128]{1,0:T(8,128)S(1)} %get-tuple-element.21.after), custom_call_target="tpu_custom_call" | custom-call | flops 3000000 | bytes 3000000 | tf_op jit(solution)/shard_map/load/pallas_call | solution.py:592
  10.1 0.0 collective-permute-done.1.refs_1_
  10.1 2.4 %collective-permute-done.refs_0_ = f32[328,128]{1,0:T(8,128)S(1)} collective-permute-done((f32[328,128]{1,0:T(8,128)S(1)}, f32[328,128]{1,0:T(8,128)S(1)}, u32[]{:S(2)}, u32[]{:S(2)}) %collective-permute-start) | collective-permute-done | bytes 167968 | tf_op jit(solution)/shard_map/ppermute | solution.py:31
  12.5 0.2 pack_y.1
  12.7 0.1 collective-permute-start.2
  12.8 0.7 %collective-permute-start.3 = (f32[27,8,128]{2,1,0:T(8,128)S(1)}, f32[27,8,128]{2,1,0:T(8,128)S(1)}, u32[]{:S(2)}, u32[]{:S(2)}) collective-permute-start(f32[27,8,128]{2,1,0:T(8,128)S(1)} %get-tuple-element.28), channel_id=1, source_target_pairs={{2,4},{4,2},{3,5},{5,3},{10,12},{12,10},{11,13},{13,11},{18,20},{2... | collective-permute-start | bytes 331784 | tf_op jit(solution)/shard_map/ppermute | solution.py:31
  13.4 0.6 %collective-permute-done.2.refs_2_ = f32[27,8,128]{2,1,0:T(8,128)S(1)} collective-permute-done((f32[27,8,128]{2,1,0:T(8,128)S(1)}, f32[27,8,128]{2,1,0:T(8,128)S(1)}, u32[]{:S(2)}, u32[]{:S(2)}) %collective-permute-start.2) | collective-permute-done | bytes 110624 | tf_op jit(solution)/shard_map/ppermute | solution.py:31
  14.1 0.0 collective-permute-done.3.refs_3_
  14.1 0.5 %pack_z.1 = (f32[24,40,128]{2,1,0:T(8,128)S(1)}, f32[24,40,128]{2,1,0:T(8,128)S(1)}, f32[2,40,128]{2,1,0:T(8,128)S(1)}) custom-call(f32[16,32,128]{2,1,0:T(8,128)S(1)} %get-tuple-element.22.coef, f32[16,32,128]{2,1,0:T(8,128)S(1)} %get-tuple-element.25.press, f32[3,16,32,128]{3,2,1,0:T(8,128)S(1)} %get-tuple-element.23.vel, ...), custom_call_target="tpu_custom_call" | custom-call | flops 3000000 | bytes 3000000 | tf_op jit(solution)/shard_map/pack_z/pallas_call | solution.py:592
  14.6 1.6 %collective-permute-start.4 = (f32[2,40,128]{2,1,0:T(8,128)S(1)}, f32[2,40,128]{2,1,0:T(8,128)S(1)}, u32[]{:S(2)}, u32[]{:S(2)}) collective-permute-start(f32[2,40,128]{2,1,0:T(8,128)S(1)} %get-tuple-element.36), channel_id=1, source_target_pairs={{0,1},{1,0},{2,3},{3,2},{4,5},{5,4},{6,7},{7,6},{8,9},{9,8},{10,11... | collective-permute-start | bytes 122888 | tf_op jit(solution)/shard_map/ppermute | solution.py:31
  16.2 1.0 %prepare.1 = (f32[24,40,128]{2,1,0:T(8,128)S(1)}, f32[2,24,40,128]{3,2,1,0:T(8,128)S(1)}, f32[2,24,40,128]{3,2,1,0:T(8,128)S(1)}, f32[24,40,128]{2,1,0:T(8,128)S(1)}, f32[3,3,40,128]{3,2,1,0:T(8,128)S(1)}) custom-call(f32[16,32,128]{2,1,0:T(8,128)S(1)} %get-tuple-element.22.coef, f32[3,16,32,128]{3,2,1,0:T(8,128)S(1)} %get-tuple-element.23.vel, ...), custom_call_target="tpu_custom_call" | custom-call | flops 3000000 | bytes 3000000 | tf_op jit(solution)/shard_map/prepare/pallas_call | solution.py:592
  17.2 1.5 %collective-permute-done.4.refs_0_.refs_4_ = f32[2,40,128]{2,1,0:T(8,128)S(1)} collective-permute-done((f32[2,40,128]{2,1,0:T(8,128)S(1)}, f32[2,40,128]{2,1,0:T(8,128)S(1)}, u32[]{:S(2)}, u32[]{:S(2)}) %collective-permute-start.4) | collective-permute-done | bytes 40992 | tf_op jit(solution)/shard_map/ppermute | solution.py:31
  18.7 1.9 %krylov.1 = (f32[3,24,40,128]{3,2,1,0:T(8,128)S(1)}, f32[4,3,40,128]{3,2,1,0:T(8,128)S(1)}, f32[1,128]{1,0:T(1,128)S(1)}) custom-call(f32[24,40,128]{2,1,0:T(8,128)S(1)} %get-tuple-element.31.wx, f32[2,24,40,128]{3,2,1,0:T(8,128)S(1)} %get-tuple-element.32.wy, f32[2,24,40,128]{3,2,1,0:T(8,128)S(1)} %get-tuple-element.33.wz, ...), custom_call_target="tpu_custom_call" | custom-call | flops 3000000 | bytes 3000000 | tf_op jit(solution)/shard_map/krylov/pallas_call | solution.py:592
  20.6 15.8 %all_to_all.5 = f32[32,1,128]{2,1,0:T(1,128)S(1)} all-to-all(f32[32,1,128]{2,1,0:T(1,128)S(1)} %broadcast_in_dim.9), channel_id=1, replica_groups=mesh['gx'=4,'gy'=4,'gz'=2] {'gx','gy','gz'}, dimensions={0} | all-to-all | bytes 32768 | tf_op jit(solution)/shard_map/all_to_all | solution.py:655
  36.3 1.6 %finish.1 = (f32[3,16,32,128]{3,2,1,0:T(8,128)}, f32[16,32,128]{2,1,0:T(8,128)}) custom-call(f32[32,128]{1,0:T(8,128)S(1)} %bitcast.2, f32[16,32,128]{2,1,0:T(8,128)S(1)} %get-tuple-element.25.press, f32[3,16,32,128]{3,2,1,0:T(8,128)S(1)} %get-tuple-element.23.vel, f32[3,24,40,128]{3,2,1,0:T(8,128)S(1)} %get-tuple-element.38.basis, ...), custom_call_target="tpu_custom_call" | custom-call | flops 3000000 | bytes 3000000 | tf_op jit(solution)/shard_map/finish/pallas_call | solution.py:592
  (1 shorter events, 0.0 us)
Async XLA Ops:
  1.9 8.2 %collective-permute-start.1 = (f32[328,128]{1,0:T(8,128)S(1)}, f32[328,128]{1,0:T(8,128)S(1)}, u32[]{:S(2)}, u32[]{:S(2)}) collective-permute-start(f32[328,128]{1,0:T(8,128)S(1)} %get-tuple-element.26), channel_id=1, source_target_pairs={{8,16},{16,8},{9,17},{17,9},{10,18},{18,10},{11,19},{19,11},{12,20... | collective-permute-start | bytes 503816 | tf_op jit(solution)/shard_map/ppermute | solution.py:31
  2.6 9.9 %collective-permute-start = (f32[328,128]{1,0:T(8,128)S(1)}, f32[328,128]{1,0:T(8,128)S(1)}, u32[]{:S(2)}, u32[]{:S(2)}) collective-permute-start(f32[328,128]{1,0:T(8,128)S(1)} %get-tuple-element.21.after), channel_id=1, source_target_pairs={{0,8},{8,0},{16,24},{24,16},{1,9},{9,1},{17,25},{25,17},{2,10},{10... | collective-permute-start | bytes 503816 | tf_op jit(solution)/shard_map/ppermute | solution.py:31
  12.7 1.4 %collective-permute-start.2 = (f32[27,8,128]{2,1,0:T(8,128)S(1)}, f32[27,8,128]{2,1,0:T(8,128)S(1)}, u32[]{:S(2)}, u32[]{:S(2)}) collective-permute-start(f32[27,8,128]{2,1,0:T(8,128)S(1)} %get-tuple-element.27), channel_id=1, source_target_pairs={{0,2},{2,0},{4,6},{6,4},{1,3},{3,1},{5,7},{7,5},{8,10},{10,8},{12,... | collective-permute-start | bytes 331784 | tf_op jit(solution)/shard_map/ppermute | solution.py:31
  12.8 1.3 %collective-permute-start.3 = (f32[27,8,128]{2,1,0:T(8,128)S(1)}, f32[27,8,128]{2,1,0:T(8,128)S(1)}, u32[]{:S(2)}, u32[]{:S(2)}) collective-permute-start(f32[27,8,128]{2,1,0:T(8,128)S(1)} %get-tuple-element.28), channel_id=1, source_target_pairs={{2,4},{4,2},{3,5},{5,3},{10,12},{12,10},{11,13},{13,11},{18,20},{2... | collective-permute-start | bytes 331784 | tf_op jit(solution)/shard_map/ppermute | solution.py:31
  14.6 4.1 %collective-permute-start.4 = (f32[2,40,128]{2,1,0:T(8,128)S(1)}, f32[2,40,128]{2,1,0:T(8,128)S(1)}, u32[]{:S(2)}, u32[]{:S(2)}) collective-permute-start(f32[2,40,128]{2,1,0:T(8,128)S(1)} %get-tuple-element.36), channel_id=1, source_target_pairs={{0,1},{1,0},{2,3},{3,2},{4,5},{5,4},{6,7},{7,6},{8,9},{9,8},{10,11... | collective-permute-start | bytes 122888 | tf_op jit(solution)/shard_map/ppermute | solution.py:31

commit v5 on v4

--- a/solution.py
+++ b/solution.py
@@ -1,4 +1,5 @@
 import functools
+import itertools
 
 import jax
 import jax.numpy as jnp
@@ -8,6 +9,7 @@
 from jax.sharding import PartitionSpec as P
 
 AXES = ("gx", "gy", "gz")
+SPARE = dict(gx="gy", gy="gz", gz="gx")
 DEPTH = 4
 GROUP = 4 * DEPTH
 LANES = 128
@@ -19,16 +21,40 @@
 PARAMS = pltpu.CompilerParams(vmem_limit_bytes=40 * 1024 * 1024)
 
 
-def swaps(count, first):
+def swaps(axis, turn):
+    sizes = [lax.axis_size(name) for name in AXES]
+    along, spare = AXES.index(axis), AXES.index(SPARE[axis])
+    number = lambda place: (place[0] * sizes[1] + place[1]) * sizes[2] + place[2]
     pairs = []
-    for i in range(first, count - 1, 2):
-        pairs += [(i, i + 1), (i + 1, i)]
+    for place in itertools.product(*map(range, sizes)):
+        partner = list(place)
+        other = place[along] + (1 if (place[along] - turn) % 2 == 0 else -1)
+        if 0 <= other < sizes[along]:
+            partner[along] = other
+        elif sizes[spare] % 2 == 0:
+            partner[spare] ^= 1
+        else:
+            continue
+        pairs.append((number(place), number(partner)))
     return pairs
 
 
 def exchange(sends, axis):
-    count = lax.axis_size(axis)
-    return [lax.ppermute(send, axis, swaps(count, turn)) for turn, send in enumerate(sends)]
+    return [lax.ppermute(send, AXES, swaps(axis, turn)) for turn, send in enumerate(sends)]
+
+
+def clear_if_alone(axis, turn, out):
+    count, place = lax.axis_size(axis), lax.axis_index(axis)
+    alone = []
+    if turn == 1:
+        alone.append(place == 0)
+    if count % 2 != turn:
+        alone.append(place == count - 1)
+    for case in alone:
+
+        @pl.when(case)
+        def _():
+            out[...] = jnp.zeros(out.shape, out.dtype)
 
 
 def even(axis):
@@ -74,7 +100,7 @@
     return (up * vy - down * roll_rows(vy, 1)) + (right * vz - left * roll_lanes(vz, 1))
 
 
-RHS, VX, PRESS, VZ, VY = DEPTH, 2 * DEPTH - 1, 2 * DEPTH, 2 * DEPTH + 1, 2 * DEPTH + 2
+RHS, VX, PRESS, VY = DEPTH, 2 * DEPTH - 1, 2 * DEPTH, 2 * DEPTH + 1
 
 
 def pack_x(nx, ny, phase, press, vel, *refs):
@@ -97,13 +123,13 @@
             copies.append(copy)
     for copy in copies:
         copy.wait()
-    lanes = lane_index((ny, LANES))
+    lanes = lane_index((ROWS, LANES))
     rows = row_index((ROWS, LANES))
     for turn, out in enumerate(outs):
         top = even("gx") == (turn == 0)
         coefs = [coefficient(held[turn, j]) for j in range(DEPTH)]
         flux = [0.5 * (coefs[j] + coefs[j + 1]) * held_vel[turn, 0, j] for j in range(DEPTH - 1)]
-        columns = jnp.zeros((ny, LANES), jnp.float32)
+        columns = jnp.zeros((ROWS, LANES), jnp.float32)
         lines = jnp.zeros((ROWS, LANES), jnp.float32)
         for j in range(DEPTH):
             out[j * ny : (j + 1) * ny, :] = coefs[j]
@@ -114,11 +140,14 @@
             lower = (flux[j] - flux[j - 1]) if j else flux[j]
             inner = inner_rhs(jnp.where(top, coefs[j + 1], coefs[j]), vy, vz)
             out[(RHS + j) * ny : (RHS + j + 1) * ny, :] = jnp.where(top, upper, lower) + inner
-            columns = jnp.where(lanes == j, roll_lanes(vz, j + 1), columns)
+            for t in range(ny // ROWS):
+                lane = DEPTH * t + j
+                columns = jnp.where(lanes == lane, roll_lanes(vz[t * ROWS : (t + 1) * ROWS], lane + 1), columns)
             lines = jnp.where(rows == j, roll_rows(vy[ny - ROWS :], j + 1), lines)
         out[VX * ny : (VX + 1) * ny, :] = held_vel[turn, 0, DEPTH - 1]
-        out[VZ * ny : (VZ + 1) * ny, :] = columns
-        out[VY * ny :, :] = lines
+        out[VY * ny : VY * ny + ROWS, :] = lines
+        out[VY * ny + ROWS :, :] = columns
+        clear_if_alone("gx", turn, out)
 
 
 def load(phase, press, vel, after, coef, press_out, vel_out, rhs, held, sem):
@@ -194,13 +223,20 @@
             place = (0, plane - self.nx - DEPTH - 1)
         return place if 0 <= place[1] < DEPTH - 1 else None
 
-    def vz_end(self, plane):
+    def columns(self):
+        at = VY * self.ny + ROWS
+        return sides(self.even, self.got_x, lambda ref: ref[at : at + ROWS, :])
+
+    def vz_end(self, plane, lane):
         if plane < self.nx:
-            return self.vel[2, plane], LANES - 1
+            return roll_lanes(self.vel[2, plane], lane + 1)
         place = self.layer(plane)
         if place is None:
-            return jnp.zeros((self.ny, LANES), jnp.float32), 0
-        return self.halo(VZ)[place[0]], place[1]
+            return jnp.zeros((self.ny, LANES), jnp.float32)
+        source = self.columns()[place[0]]
+        return jnp.concatenate(
+            [roll_lanes(source, lane - DEPTH * t - place[1]) for t in range(self.ny // ROWS)], 0
+        )
 
     def vy_end(self, plane):
         if plane < self.nx:
@@ -221,7 +257,7 @@
         row = pl.multiple_of(jnp.where(top, ny - ROWS, 0), ROWS)
         block = Block(nx, ny, coef, vel, rhs, got_x, row, ROWS)
         columns = jnp.zeros((ROWS, LANES), jnp.float32)
-        low_end, high_end = block.halo(VZ)
+        ends = block.columns()
         for plane in range(total):
             one, two = block.coef(plane), block.rhs(plane)
             one = jnp.where(top, roll_rows(one, DEPTH), one)
@@ -229,23 +265,24 @@
             tile = jnp.where(rows < DEPTH, one, two)
             out[plane] = jnp.where(rows == ROWS - 1, block.vy_end(plane), tile)
             if plane < nx:
-                source, lane = vel[2, plane, pl.ds(row, ROWS), :], LANES - 1
+                source = roll_lanes(vel[2, plane, pl.ds(row, ROWS), :], plane + 1)
             elif block.layer(plane) is None:
                 continue
             else:
-                side, lane = block.layer(plane)
-                source = (low_end, high_end)[side]
-            columns = jnp.where(lanes == plane, roll_lanes(source, plane - lane), columns)
+                side, layer = block.layer(plane)
+                high = (plane - layer - DEPTH * (ny // ROWS - 1)) % LANES
+                source = pltpu.roll(ends[side], jnp.where(top, high, (plane - layer) % LANES), 1)
+            columns = jnp.where(lanes == plane, source, columns)
         out[total + nx // ROWS] = jnp.where(top, roll_rows(columns, DEPTH - 1), columns)
         for plane in range(nx):
             tile = press[plane, pl.ds(row, ROWS), :]
             edge = jnp.where(top, tile[ROWS - 1 : ROWS], tile[0:1])
             out[total + plane // ROWS, plane % ROWS : plane % ROWS + 1, :] = edge
+        clear_if_alone("gy", turn, out)
 
 
 def tall_end(block, tile_end, plane, lane):
-    source, at = block.vz_end(plane)
-    return jnp.concatenate([roll_lanes(source, lane - at), roll_lanes(tile_end, lane - plane)], 0)
+    return jnp.concatenate([block.vz_end(plane, lane), roll_lanes(tile_end, lane - plane)], 0)
 
 
 def tile_of_ends(nx, even_y, got_y):
@@ -309,6 +346,7 @@
         made[turn][groups // 2] = jnp.concatenate([value, made[turn][groups // 2][ny:]], 0)
         for which, value in enumerate(made[turn]):
             send[which] = value
+        clear_if_alone("gz", turn, send)
 
 
 def prepare(nx, ny, n_x, n_y, coef, vel, rhs, full_coef, full_rhs, *refs):
@@ -604,7 +642,7 @@
         functools.partial(pack_x, nx, ny),
         inputs,
         [HBM] * 3,
-        [f32(VY * ny + ROWS, nz)] * n_x,
+        [f32(VY * ny + 2 * ROWS, nz)] * n_x,
         "pack_x",
         [pltpu.VMEM((n_x, DEPTH, ny, nz), jnp.int32), scratch(n_x, 3, DEPTH, ny, nz)]
         + [pltpu.SemaphoreType.DMA((n_x, 3))],

time: 38.1 us -> 35.5 us (0.932)
  blocking collectives: 15.8 us -> 11.8 us
  waiting for transfers between devices: 4.48 us -> 6.81 us
  starting transfers between devices: 8.89 us -> 7.9 us
    all_to_all x1, blocking collectives: 15.8 us -> 11.8 us  [on_device(): gathered = lax.all_to_all(spread, AXES, 0, 0).reshape(devices, LANES)]
    ppermute x5, waiting for transfers between devices: 4.48 us -> 6.81 us  [exchange(): lax.ppermute(send, AXES, swaps(axis, turn))]
    ppermute x5, starting transfers between devices: 8.89 us -> 7.9 us  [exchange(): lax.ppermute(send, AXES, swaps(axis, turn))]
where the time goes in v5:
time: 35.5 us; the launch traced here: 35.3 us
  blocking collectives  11.8 us (33%)
  Pallas kernels  8.06 us (23%)
  starting transfers between devices  7.9 us (22%)
  waiting for transfers between devices  6.81 us (19%)
  between operations  0.69 us (2%)
    all_to_all x1, blocking collectives, on_device(): gathered = lax.all_to_all(spread, AXES, 0, 0).reshape(devices, LANES)  11.8 us
    pallas_call x7, Pallas kernels, call(): pl.pallas_call(kernel, out_shape=shapes, in_specs=in_specs, out_specs=[ou...  8.06 us
    ppermute x5, starting transfers between devices, exchange(): lax.ppermute(send, AXES, swaps(axis, turn))  7.9 us
    ppermute x5, waiting for transfers between devices, exchange(): lax.ppermute(send, AXES, swaps(axis, turn))  6.81 us
  transfers between devices with their start and end apart: 5, of which 3 were waited for; matrix products, arithmetic and copies ran while one was open for 0% of the time, Pallas kernels for 7%

profile of v5, /device:TPU:0, one launch (start us, length us, event | category | flops | bytes accessed | tf_op | source)
XLA Modules:
  0.0 35.3 jit_solution(6761652764084989185)
XLA Ops:
  0.6 1.3 %pack_x.1 = (f32[304,128]{1,0:T(8,128)S(1)}, f32[304,128]{1,0:T(8,128)S(1)}) custom-call(s32[16,32,128]{2,1,0:T(8,128)} %phase.3, f32[16,32,128]{2,1,0:T(8,128)} %press.3, f32[3,16,32,128]{3,2,1,0:T(8,128)} %vel.3), custom_call_target="tpu_custom_call" | custom-call | flops 3000000 | bytes 3000000 | tf_op jit(solution)/shard_map/pack_x/pallas_call | solution.py:630
  1.9 0.5 %collective-permute-start.1 = (f32[304,128]{1,0:T(8,128)S(1)}, f32[304,128]{1,0:T(8,128)S(1)}, u32[]{:S(2)}, u32[]{:S(2)}) collective-permute-start(f32[304,128]{1,0:T(8,128)S(1)} %get-tuple-element.26), channel_id=1, source_target_pairs={{0,2},{1,3},{2,0},{3,1},{4,6},{5,7},{6,4},{7,5},{8,16},{9,17},{10,... | collective-permute-start | bytes 466952 | tf_op jit(solution)/shard_map/ppermute | solution.py:43
  2.5 4.1 %collective-permute-start = (f32[304,128]{1,0:T(8,128)S(1)}, f32[304,128]{1,0:T(8,128)S(1)}, u32[]{:S(2)}, u32[]{:S(2)}) collective-permute-start(f32[304,128]{1,0:T(8,128)S(1)} %get-tuple-element.21.after), channel_id=1, source_target_pairs={{0,8},{1,9},{2,10},{3,11},{4,12},{5,13},{6,14},{7,15},{8,0},{9,1},... | collective-permute-start | bytes 466952 | tf_op jit(solution)/shard_map/ppermute | solution.py:43
  6.6 1.6 %load.1 = (f32[16,32,128]{2,1,0:T(8,128)S(1)}, f32[16,32,128]{2,1,0:T(8,128)S(1)}, f32[3,16,32,128]{3,2,1,0:T(8,128)S(1)}, f32[16,32,128]{2,1,0:T(8,128)S(1)}) custom-call(s32[16,32,128]{2,1,0:T(8,128)} %phase.3, f32[16,32,128]{2,1,0:T(8,128)} %press.3, f32[3,16,32,128]{3,2,1,0:T(8,128)} %vel.3, f32[304,128]{1,0:T(8,128)S(1)} %get-tuple-element.21.after), custom_call_target="tpu_custom_call" | custom-call | flops 3000000 | bytes 3000000 | tf_op jit(solution)/shard_map/load/pallas_call | solution.py:630
  8.2 0.0 collective-permute-done.1.refs_1_
  8.2 2.1 %collective-permute-done.refs_0_ = f32[304,128]{1,0:T(8,128)S(1)} collective-permute-done((f32[304,128]{1,0:T(8,128)S(1)}, f32[304,128]{1,0:T(8,128)S(1)}, u32[]{:S(2)}, u32[]{:S(2)}) %collective-permute-start) | collective-permute-done | bytes 155680 | tf_op jit(solution)/shard_map/ppermute | solution.py:43
  10.3 0.2 pack_y.1
  10.5 0.1 collective-permute-start.2
  10.6 1.6 %collective-permute-start.3 = (f32[27,8,128]{2,1,0:T(8,128)S(1)}, f32[27,8,128]{2,1,0:T(8,128)S(1)}, u32[]{:S(2)}, u32[]{:S(2)}) collective-permute-start(f32[27,8,128]{2,1,0:T(8,128)S(1)} %get-tuple-element.28), channel_id=1, source_target_pairs={{0,1},{1,0},{2,4},{3,5},{4,2},{5,3},{6,7},{7,6},{8,9},{9,8},{10,12... | collective-permute-start | bytes 331784 | tf_op jit(solution)/shard_map/ppermute | solution.py:43
  12.2 0.0 collective-permute-done.2.refs_2_
  12.2 3.2 %collective-permute-done.3.refs_3_ = f32[27,8,128]{2,1,0:T(8,128)S(1)} collective-permute-done((f32[27,8,128]{2,1,0:T(8,128)S(1)}, f32[27,8,128]{2,1,0:T(8,128)S(1)}, u32[]{:S(2)}, u32[]{:S(2)}) %collective-permute-start.3) | collective-permute-done | bytes 110624 | tf_op jit(solution)/shard_map/ppermute | solution.py:43
  15.4 0.5 %pack_z.1 = (f32[24,40,128]{2,1,0:T(8,128)S(1)}, f32[24,40,128]{2,1,0:T(8,128)S(1)}, f32[2,40,128]{2,1,0:T(8,128)S(1)}) custom-call(f32[16,32,128]{2,1,0:T(8,128)S(1)} %get-tuple-element.22.coef, f32[16,32,128]{2,1,0:T(8,128)S(1)} %get-tuple-element.25.press, f32[3,16,32,128]{3,2,1,0:T(8,128)S(1)} %get-tuple-element.23.vel, ...), custom_call_target="tpu_custom_call" | custom-call | flops 3000000 | bytes 3000000 | tf_op jit(solution)/shard_map/pack_z/pallas_call | solution.py:630
  15.9 1.6 %collective-permute-start.4 = (f32[2,40,128]{2,1,0:T(8,128)S(1)}, f32[2,40,128]{2,1,0:T(8,128)S(1)}, u32[]{:S(2)}, u32[]{:S(2)}) collective-permute-start(f32[2,40,128]{2,1,0:T(8,128)S(1)} %get-tuple-element.36), channel_id=1, source_target_pairs={{0,1},{1,0},{2,3},{3,2},{4,5},{5,4},{6,7},{7,6},{8,9},{9,8},{10,11... | collective-permute-start | bytes 122888 | tf_op jit(solution)/shard_map/ppermute | solution.py:43
  17.5 1.0 %prepare.1 = (f32[24,40,128]{2,1,0:T(8,128)S(1)}, f32[2,24,40,128]{3,2,1,0:T(8,128)S(1)}, f32[2,24,40,128]{3,2,1,0:T(8,128)S(1)}, f32[24,40,128]{2,1,0:T(8,128)S(1)}, f32[3,3,40,128]{3,2,1,0:T(8,128)S(1)}) custom-call(f32[16,32,128]{2,1,0:T(8,128)S(1)} %get-tuple-element.22.coef, f32[3,16,32,128]{3,2,1,0:T(8,128)S(1)} %get-tuple-element.23.vel, ...), custom_call_target="tpu_custom_call" | custom-call | flops 3000000 | bytes 3000000 | tf_op jit(solution)/shard_map/prepare/pallas_call | solution.py:630
  18.5 1.5 %collective-permute-done.4.refs_0_.refs_4_ = f32[2,40,128]{2,1,0:T(8,128)S(1)} collective-permute-done((f32[2,40,128]{2,1,0:T(8,128)S(1)}, f32[2,40,128]{2,1,0:T(8,128)S(1)}, u32[]{:S(2)}, u32[]{:S(2)}) %collective-permute-start.4) | collective-permute-done | bytes 40992 | tf_op jit(solution)/shard_map/ppermute | solution.py:43
  20.0 1.9 %krylov.1 = (f32[3,24,40,128]{3,2,1,0:T(8,128)S(1)}, f32[4,3,40,128]{3,2,1,0:T(8,128)S(1)}, f32[1,128]{1,0:T(1,128)S(1)}) custom-call(f32[24,40,128]{2,1,0:T(8,128)S(1)} %get-tuple-element.31.wx, f32[2,24,40,128]{3,2,1,0:T(8,128)S(1)} %get-tuple-element.32.wy, f32[2,24,40,128]{3,2,1,0:T(8,128)S(1)} %get-tuple-element.33.wz, ...), custom_call_target="tpu_custom_call" | custom-call | flops 3000000 | bytes 3000000 | tf_op jit(solution)/shard_map/krylov/pallas_call | solution.py:630
  21.9 11.8 %all_to_all.5 = f32[32,1,128]{2,1,0:T(1,128)S(1)} all-to-all(f32[32,1,128]{2,1,0:T(1,128)S(1)} %broadcast_in_dim.9), channel_id=1, replica_groups=mesh['gx'=4,'gy'=4,'gz'=2] {'gx','gy','gz'}, dimensions={0} | all-to-all | bytes 32768 | tf_op jit(solution)/shard_map/all_to_all | solution.py:693
  33.8 1.6 %finish.1 = (f32[3,16,32,128]{3,2,1,0:T(8,128)}, f32[16,32,128]{2,1,0:T(8,128)}) custom-call(f32[32,128]{1,0:T(8,128)S(1)} %bitcast.2, f32[16,32,128]{2,1,0:T(8,128)S(1)} %get-tuple-element.25.press, f32[3,16,32,128]{3,2,1,0:T(8,128)S(1)} %get-tuple-element.23.vel, f32[3,24,40,128]{3,2,1,0:T(8,128)S(1)} %get-tuple-element.38.basis, ...), custom_call_target="tpu_custom_call" | custom-call | flops 3000000 | bytes 3000000 | tf_op jit(solution)/shard_map/finish/pallas_call | solution.py:630
  (1 shorter events, 0.0 us)
Async XLA Ops:
  1.9 6.3 %collective-permute-start.1 = (f32[304,128]{1,0:T(8,128)S(1)}, f32[304,128]{1,0:T(8,128)S(1)}, u32[]{:S(2)}, u32[]{:S(2)}) collective-permute-start(f32[304,128]{1,0:T(8,128)S(1)} %get-tuple-element.26), channel_id=1, source_target_pairs={{0,2},{1,3},{2,0},{3,1},{4,6},{5,7},{6,4},{7,5},{8,16},{9,17},{10,... | collective-permute-start | bytes 466952 | tf_op jit(solution)/shard_map/ppermute | solution.py:43
  2.5 7.9 %collective-permute-start = (f32[304,128]{1,0:T(8,128)S(1)}, f32[304,128]{1,0:T(8,128)S(1)}, u32[]{:S(2)}, u32[]{:S(2)}) collective-permute-start(f32[304,128]{1,0:T(8,128)S(1)} %get-tuple-element.21.after), channel_id=1, source_target_pairs={{0,8},{1,9},{2,10},{3,11},{4,12},{5,13},{6,14},{7,15},{8,0},{9,1},... | collective-permute-start | bytes 466952 | tf_op jit(solution)/shard_map/ppermute | solution.py:43
  10.5 1.7 %collective-permute-start.2 = (f32[27,8,128]{2,1,0:T(8,128)S(1)}, f32[27,8,128]{2,1,0:T(8,128)S(1)}, u32[]{:S(2)}, u32[]{:S(2)}) collective-permute-start(f32[27,8,128]{2,1,0:T(8,128)S(1)} %get-tuple-element.27), channel_id=1, source_target_pairs={{0,2},{1,3},{2,0},{3,1},{4,6},{5,7},{6,4},{7,5},{8,10},{9,11},{10,... | collective-permute-start | bytes 331784 | tf_op jit(solution)/shard_map/ppermute | solution.py:43
  10.6 4.8 %collective-permute-start.3 = (f32[27,8,128]{2,1,0:T(8,128)S(1)}, f32[27,8,128]{2,1,0:T(8,128)S(1)}, u32[]{:S(2)}, u32[]{:S(2)}) collective-permute-start(f32[27,8,128]{2,1,0:T(8,128)S(1)} %get-tuple-element.28), channel_id=1, source_target_pairs={{0,1},{1,0},{2,4},{3,5},{4,2},{5,3},{6,7},{7,6},{8,9},{9,8},{10,12... | collective-permute-start | bytes 331784 | tf_op jit(solution)/shard_map/ppermute | solution.py:43
  15.9 4.1 %collective-permute-start.4 = (f32[2,40,128]{2,1,0:T(8,128)S(1)}, f32[2,40,128]{2,1,0:T(8,128)S(1)}, u32[]{:S(2)}, u32[]{:S(2)}) collective-permute-start(f32[2,40,128]{2,1,0:T(8,128)S(1)} %get-tuple-element.36), channel_id=1, source_target_pairs={{0,1},{1,0},{2,3},{3,2},{4,5},{5,4},{6,7},{7,6},{8,9},{9,8},{10,11... | collective-permute-start | bytes 122888 | tf_op jit(solution)/shard_map/ppermute | solution.py:43

commit v6 on v5

--- a/solution.py
+++ b/solution.py
@@ -349,28 +349,61 @@
         clear_if_alone("gz", turn, send)
 
 
+def tree_sum(parts):
+    while len(parts) > 1:
+        parts = [parts[i] + parts[i + 1] if i + 1 < len(parts) else parts[i] for i in range(0, len(parts), 2)]
+    return parts[0]
+
+
+class Totals:
+    def __init__(self):
+        self.stack = []
+
+    def add(self, tile):
+        level = 0
+        while self.stack and self.stack[-1][0] == level:
+            tile = self.stack.pop()[1] + tile
+            level += 1
+        self.stack.append((level, tile))
+
+    def value(self):
+        tiles = [tile for _, tile in self.stack]
+        total = tiles.pop()
+        while tiles:
+            total = tiles.pop() + total
+        return total
+
+
 def prepare(nx, ny, n_x, n_y, coef, vel, rhs, full_coef, full_rhs, *refs):
     got_x, got_y = refs[:n_x], refs[n_x : n_x + n_y]
-    wx, wy, wz, diag_out, ends = refs[n_x + n_y :]
+    basis, ends, shares, wx, wy, wz, inverse = refs[n_x + n_y :]
     total, height = nx + 2 * DEPTH, ny + 2 * DEPTH
     groups = total // ROWS
     lanes = lane_index((height, LANES))
     block = Block(nx, ny, coef, vel, rhs, got_x)
     tile_end = tile_of_ends(nx, even("gy"), got_y)
     for group in range(groups):
-        made = [jnp.zeros((height, LANES), jnp.float32) for _ in range(3)]
+        made = [jnp.zeros((height, LANES), jnp.float32) for _ in range(5)]
         for seat in range(ROWS):
             plane = seat * groups + group
             at = GROUP * seat
-            upper = (lanes >= at) & (lanes < at + DEPTH)
-            lower = (lanes >= at + 3 * DEPTH) & (lanes < at + GROUP)
             for which, source in enumerate((full_coef[plane], full_rhs[plane])):
-                value = jnp.where(upper, roll_lanes(source, at + DEPTH), made[which])
-                made[which] = jnp.where(lower, roll_lanes(source, at + 3 * DEPTH), value)
-            end = tall_end(block, tile_end, plane, at + DEPTH - 1)
-            made[2] = jnp.where(lanes == at + DEPTH - 1, end, made[2])
-        for which in range(3):
+                here = (lanes >= at + DEPTH) & (lanes < at + GROUP)
+                made[2 * which] = jnp.where(here, roll_lanes(source, at + DEPTH), made[2 * which])
+                here = (lanes >= at) & (lanes < at + GROUP - DEPTH)
+                made[2 * which + 1] = jnp.where(here, roll_lanes(source, at + GROUP - DEPTH), made[2 * which + 1])
+            lane = at + GROUP - DEPTH - 1
+            made[4] = jnp.where(lanes == lane, tall_end(block, tile_end, plane, lane), made[4])
+        for which in range(5):
             ends[which, group] = made[which]
+    totals = [Totals() for _ in range(6)]
+    trusted = (lanes[:ROWS] >= DEPTH) & (lanes[:ROWS] < LANES - DEPTH)
+
+    def count(which, left, right):
+        product = left[:ny] * right[:ny]
+        tile = tree_sum([product[i : i + ROWS] for i in range(0, ny, ROWS)])
+        totals[which].add(jnp.where(trusted, tile, 0.0))
+
     old_weight = None
     here = full_coef[nx + DEPTH]
     for x in range(-DEPTH, nx + DEPTH - 1):
@@ -383,117 +416,16 @@
             right = jnp.where(lanes == LANES - 1, 0.0, 0.5 * (here + roll_lanes(here, -1)))
             left = jnp.where(lanes == 0, 0.0, 0.5 * (here + roll_lanes(here, 1)))
             wy[0, e], wy[1, e], wz[0, e], wz[1, e] = up, down, right, left
-            diag_out[e] = jnp.where(here > 0, (weight + old_weight) + (up + down) + (right + left), 0.0)
+            diag = (weight + old_weight) + (up + down) + (right + left)
+            inside = here > 0
+            scale = jnp.where(inside, 1.0 / jnp.where(inside, diag, 1.0), 0.0)
+            inverse[e] = scale
+            source = full_rhs[e]
+            field = scale * source
+            basis[0, e] = field
+            if 0 <= x < nx:
+                count(0, field, source)
         old_weight, here = weight, above
-
-
-def tree_sum(parts):
-    while len(parts) > 1:
-        parts = [parts[i] + parts[i + 1] if i + 1 < len(parts) else parts[i] for i in range(0, len(parts), 2)]
-    return parts[0]
-
-
-class Totals:
-    def __init__(self):
-        self.stack = []
-
-    def add(self, tile):
-        level = 0
-        while self.stack and self.stack[-1][0] == level:
-            tile = self.stack.pop()[1] + tile
-            level += 1
-        self.stack.append((level, tile))
-
-    def value(self):
-        tiles = [tile for _, tile in self.stack]
-        total = tiles.pop()
-        while tiles:
-            total = tiles.pop() + total
-        return total
-
-
-def krylov(nx, ny, n_z, wx, wy, wz, diag_in, rhs_in, ends, *refs):
-    got_z = refs[:n_z]
-    basis, basis_z, sums = refs[n_z : n_z + 3]
-    inverse, pw, pinv, spill = refs[n_z + 3 :]
-    even_z = even("gz")
-    total, height = nx + 2 * DEPTH, ny + 2 * DEPTH
-    groups = total // ROWS
-    lanes = lane_index((height, LANES))
-    seat_lane = lanes % GROUP
-    edge = (lanes == 0) | (lanes == LANES - 1)
-
-    def along(planes, group, step):
-        if 0 <= group + step < groups:
-            return planes[group + step]
-        return roll_lanes(planes[(group + step) % groups], -GROUP * step)
-
-    def spilled(which, group, up, down):
-        spill[which, group] = jnp.where(seat_lane == 10, roll_lanes(up, 7), down)
-
-    coef, rhs_z, vz = [], [], []
-    for g in range(groups):
-        low, high = sides(even_z, got_z, lambda ref: ref[g // 2])
-        skip = ROWS * (g % 2)
-        above = (seat_lane >= DEPTH) & (seat_lane < 2 * DEPTH)
-        below = (seat_lane >= 2 * DEPTH) & (seat_lane < 3 * DEPTH)
-        value = jnp.where(above, roll_lanes(high, DEPTH - skip), ends[0, g])
-        coef.append(jnp.where(below, roll_lanes(low, 2 * DEPTH - skip), value))
-        value = jnp.where(above, roll_lanes(high, -skip), ends[1, g])
-        rhs_z.append(jnp.where(below, roll_lanes(low, DEPTH + 1 - skip), value))
-        vz.append(jnp.where(below, roll_lanes(low, DEPTH - skip), ends[2, g]))
-    for g in range(groups):
-        here = coef[g]
-        neighbours = (along(coef, g, 1), along(coef, g, -1), roll_rows(here, -1), roll_rows(here, 1))
-        neighbours += (roll_lanes(here, -1), roll_lanes(here, 1))
-        weights = [0.5 * (here + other) for other in neighbours]
-        for which, weight in enumerate(weights):
-            pw[which, g] = weight
-        diag = (weights[0] + weights[1]) + (weights[2] + weights[3]) + (weights[4] + weights[5])
-        face = (seat_lane == DEPTH - 1) | (seat_lane == 3 * DEPTH - 1)
-        next_face = (seat_lane == DEPTH) | (seat_lane == 3 * DEPTH)
-        fz = weights[4] * vz[g]
-        spilled(0, g, weights[4], weights[4])
-        spilled(1, g, fz, -fz)
-        rhs = rhs_z[g] + jnp.where(face, fz, 0.0)
-        rhs = rhs - jnp.where(next_face, weights[5] * roll_lanes(vz[g], 1), 0.0)
-        inside = here > 0
-        scale = jnp.where(inside, 1.0 / jnp.where(inside, diag, 1.0), 0.0)
-        pinv[g] = scale
-        basis_z[0, g] = scale * rhs
-        basis_z[3, g] = vz[g]
-    for n in range(3):
-        field = [basis_z[n, g] for g in range(groups)]
-        for g in range(groups):
-            here = field[g]
-            fz = pw[4, g] * (roll_lanes(here, -1) - here)
-            spilled(2 + n, g, -fz, fz)
-            if n < 2:
-                image = pw[0, g] * (here - along(field, g, 1)) + pw[1, g] * (here - along(field, g, -1))
-                image = image + (pw[2, g] * (here - roll_rows(here, -1)) + pw[3, g] * (here - roll_rows(here, 1)))
-                image = image + (pw[5, g] * (here - roll_lanes(here, 1)) - fz)
-                basis_z[n + 1, g] = pinv[g] * image
-
-    def inject(which, plane):
-        group, seat = plane % groups, plane // groups
-        return jnp.where(edge, roll_lanes(spill[which, group], LANES - 1 - 10 - GROUP * seat), 0.0)
-
-    totals = [Totals() for _ in range(6)]
-
-    def count(which, left, right):
-        product = left[:ny] * right[:ny]
-        totals[which].add(tree_sum([product[i : i + ROWS] for i in range(0, ny, ROWS)]))
-
-    for x in range(-DEPTH + 1, nx + DEPTH - 1):
-        e = x % total
-        diag, rhs = diag_in[e], rhs_in[e] + inject(1, e)
-        inside = diag > 0
-        scale = jnp.where(inside, 1.0 / jnp.where(inside, diag + inject(0, e), 1.0), 0.0)
-        inverse[e] = scale
-        field = scale * rhs
-        basis[0, e] = field
-        if 0 <= x < nx:
-            count(0, field, rhs)
     for n in range(3):
         reach = 2 - n
         old_flux = None
@@ -503,7 +435,7 @@
             above = basis[n, (e + 1) % total]
             flux = wx[e] * (above - here)
             if x >= -reach:
-                image = (old_flux - flux) + inject(2 + n, e)
+                image = old_flux - flux
                 image = image + (
                     wy[0, e] * (here - roll_rows(here, -1)) + wy[1, e] * (here - roll_rows(here, 1))
                 )
@@ -519,15 +451,95 @@
                     if own:
                         count(2 * n + 2, following, image)
             old_flux, here = flux, above
+    for which, total_ in enumerate(totals):
+        shares[which] = total_.value()
+
+
+def join(nx, ny, n_z, ends, shares, *refs):
+    got_z = refs[:n_z]
+    basis_z, vz_z, sums, weight_z, inverse_z = refs[n_z:]
+    total, height = nx + 2 * DEPTH, ny + 2 * DEPTH
+    groups = total // ROWS
+    lanes = lane_index((height, LANES))
+    seat_lane, seat = lanes % GROUP, lanes // GROUP
+    coef, rhs, vz = [], [], []
+    for side in range(2):
+        for g in range(groups):
+            got = sides(even("gz"), got_z, lambda ref: ref[g // 2])[side]
+            skip = ROWS * (g % 2)
+            if side == 0:
+                outer = seat_lane < DEPTH
+                coef.append(jnp.where(outer, roll_lanes(got, -skip), ends[0, g]))
+                rhs.append(jnp.where(outer, roll_lanes(got, 1 - DEPTH - skip), ends[2, g]))
+                vz.append(roll_lanes(got, -DEPTH - skip))
+                vz_z[g] = vz[-1]
+            else:
+                outer = seat_lane >= GROUP - DEPTH
+                coef.append(jnp.where(outer, roll_lanes(got, GROUP - DEPTH - skip), ends[1, g]))
+                rhs.append(jnp.where(outer, roll_lanes(got, GROUP - 2 * DEPTH - skip), ends[3, g]))
+                vz.append(ends[4, g])
+
+    def along(planes, q, step):
+        g = q % groups
+        if 0 <= g + step < groups:
+            return planes[q + step]
+        return roll_lanes(planes[q - g + (g + step) % groups], -GROUP * step)
+
+    totals = [Totals() for _ in range(6)]
+
+    def count(which, q, left, right):
+        first = DEPTH if q < groups else GROUP - 2 * DEPTH
+        spot = seat_lane[:ROWS]
+        mine = (spot >= first) & (spot < first + DEPTH) & (seat[:ROWS] * groups + q % groups < nx)
+        product = left[:ny] * right[:ny]
+        tile = tree_sum([product[i : i + ROWS] for i in range(0, ny, ROWS)])
+        totals[which].add(jnp.where(mine, tile, 0.0))
+
+    field = []
+    for q in range(2 * groups):
+        here = coef[q]
+        neighbours = (along(coef, q, 1), along(coef, q, -1), roll_rows(here, -1), roll_rows(here, 1))
+        neighbours += (roll_lanes(here, -1), roll_lanes(here, 1))
+        weights = [0.5 * (here + other) for other in neighbours]
+        for which, weight in enumerate(weights):
+            weight_z[which, q] = weight
+        diag = (weights[0] + weights[1]) + (weights[2] + weights[3]) + (weights[4] + weights[5])
+        face = DEPTH - 1 if q < groups else GROUP - DEPTH - 1
+        source = rhs[q] + jnp.where(seat_lane == face, weights[4] * vz[q], 0.0)
+        source = source - jnp.where(seat_lane == face + 1, weights[5] * roll_lanes(vz[q], 1), 0.0)
+        inside = here > 0
+        scale = jnp.where(inside, 1.0 / jnp.where(inside, diag, 1.0), 0.0)
+        inverse_z[q] = scale
+        field.append(scale * source)
+        basis_z[0, q] = field[q]
+        count(0, q, field[q], source)
+    for n in range(3):
+        following = []
+        for q in range(2 * groups):
+            here = field[q]
+            image = weight_z[0, q] * (here - along(field, q, 1)) + weight_z[1, q] * (here - along(field, q, -1))
+            image = image + (
+                weight_z[2, q] * (here - roll_rows(here, -1)) + weight_z[3, q] * (here - roll_rows(here, 1))
+            )
+            image = image + (
+                weight_z[4, q] * (here - roll_lanes(here, -1)) + weight_z[5, q] * (here - roll_lanes(here, 1))
+            )
+            count(2 * n + 1, q, here, image)
+            if n < 2:
+                following.append(inverse_z[q] * image)
+                basis_z[n + 1, q] = following[q]
+                count(2 * n + 2, q, following[q], image)
+        field = following
     lane = lane_index((1, LANES))
     row = jnp.zeros((1, LANES), jnp.float32)
     for which, total_ in enumerate(totals):
-        value = jnp.sum(jnp.sum(total_.value(), 0, keepdims=True), 1, keepdims=True)
+        value = total_.value() + shares[which]
+        value = jnp.sum(jnp.sum(value, 0, keepdims=True), 1, keepdims=True)
         row = jnp.where(lane == which, value, row)
     sums[...] = row
 
 
-def finish(nx, ny, n_x, n_y, n_z, gathered, press, vel, basis, basis_z, *refs):
+def finish(nx, ny, n_x, n_y, n_z, gathered, press, vel, basis, basis_z, vz_z, *refs):
     got_x, got_y, got_z = refs[:n_x], refs[n_x : n_x + n_y], refs[n_x + n_y : n_x + n_y + n_z]
     ustar_out, coef_out, ustar, coef_cot, sem = refs[n_x + n_y + n_z :]
     even_x, even_y, even_z = even("gx"), even("gy"), even("gz")
@@ -557,8 +569,13 @@
     seat_lane = lanes % GROUP
     spill = []
     for g in range(groups):
-        cells = c0 * basis_z[0, g] + c1 * basis_z[1, g] + c2 * basis_z[2, g]
-        spill.append(jnp.where(seat_lane == 10, roll_lanes(cells, 6), cells))
+        low, high = [
+            c0 * basis_z[0, q] + c1 * basis_z[1, q] + c2 * basis_z[2, q] for q in (g, groups + g)
+        ]
+        cells = jnp.where(seat_lane < DEPTH - 1, roll_lanes(high, DEPTH - GROUP + DEPTH - 1), roll_lanes(low, -1))
+        cells = jnp.where(seat_lane == 2 * DEPTH - 2, roll_lanes(high, 2 * DEPTH - 2 - (GROUP - DEPTH)), cells)
+        spill.append(jnp.where(seat_lane == 2 * DEPTH - 1, roll_lanes(low, DEPTH), cells))
+    spoiled = (lanes < DEPTH - 1) | (lanes > LANES - DEPTH)
     lanes = lane_index((ny, LANES))
     at_low, at_high = lanes == 0, lanes == LANES - 1
     low_z, high_z = sides(even_z, got_z, lambda ref: ref[groups // 2, :ny, :])
@@ -568,7 +585,8 @@
 
     def solved(x):
         e = x % total
-        return c0 * basis[0, e] + c1 * basis[1, e] + c2 * basis[2, e]
+        cells = c0 * basis[0, e] + c1 * basis[1, e] + c2 * basis[2, e]
+        return jnp.where(spoiled, roll_lanes(spill[e % groups], 1 - DEPTH - GROUP * (e // groups)), cells)
 
     copies = []
     rows = row_index((ROWS, LANES))
@@ -593,9 +611,8 @@
         ustar[1, x] = out
         back = roll_rows(u_tall, 1)[:ny] + (own - roll_rows(here, 1)[:ny])
         answer = answer + ((p - roll_rows(p_tall, -1)[:ny]) * out + (roll_rows(p_tall, 1)[:ny] - p) * back)
-        shift = LANES - 1 - 10 - GROUP * seat
-        lam_end = roll_lanes(spill[group][:ny], shift)
-        u_end = roll_lanes(basis_z[3, group, :ny, :], shift)
+        lam_end = roll_lanes(spill[group][:ny], 1 - 2 * DEPTH - GROUP * seat)
+        u_end = roll_lanes(vz_z[group, :ny, :], 1 - DEPTH - GROUP * seat)
         p_end = roll_lanes(press_z, LANES - 1 - press_lane(x))
         out = vel[2, x] + (jnp.where(at_high, lam_end, roll_lanes(own, -1)) - own)
         ustar[2, x] = out
@@ -673,28 +690,28 @@
         "pack_z",
     )
     got_z = exchange(to_z, "gz")
-    wx, wy, wz, diag, ends = call(
+    basis, ends, shares = call(
         functools.partial(prepare, nx, ny, n_x, n_y),
         [coef, vel, rhs, full_coef, full_rhs, *got_x, *got_y],
         [VMEM] * (5 + n_x + n_y),
-        [f32(*cube), f32(2, *cube), f32(2, *cube), f32(*cube), f32(3, groups, height, LANES)],
+        [f32(3, *cube), f32(5, groups, height, LANES), f32(6, ROWS, LANES)],
         "prepare",
+        [scratch(*cube), scratch(2, *cube), scratch(2, *cube), scratch(*cube)],
     )
-    basis, basis_z, sums = call(
-        functools.partial(krylov, nx, ny, n_z),
-        [wx, wy, wz, diag, full_rhs, ends, *got_z],
-        [VMEM] * (6 + n_z),
-        [f32(3, *cube), f32(4, groups, height, LANES), f32(1, LANES)],
-        "krylov",
-        [scratch(*cube), scratch(6, groups, height, LANES), scratch(groups, height, LANES)]
-        + [scratch(5, groups, height, LANES)],
+    basis_z, vz_z, sums = call(
+        functools.partial(join, nx, ny, n_z),
+        [ends, shares, *got_z],
+        [VMEM] * (2 + n_z),
+        [f32(3, 2 * groups, height, LANES), f32(groups, height, LANES), f32(1, LANES)],
+        "join",
+        [scratch(6, 2 * groups, height, LANES), scratch(2 * groups, height, LANES)],
     )
     spread = jnp.broadcast_to(sums[None], (devices, 1, LANES))
     gathered = lax.all_to_all(spread, AXES, 0, 0).reshape(devices, LANES)
     return call(
         functools.partial(finish, nx, ny, n_x, n_y, n_z),
-        [gathered, press, vel, basis, basis_z, *got_x, *got_y, *got_z],
-        [VMEM] * (5 + n_x + n_y + n_z),
+        [gathered, press, vel, basis, basis_z, vz_z, *got_x, *got_y, *got_z],
+        [VMEM] * (6 + n_x + n_y + n_z),
         [f32(*vel.shape), f32(nx, ny, nz)],
         "finish",
         [scratch(*vel.shape), scratch(nx, ny, nz), pltpu.SemaphoreType.DMA((2, nx // STRIDE))],

time: 35.5 us -> 34.6 us (0.975)
  waiting for transfers between devices: 6.81 us -> 5.74 us
    ppermute x5, waiting for transfers between devices: 6.81 us -> 5.74 us  [exchange(): lax.ppermute(send, AXES, swaps(axis, turn))]
  transfers between devices with their start and end apart: 5 -> 5, of which waited for: 3 -> 3; matrix products, arithmetic and copies ran while one was open for 0% -> 0% of each run, Pallas kernels for 7% -> 11%
where the time goes in v6:
time: 34.6 us; the launch traced here: 34.4 us
  blocking collectives  11.8 us (34%)
  Pallas kernels  8.23 us (24%)
  starting transfers between devices  7.9 us (23%)
  waiting for transfers between devices  5.74 us (17%)
  between operations  0.69 us (2%)
    all_to_all x1, blocking collectives, on_device(): gathered = lax.all_to_all(spread, AXES, 0, 0).reshape(devices, LANES)  11.8 us
    pallas_call x7, Pallas kernels, call(): pl.pallas_call(kernel, out_shape=shapes, in_specs=in_specs, out_specs=[ou...  8.23 us
    ppermute x5, starting transfers between devices, exchange(): lax.ppermute(send, AXES, swaps(axis, turn))  7.9 us
    ppermute x5, waiting for transfers between devices, exchange(): lax.ppermute(send, AXES, swaps(axis, turn))  5.74 us
  transfers between devices with their start and end apart: 5, of which 3 were waited for; matrix products, arithmetic and copies ran while one was open for 0% of the time, Pallas kernels for 11%

profile of v6, /device:TPU:0, one launch (start us, length us, event | category | flops | bytes accessed | tf_op | source)
XLA Modules:
  0.0 34.4 jit_solution(15256272789266820256)
XLA Ops:
  0.6 1.3 %pack_x.1 = (f32[304,128]{1,0:T(8,128)S(1)}, f32[304,128]{1,0:T(8,128)S(1)}) custom-call(s32[16,32,128]{2,1,0:T(8,128)} %phase.3, f32[16,32,128]{2,1,0:T(8,128)} %press.3, f32[3,16,32,128]{3,2,1,0:T(8,128)} %vel.3), custom_call_target="tpu_custom_call" | custom-call | flops 3000000 | bytes 3000000 | tf_op jit(solution)/shard_map/pack_x/pallas_call | solution.py:647
  1.9 0.5 %collective-permute-start.1 = (f32[304,128]{1,0:T(8,128)S(1)}, f32[304,128]{1,0:T(8,128)S(1)}, u32[]{:S(2)}, u32[]{:S(2)}) collective-permute-start(f32[304,128]{1,0:T(8,128)S(1)} %get-tuple-element.24), channel_id=1, source_target_pairs={{0,2},{1,3},{2,0},{3,1},{4,6},{5,7},{6,4},{7,5},{8,16},{9,17},{10,... | collective-permute-start | bytes 466952 | tf_op jit(solution)/shard_map/ppermute | solution.py:43
  2.5 4.1 %collective-permute-start = (f32[304,128]{1,0:T(8,128)S(1)}, f32[304,128]{1,0:T(8,128)S(1)}, u32[]{:S(2)}, u32[]{:S(2)}) collective-permute-start(f32[304,128]{1,0:T(8,128)S(1)} %get-tuple-element.19.after), channel_id=1, source_target_pairs={{0,8},{1,9},{2,10},{3,11},{4,12},{5,13},{6,14},{7,15},{8,0},{9,1},... | collective-permute-start | bytes 466952 | tf_op jit(solution)/shard_map/ppermute | solution.py:43
  6.6 1.6 %load.1 = (f32[16,32,128]{2,1,0:T(8,128)S(1)}, f32[16,32,128]{2,1,0:T(8,128)S(1)}, f32[3,16,32,128]{3,2,1,0:T(8,128)S(1)}, f32[16,32,128]{2,1,0:T(8,128)S(1)}) custom-call(s32[16,32,128]{2,1,0:T(8,128)} %phase.3, f32[16,32,128]{2,1,0:T(8,128)} %press.3, f32[3,16,32,128]{3,2,1,0:T(8,128)} %vel.3, f32[304,128]{1,0:T(8,128)S(1)} %get-tuple-element.19.after), custom_call_target="tpu_custom_call" | custom-call | flops 3000000 | bytes 3000000 | tf_op jit(solution)/shard_map/load/pallas_call | solution.py:647
  8.2 0.0 collective-permute-done.1.refs_1_
  8.2 2.1 %collective-permute-done.refs_0_ = f32[304,128]{1,0:T(8,128)S(1)} collective-permute-done((f32[304,128]{1,0:T(8,128)S(1)}, f32[304,128]{1,0:T(8,128)S(1)}, u32[]{:S(2)}, u32[]{:S(2)}) %collective-permute-start) | collective-permute-done | bytes 155680 | tf_op jit(solution)/shard_map/ppermute | solution.py:43
  10.3 0.2 pack_y.1
  10.5 0.1 collective-permute-start.2
  10.6 1.6 %collective-permute-start.3 = (f32[27,8,128]{2,1,0:T(8,128)S(1)}, f32[27,8,128]{2,1,0:T(8,128)S(1)}, u32[]{:S(2)}, u32[]{:S(2)}) collective-permute-start(f32[27,8,128]{2,1,0:T(8,128)S(1)} %get-tuple-element.26), channel_id=1, source_target_pairs={{0,1},{1,0},{2,4},{3,5},{4,2},{5,3},{6,7},{7,6},{8,9},{9,8},{10,12... | collective-permute-start | bytes 331784 | tf_op jit(solution)/shard_map/ppermute | solution.py:43
  12.2 0.0 collective-permute-done.2.refs_2_
  12.2 3.2 %collective-permute-done.3.refs_3_ = f32[27,8,128]{2,1,0:T(8,128)S(1)} collective-permute-done((f32[27,8,128]{2,1,0:T(8,128)S(1)}, f32[27,8,128]{2,1,0:T(8,128)S(1)}, u32[]{:S(2)}, u32[]{:S(2)}) %collective-permute-start.3) | collective-permute-done | bytes 110624 | tf_op jit(solution)/shard_map/ppermute | solution.py:43
  15.4 0.5 %pack_z.1 = (f32[24,40,128]{2,1,0:T(8,128)S(1)}, f32[24,40,128]{2,1,0:T(8,128)S(1)}, f32[2,40,128]{2,1,0:T(8,128)S(1)}) custom-call(f32[16,32,128]{2,1,0:T(8,128)S(1)} %get-tuple-element.20.coef, f32[16,32,128]{2,1,0:T(8,128)S(1)} %get-tuple-element.23.press, f32[3,16,32,128]{3,2,1,0:T(8,128)S(1)} %get-tuple-element.21.vel, ...), custom_call_target="tpu_custom_call" | custom-call | flops 3000000 | bytes 3000000 | tf_op jit(solution)/shard_map/pack_z/pallas_call | solution.py:647
  15.9 1.6 %collective-permute-start.4 = (f32[2,40,128]{2,1,0:T(8,128)S(1)}, f32[2,40,128]{2,1,0:T(8,128)S(1)}, u32[]{:S(2)}, u32[]{:S(2)}) collective-permute-start(f32[2,40,128]{2,1,0:T(8,128)S(1)} %get-tuple-element.31), channel_id=1, source_target_pairs={{0,1},{1,0},{2,3},{3,2},{4,5},{5,4},{6,7},{7,6},{8,9},{9,8},{10,11... | collective-permute-start | bytes 122888 | tf_op jit(solution)/shard_map/ppermute | solution.py:43
  17.5 2.1 %prepare.1 = (f32[3,24,40,128]{3,2,1,0:T(8,128)S(1)}, f32[5,3,40,128]{3,2,1,0:T(8,128)S(1)}, f32[6,8,128]{2,1,0:T(8,128)S(1)}) custom-call(f32[16,32,128]{2,1,0:T(8,128)S(1)} %get-tuple-element.20.coef, f32[3,16,32,128]{3,2,1,0:T(8,128)S(1)} %get-tuple-element.21.vel, f32[16,32,128]{2,1,0:T(8,128)S(1)} %get-tuple-element.22.rhs, ...), custom_call_target="tpu_custom_call" | custom-call | flops 3000000 | bytes 3000000 | tf_op jit(solution)/shard_map/prepare/pallas_call | solution.py:647
  19.6 0.4 %collective-permute-done.4.refs_0_.refs_4_ = f32[2,40,128]{2,1,0:T(8,128)S(1)} collective-permute-done((f32[2,40,128]{2,1,0:T(8,128)S(1)}, f32[2,40,128]{2,1,0:T(8,128)S(1)}, u32[]{:S(2)}, u32[]{:S(2)}) %collective-permute-start.4) | collective-permute-done | bytes 40992 | tf_op jit(solution)/shard_map/ppermute | solution.py:43
  20.0 0.7 %join.1 = (f32[3,6,40,128]{3,2,1,0:T(8,128)S(1)}, f32[3,40,128]{2,1,0:T(8,128)S(1)}, f32[1,128]{1,0:T(1,128)S(1)}) custom-call(f32[5,3,40,128]{3,2,1,0:T(8,128)S(1)} %get-tuple-element.29.ends, f32[6,8,128]{2,1,0:T(8,128)S(1)} %get-tuple-element.30.shares, f32[2,40,128]{2,1,0:T(8,128)S(1)} %collective-permute-done.4.refs_0_.refs_4_), custom_call_target="tpu_custom_call" | custom-call | flops 3000000 | bytes 3000000 | tf_op jit(solution)/shard_map/join/pallas_call | solution.py:647
  20.8 11.8 %all_to_all.5 = f32[32,1,128]{2,1,0:T(1,128)S(1)} all-to-all(f32[32,1,128]{2,1,0:T(1,128)S(1)} %broadcast_in_dim.9), channel_id=1, replica_groups=mesh['gx'=4,'gy'=4,'gz'=2] {'gx','gy','gz'}, dimensions={0} | all-to-all | bytes 32768 | tf_op jit(solution)/shard_map/all_to_all | solution.py:710
  32.6 1.8 %finish.1 = (f32[3,16,32,128]{3,2,1,0:T(8,128)}, f32[16,32,128]{2,1,0:T(8,128)}) custom-call(f32[32,128]{1,0:T(8,128)S(1)} %bitcast.2, f32[16,32,128]{2,1,0:T(8,128)S(1)} %get-tuple-element.23.press, f32[3,16,32,128]{3,2,1,0:T(8,128)S(1)} %get-tuple-element.21.vel, f32[3,24,40,128]{3,2,1,0:T(8,128)S(1)} %get-tuple-element.33.basis, ...), custom_call_target="tpu_custom_call" | custom-call | flops 3000000 | bytes 3000000 | tf_op jit(solution)/shard_map/finish/pallas_call | solution.py:647
  (1 shorter events, 0.0 us)
Async XLA Ops:
  1.9 6.3 %collective-permute-start.1 = (f32[304,128]{1,0:T(8,128)S(1)}, f32[304,128]{1,0:T(8,128)S(1)}, u32[]{:S(2)}, u32[]{:S(2)}) collective-permute-start(f32[304,128]{1,0:T(8,128)S(1)} %get-tuple-element.24), channel_id=1, source_target_pairs={{0,2},{1,3},{2,0},{3,1},{4,6},{5,7},{6,4},{7,5},{8,16},{9,17},{10,... | collective-permute-start | bytes 466952 | tf_op jit(solution)/shard_map/ppermute | solution.py:43
  2.5 7.9 %collective-permute-start = (f32[304,128]{1,0:T(8,128)S(1)}, f32[304,128]{1,0:T(8,128)S(1)}, u32[]{:S(2)}, u32[]{:S(2)}) collective-permute-start(f32[304,128]{1,0:T(8,128)S(1)} %get-tuple-element.19.after), channel_id=1, source_target_pairs={{0,8},{1,9},{2,10},{3,11},{4,12},{5,13},{6,14},{7,15},{8,0},{9,1},... | collective-permute-start | bytes 466952 | tf_op jit(solution)/shard_map/ppermute | solution.py:43
  10.5 1.7 %collective-permute-start.2 = (f32[27,8,128]{2,1,0:T(8,128)S(1)}, f32[27,8,128]{2,1,0:T(8,128)S(1)}, u32[]{:S(2)}, u32[]{:S(2)}) collective-permute-start(f32[27,8,128]{2,1,0:T(8,128)S(1)} %get-tuple-element.25), channel_id=1, source_target_pairs={{0,2},{1,3},{2,0},{3,1},{4,6},{5,7},{6,4},{7,5},{8,10},{9,11},{10,... | collective-permute-start | bytes 331784 | tf_op jit(solution)/shard_map/ppermute | solution.py:43
  10.6 4.8 %collective-permute-start.3 = (f32[27,8,128]{2,1,0:T(8,128)S(1)}, f32[27,8,128]{2,1,0:T(8,128)S(1)}, u32[]{:S(2)}, u32[]{:S(2)}) collective-permute-start(f32[27,8,128]{2,1,0:T(8,128)S(1)} %get-tuple-element.26), channel_id=1, source_target_pairs={{0,1},{1,0},{2,4},{3,5},{4,2},{5,3},{6,7},{7,6},{8,9},{9,8},{10,12... | collective-permute-start | bytes 331784 | tf_op jit(solution)/shard_map/ppermute | solution.py:43
  15.9 4.1 %collective-permute-start.4 = (f32[2,40,128]{2,1,0:T(8,128)S(1)}, f32[2,40,128]{2,1,0:T(8,128)S(1)}, u32[]{:S(2)}, u32[]{:S(2)}) collective-permute-start(f32[2,40,128]{2,1,0:T(8,128)S(1)} %get-tuple-element.31), channel_id=1, source_target_pairs={{0,1},{1,0},{2,3},{3,2},{4,5},{5,4},{6,7},{7,6},{8,9},{9,8},{10,11... | collective-permute-start | bytes 122888 | tf_op jit(solution)/shard_map/ppermute | solution.py:43

commit v7 on v6

--- a/solution.py
+++ b/solution.py
@@ -21,40 +21,43 @@
 PARAMS = pltpu.CompilerParams(vmem_limit_bytes=40 * 1024 * 1024)
 
 
-def swaps(axis, turn):
+def swaps(moves):
     sizes = [lax.axis_size(name) for name in AXES]
-    along, spare = AXES.index(axis), AXES.index(SPARE[axis])
     number = lambda place: (place[0] * sizes[1] + place[1]) * sizes[2] + place[2]
+    spare = AXES.index("gz" if len(moves) > 1 else SPARE[moves[0][0]])
     pairs = []
     for place in itertools.product(*map(range, sizes)):
-        partner = list(place)
-        other = place[along] + (1 if (place[along] - turn) % 2 == 0 else -1)
-        if 0 <= other < sizes[along]:
-            partner[along] = other
-        elif sizes[spare] % 2 == 0:
+        partner, met = list(place), True
+        for axis, turn in moves:
+            along = AXES.index(axis)
+            partner[along] += 1 if (place[along] - turn) % 2 == 0 else -1
+            met = met and 0 <= partner[along] < sizes[along]
+        if not met:
+            if sizes[spare] % 2:
+                continue
+            partner = list(place)
             partner[spare] ^= 1
-        else:
-            continue
         pairs.append((number(place), number(partner)))
     return pairs
 
 
-def exchange(sends, axis):
-    return [lax.ppermute(send, AXES, swaps(axis, turn)) for turn, send in enumerate(sends)]
-
-
-def clear_if_alone(axis, turn, out):
-    count, place = lax.axis_size(axis), lax.axis_index(axis)
-    alone = []
-    if turn == 1:
-        alone.append(place == 0)
-    if count % 2 != turn:
-        alone.append(place == count - 1)
-    for case in alone:
-
-        @pl.when(case)
-        def _():
-            out[...] = jnp.zeros(out.shape, out.dtype)
+def exchange(send, *moves):
+    return lax.ppermute(send, AXES, swaps(moves))
+
+
+def clear_if_alone(out, *moves):
+    for axis, turn in moves:
+        count, place = lax.axis_size(axis), lax.axis_index(axis)
+        alone = []
+        if turn == 1:
+            alone.append(place == 0)
+        if count % 2 != turn:
+            alone.append(place == count - 1)
+        for case in alone:
+
+            @pl.when(case)
+            def _():
+                out[...] = jnp.zeros(out.shape, out.dtype)
 
 
 def even(axis):
@@ -103,10 +106,10 @@
 RHS, VX, PRESS, VY = DEPTH, 2 * DEPTH - 1, 2 * DEPTH, 2 * DEPTH + 1
 
 
-def pack_x(nx, ny, phase, press, vel, *refs):
-    count = len(refs) - 3
-    outs = refs[:count]
-    held, held_vel, sem = refs[count:]
+def pack_first(nx, ny, n_x, n_y, phase, press, vel, *refs):
+    outs, odd_outs, (held, held_vel, sem) = refs[:n_x], refs[n_x:-3], refs[-3:]
+    if n_y > 1:
+        *odd_outs, tile_phase, tile_vel, tile_press, tile_sem = odd_outs
     copies = []
     for turn, out in enumerate(outs):
         top = even("gx") == (turn == 0)
@@ -119,6 +122,17 @@
         ]
         for which, (src, dst) in enumerate(parts):
             copy = pltpu.make_async_copy(src, dst, sem.at[turn, which])
+            copy.start()
+            copies.append(copy)
+    if n_y > 1:
+        row = pl.multiple_of(jnp.where(even("gy"), 0, ny - ROWS), ROWS)
+        parts = [
+            (phase.at[:, pl.ds(row, ROWS)], tile_phase),
+            (vel.at[:, :, pl.ds(row, ROWS)], tile_vel),
+            (press.at[:, pl.ds(row, ROWS)], tile_press),
+        ]
+        for which, (src, dst) in enumerate(parts):
+            copy = pltpu.make_async_copy(src, dst, tile_sem.at[which])
             copy.start()
             copies.append(copy)
     for copy in copies:
@@ -147,7 +161,84 @@
         out[VX * ny : (VX + 1) * ny, :] = held_vel[turn, 0, DEPTH - 1]
         out[VY * ny : VY * ny + ROWS, :] = lines
         out[VY * ny + ROWS :, :] = columns
-        clear_if_alone("gx", turn, out)
+        clear_if_alone(out, ("gx", turn))
+    if n_y > 1:
+        pack_odd(nx, tile_phase, tile_vel, tile_press, odd_outs)
+
+
+def row_tile(coef, rhs, vy, top):
+    rows = row_index((ROWS, LANES))
+    coef = jnp.where(top, roll_rows(coef, DEPTH), coef)
+    rhs = jnp.where(top, roll_rows(rhs, -1), roll_rows(rhs, DEPTH))
+    return jnp.where(rows == ROWS - 1, vy, jnp.where(rows < DEPTH, coef, rhs))
+
+
+def pack_odd(nx, tile_phase, tile_vel, tile_press, outs):
+    out, *corners = outs
+    top = jnp.logical_not(even("gy"))
+    lanes = lane_index((ROWS, LANES))
+    ends_at, vx_at = nx + nx // ROWS, nx + nx // ROWS + 1
+    ends = jnp.zeros((ROWS, LANES), jnp.float32)
+    here, old_flux = coefficient(tile_phase[0]), None
+    for x in range(nx):
+        vy, vz = tile_vel[1, x], tile_vel[2, x]
+        answer = inner_rhs(here, vy, vz)
+        if old_flux is not None:
+            answer = answer - old_flux
+        coef = here
+        if x + 1 < nx:
+            above = coefficient(tile_phase[x + 1])
+            old_flux = 0.5 * (here + above) * tile_vel[0, x]
+            answer = answer + old_flux
+            here = above
+        out[x] = row_tile(coef, answer, vy, top)
+        ends = jnp.where(lanes == x, roll_lanes(vz, x + 1), ends)
+        tile = tile_press[x]
+        at = nx + x // ROWS
+        out[at, x % ROWS : x % ROWS + 1, :] = jnp.where(top, tile[ROWS - 1 : ROWS], tile[0:1])
+    shift = lambda tile: jnp.where(top, roll_rows(tile, -1), roll_rows(tile, DEPTH))
+    ends = jnp.where(top, roll_rows(ends, DEPTH - 1), ends)
+    out[ends_at] = ends
+    out[vx_at] = shift(tile_vel[0, nx - 1])
+    for turn, corner in enumerate(corners):
+        first = jnp.where(even("gx") == (turn == 0), nx - DEPTH, 0)
+        for j in range(DEPTH):
+            corner[j] = out[first + j]
+        corner[DEPTH] = pltpu.roll(ends, jnp.where(first == 0, 0, (DEPTH - nx) % LANES), 1)
+        corner[DEPTH + 1] = out[vx_at]
+        clear_if_alone(corner, ("gx", turn), ("gy", 1))
+    clear_if_alone(out, ("gy", 1))
+
+
+def merge_odd(nx, got, *refs):
+    corners, out = refs[:-1], refs[-1]
+    total = nx + 2 * DEPTH
+    rows, lanes = row_index((ROWS, LANES)), lane_index((ROWS, LANES))
+    ends_at, vx_at = nx + nx // ROWS, nx + nx // ROWS + 1
+    low, high = zip(*[sides(even("gx"), corners, lambda ref: ref[j]) for j in range(DEPTH + 2)])
+    tiles = [got[x] for x in range(nx)] + list(high[:DEPTH]) + list(low[:DEPTH])
+    inner = (rows >= DEPTH) & (rows < ROWS - 1)
+
+    def face(below, above, vx):
+        weight = 0.5 * (tiles[below] + tiles[above])
+        weight = jnp.where(even("gy"), roll_rows(weight, DEPTH - 1), roll_rows(weight, DEPTH))
+        return jnp.where(inner, weight * vx, 0.0)
+
+    low_face, high_face = face(total - 1, 0, low[DEPTH + 1]), face(nx - 1, nx, got[vx_at])
+    for plane, tile in enumerate(tiles):
+        if plane == 0:
+            tile = tile - low_face
+        if plane == total - 1:
+            tile = tile + low_face
+        if plane == nx - 1:
+            tile = tile + high_face
+        if plane == nx:
+            tile = tile - high_face
+        out[plane] = tile
+    for at in range(nx // ROWS):
+        out[total + at] = got[nx + at]
+    ends = jnp.where(lanes < nx, got[ends_at], roll_lanes(high[DEPTH], nx))
+    out[total + nx // ROWS] = jnp.where(lanes < nx + DEPTH, ends, roll_lanes(low[DEPTH], nx + DEPTH))
 
 
 def load(phase, press, vel, after, coef, press_out, vel_out, rhs, held, sem):
@@ -249,36 +340,31 @@
 
 
 def pack_y(nx, ny, n_x, coef, press, vel, rhs, *refs):
-    got_x, outs = refs[:n_x], refs[n_x:]
+    got_x, out = refs[:n_x], refs[-1]
     total = nx + 2 * DEPTH
-    rows, lanes = row_index((ROWS, LANES)), lane_index((ROWS, LANES))
-    for turn, out in enumerate(outs):
-        top = even("gy") == (turn == 0)
-        row = pl.multiple_of(jnp.where(top, ny - ROWS, 0), ROWS)
-        block = Block(nx, ny, coef, vel, rhs, got_x, row, ROWS)
-        columns = jnp.zeros((ROWS, LANES), jnp.float32)
-        ends = block.columns()
-        for plane in range(total):
-            one, two = block.coef(plane), block.rhs(plane)
-            one = jnp.where(top, roll_rows(one, DEPTH), one)
-            two = jnp.where(top, roll_rows(two, -1), roll_rows(two, DEPTH))
-            tile = jnp.where(rows < DEPTH, one, two)
-            out[plane] = jnp.where(rows == ROWS - 1, block.vy_end(plane), tile)
-            if plane < nx:
-                source = roll_lanes(vel[2, plane, pl.ds(row, ROWS), :], plane + 1)
-            elif block.layer(plane) is None:
-                continue
-            else:
-                side, layer = block.layer(plane)
-                high = (plane - layer - DEPTH * (ny // ROWS - 1)) % LANES
-                source = pltpu.roll(ends[side], jnp.where(top, high, (plane - layer) % LANES), 1)
-            columns = jnp.where(lanes == plane, source, columns)
-        out[total + nx // ROWS] = jnp.where(top, roll_rows(columns, DEPTH - 1), columns)
-        for plane in range(nx):
-            tile = press[plane, pl.ds(row, ROWS), :]
-            edge = jnp.where(top, tile[ROWS - 1 : ROWS], tile[0:1])
-            out[total + plane // ROWS, plane % ROWS : plane % ROWS + 1, :] = edge
-        clear_if_alone("gy", turn, out)
+    lanes = lane_index((ROWS, LANES))
+    top = even("gy")
+    row = pl.multiple_of(jnp.where(top, ny - ROWS, 0), ROWS)
+    block = Block(nx, ny, coef, vel, rhs, got_x, row, ROWS)
+    columns = jnp.zeros((ROWS, LANES), jnp.float32)
+    ends = block.columns()
+    for plane in range(total):
+        out[plane] = row_tile(block.coef(plane), block.rhs(plane), block.vy_end(plane), top)
+        if plane < nx:
+            source = roll_lanes(vel[2, plane, pl.ds(row, ROWS), :], plane + 1)
+        elif block.layer(plane) is None:
+            continue
+        else:
+            side, layer = block.layer(plane)
+            high = (plane - layer - DEPTH * (ny // ROWS - 1)) % LANES
+            source = pltpu.roll(ends[side], jnp.where(top, high, (plane - layer) % LANES), 1)
+        columns = jnp.where(lanes == plane, source, columns)
+    out[total + nx // ROWS] = jnp.where(top, roll_rows(columns, DEPTH - 1), columns)
+    for plane in range(nx):
+        tile = press[plane, pl.ds(row, ROWS), :]
+        edge = jnp.where(top, tile[ROWS - 1 : ROWS], tile[0:1])
+        out[total + plane // ROWS, plane % ROWS : plane % ROWS + 1, :] = edge
+    clear_if_alone(out, ("gy", 0))
 
 
 def tall_end(block, tile_end, plane, lane):
@@ -346,7 +432,7 @@
         made[turn][groups // 2] = jnp.concatenate([value, made[turn][groups // 2][ny:]], 0)
         for which, value in enumerate(made[turn]):
             send[which] = value
-        clear_if_alone("gz", turn, send)
+        clear_if_alone(send, ("gz", turn))
 
 
 def tree_sum(parts):
@@ -655,16 +741,28 @@
             name=name,
         )(*args)
 
-    to_x = call(
-        functools.partial(pack_x, nx, ny),
+    odd = n_y > 1
+    sent = call(
+        functools.partial(pack_first, nx, ny, n_x, n_y),
         inputs,
         [HBM] * 3,
-        [f32(VY * ny + 2 * ROWS, nz)] * n_x,
-        "pack_x",
-        [pltpu.VMEM((n_x, DEPTH, ny, nz), jnp.int32), scratch(n_x, 3, DEPTH, ny, nz)]
+        [f32(VY * ny + 2 * ROWS, nz)] * n_x
+        + ([f32(nx + nx // ROWS + 2, ROWS, nz)] + [f32(DEPTH + 2, ROWS, nz)] * n_x if odd else []),
+        "pack_first",
+        (
+            [pltpu.VMEM((nx, ROWS, nz), jnp.int32), scratch(3, nx, ROWS, nz), scratch(nx, ROWS, nz)]
+            + [pltpu.SemaphoreType.DMA((3,))]
+            if odd
+            else []
+        )
+        + [pltpu.VMEM((n_x, DEPTH, ny, nz), jnp.int32), scratch(n_x, 3, DEPTH, ny, nz)]
         + [pltpu.SemaphoreType.DMA((n_x, 3))],
     )
-    got_x = exchange(to_x, "gx")
+    to_x = sent[:n_x]
+    got_x = [exchange(send, ("gx", turn)) for turn, send in enumerate(to_x)]
+    if odd:
+        got_odd = exchange(sent[n_x], ("gy", 1))
+        corners = [exchange(send, ("gx", turn), ("gy", 1)) for turn, send in enumerate(sent[n_x + 1 :])]
     coef, press, vel, rhs = call(
         load,
         inputs + [to_x[0]],
@@ -673,14 +771,25 @@
         "load",
         [pltpu.VMEM(phase.shape, jnp.int32), pltpu.SemaphoreType.DMA((3,))],
     )
-    to_y = call(
-        functools.partial(pack_y, nx, ny, n_x),
-        [coef, press, vel, rhs, *got_x],
-        [VMEM] * (4 + n_x),
-        [f32(total + nx // ROWS + 1, ROWS, nz)] * n_y,
-        "pack_y",
-    )
-    got_y = exchange(to_y, "gy")
+    rows_y = f32(total + nx // ROWS + 1, ROWS, nz)
+    got_y, odd_rows = [], []
+    if odd:
+        odd_rows = call(
+            functools.partial(merge_odd, nx),
+            [got_odd, *corners],
+            [VMEM] * (1 + n_x),
+            [rows_y],
+            "merge_odd",
+        )
+    if n_y:
+        to_y = call(
+            functools.partial(pack_y, nx, ny, n_x),
+            [coef, press, vel, rhs, *got_x, *odd_rows],
+            [VMEM] * (4 + n_x) + [ANY] * len(odd_rows),
+            [rows_y],
+            "pack_y",
+        )
+        got_y = [exchange(to_y[0], ("gy", 0)), *odd_rows]
     cube = (total, height, nz)
     full_coef, full_rhs, *to_z = call(
         functools.partial(pack_z, nx, ny, n_x, n_y, n_z),
@@ -689,7 +798,7 @@
         [f32(*cube)] * 2 + [f32(groups // 2 + 1, height, LANES)] * n_z,
         "pack_z",
     )
-    got_z = exchange(to_z, "gz")
+    got_z = [exchange(send, ("gz", turn)) for turn, send in enumerate(to_z)]
     basis, ends, shares = call(
         functools.partial(prepare, nx, ny, n_x, n_y),
         [coef, vel, rhs, full_coef, full_rhs, *got_x, *got_y],

time: 34.6 us -> 32.8 us (0.948)
  waiting for transfers between devices: 5.74 us -> 2.41 us
  starting transfers between devices: 7.9 us -> 9.86 us
  blocking collectives: 11.8 us -> 11 us
  Pallas kernels: 8.23 us -> 8.68 us
    ppermute x5 -> x7, waiting for transfers between devices: 5.74 us -> 2.41 us  [exchange(): return lax.ppermute(send, AXES, swaps(moves))]
    ppermute x5 -> x7, starting transfers between devices: 7.9 us -> 9.86 us  [exchange(): return lax.ppermute(send, AXES, swaps(moves))]
    all_to_all x1, blocking collectives: 11.8 us -> 11 us  [on_device(): gathered = lax.all_to_all(spread, AXES, 0, 0).reshape(devices, LANES)]
    pallas_call x7 -> x8, Pallas kernels: 8.23 us -> 8.68 us  [call(): pl.pallas_call(kernel, out_shape=shapes, in_specs=in_specs, out_specs=[ou...]
  transfers between devices with their start and end apart: 5 -> 7, of which waited for: 3 -> 4; matrix products, arithmetic and copies ran while one was open for 0% -> 0% of each run, Pallas kernels for 11% -> 12%
where the time goes in v7:
time: 32.8 us; the launch traced here: 32.6 us
  blocking collectives  11 us (34%)
  starting transfers between devices  9.86 us (30%)
  Pallas kernels  8.68 us (26%)
  waiting for transfers between devices  2.41 us (7%)
  between operations  0.68 us (2%)
    all_to_all x1, blocking collectives, on_device(): gathered = lax.all_to_all(spread, AXES, 0, 0).reshape(devices, LANES)  11 us
    ppermute x7, starting transfers between devices, exchange(): return lax.ppermute(send, AXES, swaps(moves))  9.86 us
    pallas_call x8, Pallas kernels, call(): pl.pallas_call(kernel, out_shape=shapes, in_specs=in_specs, out_specs=[ou...  8.68 us
    ppermute x7, waiting for transfers between devices, exchange(): return lax.ppermute(send, AXES, swaps(moves))  2.41 us
  transfers between devices with their start and end apart: 7, of which 4 were waited for; matrix products, arithmetic and copies ran while one was open for 0% of the time, Pallas kernels for 12%

profile of v7, /device:TPU:0, one launch (start us, length us, event | category | flops | bytes accessed | tf_op | source)
XLA Modules:
  0.0 32.6 jit_solution(9891109034226304708)
XLA Ops:
  0.6 1.7 %pack_first.1 = (f32[304,128]{1,0:T(8,128)S(1)}, f32[304,128]{1,0:T(8,128)S(1)}, f32[20,8,128]{2,1,0:T(8,128)S(1)}, f32[6,8,128]{2,1,0:T(8,128)S(1)}, f32[6,8,128]{2,1,0:T(8,128)S(1)}) custom-call(s32[16,32,128]{2,1,0:T(8,128)} %phase.3, f32[16,32,128]{2,1,0:T(8,128)} %press.3, f32[3,16,32,128]{3,2,1,0:T(8,128)} %vel.3), custom_call_target="tpu_custom_call" | custom-call | flops 3000000 | bytes 3000000 | tf_op jit(solution)/shard_map/pack_first/pallas_call | solution.py:733
  2.3 0.5 %collective-permute-start.1 = (f32[304,128]{1,0:T(8,128)S(1)}, f32[304,128]{1,0:T(8,128)S(1)}, u32[]{:S(2)}, u32[]{:S(2)}) collective-permute-start(f32[304,128]{1,0:T(8,128)S(1)} %get-tuple-element.25), channel_id=1, source_target_pairs={{0,2},{1,3},{2,0},{3,1},{4,6},{5,7},{6,4},{7,5},{8,16},{9,17},{10,... | collective-permute-start | bytes 466952 | tf_op jit(solution)/shard_map/ppermute | solution.py:45
  2.9 4.1 %collective-permute-start = (f32[304,128]{1,0:T(8,128)S(1)}, f32[304,128]{1,0:T(8,128)S(1)}, u32[]{:S(2)}, u32[]{:S(2)}) collective-permute-start(f32[304,128]{1,0:T(8,128)S(1)} %get-tuple-element.20.after), channel_id=1, source_target_pairs={{0,8},{1,9},{2,10},{3,11},{4,12},{5,13},{6,14},{7,15},{8,0},{9,1},... | collective-permute-start | bytes 466952 | tf_op jit(solution)/shard_map/ppermute | solution.py:45
  7.0 1.5 %collective-permute-start.2 = (f32[20,8,128]{2,1,0:T(8,128)S(1)}, f32[20,8,128]{2,1,0:T(8,128)S(1)}, u32[]{:S(2)}, u32[]{:S(2)}) collective-permute-start(f32[20,8,128]{2,1,0:T(8,128)S(1)} %get-tuple-element.26), channel_id=1, source_target_pairs={{0,1},{1,0},{2,4},{3,5},{4,2},{5,3},{6,7},{7,6},{8,9},{9,8},{10,12... | collective-permute-start | bytes 245768 | tf_op jit(solution)/shard_map/ppermute | solution.py:45
  8.5 0.5 %collective-permute-start.3 = (f32[6,8,128]{2,1,0:T(8,128)S(1)}, f32[6,8,128]{2,1,0:T(8,128)S(1)}, u32[]{:S(2)}, u32[]{:S(2)}) collective-permute-start(f32[6,8,128]{2,1,0:T(8,128)S(1)} %get-tuple-element.27), channel_id=1, source_target_pairs={{0,1},{1,0},{2,12},{3,13},{4,10},{5,11},{6,7},{7,6},{8,9},{9,8},{1... | collective-permute-start | bytes 73736 | tf_op jit(solution)/shard_map/ppermute | solution.py:45
  9.0 1.5 %collective-permute-start.4 = (f32[6,8,128]{2,1,0:T(8,128)S(1)}, f32[6,8,128]{2,1,0:T(8,128)S(1)}, u32[]{:S(2)}, u32[]{:S(2)}) collective-permute-start(f32[6,8,128]{2,1,0:T(8,128)S(1)} %get-tuple-element.28), channel_id=1, source_target_pairs={{0,1},{1,0},{2,3},{3,2},{4,5},{5,4},{6,7},{7,6},{8,9},{9,8},{10,20... | collective-permute-start | bytes 73736 | tf_op jit(solution)/shard_map/ppermute | solution.py:45
  10.6 1.6 %load.1 = (f32[16,32,128]{2,1,0:T(8,128)S(1)}, f32[16,32,128]{2,1,0:T(8,128)S(1)}, f32[3,16,32,128]{3,2,1,0:T(8,128)S(1)}, f32[16,32,128]{2,1,0:T(8,128)S(1)}) custom-call(s32[16,32,128]{2,1,0:T(8,128)} %phase.3, f32[16,32,128]{2,1,0:T(8,128)} %press.3, f32[3,16,32,128]{3,2,1,0:T(8,128)} %vel.3, f32[304,128]{1,0:T(8,128)S(1)} %get-tuple-element.20.after), custom_call_target="tpu_custom_call" | custom-call | flops 3000000 | bytes 3000000 | tf_op jit(solution)/shard_map/load/pallas_call | solution.py:733
  12.2 0.2 collective-permute-done.3.refs_0_
  12.4 0.5 %collective-permute-done.4.refs_1_ = f32[6,8,128]{2,1,0:T(8,128)S(1)} collective-permute-done((f32[6,8,128]{2,1,0:T(8,128)S(1)}, f32[6,8,128]{2,1,0:T(8,128)S(1)}, u32[]{:S(2)}, u32[]{:S(2)}) %collective-permute-start.4) | collective-permute-done | bytes 24608 | tf_op jit(solution)/shard_map/ppermute | solution.py:45
  12.9 0.0 collective-permute-done.2.got
  12.9 0.1 merge_odd.1.refs_2_.refs_3_
  12.9 0.0 collective-permute-done.1.refs_1_
  13.0 0.0 collective-permute-done.refs_0_
  13.0 0.1 pack_y.1
  13.1 0.1 collective-permute-start.5
  13.2 1.3 %collective-permute-done.5.refs_2_ = f32[27,8,128]{2,1,0:T(8,128)S(1)} collective-permute-done((f32[27,8,128]{2,1,0:T(8,128)S(1)}, f32[27,8,128]{2,1,0:T(8,128)S(1)}, u32[]{:S(2)}, u32[]{:S(2)}) %collective-permute-start.5) | collective-permute-done | bytes 110624 | tf_op jit(solution)/shard_map/ppermute | solution.py:45
  14.5 0.5 %pack_z.1 = (f32[24,40,128]{2,1,0:T(8,128)S(1)}, f32[24,40,128]{2,1,0:T(8,128)S(1)}, f32[2,40,128]{2,1,0:T(8,128)S(1)}) custom-call(f32[16,32,128]{2,1,0:T(8,128)S(1)} %get-tuple-element.21.coef, f32[16,32,128]{2,1,0:T(8,128)S(1)} %get-tuple-element.24.press, f32[3,16,32,128]{3,2,1,0:T(8,128)S(1)} %get-tuple-element.22.vel, ...), custom_call_target="tpu_custom_call" | custom-call | flops 3000000 | bytes 3000000 | tf_op jit(solution)/shard_map/pack_z/pallas_call | solution.py:733
  15.0 1.6 %collective-permute-start.6 = (f32[2,40,128]{2,1,0:T(8,128)S(1)}, f32[2,40,128]{2,1,0:T(8,128)S(1)}, u32[]{:S(2)}, u32[]{:S(2)}) collective-permute-start(f32[2,40,128]{2,1,0:T(8,128)S(1)} %get-tuple-element.33), channel_id=1, source_target_pairs={{0,1},{1,0},{2,3},{3,2},{4,5},{5,4},{6,7},{7,6},{8,9},{9,8},{10,11... | collective-permute-start | bytes 122888 | tf_op jit(solution)/shard_map/ppermute | solution.py:45
  16.6 2.1 %prepare.1 = (f32[3,24,40,128]{3,2,1,0:T(8,128)S(1)}, f32[5,3,40,128]{3,2,1,0:T(8,128)S(1)}, f32[6,8,128]{2,1,0:T(8,128)S(1)}) custom-call(f32[16,32,128]{2,1,0:T(8,128)S(1)} %get-tuple-element.21.coef, f32[3,16,32,128]{3,2,1,0:T(8,128)S(1)} %get-tuple-element.22.vel, f32[16,32,128]{2,1,0:T(8,128)S(1)} %get-tuple-element.23.rhs, ...), custom_call_target="tpu_custom_call" | custom-call | flops 3000000 | bytes 3000000 | tf_op jit(solution)/shard_map/prepare/pallas_call | solution.py:733
  18.7 0.4 %collective-permute-done.6.refs_0_.refs_4_ = f32[2,40,128]{2,1,0:T(8,128)S(1)} collective-permute-done((f32[2,40,128]{2,1,0:T(8,128)S(1)}, f32[2,40,128]{2,1,0:T(8,128)S(1)}, u32[]{:S(2)}, u32[]{:S(2)}) %collective-permute-start.6) | collective-permute-done | bytes 40992 | tf_op jit(solution)/shard_map/ppermute | solution.py:45
  19.1 0.7 %join.1 = (f32[3,6,40,128]{3,2,1,0:T(8,128)S(1)}, f32[3,40,128]{2,1,0:T(8,128)S(1)}, f32[1,128]{1,0:T(1,128)S(1)}) custom-call(f32[5,3,40,128]{3,2,1,0:T(8,128)S(1)} %get-tuple-element.31.ends, f32[6,8,128]{2,1,0:T(8,128)S(1)} %get-tuple-element.32.shares, f32[2,40,128]{2,1,0:T(8,128)S(1)} %collective-permute-done.6.refs_0_.refs_4_), custom_call_target="tpu_custom_call" | custom-call | flops 3000000 | bytes 3000000 | tf_op jit(solution)/shard_map/join/pallas_call | solution.py:733
  19.8 11.0 %all_to_all.5 = f32[32,1,128]{2,1,0:T(1,128)S(1)} all-to-all(f32[32,1,128]{2,1,0:T(1,128)S(1)} %broadcast_in_dim.9), channel_id=1, replica_groups=mesh['gx'=4,'gy'=4,'gz'=2] {'gx','gy','gz'}, dimensions={0} | all-to-all | bytes 32768 | tf_op jit(solution)/shard_map/all_to_all | solution.py:819
  30.8 1.8 %finish.1 = (f32[3,16,32,128]{3,2,1,0:T(8,128)}, f32[16,32,128]{2,1,0:T(8,128)}) custom-call(f32[32,128]{1,0:T(8,128)S(1)} %bitcast.2, f32[16,32,128]{2,1,0:T(8,128)S(1)} %get-tuple-element.24.press, f32[3,16,32,128]{3,2,1,0:T(8,128)S(1)} %get-tuple-element.22.vel, f32[3,24,40,128]{3,2,1,0:T(8,128)S(1)} %get-tuple-element.35.basis, ...), custom_call_target="tpu_custom_call" | custom-call | flops 3000000 | bytes 3000000 | tf_op jit(solution)/shard_map/finish/pallas_call | solution.py:733
  (1 shorter events, 0.0 us)
Async XLA Ops:
  2.3 10.6 %collective-permute-start.1 = (f32[304,128]{1,0:T(8,128)S(1)}, f32[304,128]{1,0:T(8,128)S(1)}, u32[]{:S(2)}, u32[]{:S(2)}) collective-permute-start(f32[304,128]{1,0:T(8,128)S(1)} %get-tuple-element.25), channel_id=1, source_target_pairs={{0,2},{1,3},{2,0},{3,1},{4,6},{5,7},{6,4},{7,5},{8,16},{9,17},{10,... | collective-permute-start | bytes 466952 | tf_op jit(solution)/shard_map/ppermute | solution.py:45
  2.9 10.1 %collective-permute-start = (f32[304,128]{1,0:T(8,128)S(1)}, f32[304,128]{1,0:T(8,128)S(1)}, u32[]{:S(2)}, u32[]{:S(2)}) collective-permute-start(f32[304,128]{1,0:T(8,128)S(1)} %get-tuple-element.20.after), channel_id=1, source_target_pairs={{0,8},{1,9},{2,10},{3,11},{4,12},{5,13},{6,14},{7,15},{8,0},{9,1},... | collective-permute-start | bytes 466952 | tf_op jit(solution)/shard_map/ppermute | solution.py:45
  7.0 5.9 %collective-permute-start.2 = (f32[20,8,128]{2,1,0:T(8,128)S(1)}, f32[20,8,128]{2,1,0:T(8,128)S(1)}, u32[]{:S(2)}, u32[]{:S(2)}) collective-permute-start(f32[20,8,128]{2,1,0:T(8,128)S(1)} %get-tuple-element.26), channel_id=1, source_target_pairs={{0,1},{1,0},{2,4},{3,5},{4,2},{5,3},{6,7},{7,6},{8,9},{9,8},{10,12... | collective-permute-start | bytes 245768 | tf_op jit(solution)/shard_map/ppermute | solution.py:45
  8.5 3.8 %collective-permute-start.3 = (f32[6,8,128]{2,1,0:T(8,128)S(1)}, f32[6,8,128]{2,1,0:T(8,128)S(1)}, u32[]{:S(2)}, u32[]{:S(2)}) collective-permute-start(f32[6,8,128]{2,1,0:T(8,128)S(1)} %get-tuple-element.27), channel_id=1, source_target_pairs={{0,1},{1,0},{2,12},{3,13},{4,10},{5,11},{6,7},{7,6},{8,9},{9,8},{1... | collective-permute-start | bytes 73736 | tf_op jit(solution)/shard_map/ppermute | solution.py:45
  9.0 3.8 %collective-permute-start.4 = (f32[6,8,128]{2,1,0:T(8,128)S(1)}, f32[6,8,128]{2,1,0:T(8,128)S(1)}, u32[]{:S(2)}, u32[]{:S(2)}) collective-permute-start(f32[6,8,128]{2,1,0:T(8,128)S(1)} %get-tuple-element.28), channel_id=1, source_target_pairs={{0,1},{1,0},{2,3},{3,2},{4,5},{5,4},{6,7},{7,6},{8,9},{9,8},{10,20... | collective-permute-start | bytes 73736 | tf_op jit(solution)/shard_map/ppermute | solution.py:45
  13.1 1.4 %collective-permute-start.5 = (f32[27,8,128]{2,1,0:T(8,128)S(1)}, f32[27,8,128]{2,1,0:T(8,128)S(1)}, u32[]{:S(2)}, u32[]{:S(2)}) collective-permute-start(f32[27,8,128]{2,1,0:T(8,128)S(1)} %pack_y.1), channel_id=1, source_target_pairs={{0,2},{1,3},{2,0},{3,1},{4,6},{5,7},{6,4},{7,5},{8,10},{9,11},{10,... | collective-permute-start | bytes 331784 | tf_op jit(solution)/shard_map/ppermute | solution.py:45
  15.0 4.1 %collective-permute-start.6 = (f32[2,40,128]{2,1,0:T(8,128)S(1)}, f32[2,40,128]{2,1,0:T(8,128)S(1)}, u32[]{:S(2)}, u32[]{:S(2)}) collective-permute-start(f32[2,40,128]{2,1,0:T(8,128)S(1)} %get-tuple-element.33), channel_id=1, source_target_pairs={{0,1},{1,0},{2,3},{3,2},{4,5},{5,4},{6,7},{7,6},{8,9},{9,8},{10,11... | collective-permute-start | bytes 122888 | tf_op jit(solution)/shard_map/ppermute | solution.py:45

commit v8 on v7

--- a/solution.py
+++ b/solution.py
@@ -267,11 +267,13 @@
 
 
 class Block:
-    def __init__(self, nx, ny, coef, vel, rhs, got_x, row=0, height=None):
+    def __init__(self, nx, ny, coef, vel, rhs, got_x, row=0, height=None, faces=True):
         self.nx, self.ny = nx, ny
         self.own_coef, self.vel, self.own_rhs, self.got_x = coef, vel, rhs, got_x
         self.even = even("gx")
         self.row, self.height = row, height or ny
+        if not faces:
+            return
         self.low_face = 0.5 * (self.coef(nx + 2 * DEPTH - 1) + self.coef(0)) * self.halo(VX)[0]
         self.high_face = 0.5 * (self.coef(nx - 1) + self.coef(nx)) * self.take(vel, 0, nx - 1)
 
@@ -381,47 +383,72 @@
     return GROUP * (x % ROWS) + ROWS + 2 * (x // ROWS)
 
 
-def pack_z(nx, ny, n_x, n_y, n_z, coef, press, vel, rhs, *refs):
-    got_x, got_y = refs[:n_x], refs[n_x : n_x + n_y]
-    full_coef, full_rhs, *sends = refs[n_x + n_y :]
+def pack_plane(lanes, at, top, coef, rhs, end):
+    coef = pltpu.roll(coef, jnp.where(top, (at + DEPTH) % LANES, at), 1)
+    rhs = pltpu.roll(rhs, jnp.where(top, (at + ROWS - 1) % LANES, at + DEPTH), 1)
+    value = jnp.where(lanes == at + ROWS - 1, end, 0.0)
+    value = jnp.where((lanes >= at + DEPTH) & (lanes < at + ROWS - 1), rhs, value)
+    return jnp.where((lanes >= at) & (lanes < at + DEPTH), coef, value)
+
+
+def half_tile(tile, below):
+    rows = row_index((ROWS, LANES))
+    coef = jnp.where(below, jnp.where(rows >= DEPTH, roll_rows(tile, DEPTH), 0.0), jnp.where(rows < DEPTH, tile, 0.0))
+    rhs = jnp.where(
+        below,
+        jnp.where(rows > DEPTH, roll_rows(tile, 1), 0.0),
+        jnp.where(rows < DEPTH - 1, roll_rows(tile, -DEPTH), 0.0),
+    )
+    return coef, rhs
+
+
+def half_ends(tile, below):
+    rows = row_index((ROWS, LANES))
+    return jnp.where(
+        below, jnp.where(rows > DEPTH, roll_rows(tile, DEPTH + 1), 0.0), jnp.where(rows < DEPTH - 1, tile, 0.0)
+    )
+
+
+def face_y(own_low, own_high, coef_tile, tile, vy_end, below):
+    rows = row_index((ROWS, LANES))
+    down = 0.5 * (coef_tile[ROWS - 1 :] + own_low) * tile[ROWS - 1 :]
+    up = 0.5 * (own_high + coef_tile[:1]) * vy_end
+    outside = jnp.where(below, jnp.where(rows == ROWS - 1, down, 0.0), jnp.where(rows == 0, -up, 0.0))
+    inside = jnp.where(below, jnp.where(rows == 0, -down, 0.0), jnp.where(rows == ROWS - 1, up, 0.0))
+    return outside, inside
+
+
+def stage_z(nx, ny, n_x, n_z, coef, press, vel, rhs, *refs):
+    got_x, (*got_odd, full_coef, full_rhs), sends = refs[:n_x], refs[n_x : len(refs) - n_z], refs[len(refs) - n_z :]
     total, height = nx + 2 * DEPTH, ny + 2 * DEPTH
     groups = total // ROWS
-    even_y = even("gy")
-    rows = row_index((ROWS, LANES))
+    below = even("gy")
     lanes = lane_index((height, LANES))
     block = Block(nx, ny, coef, vel, rhs, got_x)
-    tile_end = tile_of_ends(nx, even_y, got_y)
-    parts = [jnp.zeros((height, LANES), jnp.float32) for _ in range(groups // 2 + 1)]
-    made = [list(parts) for _ in sends]
+    nothing = jnp.zeros((ROWS, LANES), jnp.float32)
+    tile_end = half_ends(got_odd[0][total + nx // ROWS], below) if got_odd else nothing
+    made = [[jnp.zeros((height, LANES), jnp.float32) for _ in range(groups // 2 + 1)] for _ in sends]
+    row = pl.ds(pl.multiple_of(jnp.where(below, 0, ny - ROWS), ROWS), ROWS)
     for plane in range(total):
-        low, high = sides(even_y, got_y, lambda ref: ref[plane])
-        c_own, c_tile = block.coef(plane), jnp.where(rows < DEPTH, high, roll_rows(low, DEPTH))
-        r_own, r_tile = block.rhs(plane), jnp.where(rows < DEPTH, roll_rows(high, -DEPTH), roll_rows(low, 1))
-        up = 0.5 * (c_own[ny - 1 :] + c_tile[:1]) * block.vy_end(plane)
-        down = 0.5 * (c_tile[ROWS - 1 :] + c_own[:1]) * low[ROWS - 1 :]
-        first, last = r_own[:ROWS], r_own[ny - ROWS :]
-        r_tile = jnp.where(rows == 0, r_tile - up, jnp.where(rows == ROWS - 1, r_tile + down, r_tile))
-        middle = [r_own[ROWS : ny - ROWS]] if ny > 2 * ROWS else []
-        if ny > ROWS:
-            first = jnp.where(rows == 0, first - down, first)
-            last = jnp.where(rows == ROWS - 1, last + up, last)
-            r_all = jnp.concatenate([first] + middle + [last, r_tile], 0)
-        else:
-            only = jnp.where(rows == 0, first - down, jnp.where(rows == ROWS - 1, first + up, first))
-            r_all = jnp.concatenate([only, r_tile], 0)
+        c_own, r_own = block.coef(plane), block.rhs(plane)
+        c_tile = r_tile = nothing
+        full_rhs[plane, :ny, :] = r_own
+        if got_odd:
+            tile = got_odd[0][plane]
+            c_tile, r_tile = half_tile(tile, below)
+            outside, inside = face_y(c_own[:1], c_own[ny - 1 :], c_tile, tile, block.vy_end(plane), below)
+            r_tile = r_tile + outside
+            full_rhs[plane, row, :] = full_rhs[plane, row, :] + inside
         c_all = jnp.concatenate([c_own, c_tile], 0)
-        full_coef[plane], full_rhs[plane] = c_all, r_all
+        full_coef[plane] = c_all
+        full_rhs[plane, ny:, :] = r_tile
+        r_all = full_rhs[plane]
         group, seat = plane % groups, plane // groups
         at = GROUP * seat + ROWS * (group % 2)
         end = tall_end(block, tile_end, plane, at + ROWS - 1)
-        for turn in range(len(sends)):
-            top = even("gz") == (turn == 0)
-            c_move = pltpu.roll(c_all, jnp.where(top, (at + DEPTH) % LANES, at), 1)
-            r_move = pltpu.roll(r_all, jnp.where(top, (at + ROWS - 1) % LANES, at + DEPTH), 1)
-            value = made[turn][group // 2]
-            value = jnp.where((lanes >= at) & (lanes < at + DEPTH), c_move, value)
-            value = jnp.where((lanes >= at + DEPTH) & (lanes < at + ROWS - 1), r_move, value)
-            made[turn][group // 2] = jnp.where(lanes == at + ROWS - 1, end, value)
+        for turn in range(n_z):
+            value = pack_plane(lanes, at, even("gz") == (turn == 0), c_all, r_all, end)
+            made[turn][group // 2] = made[turn][group // 2] + value
     for turn, send in enumerate(sends):
         top = even("gz") == (turn == 0)
         value = made[turn][groups // 2][:ny]
@@ -432,6 +459,41 @@
         made[turn][groups // 2] = jnp.concatenate([value, made[turn][groups // 2][ny:]], 0)
         for which, value in enumerate(made[turn]):
             send[which] = value
+
+
+def pack_z(nx, ny, n_x, n_z, vel, *refs):
+    got_x, got, (full_coef, full_rhs, *sends) = refs[:n_x], refs[n_x], refs[-2 - n_z :]
+    total = nx + 2 * DEPTH
+    groups = total // ROWS
+    below = jnp.logical_not(even("gy"))
+    lanes = lane_index((ROWS, LANES))
+    block = Block(nx, ny, full_coef, vel, full_rhs, got_x, faces=False)
+    tile_end = half_ends(got[total + nx // ROWS], below)
+    row = pl.ds(pl.multiple_of(jnp.where(below, 0, ny - ROWS), ROWS), ROWS)
+    added = [[[jnp.zeros((ROWS, LANES), jnp.float32) for _ in range(2)] for _ in range(groups // 2 + 1)] for _ in sends]
+    for plane in range(total):
+        tile = got[plane]
+        c_tile, r_tile = half_tile(tile, below)
+        low, high = full_coef[plane, :1, :], full_coef[plane, ny - 1 : ny, :]
+        outside, inside = face_y(low, high, c_tile, tile, block.vy_end(plane), below)
+        r_tile = r_tile + outside
+        full_coef[plane, ny:, :] = full_coef[plane, ny:, :] + c_tile
+        full_rhs[plane, ny:, :] = full_rhs[plane, ny:, :] + r_tile
+        full_rhs[plane, row, :] = full_rhs[plane, row, :] + inside
+        group, seat = plane % groups, plane // groups
+        at = GROUP * seat + ROWS * (group % 2)
+        end = roll_lanes(tile_end, at + ROWS - 1 - plane)
+        for turn in range(n_z):
+            top = even("gz") == (turn == 0)
+            inside_move = pltpu.roll(inside, jnp.where(top, (at + ROWS - 1) % LANES, at + DEPTH), 1)
+            inside_move = jnp.where((lanes >= at + DEPTH) & (lanes < at + ROWS - 1), inside_move, 0.0)
+            slot = added[turn][group // 2]
+            slot[0] = slot[0] + pack_plane(lanes, at, top, c_tile, r_tile, end)
+            slot[1] = slot[1] + inside_move
+    for turn, send in enumerate(sends):
+        for which, (tile, inside) in enumerate(added[turn]):
+            send[which, ny:, :] = send[which, ny:, :] + tile
+            send[which, row, :] = send[which, row, :] + inside
         clear_if_alone(send, ("gz", turn))
 
 
@@ -729,13 +791,14 @@
     scratch = lambda *shape: pltpu.VMEM(shape, jnp.float32)
     inputs = [pltpu.with_memory_space_constraint(array, pltpu.HBM) for array in (phase, press, vel)]
 
-    def call(kernel, args, in_specs, shapes, name, scratch_shapes=(), out_spec=VMEM):
+    def call(kernel, args, in_specs, shapes, name, scratch_shapes=(), out_spec=VMEM, aliases={}):
         return pl.pallas_call(
             kernel,
             out_shape=shapes,
             in_specs=in_specs,
             out_specs=[out_spec] * len(shapes),
             scratch_shapes=list(scratch_shapes),
+            input_output_aliases=aliases,
             compiler_params=PARAMS,
             cost_estimate=pl.CostEstimate(flops=3_000_000, bytes_accessed=3_000_000, transcendentals=0),
             name=name,
@@ -791,12 +854,21 @@
         )
         got_y = [exchange(to_y[0], ("gy", 0)), *odd_rows]
     cube = (total, height, nz)
+    packs = [f32(groups // 2 + 1, height, LANES)] * n_z
+    staged = call(
+        functools.partial(stage_z, nx, ny, n_x, n_z),
+        [coef, press, vel, rhs, *got_x, *odd_rows],
+        [VMEM] * (4 + n_x + len(odd_rows)),
+        [f32(*cube)] * 2 + packs,
+        "stage_z",
+    )
     full_coef, full_rhs, *to_z = call(
-        functools.partial(pack_z, nx, ny, n_x, n_y, n_z),
-        [coef, press, vel, rhs, *got_x, *got_y],
-        [VMEM] * (4 + n_x + n_y),
-        [f32(*cube)] * 2 + [f32(groups // 2 + 1, height, LANES)] * n_z,
+        functools.partial(pack_z, nx, ny, n_x, n_z),
+        [vel, *got_x, got_y[0], *staged],
+        [VMEM] * (4 + n_x + n_z),
+        [f32(*cube)] * 2 + packs,
         "pack_z",
+        aliases={2 + n_x + which: which for which in range(2 + n_z)},
     )
     got_z = [exchange(send, ("gz", turn)) for turn, send in enumerate(to_z)]
     basis, ends, shares = call(

time: 32.8 us -> 32.5 us (level)
  waiting for transfers between devices: 2.41 us -> 1.84 us
    ppermute x7, waiting for transfers between devices: 2.41 us -> 1.84 us  [exchange(): return lax.ppermute(send, AXES, swaps(moves))]
    pallas_call x8 -> x9, Pallas kernels: 8.68 us -> 8.91 us  [call(): pl.pallas_call(kernel, out_shape=shapes, in_specs=in_specs, out_specs=[ou...]
  transfers between devices with their start and end apart: 7 -> 7, of which waited for: 4 -> 4; matrix products, arithmetic and copies ran while one was open for 0% -> 0% of each run, Pallas kernels for 12% -> 13%
where the time goes in v8:
time: 32.5 us; the launch traced here: 32.3 us
  blocking collectives  11 us (34%)
  starting transfers between devices  9.86 us (30%)
  Pallas kernels  8.91 us (27%)
  waiting for transfers between devices  1.84 us (6%)
  between operations  0.68 us (2%)
    all_to_all x1, blocking collectives, on_device(): gathered = lax.all_to_all(spread, AXES, 0, 0).reshape(devices, LANES)  11 us
    ppermute x7, starting transfers between devices, exchange(): return lax.ppermute(send, AXES, swaps(moves))  9.86 us
    pallas_call x9, Pallas kernels, call(): pl.pallas_call(kernel, out_shape=shapes, in_specs=in_specs, out_specs=[ou...  8.91 us
    ppermute x7, waiting for transfers between devices, exchange(): return lax.ppermute(send, AXES, swaps(moves))  1.84 us
  transfers between devices with their start and end apart: 7, of which 4 were waited for; matrix products, arithmetic and copies ran while one was open for 0% of the time, Pallas kernels for 13%

profile of v8, /device:TPU:0, one launch (start us, length us, event | category | flops | bytes accessed | tf_op | source)
XLA Modules:
  0.0 32.3 jit_solution(3562914981866440866)
XLA Ops:
  0.6 1.7 %pack_first.1 = (f32[304,128]{1,0:T(8,128)S(1)}, f32[304,128]{1,0:T(8,128)S(1)}, f32[20,8,128]{2,1,0:T(8,128)S(1)}, f32[6,8,128]{2,1,0:T(8,128)S(1)}, f32[6,8,128]{2,1,0:T(8,128)S(1)}) custom-call(s32[16,32,128]{2,1,0:T(8,128)} %phase.3, f32[16,32,128]{2,1,0:T(8,128)} %press.3, f32[3,16,32,128]{3,2,1,0:T(8,128)} %vel.3), custom_call_target="tpu_custom_call" | custom-call | flops 3000000 | bytes 3000000 | tf_op jit(solution)/shard_map/pack_first/pallas_call | solution.py:795
  2.3 0.5 %collective-permute-start.1 = (f32[304,128]{1,0:T(8,128)S(1)}, f32[304,128]{1,0:T(8,128)S(1)}, u32[]{:S(2)}, u32[]{:S(2)}) collective-permute-start(f32[304,128]{1,0:T(8,128)S(1)} %get-tuple-element.27), channel_id=1, source_target_pairs={{0,2},{1,3},{2,0},{3,1},{4,6},{5,7},{6,4},{7,5},{8,16},{9,17},{10,... | collective-permute-start | bytes 466952 | tf_op jit(solution)/shard_map/ppermute | solution.py:45
  2.9 4.1 %collective-permute-start = (f32[304,128]{1,0:T(8,128)S(1)}, f32[304,128]{1,0:T(8,128)S(1)}, u32[]{:S(2)}, u32[]{:S(2)}) collective-permute-start(f32[304,128]{1,0:T(8,128)S(1)} %get-tuple-element.23.after), channel_id=1, source_target_pairs={{0,8},{1,9},{2,10},{3,11},{4,12},{5,13},{6,14},{7,15},{8,0},{9,1},... | collective-permute-start | bytes 466952 | tf_op jit(solution)/shard_map/ppermute | solution.py:45
  7.0 1.5 %collective-permute-start.2 = (f32[20,8,128]{2,1,0:T(8,128)S(1)}, f32[20,8,128]{2,1,0:T(8,128)S(1)}, u32[]{:S(2)}, u32[]{:S(2)}) collective-permute-start(f32[20,8,128]{2,1,0:T(8,128)S(1)} %get-tuple-element.29), channel_id=1, source_target_pairs={{0,1},{1,0},{2,4},{3,5},{4,2},{5,3},{6,7},{7,6},{8,9},{9,8},{10,12... | collective-permute-start | bytes 245768 | tf_op jit(solution)/shard_map/ppermute | solution.py:45
  8.5 0.5 %collective-permute-start.3 = (f32[6,8,128]{2,1,0:T(8,128)S(1)}, f32[6,8,128]{2,1,0:T(8,128)S(1)}, u32[]{:S(2)}, u32[]{:S(2)}) collective-permute-start(f32[6,8,128]{2,1,0:T(8,128)S(1)} %get-tuple-element.30), channel_id=1, source_target_pairs={{0,1},{1,0},{2,12},{3,13},{4,10},{5,11},{6,7},{7,6},{8,9},{9,8},{1... | collective-permute-start | bytes 73736 | tf_op jit(solution)/shard_map/ppermute | solution.py:45
  9.0 1.5 %collective-permute-start.4 = (f32[6,8,128]{2,1,0:T(8,128)S(1)}, f32[6,8,128]{2,1,0:T(8,128)S(1)}, u32[]{:S(2)}, u32[]{:S(2)}) collective-permute-start(f32[6,8,128]{2,1,0:T(8,128)S(1)} %get-tuple-element.31), channel_id=1, source_target_pairs={{0,1},{1,0},{2,3},{3,2},{4,5},{5,4},{6,7},{7,6},{8,9},{9,8},{10,20... | collective-permute-start | bytes 73736 | tf_op jit(solution)/shard_map/ppermute | solution.py:45
  10.6 1.6 %load.1 = (f32[16,32,128]{2,1,0:T(8,128)S(1)}, f32[16,32,128]{2,1,0:T(8,128)S(1)}, f32[3,16,32,128]{3,2,1,0:T(8,128)S(1)}, f32[16,32,128]{2,1,0:T(8,128)S(1)}) custom-call(s32[16,32,128]{2,1,0:T(8,128)} %phase.3, f32[16,32,128]{2,1,0:T(8,128)} %press.3, f32[3,16,32,128]{3,2,1,0:T(8,128)} %vel.3, f32[304,128]{1,0:T(8,128)S(1)} %get-tuple-element.23.after), custom_call_target="tpu_custom_call" | custom-call | flops 3000000 | bytes 3000000 | tf_op jit(solution)/shard_map/load/pallas_call | solution.py:795
  12.2 0.2 collective-permute-done.3.refs_0_
  12.4 0.5 %collective-permute-done.4.refs_1_ = f32[6,8,128]{2,1,0:T(8,128)S(1)} collective-permute-done((f32[6,8,128]{2,1,0:T(8,128)S(1)}, f32[6,8,128]{2,1,0:T(8,128)S(1)}, u32[]{:S(2)}, u32[]{:S(2)}) %collective-permute-start.4) | collective-permute-done | bytes 24608 | tf_op jit(solution)/shard_map/ppermute | solution.py:45
  12.9 0.0 collective-permute-done.2.got
  12.9 0.1 merge_odd.1.refs_2_.refs_3_
  12.9 0.0 collective-permute-done.1.refs_1_
  13.0 0.0 collective-permute-done.refs_0_
  13.0 0.1 pack_y.1
  13.1 0.1 collective-permute-start.5
  13.2 0.6 %stage_z.1 = (f32[24,40,128]{2,1,0:T(8,128)S(1)}, f32[24,40,128]{2,1,0:T(8,128)S(1)}, f32[2,40,128]{2,1,0:T(8,128)S(1)}) custom-call(f32[16,32,128]{2,1,0:T(8,128)S(1)} %get-tuple-element.24.coef, f32[16,32,128]{2,1,0:T(8,128)S(1)} %get-tuple-element.28.press, f32[3,16,32,128]{3,2,1,0:T(8,128)S(1)} %get-tuple-element.25.vel, ...), custom_call_target="tpu_custom_call" | custom-call | flops 3000000 | bytes 3000000 | tf_op jit(solution)/shard_map/stage_z/pallas_call | solution.py:795
  13.7 0.7 %collective-permute-done.5.refs_2_ = f32[27,8,128]{2,1,0:T(8,128)S(1)} collective-permute-done((f32[27,8,128]{2,1,0:T(8,128)S(1)}, f32[27,8,128]{2,1,0:T(8,128)S(1)}, u32[]{:S(2)}, u32[]{:S(2)}) %collective-permute-start.5) | collective-permute-done | bytes 110624 | tf_op jit(solution)/shard_map/ppermute | solution.py:45
  14.5 0.2 pack_z.1
  14.7 1.6 %collective-permute-start.6 = (f32[2,40,128]{2,1,0:T(8,128)S(1)}, f32[2,40,128]{2,1,0:T(8,128)S(1)}, u32[]{:S(2)}, u32[]{:S(2)}) collective-permute-start(f32[2,40,128]{2,1,0:T(8,128)S(1)} %get-tuple-element.39), channel_id=1, source_target_pairs={{0,1},{1,0},{2,3},{3,2},{4,5},{5,4},{6,7},{7,6},{8,9},{9,8},{10,11... | collective-permute-start | bytes 122888 | tf_op jit(solution)/shard_map/ppermute | solution.py:45
  16.3 2.1 %prepare.1 = (f32[3,24,40,128]{3,2,1,0:T(8,128)S(1)}, f32[5,3,40,128]{3,2,1,0:T(8,128)S(1)}, f32[6,8,128]{2,1,0:T(8,128)S(1)}) custom-call(f32[16,32,128]{2,1,0:T(8,128)S(1)} %get-tuple-element.24.coef, f32[3,16,32,128]{3,2,1,0:T(8,128)S(1)} %get-tuple-element.25.vel, f32[16,32,128]{2,1,0:T(8,128)S(1)} %get-tuple-element.26.rhs, ...), custom_call_target="tpu_custom_call" | custom-call | flops 3000000 | bytes 3000000 | tf_op jit(solution)/shard_map/prepare/pallas_call | solution.py:795
  18.3 0.4 %collective-permute-done.6.refs_0_.refs_4_ = f32[2,40,128]{2,1,0:T(8,128)S(1)} collective-permute-done((f32[2,40,128]{2,1,0:T(8,128)S(1)}, f32[2,40,128]{2,1,0:T(8,128)S(1)}, u32[]{:S(2)}, u32[]{:S(2)}) %collective-permute-start.6) | collective-permute-done | bytes 40992 | tf_op jit(solution)/shard_map/ppermute | solution.py:45
  18.8 0.7 %join.1 = (f32[3,6,40,128]{3,2,1,0:T(8,128)S(1)}, f32[3,40,128]{2,1,0:T(8,128)S(1)}, f32[1,128]{1,0:T(1,128)S(1)}) custom-call(f32[5,3,40,128]{3,2,1,0:T(8,128)S(1)} %get-tuple-element.37.ends, f32[6,8,128]{2,1,0:T(8,128)S(1)} %get-tuple-element.38.shares, f32[2,40,128]{2,1,0:T(8,128)S(1)} %collective-permute-done.6.refs_0_.refs_4_), custom_call_target="tpu_custom_call" | custom-call | flops 3000000 | bytes 3000000 | tf_op jit(solution)/shard_map/join/pallas_call | solution.py:795
  19.5 11.0 %all_to_all.5 = f32[32,1,128]{2,1,0:T(1,128)S(1)} all-to-all(f32[32,1,128]{2,1,0:T(1,128)S(1)} %broadcast_in_dim.9), channel_id=1, replica_groups=mesh['gx'=4,'gy'=4,'gz'=2] {'gx','gy','gz'}, dimensions={0} | all-to-all | bytes 32768 | tf_op jit(solution)/shard_map/all_to_all | solution.py:891
  30.5 1.8 %finish.1 = (f32[3,16,32,128]{3,2,1,0:T(8,128)}, f32[16,32,128]{2,1,0:T(8,128)}) custom-call(f32[32,128]{1,0:T(8,128)S(1)} %bitcast.2, f32[16,32,128]{2,1,0:T(8,128)S(1)} %get-tuple-element.28.press, f32[3,16,32,128]{3,2,1,0:T(8,128)S(1)} %get-tuple-element.25.vel, f32[3,24,40,128]{3,2,1,0:T(8,128)S(1)} %get-tuple-element.41.basis, ...), custom_call_target="tpu_custom_call" | custom-call | flops 3000000 | bytes 3000000 | tf_op jit(solution)/shard_map/finish/pallas_call | solution.py:795
  (1 shorter events, 0.0 us)
Async XLA Ops:
  2.3 10.6 %collective-permute-start.1 = (f32[304,128]{1,0:T(8,128)S(1)}, f32[304,128]{1,0:T(8,128)S(1)}, u32[]{:S(2)}, u32[]{:S(2)}) collective-permute-start(f32[304,128]{1,0:T(8,128)S(1)} %get-tuple-element.27), channel_id=1, source_target_pairs={{0,2},{1,3},{2,0},{3,1},{4,6},{5,7},{6,4},{7,5},{8,16},{9,17},{10,... | collective-permute-start | bytes 466952 | tf_op jit(solution)/shard_map/ppermute | solution.py:45
  2.9 10.1 %collective-permute-start = (f32[304,128]{1,0:T(8,128)S(1)}, f32[304,128]{1,0:T(8,128)S(1)}, u32[]{:S(2)}, u32[]{:S(2)}) collective-permute-start(f32[304,128]{1,0:T(8,128)S(1)} %get-tuple-element.23.after), channel_id=1, source_target_pairs={{0,8},{1,9},{2,10},{3,11},{4,12},{5,13},{6,14},{7,15},{8,0},{9,1},... | collective-permute-start | bytes 466952 | tf_op jit(solution)/shard_map/ppermute | solution.py:45
  7.0 5.9 %collective-permute-start.2 = (f32[20,8,128]{2,1,0:T(8,128)S(1)}, f32[20,8,128]{2,1,0:T(8,128)S(1)}, u32[]{:S(2)}, u32[]{:S(2)}) collective-permute-start(f32[20,8,128]{2,1,0:T(8,128)S(1)} %get-tuple-element.29), channel_id=1, source_target_pairs={{0,1},{1,0},{2,4},{3,5},{4,2},{5,3},{6,7},{7,6},{8,9},{9,8},{10,12... | collective-permute-start | bytes 245768 | tf_op jit(solution)/shard_map/ppermute | solution.py:45
  8.5 3.8 %collective-permute-start.3 = (f32[6,8,128]{2,1,0:T(8,128)S(1)}, f32[6,8,128]{2,1,0:T(8,128)S(1)}, u32[]{:S(2)}, u32[]{:S(2)}) collective-permute-start(f32[6,8,128]{2,1,0:T(8,128)S(1)} %get-tuple-element.30), channel_id=1, source_target_pairs={{0,1},{1,0},{2,12},{3,13},{4,10},{5,11},{6,7},{7,6},{8,9},{9,8},{1... | collective-permute-start | bytes 73736 | tf_op jit(solution)/shard_map/ppermute | solution.py:45
  9.0 3.8 %collective-permute-start.4 = (f32[6,8,128]{2,1,0:T(8,128)S(1)}, f32[6,8,128]{2,1,0:T(8,128)S(1)}, u32[]{:S(2)}, u32[]{:S(2)}) collective-permute-start(f32[6,8,128]{2,1,0:T(8,128)S(1)} %get-tuple-element.31), channel_id=1, source_target_pairs={{0,1},{1,0},{2,3},{3,2},{4,5},{5,4},{6,7},{7,6},{8,9},{9,8},{10,20... | collective-permute-start | bytes 73736 | tf_op jit(solution)/shard_map/ppermute | solution.py:45
  13.1 1.4 %collective-permute-start.5 = (f32[27,8,128]{2,1,0:T(8,128)S(1)}, f32[27,8,128]{2,1,0:T(8,128)S(1)}, u32[]{:S(2)}, u32[]{:S(2)}) collective-permute-start(f32[27,8,128]{2,1,0:T(8,128)S(1)} %pack_y.1), channel_id=1, source_target_pairs={{0,2},{1,3},{2,0},{3,1},{4,6},{5,7},{6,4},{7,5},{8,10},{9,11},{10,... | collective-permute-start | bytes 331784 | tf_op jit(solution)/shard_map/ppermute | solution.py:45
  14.7 4.1 %collective-permute-start.6 = (f32[2,40,128]{2,1,0:T(8,128)S(1)}, f32[2,40,128]{2,1,0:T(8,128)S(1)}, u32[]{:S(2)}, u32[]{:S(2)}) collective-permute-start(f32[2,40,128]{2,1,0:T(8,128)S(1)} %get-tuple-element.39), channel_id=1, source_target_pairs={{0,1},{1,0},{2,3},{3,2},{4,5},{5,4},{6,7},{7,6},{8,9},{9,8},{10,11... | collective-permute-start | bytes 122888 | tf_op jit(solution)/shard_map/ppermute | solution.py:45

commit v9 on v8

--- a/solution.py
+++ b/solution.py
@@ -603,7 +603,8 @@
         shares[which] = total_.value()
 
 
-def join(nx, ny, n_z, ends, shares, *refs):
+def join(nx, ny, n_z, after, ends, shares, *refs):
+    del after
     got_z = refs[:n_z]
     basis_z, vz_z, sums, weight_z, inverse_z = refs[n_z:]
     total, height = nx + 2 * DEPTH, ny + 2 * DEPTH
@@ -687,10 +688,39 @@
     sums[...] = row
 
 
-def finish(nx, ny, n_x, n_y, n_z, gathered, press, vel, basis, basis_z, vz_z, *refs):
-    got_x, got_y, got_z = refs[:n_x], refs[n_x : n_x + n_y], refs[n_x + n_y : n_x + n_y + n_z]
-    ustar_out, coef_out, ustar, coef_cot, sem = refs[n_x + n_y + n_z :]
-    even_x, even_y, even_z = even("gx"), even("gy"), even("gz")
+def slopes(nx, ny, n_x, n_y, press, vel, *refs):
+    got_x, got_y, (slope_x, slope_y, slope_z, base) = refs[:n_x], refs[n_x : n_x + n_y], refs[n_x + n_y :]
+    total = nx + 2 * DEPTH
+    rows, shape = row_index((ROWS, LANES)), (ROWS, LANES)
+    lanes = lane_index((ny, LANES))
+    at_low, at_high = lanes == 0, lanes == LANES - 1
+    p_low, p_high = sides(even("gx"), got_x, lambda ref: ref[PRESS * ny : (PRESS + 1) * ny, :])
+    u_low, _ = sides(even("gx"), got_x, lambda ref: ref[VX * ny : (VX + 1) * ny, :])
+    old = p_low - press[0]
+    slope_x[0] = old
+    old = old * u_low
+    for x in range(nx):
+        p = press[x]
+        slope = p - (press[x + 1] if x + 1 < nx else p_high)
+        slope_x[x + 1] = slope
+        new = slope * vel[0, x]
+        answer, old = old + new, new
+        low, high = sides(even("gy"), got_y, lambda ref: ref[total + x // ROWS, x % ROWS : x % ROWS + 1, :])
+        p_tile = jnp.where(rows == 0, jnp.broadcast_to(high, shape), jnp.broadcast_to(low, shape))
+        p_tall = jnp.concatenate([p, p_tile], 0)
+        u_row, _ = sides(even("gy"), got_y, lambda ref: ref[x, ROWS - 1 :, :])
+        u_tall = jnp.concatenate([vel[1, x], jnp.broadcast_to(u_row, shape)], 0)
+        up, down = p - roll_rows(p_tall, -1)[:ny], roll_rows(p_tall, 1)[:ny] - p
+        slope_y[0, x], slope_y[1, x] = up, down
+        answer = answer + (up * vel[1, x] + down * roll_rows(u_tall, 1)[:ny])
+        up = p - jnp.where(at_high, 0.0, roll_lanes(p, -1))
+        down = jnp.where(at_low, 0.0, roll_lanes(p, 1)) - p
+        slope_z[0, x], slope_z[1, x] = up, down
+        base[x] = answer + (up * vel[2, x] + down * jnp.where(at_low, 0.0, roll_lanes(vel[2, x], 1)))
+
+
+def finish(nx, ny, n_z, gathered, vel, basis, basis_z, vz_z, slope_x, slope_y, slope_z, base, *refs):
+    got_z, (ustar_out, coef_out, ustar, coef_cot, sem) = refs[:n_z], refs[n_z:]
     total, height = nx + 2 * DEPTH, ny + 2 * DEPTH
     groups = total // ROWS
     parts = gathered[...]
@@ -726,10 +756,8 @@
     spoiled = (lanes < DEPTH - 1) | (lanes > LANES - DEPTH)
     lanes = lane_index((ny, LANES))
     at_low, at_high = lanes == 0, lanes == LANES - 1
-    low_z, high_z = sides(even_z, got_z, lambda ref: ref[groups // 2, :ny, :])
+    low_z, high_z = sides(even("gz"), got_z, lambda ref: ref[groups // 2, :ny, :])
     press_z = jnp.where(lanes % 2 == 0, high_z, roll_lanes(low_z, 1))
-    p_low, p_high = sides(even_x, got_x, lambda ref: ref[PRESS * ny : (PRESS + 1) * ny, :])
-    u_low, _ = sides(even_x, got_x, lambda ref: ref[VX * ny : (VX + 1) * ny, :])
 
     def solved(x):
         e = x % total
@@ -737,37 +765,30 @@
         return jnp.where(spoiled, roll_lanes(spill[e % groups], 1 - DEPTH - GROUP * (e // groups)), cells)
 
     copies = []
-    rows = row_index((ROWS, LANES))
     below, here = solved(-1), solved(0)
-    face_low = (p_low - press[0]) * (u_low + here[:ny] - below[:ny])
+    down = here[:ny] - below[:ny]
     for x in range(nx):
         above = solved(x + 1)
         group, seat = x % groups, x // groups
-        own, p = here[:ny], press[x]
-        out = vel[0, x] + (above[:ny] - own)
-        ustar[0, x] = out
-        face = (p - (press[x + 1] if x + 1 < nx else p_high)) * out
-        answer = face_low + face
-        face_low = face
-        low, high = sides(even_y, got_y, lambda ref: ref[total + x // ROWS, x % ROWS : x % ROWS + 1, :])
-        shape = (ROWS, LANES)
-        p_tile = jnp.where(rows == 0, jnp.broadcast_to(high, shape), jnp.broadcast_to(low, shape))
-        p_tall = jnp.concatenate([p, p_tile], 0)
-        u_row, _ = sides(even_y, got_y, lambda ref: ref[x, ROWS - 1 :, :])
-        u_tall = jnp.concatenate([vel[1, x], jnp.broadcast_to(u_row, shape)], 0)
-        out = vel[1, x] + (roll_rows(here, -1)[:ny] - own)
-        ustar[1, x] = out
-        back = roll_rows(u_tall, 1)[:ny] + (own - roll_rows(here, 1)[:ny])
-        answer = answer + ((p - roll_rows(p_tall, -1)[:ny]) * out + (roll_rows(p_tall, 1)[:ny] - p) * back)
+        own = here[:ny]
+        up = above[:ny] - own
+        ustar[0, x] = vel[0, x] + up
+        answer = base[x] + (slope_x[x + 1] * up + slope_x[x] * down)
+        next_down = up
+        up, down = roll_rows(here, -1)[:ny] - own, own - roll_rows(here, 1)[:ny]
+        ustar[1, x] = vel[1, x] + up
+        answer = answer + (slope_y[0, x] * up + slope_y[1, x] * down)
         lam_end = roll_lanes(spill[group][:ny], 1 - 2 * DEPTH - GROUP * seat)
         u_end = roll_lanes(vz_z[group, :ny, :], 1 - DEPTH - GROUP * seat)
         p_end = roll_lanes(press_z, LANES - 1 - press_lane(x))
-        out = vel[2, x] + (jnp.where(at_high, lam_end, roll_lanes(own, -1)) - own)
+        up = jnp.where(at_high, lam_end, roll_lanes(own, -1)) - own
+        down = own - jnp.where(at_low, lam_end, roll_lanes(own, 1))
+        out = vel[2, x] + up
         ustar[2, x] = out
-        answer = answer + (p - jnp.where(at_high, p_end, roll_lanes(p, -1))) * out
-        back = jnp.where(at_low, u_end, roll_lanes(vel[2, x], 1))
-        back = back + (own - jnp.where(at_low, lam_end, roll_lanes(own, 1)))
-        answer = answer + (jnp.where(at_low, p_end, roll_lanes(p, 1)) - p) * back
+        answer = answer + (slope_z[0, x] * up + slope_z[1, x] * down)
+        beyond = jnp.where(at_low, p_end * (u_end + down) + slope_z[1, x] * u_end, 0.0)
+        answer = answer + jnp.where(at_high, -p_end * out, beyond)
+        down = next_down
         coef_cot[x] = 0.5 * answer
         here = above
         if (x + 1) % STRIDE == 0:
@@ -879,10 +900,17 @@
         "prepare",
         [scratch(*cube), scratch(2, *cube), scratch(2, *cube), scratch(*cube)],
     )
+    slope = call(
+        functools.partial(slopes, nx, ny, n_x, n_y),
+        [press, vel, *got_x, *got_y],
+        [VMEM] * (2 + n_x + n_y),
+        [f32(nx + 1, ny, nz), f32(2, nx, ny, nz), f32(2, nx, ny, nz), f32(nx, ny, nz)],
+        "slopes",
+    )
     basis_z, vz_z, sums = call(
         functools.partial(join, nx, ny, n_z),
-        [ends, shares, *got_z],
-        [VMEM] * (2 + n_z),
+        [slope[-1], ends, shares, *got_z],
+        [ANY] + [VMEM] * (2 + n_z),
         [f32(3, 2 * groups, height, LANES), f32(groups, height, LANES), f32(1, LANES)],
         "join",
         [scratch(6, 2 * groups, height, LANES), scratch(2 * groups, height, LANES)],
@@ -890,9 +918,9 @@
     spread = jnp.broadcast_to(sums[None], (devices, 1, LANES))
     gathered = lax.all_to_all(spread, AXES, 0, 0).reshape(devices, LANES)
     return call(
-        functools.partial(finish, nx, ny, n_x, n_y, n_z),
-        [gathered, press, vel, basis, basis_z, vz_z, *got_x, *got_y, *got_z],
-        [VMEM] * (6 + n_x + n_y + n_z),
+        functools.partial(finish, nx, ny, n_z),
+        [gathered, vel, basis, basis_z, vz_z, *slope, *got_z],
+        [VMEM] * (9 + n_z),
         [f32(*vel.shape), f32(nx, ny, nz)],
         "finish",
         [scratch(*vel.shape), scratch(nx, ny, nz), pltpu.SemaphoreType.DMA((2, nx // STRIDE))],

time: 32.5 us -> 32.3 us (level)
    pallas_call x9 -> x10, Pallas kernels: 8.91 us -> 9 us  [call(): pl.pallas_call(kernel, out_shape=shapes, in_specs=in_specs, out_specs=[ou...]
  transfers between devices with their start and end apart: 7 -> 7, of which waited for: 4 -> 4; matrix products, arithmetic and copies ran while one was open for 0% -> 0% of each run, Pallas kernels for 13% -> 14%
where the time goes in v9:
time: 32.3 us; the launch traced here: 32.1 us
  blocking collectives  11 us (34%)
  starting transfers between devices  9.86 us (31%)
  Pallas kernels  9 us (28%)
  waiting for transfers between devices  1.59 us (5%)
  between operations  0.69 us (2%)
    all_to_all x1, blocking collectives, on_device(): gathered = lax.all_to_all(spread, AXES, 0, 0).reshape(devices, LANES)  11 us
    ppermute x7, starting transfers between devices, exchange(): return lax.ppermute(send, AXES, swaps(moves))  9.86 us
    pallas_call x10, Pallas kernels, call(): pl.pallas_call(kernel, out_shape=shapes, in_specs=in_specs, out_specs=[ou...  9 us
    ppermute x7, waiting for transfers between devices, exchange(): return lax.ppermute(send, AXES, swaps(moves))  1.59 us
  transfers between devices with their start and end apart: 7, of which 4 were waited for; matrix products, arithmetic and copies ran while one was open for 0% of the time, Pallas kernels for 14%

profile of v9, /device:TPU:0, one launch (start us, length us, event | category | flops | bytes accessed | tf_op | source)
XLA Modules:
  0.0 32.1 jit_solution(5028659694080003525)
XLA Ops:
  0.6 1.7 %pack_first.1 = (f32[304,128]{1,0:T(8,128)S(1)}, f32[304,128]{1,0:T(8,128)S(1)}, f32[20,8,128]{2,1,0:T(8,128)S(1)}, f32[6,8,128]{2,1,0:T(8,128)S(1)}, f32[6,8,128]{2,1,0:T(8,128)S(1)}) custom-call(s32[16,32,128]{2,1,0:T(8,128)} %phase.3, f32[16,32,128]{2,1,0:T(8,128)} %press.3, f32[3,16,32,128]{3,2,1,0:T(8,128)} %vel.3), custom_call_target="tpu_custom_call" | custom-call | flops 3000000 | bytes 3000000 | tf_op jit(solution)/shard_map/pack_first/pallas_call | solution.py:816
  2.3 0.5 %collective-permute-start.1 = (f32[304,128]{1,0:T(8,128)S(1)}, f32[304,128]{1,0:T(8,128)S(1)}, u32[]{:S(2)}, u32[]{:S(2)}) collective-permute-start(f32[304,128]{1,0:T(8,128)S(1)} %get-tuple-element.30), channel_id=1, source_target_pairs={{0,2},{1,3},{2,0},{3,1},{4,6},{5,7},{6,4},{7,5},{8,16},{9,17},{10,... | collective-permute-start | bytes 466952 | tf_op jit(solution)/shard_map/ppermute | solution.py:45
  2.9 4.1 %collective-permute-start = (f32[304,128]{1,0:T(8,128)S(1)}, f32[304,128]{1,0:T(8,128)S(1)}, u32[]{:S(2)}, u32[]{:S(2)}) collective-permute-start(f32[304,128]{1,0:T(8,128)S(1)} %get-tuple-element.27.after), channel_id=1, source_target_pairs={{0,8},{1,9},{2,10},{3,11},{4,12},{5,13},{6,14},{7,15},{8,0},{9,1},... | collective-permute-start | bytes 466952 | tf_op jit(solution)/shard_map/ppermute | solution.py:45
  7.0 1.5 %collective-permute-start.2 = (f32[20,8,128]{2,1,0:T(8,128)S(1)}, f32[20,8,128]{2,1,0:T(8,128)S(1)}, u32[]{:S(2)}, u32[]{:S(2)}) collective-permute-start(f32[20,8,128]{2,1,0:T(8,128)S(1)} %get-tuple-element.33), channel_id=1, source_target_pairs={{0,1},{1,0},{2,4},{3,5},{4,2},{5,3},{6,7},{7,6},{8,9},{9,8},{10,12... | collective-permute-start | bytes 245768 | tf_op jit(solution)/shard_map/ppermute | solution.py:45
  8.5 0.5 %collective-permute-start.3 = (f32[6,8,128]{2,1,0:T(8,128)S(1)}, f32[6,8,128]{2,1,0:T(8,128)S(1)}, u32[]{:S(2)}, u32[]{:S(2)}) collective-permute-start(f32[6,8,128]{2,1,0:T(8,128)S(1)} %get-tuple-element.34), channel_id=1, source_target_pairs={{0,1},{1,0},{2,12},{3,13},{4,10},{5,11},{6,7},{7,6},{8,9},{9,8},{1... | collective-permute-start | bytes 73736 | tf_op jit(solution)/shard_map/ppermute | solution.py:45
  9.0 1.5 %collective-permute-start.4 = (f32[6,8,128]{2,1,0:T(8,128)S(1)}, f32[6,8,128]{2,1,0:T(8,128)S(1)}, u32[]{:S(2)}, u32[]{:S(2)}) collective-permute-start(f32[6,8,128]{2,1,0:T(8,128)S(1)} %get-tuple-element.35), channel_id=1, source_target_pairs={{0,1},{1,0},{2,3},{3,2},{4,5},{5,4},{6,7},{7,6},{8,9},{9,8},{10,20... | collective-permute-start | bytes 73736 | tf_op jit(solution)/shard_map/ppermute | solution.py:45
  10.6 1.6 %load.1 = (f32[16,32,128]{2,1,0:T(8,128)S(1)}, f32[16,32,128]{2,1,0:T(8,128)S(1)}, f32[3,16,32,128]{3,2,1,0:T(8,128)S(1)}, f32[16,32,128]{2,1,0:T(8,128)S(1)}) custom-call(s32[16,32,128]{2,1,0:T(8,128)} %phase.3, f32[16,32,128]{2,1,0:T(8,128)} %press.3, f32[3,16,32,128]{3,2,1,0:T(8,128)} %vel.3, f32[304,128]{1,0:T(8,128)S(1)} %get-tuple-element.27.after), custom_call_target="tpu_custom_call" | custom-call | flops 3000000 | bytes 3000000 | tf_op jit(solution)/shard_map/load/pallas_call | solution.py:816
  12.2 0.2 collective-permute-done.3.refs_0_
  12.4 0.5 %collective-permute-done.4.refs_1_ = f32[6,8,128]{2,1,0:T(8,128)S(1)} collective-permute-done((f32[6,8,128]{2,1,0:T(8,128)S(1)}, f32[6,8,128]{2,1,0:T(8,128)S(1)}, u32[]{:S(2)}, u32[]{:S(2)}) %collective-permute-start.4) | collective-permute-done | bytes 24608 | tf_op jit(solution)/shard_map/ppermute | solution.py:45
  12.9 0.0 collective-permute-done.2.got
  12.9 0.1 merge_odd.1.refs_2_.refs_3_
  13.0 0.0 collective-permute-done.refs_0_
  13.0 0.1 pack_y.1
  13.1 0.1 collective-permute-start.5
  13.2 0.6 %stage_z.1 = (f32[24,40,128]{2,1,0:T(8,128)S(1)}, f32[24,40,128]{2,1,0:T(8,128)S(1)}, f32[2,40,128]{2,1,0:T(8,128)S(1)}) custom-call(f32[16,32,128]{2,1,0:T(8,128)S(1)} %get-tuple-element.31.coef, f32[16,32,128]{2,1,0:T(8,128)S(1)} %get-tuple-element.28.press, f32[3,16,32,128]{3,2,1,0:T(8,128)S(1)} %get-tuple-element.29.vel, ...), custom_call_target="tpu_custom_call" | custom-call | flops 3000000 | bytes 3000000 | tf_op jit(solution)/shard_map/stage_z/pallas_call | solution.py:816
  13.7 0.7 %collective-permute-done.5.refs_2_ = f32[27,8,128]{2,1,0:T(8,128)S(1)} collective-permute-done((f32[27,8,128]{2,1,0:T(8,128)S(1)}, f32[27,8,128]{2,1,0:T(8,128)S(1)}, u32[]{:S(2)}, u32[]{:S(2)}) %collective-permute-start.5) | collective-permute-done | bytes 110624 | tf_op jit(solution)/shard_map/ppermute | solution.py:45
  14.5 0.2 pack_z.1
  14.7 1.6 %collective-permute-start.6 = (f32[2,40,128]{2,1,0:T(8,128)S(1)}, f32[2,40,128]{2,1,0:T(8,128)S(1)}, u32[]{:S(2)}, u32[]{:S(2)}) collective-permute-start(f32[2,40,128]{2,1,0:T(8,128)S(1)} %get-tuple-element.44), channel_id=1, source_target_pairs={{0,1},{1,0},{2,3},{3,2},{4,5},{5,4},{6,7},{7,6},{8,9},{9,8},{10,11... | collective-permute-start | bytes 122888 | tf_op jit(solution)/shard_map/ppermute | solution.py:45
  16.3 0.3 slopes.1
  16.6 2.0 %prepare.1 = (f32[3,24,40,128]{3,2,1,0:T(8,128)S(1)}, f32[5,3,40,128]{3,2,1,0:T(8,128)S(1)}, f32[6,8,128]{2,1,0:T(8,128)S(1)}) custom-call(f32[16,32,128]{2,1,0:T(8,128)S(1)} %get-tuple-element.31.coef, f32[3,16,32,128]{3,2,1,0:T(8,128)S(1)} %get-tuple-element.29.vel, f32[16,32,128]{2,1,0:T(8,128)S(1)} %get-tuple-element.32.rhs, ...), custom_call_target="tpu_custom_call" | custom-call | flops 3000000 | bytes 3000000 | tf_op jit(solution)/shard_map/prepare/pallas_call | solution.py:816
  18.6 0.2 collective-permute-done.6.refs_0_
  18.8 0.7 %join.1 = (f32[3,6,40,128]{3,2,1,0:T(8,128)S(1)}, f32[3,40,128]{2,1,0:T(8,128)S(1)}, f32[1,128]{1,0:T(1,128)S(1)}) custom-call(f32[16,32,128]{2,1,0:T(8,128)S(1)} %get-tuple-element.36.after.base, f32[5,3,40,128]{3,2,1,0:T(8,128)S(1)} %get-tuple-element.42.ends, f32[6,8,128]{2,1,0:T(8,128)S(1)} %get-tuple-element.43.shares, ...), custom_call_target="tpu_custom_call" | custom-call | flops 3000000 | bytes 3000000 | tf_op jit(solution)/shard_map/join/pallas_call | solution.py:816
  19.5 11.0 %all_to_all.5 = f32[32,1,128]{2,1,0:T(1,128)S(1)} all-to-all(f32[32,1,128]{2,1,0:T(1,128)S(1)} %broadcast_in_dim.9), channel_id=1, replica_groups=mesh['gx'=4,'gy'=4,'gz'=2] {'gx','gy','gz'}, dimensions={0} | all-to-all | bytes 32768 | tf_op jit(solution)/shard_map/all_to_all | solution.py:919
  30.5 1.6 %finish.1 = (f32[3,16,32,128]{3,2,1,0:T(8,128)}, f32[16,32,128]{2,1,0:T(8,128)}) custom-call(f32[32,128]{1,0:T(8,128)S(1)} %bitcast.2, f32[3,16,32,128]{3,2,1,0:T(8,128)S(1)} %get-tuple-element.29.vel, f32[3,24,40,128]{3,2,1,0:T(8,128)S(1)} %get-tuple-element.46.basis, f32[3,6,40,128]{3,2,1,0:T(8,128)S(1)} %get-tuple-element.47.basis_z, ...), custom_call_target="tpu_custom_call" | custom-call | flops 3000000 | bytes 3000000 | tf_op jit(solution)/shard_map/finish/pallas_call | solution.py:816
  (2 shorter events, 0.0 us)
Async XLA Ops:
  2.3 10.6 %collective-permute-start.1 = (f32[304,128]{1,0:T(8,128)S(1)}, f32[304,128]{1,0:T(8,128)S(1)}, u32[]{:S(2)}, u32[]{:S(2)}) collective-permute-start(f32[304,128]{1,0:T(8,128)S(1)} %get-tuple-element.30), channel_id=1, source_target_pairs={{0,2},{1,3},{2,0},{3,1},{4,6},{5,7},{6,4},{7,5},{8,16},{9,17},{10,... | collective-permute-start | bytes 466952 | tf_op jit(solution)/shard_map/ppermute | solution.py:45
  2.9 10.1 %collective-permute-start = (f32[304,128]{1,0:T(8,128)S(1)}, f32[304,128]{1,0:T(8,128)S(1)}, u32[]{:S(2)}, u32[]{:S(2)}) collective-permute-start(f32[304,128]{1,0:T(8,128)S(1)} %get-tuple-element.27.after), channel_id=1, source_target_pairs={{0,8},{1,9},{2,10},{3,11},{4,12},{5,13},{6,14},{7,15},{8,0},{9,1},... | collective-permute-start | bytes 466952 | tf_op jit(solution)/shard_map/ppermute | solution.py:45
  7.0 5.9 %collective-permute-start.2 = (f32[20,8,128]{2,1,0:T(8,128)S(1)}, f32[20,8,128]{2,1,0:T(8,128)S(1)}, u32[]{:S(2)}, u32[]{:S(2)}) collective-permute-start(f32[20,8,128]{2,1,0:T(8,128)S(1)} %get-tuple-element.33), channel_id=1, source_target_pairs={{0,1},{1,0},{2,4},{3,5},{4,2},{5,3},{6,7},{7,6},{8,9},{9,8},{10,12... | collective-permute-start | bytes 245768 | tf_op jit(solution)/shard_map/ppermute | solution.py:45
  8.5 3.8 %collective-permute-start.3 = (f32[6,8,128]{2,1,0:T(8,128)S(1)}, f32[6,8,128]{2,1,0:T(8,128)S(1)}, u32[]{:S(2)}, u32[]{:S(2)}) collective-permute-start(f32[6,8,128]{2,1,0:T(8,128)S(1)} %get-tuple-element.34), channel_id=1, source_target_pairs={{0,1},{1,0},{2,12},{3,13},{4,10},{5,11},{6,7},{7,6},{8,9},{9,8},{1... | collective-permute-start | bytes 73736 | tf_op jit(solution)/shard_map/ppermute | solution.py:45
  9.0 3.8 %collective-permute-start.4 = (f32[6,8,128]{2,1,0:T(8,128)S(1)}, f32[6,8,128]{2,1,0:T(8,128)S(1)}, u32[]{:S(2)}, u32[]{:S(2)}) collective-permute-start(f32[6,8,128]{2,1,0:T(8,128)S(1)} %get-tuple-element.35), channel_id=1, source_target_pairs={{0,1},{1,0},{2,3},{3,2},{4,5},{5,4},{6,7},{7,6},{8,9},{9,8},{10,20... | collective-permute-start | bytes 73736 | tf_op jit(solution)/shard_map/ppermute | solution.py:45
  13.1 1.4 %collective-permute-start.5 = (f32[27,8,128]{2,1,0:T(8,128)S(1)}, f32[27,8,128]{2,1,0:T(8,128)S(1)}, u32[]{:S(2)}, u32[]{:S(2)}) collective-permute-start(f32[27,8,128]{2,1,0:T(8,128)S(1)} %pack_y.1), channel_id=1, source_target_pairs={{0,2},{1,3},{2,0},{3,1},{4,6},{5,7},{6,4},{7,5},{8,10},{9,11},{10,... | collective-permute-start | bytes 331784 | tf_op jit(solution)/shard_map/ppermute | solution.py:45
  14.7 4.1 %collective-permute-start.6 = (f32[2,40,128]{2,1,0:T(8,128)S(1)}, f32[2,40,128]{2,1,0:T(8,128)S(1)}, u32[]{:S(2)}, u32[]{:S(2)}) collective-permute-start(f32[2,40,128]{2,1,0:T(8,128)S(1)} %get-tuple-element.44), channel_id=1, source_target_pairs={{0,1},{1,0},{2,3},{3,2},{4,5},{5,4},{6,7},{7,6},{8,9},{9,8},{10,11... | collective-permute-start | bytes 122888 | tf_op jit(solution)/shard_map/ppermute | solution.py:45

commit v10 on v9

--- a/solution.py
+++ b/solution.py
@@ -110,7 +110,7 @@
     outs, odd_outs, (held, held_vel, sem) = refs[:n_x], refs[n_x:-3], refs[-3:]
     if n_y > 1:
         *odd_outs, tile_phase, tile_vel, tile_press, tile_sem = odd_outs
-    copies = []
+    copies, late = [], []
     for turn, out in enumerate(outs):
         top = even("gx") == (turn == 0)
         deep = jnp.where(top, nx - DEPTH, 0)
@@ -134,12 +134,12 @@
         for which, (src, dst) in enumerate(parts):
             copy = pltpu.make_async_copy(src, dst, tile_sem.at[which])
             copy.start()
-            copies.append(copy)
-    for copy in copies:
-        copy.wait()
+            late.append(copy)
     lanes = lane_index((ROWS, LANES))
     rows = row_index((ROWS, LANES))
     for turn, out in enumerate(outs):
+        for copy in copies[3 * turn : 3 * turn + 3]:
+            copy.wait()
         top = even("gx") == (turn == 0)
         coefs = [coefficient(held[turn, j]) for j in range(DEPTH)]
         flux = [0.5 * (coefs[j] + coefs[j + 1]) * held_vel[turn, 0, j] for j in range(DEPTH - 1)]
@@ -162,6 +162,8 @@
         out[VY * ny : VY * ny + ROWS, :] = lines
         out[VY * ny + ROWS :, :] = columns
         clear_if_alone(out, ("gx", turn))
+    for copy in late:
+        copy.wait()
     if n_y > 1:
         pack_odd(nx, tile_phase, tile_vel, tile_press, odd_outs)
 
@@ -603,87 +605,108 @@
         shares[which] = total_.value()
 
 
-def join(nx, ny, n_z, after, ends, shares, *refs):
-    del after
-    got_z = refs[:n_z]
-    basis_z, vz_z, sums, weight_z, inverse_z = refs[n_z:]
+def beside_z(side):
+    place = lax.axis_index("gz")
+    return place > 0 if side == 0 else place < lax.axis_size("gz") - 1
+
+
+def solve_end(nx, ny, side, received, ends, basis_z, vz_z, shares, weight_z, inverse_z):
     total, height = nx + 2 * DEPTH, ny + 2 * DEPTH
     groups = total // ROWS
     lanes = lane_index((height, LANES))
     seat_lane, seat = lanes % GROUP, lanes // GROUP
+    outer = seat_lane < DEPTH if side == 0 else seat_lane >= GROUP - DEPTH
     coef, rhs, vz = [], [], []
-    for side in range(2):
-        for g in range(groups):
-            got = sides(even("gz"), got_z, lambda ref: ref[g // 2])[side]
-            skip = ROWS * (g % 2)
-            if side == 0:
-                outer = seat_lane < DEPTH
-                coef.append(jnp.where(outer, roll_lanes(got, -skip), ends[0, g]))
-                rhs.append(jnp.where(outer, roll_lanes(got, 1 - DEPTH - skip), ends[2, g]))
-                vz.append(roll_lanes(got, -DEPTH - skip))
-                vz_z[g] = vz[-1]
-            else:
-                outer = seat_lane >= GROUP - DEPTH
-                coef.append(jnp.where(outer, roll_lanes(got, GROUP - DEPTH - skip), ends[1, g]))
-                rhs.append(jnp.where(outer, roll_lanes(got, GROUP - 2 * DEPTH - skip), ends[3, g]))
-                vz.append(ends[4, g])
-
-    def along(planes, q, step):
-        g = q % groups
+    for g in range(groups):
+        got, skip = received(g // 2), ROWS * (g % 2)
+        start = 0 if side == 0 else GROUP - DEPTH
+        less = 1 if side == 0 else 0
+        coef.append(jnp.where(outer, roll_lanes(got, start - skip), ends[side, g]))
+        rhs.append(jnp.where(outer, roll_lanes(got, start + less - DEPTH - skip), ends[2 + side, g]))
+        if side == 0:
+            vz.append(roll_lanes(got, -DEPTH - skip))
+            vz_z[g] = vz[-1]
+        else:
+            vz.append(ends[4, g])
+
+    def along(planes, g, step):
         if 0 <= g + step < groups:
-            return planes[q + step]
-        return roll_lanes(planes[q - g + (g + step) % groups], -GROUP * step)
+            return planes[g + step]
+        return roll_lanes(planes[(g + step) % groups], -GROUP * step)
 
     totals = [Totals() for _ in range(6)]
 
-    def count(which, q, left, right):
-        first = DEPTH if q < groups else GROUP - 2 * DEPTH
+    def count(which, g, left, right):
+        first = DEPTH if side == 0 else GROUP - 2 * DEPTH
         spot = seat_lane[:ROWS]
-        mine = (spot >= first) & (spot < first + DEPTH) & (seat[:ROWS] * groups + q % groups < nx)
+        mine = (spot >= first) & (spot < first + DEPTH) & (seat[:ROWS] * groups + g < nx)
         product = left[:ny] * right[:ny]
         tile = tree_sum([product[i : i + ROWS] for i in range(0, ny, ROWS)])
         totals[which].add(jnp.where(mine, tile, 0.0))
 
     field = []
-    for q in range(2 * groups):
-        here = coef[q]
-        neighbours = (along(coef, q, 1), along(coef, q, -1), roll_rows(here, -1), roll_rows(here, 1))
+    for g in range(groups):
+        here, q = coef[g], side * groups + g
+        neighbours = (along(coef, g, 1), along(coef, g, -1), roll_rows(here, -1), roll_rows(here, 1))
         neighbours += (roll_lanes(here, -1), roll_lanes(here, 1))
         weights = [0.5 * (here + other) for other in neighbours]
         for which, weight in enumerate(weights):
-            weight_z[which, q] = weight
+            weight_z[which, g] = weight
         diag = (weights[0] + weights[1]) + (weights[2] + weights[3]) + (weights[4] + weights[5])
-        face = DEPTH - 1 if q < groups else GROUP - DEPTH - 1
-        source = rhs[q] + jnp.where(seat_lane == face, weights[4] * vz[q], 0.0)
-        source = source - jnp.where(seat_lane == face + 1, weights[5] * roll_lanes(vz[q], 1), 0.0)
+        face = DEPTH - 1 if side == 0 else GROUP - DEPTH - 1
+        source = rhs[g] + jnp.where(seat_lane == face, weights[4] * vz[g], 0.0)
+        source = source - jnp.where(seat_lane == face + 1, weights[5] * roll_lanes(vz[g], 1), 0.0)
         inside = here > 0
         scale = jnp.where(inside, 1.0 / jnp.where(inside, diag, 1.0), 0.0)
-        inverse_z[q] = scale
+        inverse_z[g] = scale
         field.append(scale * source)
-        basis_z[0, q] = field[q]
-        count(0, q, field[q], source)
+        basis_z[0, q] = field[g]
+        count(0, g, field[g], source)
     for n in range(3):
         following = []
-        for q in range(2 * groups):
-            here = field[q]
-            image = weight_z[0, q] * (here - along(field, q, 1)) + weight_z[1, q] * (here - along(field, q, -1))
+        for g in range(groups):
+            here, q = field[g], side * groups + g
+            image = weight_z[0, g] * (here - along(field, g, 1)) + weight_z[1, g] * (here - along(field, g, -1))
             image = image + (
-                weight_z[2, q] * (here - roll_rows(here, -1)) + weight_z[3, q] * (here - roll_rows(here, 1))
+                weight_z[2, g] * (here - roll_rows(here, -1)) + weight_z[3, g] * (here - roll_rows(here, 1))
             )
             image = image + (
-                weight_z[4, q] * (here - roll_lanes(here, -1)) + weight_z[5, q] * (here - roll_lanes(here, 1))
+                weight_z[4, g] * (here - roll_lanes(here, -1)) + weight_z[5, g] * (here - roll_lanes(here, 1))
             )
-            count(2 * n + 1, q, here, image)
+            count(2 * n + 1, g, here, image)
             if n < 2:
-                following.append(inverse_z[q] * image)
-                basis_z[n + 1, q] = following[q]
-                count(2 * n + 2, q, following[q], image)
+                following.append(inverse_z[g] * image)
+                basis_z[n + 1, q] = following[g]
+                count(2 * n + 2, g, following[g], image)
         field = following
+    for which, total_ in enumerate(totals):
+        shares[which] = shares[which] + total_.value()
+
+
+def outer_ends(nx, ny, ends, shares_in, basis_z, vz_z, shares, *scratch):
+    shares[...] = shares_in[...]
+    nothing = jnp.zeros((ny + 2 * DEPTH, LANES), jnp.float32)
+    for side in range(2):
+
+        @pl.when(jnp.logical_not(beside_z(side)))
+        def _():
+            solve_end(nx, ny, side, lambda i: nothing, ends, basis_z, vz_z, shares, *scratch)
+
+
+def join(nx, ny, n_z, after, ends, *refs):
+    del after
+    got_z, (basis_z, vz_z, shares, sums, *scratch) = refs[:n_z], refs[n_z + 3 :]
+    for side in range(2):
+
+        @pl.when(beside_z(side))
+        def _():
+            received = lambda i: sides(even("gz"), got_z, lambda ref: ref[i])[side]
+            solve_end(nx, ny, side, received, ends, basis_z, vz_z, shares, *scratch)
+
     lane = lane_index((1, LANES))
     row = jnp.zeros((1, LANES), jnp.float32)
-    for which, total_ in enumerate(totals):
-        value = total_.value() + shares[which]
-        value = jnp.sum(jnp.sum(value, 0, keepdims=True), 1, keepdims=True)
+    for which in range(6):
+        value = jnp.sum(jnp.sum(shares[which], 0, keepdims=True), 1, keepdims=True)
         row = jnp.where(lane == which, value, row)
     sums[...] = row
 
@@ -907,13 +930,24 @@
         [f32(nx + 1, ny, nz), f32(2, nx, ny, nz), f32(2, nx, ny, nz), f32(nx, ny, nz)],
         "slopes",
     )
-    basis_z, vz_z, sums = call(
+    shapes_z = [f32(3, 2 * groups, height, LANES), f32(groups, height, LANES), f32(6, ROWS, LANES)]
+    scratch_z = [scratch(6, groups, height, LANES), scratch(groups, height, LANES)]
+    outer = call(
+        functools.partial(outer_ends, nx, ny),
+        [ends, shares],
+        [VMEM] * 2,
+        shapes_z,
+        "outer_ends",
+        scratch_z,
+    )
+    basis_z, vz_z, _, sums = call(
         functools.partial(join, nx, ny, n_z),
-        [slope[-1], ends, shares, *got_z],
-        [ANY] + [VMEM] * (2 + n_z),
-        [f32(3, 2 * groups, height, LANES), f32(groups, height, LANES), f32(1, LANES)],
+        [slope[-1], ends, *got_z, *outer],
+        [ANY] + [VMEM] * (4 + n_z),
+        shapes_z + [f32(1, LANES)],
         "join",
-        [scratch(6, 2 * groups, height, LANES), scratch(2 * groups, height, LANES)],
+        scratch_z,
+        aliases={2 + n_z + which: which for which in range(3)},
     )
     spread = jnp.broadcast_to(sums[None], (devices, 1, LANES))
     gathered = lax.all_to_all(spread, AXES, 0, 0).reshape(devices, LANES)

time: 32.3 us -> 32 us (level)
  blocking collectives: 11 us -> 10.6 us
    all_to_all x1, blocking collectives: 11 us -> 10.6 us  [on_device(): gathered = lax.all_to_all(spread, AXES, 0, 0).reshape(devices, LANES)]
    pallas_call x10 -> x11, Pallas kernels: 9 us -> 9.2 us  [call(): pl.pallas_call(kernel, out_shape=shapes, in_specs=in_specs, out_specs=[ou...]
  transfers between devices with their start and end apart: 7 -> 7, of which waited for: 4 -> 3; matrix products, arithmetic and copies ran while one was open for 0% -> 0% of each run, Pallas kernels for 14% -> 16%
where the time goes in v10:
time: 32 us; the launch traced here: 31.8 us
  blocking collectives  10.6 us (33%)
  starting transfers between devices  9.86 us (31%)
  Pallas kernels  9.2 us (29%)
  waiting for transfers between devices  1.42 us (4%)
  between operations  0.7 us (2%)
    all_to_all x1, blocking collectives, on_device(): gathered = lax.all_to_all(spread, AXES, 0, 0).reshape(devices, LANES)  10.6 us
    ppermute x7, starting transfers between devices, exchange(): return lax.ppermute(send, AXES, swaps(moves))  9.86 us
    pallas_call x11, Pallas kernels, call(): pl.pallas_call(kernel, out_shape=shapes, in_specs=in_specs, out_specs=[ou...  9.2 us
    ppermute x7, waiting for transfers between devices, exchange(): return lax.ppermute(send, AXES, swaps(moves))  1.42 us
  transfers between devices with their start and end apart: 7, of which 3 were waited for; matrix products, arithmetic and copies ran while one was open for 0% of the time, Pallas kernels for 16%

profile of v10, /device:TPU:0, one launch (start us, length us, event | category | flops | bytes accessed | tf_op | source)
XLA Modules:
  0.0 31.8 jit_solution(5259494279573889)
XLA Ops:
  0.6 1.6 %pack_first.1 = (f32[304,128]{1,0:T(8,128)S(1)}, f32[304,128]{1,0:T(8,128)S(1)}, f32[20,8,128]{2,1,0:T(8,128)S(1)}, f32[6,8,128]{2,1,0:T(8,128)S(1)}, f32[6,8,128]{2,1,0:T(8,128)S(1)}) custom-call(s32[16,32,128]{2,1,0:T(8,128)} %phase.3, f32[16,32,128]{2,1,0:T(8,128)} %press.3, f32[3,16,32,128]{3,2,1,0:T(8,128)} %vel.3), custom_call_target="tpu_custom_call" | custom-call | flops 3000000 | bytes 3000000 | tf_op jit(solution)/shard_map/pack_first/pallas_call | solution.py:839
  2.2 0.5 %collective-permute-start.1 = (f32[304,128]{1,0:T(8,128)S(1)}, f32[304,128]{1,0:T(8,128)S(1)}, u32[]{:S(2)}, u32[]{:S(2)}) collective-permute-start(f32[304,128]{1,0:T(8,128)S(1)} %get-tuple-element.33), channel_id=1, source_target_pairs={{0,2},{1,3},{2,0},{3,1},{4,6},{5,7},{6,4},{7,5},{8,16},{9,17},{10,... | collective-permute-start | bytes 466952 | tf_op jit(solution)/shard_map/ppermute | solution.py:45
  2.7 4.2 %collective-permute-start = (f32[304,128]{1,0:T(8,128)S(1)}, f32[304,128]{1,0:T(8,128)S(1)}, u32[]{:S(2)}, u32[]{:S(2)}) collective-permute-start(f32[304,128]{1,0:T(8,128)S(1)} %get-tuple-element.30.after), channel_id=1, source_target_pairs={{0,8},{1,9},{2,10},{3,11},{4,12},{5,13},{6,14},{7,15},{8,0},{9,1},... | collective-permute-start | bytes 466952 | tf_op jit(solution)/shard_map/ppermute | solution.py:45
  6.9 1.5 %collective-permute-start.2 = (f32[20,8,128]{2,1,0:T(8,128)S(1)}, f32[20,8,128]{2,1,0:T(8,128)S(1)}, u32[]{:S(2)}, u32[]{:S(2)}) collective-permute-start(f32[20,8,128]{2,1,0:T(8,128)S(1)} %get-tuple-element.36), channel_id=1, source_target_pairs={{0,1},{1,0},{2,4},{3,5},{4,2},{5,3},{6,7},{7,6},{8,9},{9,8},{10,12... | collective-permute-start | bytes 245768 | tf_op jit(solution)/shard_map/ppermute | solution.py:45
  8.4 0.5 %collective-permute-start.3 = (f32[6,8,128]{2,1,0:T(8,128)S(1)}, f32[6,8,128]{2,1,0:T(8,128)S(1)}, u32[]{:S(2)}, u32[]{:S(2)}) collective-permute-start(f32[6,8,128]{2,1,0:T(8,128)S(1)} %get-tuple-element.37), channel_id=1, source_target_pairs={{0,1},{1,0},{2,12},{3,13},{4,10},{5,11},{6,7},{7,6},{8,9},{9,8},{1... | collective-permute-start | bytes 73736 | tf_op jit(solution)/shard_map/ppermute | solution.py:45
  8.9 1.5 %collective-permute-start.4 = (f32[6,8,128]{2,1,0:T(8,128)S(1)}, f32[6,8,128]{2,1,0:T(8,128)S(1)}, u32[]{:S(2)}, u32[]{:S(2)}) collective-permute-start(f32[6,8,128]{2,1,0:T(8,128)S(1)} %get-tuple-element.38), channel_id=1, source_target_pairs={{0,1},{1,0},{2,3},{3,2},{4,5},{5,4},{6,7},{7,6},{8,9},{9,8},{10,20... | collective-permute-start | bytes 73736 | tf_op jit(solution)/shard_map/ppermute | solution.py:45
  10.4 1.6 %load.1 = (f32[16,32,128]{2,1,0:T(8,128)S(1)}, f32[16,32,128]{2,1,0:T(8,128)S(1)}, f32[3,16,32,128]{3,2,1,0:T(8,128)S(1)}, f32[16,32,128]{2,1,0:T(8,128)S(1)}) custom-call(s32[16,32,128]{2,1,0:T(8,128)} %phase.3, f32[16,32,128]{2,1,0:T(8,128)} %press.3, f32[3,16,32,128]{3,2,1,0:T(8,128)} %vel.3, f32[304,128]{1,0:T(8,128)S(1)} %get-tuple-element.30.after), custom_call_target="tpu_custom_call" | custom-call | flops 3000000 | bytes 3000000 | tf_op jit(solution)/shard_map/load/pallas_call | solution.py:839
  12.0 0.2 collective-permute-done.3.refs_0_
  12.2 0.5 %collective-permute-done.4.refs_1_ = f32[6,8,128]{2,1,0:T(8,128)S(1)} collective-permute-done((f32[6,8,128]{2,1,0:T(8,128)S(1)}, f32[6,8,128]{2,1,0:T(8,128)S(1)}, u32[]{:S(2)}, u32[]{:S(2)}) %collective-permute-start.4) | collective-permute-done | bytes 24608 | tf_op jit(solution)/shard_map/ppermute | solution.py:45
  12.7 0.0 collective-permute-done.2.got
  12.7 0.1 merge_odd.1.refs_2_.refs_3_
  12.8 0.0 collective-permute-done.1.refs_1_
  12.8 0.1 pack_y.1
  12.9 0.1 collective-permute-start.5
  13.0 0.6 %stage_z.1 = (f32[24,40,128]{2,1,0:T(8,128)S(1)}, f32[24,40,128]{2,1,0:T(8,128)S(1)}, f32[2,40,128]{2,1,0:T(8,128)S(1)}) custom-call(f32[16,32,128]{2,1,0:T(8,128)S(1)} %get-tuple-element.34.coef, f32[16,32,128]{2,1,0:T(8,128)S(1)} %get-tuple-element.31.press, f32[3,16,32,128]{3,2,1,0:T(8,128)S(1)} %get-tuple-element.32.vel, ...), custom_call_target="tpu_custom_call" | custom-call | flops 3000000 | bytes 3000000 | tf_op jit(solution)/shard_map/stage_z/pallas_call | solution.py:839
  13.6 0.7 %collective-permute-done.5.refs_2_ = f32[27,8,128]{2,1,0:T(8,128)S(1)} collective-permute-done((f32[27,8,128]{2,1,0:T(8,128)S(1)}, f32[27,8,128]{2,1,0:T(8,128)S(1)}, u32[]{:S(2)}, u32[]{:S(2)}) %collective-permute-start.5) | collective-permute-done | bytes 110624 | tf_op jit(solution)/shard_map/ppermute | solution.py:45
  14.3 0.2 pack_z.1
  14.5 1.6 %collective-permute-start.6 = (f32[2,40,128]{2,1,0:T(8,128)S(1)}, f32[2,40,128]{2,1,0:T(8,128)S(1)}, u32[]{:S(2)}, u32[]{:S(2)}) collective-permute-start(f32[2,40,128]{2,1,0:T(8,128)S(1)} %get-tuple-element.46), channel_id=1, source_target_pairs={{0,1},{1,0},{2,3},{3,2},{4,5},{5,4},{6,7},{7,6},{8,9},{9,8},{10,11... | collective-permute-start | bytes 122888 | tf_op jit(solution)/shard_map/ppermute | solution.py:45
  16.1 2.1 %prepare.1 = (f32[3,24,40,128]{3,2,1,0:T(8,128)S(1)}, f32[5,3,40,128]{3,2,1,0:T(8,128)S(1)}, f32[6,8,128]{2,1,0:T(8,128)S(1)}) custom-call(f32[16,32,128]{2,1,0:T(8,128)S(1)} %get-tuple-element.34.coef, f32[3,16,32,128]{3,2,1,0:T(8,128)S(1)} %get-tuple-element.32.vel, f32[16,32,128]{2,1,0:T(8,128)S(1)} %get-tuple-element.35.rhs, ...), custom_call_target="tpu_custom_call" | custom-call | flops 3000000 | bytes 3000000 | tf_op jit(solution)/shard_map/prepare/pallas_call | solution.py:839
  18.2 0.5 %outer_ends.1 = (f32[3,6,40,128]{3,2,1,0:T(8,128)S(1)}, f32[3,40,128]{2,1,0:T(8,128)S(1)}, f32[6,8,128]{2,1,0:T(8,128)S(1)}) custom-call(f32[5,3,40,128]{3,2,1,0:T(8,128)S(1)} %get-tuple-element.45.ends, f32[6,8,128]{2,1,0:T(8,128)S(1)} %get-tuple-element.47.shares_in), custom_call_target="tpu_custom_call" | custom-call | flops 3000000 | bytes 3000000 | tf_op jit(solution)/shard_map/outer_ends/pallas_call | solution.py:839
  18.7 0.3 slopes.1
  19.0 0.6 %join.1 = (f32[3,6,40,128]{3,2,1,0:T(8,128)S(1)}, f32[3,40,128]{2,1,0:T(8,128)S(1)}, f32[6,8,128]{2,1,0:T(8,128)S(1)}, f32[1,128]{1,0:T(1,128)S(1)}) custom-call(f32[16,32,128]{2,1,0:T(8,128)S(1)} %get-tuple-element.39.after.base, f32[5,3,40,128]{3,2,1,0:T(8,128)S(1)} %get-tuple-element.45.ends, ...), custom_call_target="tpu_custom_call", output_to_operand_aliasing={{0}: (3, {}), {1}: (4, {}), {2}: (5, {})} | custom-call | flops 3000000 | bytes 3000000 | tf_op jit(solution)/shard_map/join/pallas_call | solution.py:839
  19.6 10.6 %all_to_all.5 = f32[32,1,128]{2,1,0:T(1,128)S(1)} all-to-all(f32[32,1,128]{2,1,0:T(1,128)S(1)} %broadcast_in_dim.9), channel_id=1, replica_groups=mesh['gx'=4,'gy'=4,'gz'=2] {'gx','gy','gz'}, dimensions={0} | all-to-all | bytes 32768 | tf_op jit(solution)/shard_map/all_to_all | solution.py:953
  30.1 1.6 %finish.1 = (f32[3,16,32,128]{3,2,1,0:T(8,128)}, f32[16,32,128]{2,1,0:T(8,128)}) custom-call(f32[32,128]{1,0:T(8,128)S(1)} %bitcast.2, f32[3,16,32,128]{3,2,1,0:T(8,128)S(1)} %get-tuple-element.32.vel, f32[3,24,40,128]{3,2,1,0:T(8,128)S(1)} %get-tuple-element.52.basis, f32[3,6,40,128]{3,2,1,0:T(8,128)S(1)} %get-tuple-element.53.basis_z, ...), custom_call_target="tpu_custom_call" | custom-call | flops 3000000 | bytes 3000000 | tf_op jit(solution)/shard_map/finish/pallas_call | solution.py:839
  (3 shorter events, 0.0 us)
Async XLA Ops:
  2.2 10.6 %collective-permute-start.1 = (f32[304,128]{1,0:T(8,128)S(1)}, f32[304,128]{1,0:T(8,128)S(1)}, u32[]{:S(2)}, u32[]{:S(2)}) collective-permute-start(f32[304,128]{1,0:T(8,128)S(1)} %get-tuple-element.33), channel_id=1, source_target_pairs={{0,2},{1,3},{2,0},{3,1},{4,6},{5,7},{6,4},{7,5},{8,16},{9,17},{10,... | collective-permute-start | bytes 466952 | tf_op jit(solution)/shard_map/ppermute | solution.py:45
  2.7 10.1 %collective-permute-start = (f32[304,128]{1,0:T(8,128)S(1)}, f32[304,128]{1,0:T(8,128)S(1)}, u32[]{:S(2)}, u32[]{:S(2)}) collective-permute-start(f32[304,128]{1,0:T(8,128)S(1)} %get-tuple-element.30.after), channel_id=1, source_target_pairs={{0,8},{1,9},{2,10},{3,11},{4,12},{5,13},{6,14},{7,15},{8,0},{9,1},... | collective-permute-start | bytes 466952 | tf_op jit(solution)/shard_map/ppermute | solution.py:45
  6.9 5.9 %collective-permute-start.2 = (f32[20,8,128]{2,1,0:T(8,128)S(1)}, f32[20,8,128]{2,1,0:T(8,128)S(1)}, u32[]{:S(2)}, u32[]{:S(2)}) collective-permute-start(f32[20,8,128]{2,1,0:T(8,128)S(1)} %get-tuple-element.36), channel_id=1, source_target_pairs={{0,1},{1,0},{2,4},{3,5},{4,2},{5,3},{6,7},{7,6},{8,9},{9,8},{10,12... | collective-permute-start | bytes 245768 | tf_op jit(solution)/shard_map/ppermute | solution.py:45
  8.4 3.8 %collective-permute-start.3 = (f32[6,8,128]{2,1,0:T(8,128)S(1)}, f32[6,8,128]{2,1,0:T(8,128)S(1)}, u32[]{:S(2)}, u32[]{:S(2)}) collective-permute-start(f32[6,8,128]{2,1,0:T(8,128)S(1)} %get-tuple-element.37), channel_id=1, source_target_pairs={{0,1},{1,0},{2,12},{3,13},{4,10},{5,11},{6,7},{7,6},{8,9},{9,8},{1... | collective-permute-start | bytes 73736 | tf_op jit(solution)/shard_map/ppermute | solution.py:45
  8.9 3.8 %collective-permute-start.4 = (f32[6,8,128]{2,1,0:T(8,128)S(1)}, f32[6,8,128]{2,1,0:T(8,128)S(1)}, u32[]{:S(2)}, u32[]{:S(2)}) collective-permute-start(f32[6,8,128]{2,1,0:T(8,128)S(1)} %get-tuple-element.38), channel_id=1, source_target_pairs={{0,1},{1,0},{2,3},{3,2},{4,5},{5,4},{6,7},{7,6},{8,9},{9,8},{10,20... | collective-permute-start | bytes 73736 | tf_op jit(solution)/shard_map/ppermute | solution.py:45
  12.9 1.4 %collective-permute-start.5 = (f32[27,8,128]{2,1,0:T(8,128)S(1)}, f32[27,8,128]{2,1,0:T(8,128)S(1)}, u32[]{:S(2)}, u32[]{:S(2)}) collective-permute-start(f32[27,8,128]{2,1,0:T(8,128)S(1)} %pack_y.1), channel_id=1, source_target_pairs={{0,2},{1,3},{2,0},{3,1},{4,6},{5,7},{6,4},{7,5},{8,10},{9,11},{10,... | collective-permute-start | bytes 331784 | tf_op jit(solution)/shard_map/ppermute | solution.py:45
  14.5 4.4 %collective-permute-start.6 = (f32[2,40,128]{2,1,0:T(8,128)S(1)}, f32[2,40,128]{2,1,0:T(8,128)S(1)}, u32[]{:S(2)}, u32[]{:S(2)}) collective-permute-start(f32[2,40,128]{2,1,0:T(8,128)S(1)} %get-tuple-element.46), channel_id=1, source_target_pairs={{0,1},{1,0},{2,3},{3,2},{4,5},{5,4},{6,7},{7,6},{8,9},{9,8},{10,11... | collective-permute-start | bytes 122888 | tf_op jit(solution)/shard_map/ppermute | solution.py:45

commit v11 on v10

--- a/solution.py
+++ b/solution.py
@@ -213,7 +213,7 @@
 
 
 def merge_odd(nx, got, *refs):
-    corners, out = refs[:-1], refs[-1]
+    corners, out = refs[:-1][::-1], refs[-1]
     total = nx + 2 * DEPTH
     rows, lanes = row_index((ROWS, LANES)), lane_index((ROWS, LANES))
     ends_at, vx_at = nx + nx // ROWS, nx + nx // ROWS + 1
@@ -883,7 +883,7 @@
     if odd:
         odd_rows = call(
             functools.partial(merge_odd, nx),
-            [got_odd, *corners],
+            [got_odd, *corners[::-1]],
             [VMEM] * (1 + n_x),
             [rows_y],
             "merge_odd",

time: 32 us -> 31.4 us (0.981)
  blocking collectives: 10.6 us -> 9.57 us
  starting transfers between devices: 9.86 us -> 10.2 us
    all_to_all x1, blocking collectives: 10.6 us -> 9.57 us  [on_device(): gathered = lax.all_to_all(spread, AXES, 0, 0).reshape(devices, LANES)]
    ppermute x7, starting transfers between devices: 9.86 us -> 10.2 us  [exchange(): return lax.ppermute(send, AXES, swaps(moves))]
  transfers between devices with their start and end apart: 7 -> 7, of which waited for: 3 -> 4; matrix products, arithmetic and copies ran while one was open for 0% -> 0% of each run, Pallas kernels for 16% -> 16%
where the time goes in v11:
time: 31.4 us; the launch traced here: 31.2 us
  starting transfers between devices  10.2 us (32%)
  blocking collectives  9.57 us (30%)
  Pallas kernels  9.18 us (29%)
  waiting for transfers between devices  1.53 us (5%)
  between operations  0.69 us (2%)
    ppermute x7, starting transfers between devices, exchange(): return lax.ppermute(send, AXES, swaps(moves))  10.2 us
    all_to_all x1, blocking collectives, on_device(): gathered = lax.all_to_all(spread, AXES, 0, 0).reshape(devices, LANES)  9.57 us
    pallas_call x11, Pallas kernels, call(): pl.pallas_call(kernel, out_shape=shapes, in_specs=in_specs, out_specs=[ou...  9.18 us
    ppermute x7, waiting for transfers between devices, exchange(): return lax.ppermute(send, AXES, swaps(moves))  1.53 us
  transfers between devices with their start and end apart: 7, of which 4 were waited for; matrix products, arithmetic and copies ran while one was open for 0% of the time, Pallas kernels for 16%

profile of v11, /device:TPU:0, one launch (start us, length us, event | category | flops | bytes accessed | tf_op | source)
XLA Modules:
  0.0 31.2 jit_solution(11093958107815656594)
XLA Ops:
  0.6 1.6 %pack_first.1 = (f32[304,128]{1,0:T(8,128)S(1)}, f32[304,128]{1,0:T(8,128)S(1)}, f32[20,8,128]{2,1,0:T(8,128)S(1)}, f32[6,8,128]{2,1,0:T(8,128)S(1)}, f32[6,8,128]{2,1,0:T(8,128)S(1)}) custom-call(s32[16,32,128]{2,1,0:T(8,128)} %phase.3, f32[16,32,128]{2,1,0:T(8,128)} %press.3, f32[3,16,32,128]{3,2,1,0:T(8,128)} %vel.3), custom_call_target="tpu_custom_call" | custom-call | flops 3000000 | bytes 3000000 | tf_op jit(solution)/shard_map/pack_first/pallas_call | solution.py:839
  2.2 0.5 %collective-permute-start.1 = (f32[304,128]{1,0:T(8,128)S(1)}, f32[304,128]{1,0:T(8,128)S(1)}, u32[]{:S(2)}, u32[]{:S(2)}) collective-permute-start(f32[304,128]{1,0:T(8,128)S(1)} %get-tuple-element.33), channel_id=1, source_target_pairs={{0,2},{1,3},{2,0},{3,1},{4,6},{5,7},{6,4},{7,5},{8,16},{9,17},{10,... | collective-permute-start | bytes 466952 | tf_op jit(solution)/shard_map/ppermute | solution.py:45
  2.7 4.2 %collective-permute-start = (f32[304,128]{1,0:T(8,128)S(1)}, f32[304,128]{1,0:T(8,128)S(1)}, u32[]{:S(2)}, u32[]{:S(2)}) collective-permute-start(f32[304,128]{1,0:T(8,128)S(1)} %get-tuple-element.30.after), channel_id=1, source_target_pairs={{0,8},{1,9},{2,10},{3,11},{4,12},{5,13},{6,14},{7,15},{8,0},{9,1},... | collective-permute-start | bytes 466952 | tf_op jit(solution)/shard_map/ppermute | solution.py:45
  6.9 1.5 %collective-permute-start.2 = (f32[20,8,128]{2,1,0:T(8,128)S(1)}, f32[20,8,128]{2,1,0:T(8,128)S(1)}, u32[]{:S(2)}, u32[]{:S(2)}) collective-permute-start(f32[20,8,128]{2,1,0:T(8,128)S(1)} %get-tuple-element.36), channel_id=1, source_target_pairs={{0,1},{1,0},{2,4},{3,5},{4,2},{5,3},{6,7},{7,6},{8,9},{9,8},{10,12... | collective-permute-start | bytes 245768 | tf_op jit(solution)/shard_map/ppermute | solution.py:45
  8.4 0.5 %collective-permute-start.3 = (f32[6,8,128]{2,1,0:T(8,128)S(1)}, f32[6,8,128]{2,1,0:T(8,128)S(1)}, u32[]{:S(2)}, u32[]{:S(2)}) collective-permute-start(f32[6,8,128]{2,1,0:T(8,128)S(1)} %get-tuple-element.37), channel_id=1, source_target_pairs={{0,1},{1,0},{2,3},{3,2},{4,5},{5,4},{6,7},{7,6},{8,9},{9,8},{10,20... | collective-permute-start | bytes 73736 | tf_op jit(solution)/shard_map/ppermute | solution.py:45
  8.9 1.5 %collective-permute-start.4 = (f32[6,8,128]{2,1,0:T(8,128)S(1)}, f32[6,8,128]{2,1,0:T(8,128)S(1)}, u32[]{:S(2)}, u32[]{:S(2)}) collective-permute-start(f32[6,8,128]{2,1,0:T(8,128)S(1)} %get-tuple-element.38), channel_id=1, source_target_pairs={{0,1},{1,0},{2,12},{3,13},{4,10},{5,11},{6,7},{7,6},{8,9},{9,8},{1... | collective-permute-start | bytes 73736 | tf_op jit(solution)/shard_map/ppermute | solution.py:45
  10.4 1.6 %load.1 = (f32[16,32,128]{2,1,0:T(8,128)S(1)}, f32[16,32,128]{2,1,0:T(8,128)S(1)}, f32[3,16,32,128]{3,2,1,0:T(8,128)S(1)}, f32[16,32,128]{2,1,0:T(8,128)S(1)}) custom-call(s32[16,32,128]{2,1,0:T(8,128)} %phase.3, f32[16,32,128]{2,1,0:T(8,128)} %press.3, f32[3,16,32,128]{3,2,1,0:T(8,128)} %vel.3, f32[304,128]{1,0:T(8,128)S(1)} %get-tuple-element.30.after), custom_call_target="tpu_custom_call" | custom-call | flops 3000000 | bytes 3000000 | tf_op jit(solution)/shard_map/load/pallas_call | solution.py:839
  12.0 0.2 collective-permute-done.3.refs_0_
  12.2 0.5 %collective-permute-done.4.refs_1_ = f32[6,8,128]{2,1,0:T(8,128)S(1)} collective-permute-done((f32[6,8,128]{2,1,0:T(8,128)S(1)}, f32[6,8,128]{2,1,0:T(8,128)S(1)}, u32[]{:S(2)}, u32[]{:S(2)}) %collective-permute-start.4) | collective-permute-done | bytes 24608 | tf_op jit(solution)/shard_map/ppermute | solution.py:45
  12.7 0.0 collective-permute-done.2.got
  12.7 0.1 merge_odd.1.refs_2_.refs_3_
  12.8 0.1 pack_y.1
  12.9 1.2 %collective-permute-start.5 = (f32[27,8,128]{2,1,0:T(8,128)S(1)}, f32[27,8,128]{2,1,0:T(8,128)S(1)}, u32[]{:S(2)}, u32[]{:S(2)}) collective-permute-start(f32[27,8,128]{2,1,0:T(8,128)S(1)} %pack_y.1), channel_id=1, source_target_pairs={{0,2},{1,3},{2,0},{3,1},{4,6},{5,7},{6,4},{7,5},{8,10},{9,11},{10,... | collective-permute-start | bytes 331784 | tf_op jit(solution)/shard_map/ppermute | solution.py:45
  14.1 0.6 %stage_z.1 = (f32[24,40,128]{2,1,0:T(8,128)S(1)}, f32[24,40,128]{2,1,0:T(8,128)S(1)}, f32[2,40,128]{2,1,0:T(8,128)S(1)}) custom-call(f32[16,32,128]{2,1,0:T(8,128)S(1)} %get-tuple-element.34.coef, f32[16,32,128]{2,1,0:T(8,128)S(1)} %get-tuple-element.31.press, f32[3,16,32,128]{3,2,1,0:T(8,128)S(1)} %get-tuple-element.32.vel, ...), custom_call_target="tpu_custom_call" | custom-call | flops 3000000 | bytes 3000000 | tf_op jit(solution)/shard_map/stage_z/pallas_call | solution.py:839
  14.7 0.4 %collective-permute-done.5.refs_2_ = f32[27,8,128]{2,1,0:T(8,128)S(1)} collective-permute-done((f32[27,8,128]{2,1,0:T(8,128)S(1)}, f32[27,8,128]{2,1,0:T(8,128)S(1)}, u32[]{:S(2)}, u32[]{:S(2)}) %collective-permute-start.5) | collective-permute-done | bytes 110624 | tf_op jit(solution)/shard_map/ppermute | solution.py:45
  15.1 0.2 pack_z.1
  15.3 0.8 %collective-permute-start.6 = (f32[2,40,128]{2,1,0:T(8,128)S(1)}, f32[2,40,128]{2,1,0:T(8,128)S(1)}, u32[]{:S(2)}, u32[]{:S(2)}) collective-permute-start(f32[2,40,128]{2,1,0:T(8,128)S(1)} %get-tuple-element.46), channel_id=1, source_target_pairs={{0,1},{1,0},{2,3},{3,2},{4,5},{5,4},{6,7},{7,6},{8,9},{9,8},{10,11... | collective-permute-start | bytes 122888 | tf_op jit(solution)/shard_map/ppermute | solution.py:45
  16.1 2.1 %prepare.1 = (f32[3,24,40,128]{3,2,1,0:T(8,128)S(1)}, f32[5,3,40,128]{3,2,1,0:T(8,128)S(1)}, f32[6,8,128]{2,1,0:T(8,128)S(1)}) custom-call(f32[16,32,128]{2,1,0:T(8,128)S(1)} %get-tuple-element.34.coef, f32[3,16,32,128]{3,2,1,0:T(8,128)S(1)} %get-tuple-element.32.vel, f32[16,32,128]{2,1,0:T(8,128)S(1)} %get-tuple-element.35.rhs, ...), custom_call_target="tpu_custom_call" | custom-call | flops 3000000 | bytes 3000000 | tf_op jit(solution)/shard_map/prepare/pallas_call | solution.py:839
  18.2 0.5 %outer_ends.1 = (f32[3,6,40,128]{3,2,1,0:T(8,128)S(1)}, f32[3,40,128]{2,1,0:T(8,128)S(1)}, f32[6,8,128]{2,1,0:T(8,128)S(1)}) custom-call(f32[5,3,40,128]{3,2,1,0:T(8,128)S(1)} %get-tuple-element.45.ends, f32[6,8,128]{2,1,0:T(8,128)S(1)} %get-tuple-element.47.shares_in), custom_call_target="tpu_custom_call" | custom-call | flops 3000000 | bytes 3000000 | tf_op jit(solution)/shard_map/outer_ends/pallas_call | solution.py:839
  18.7 0.3 slopes.1
  18.9 0.5 %collective-permute-done.6.refs_0_ = f32[2,40,128]{2,1,0:T(8,128)S(1)} collective-permute-done((f32[2,40,128]{2,1,0:T(8,128)S(1)}, f32[2,40,128]{2,1,0:T(8,128)S(1)}, u32[]{:S(2)}, u32[]{:S(2)}) %collective-permute-start.6) | collective-permute-done | bytes 40992 | tf_op jit(solution)/shard_map/ppermute | solution.py:45
  19.4 0.6 %join.1 = (f32[3,6,40,128]{3,2,1,0:T(8,128)S(1)}, f32[3,40,128]{2,1,0:T(8,128)S(1)}, f32[6,8,128]{2,1,0:T(8,128)S(1)}, f32[1,128]{1,0:T(1,128)S(1)}) custom-call(f32[16,32,128]{2,1,0:T(8,128)S(1)} %get-tuple-element.39.after.base, f32[5,3,40,128]{3,2,1,0:T(8,128)S(1)} %get-tuple-element.45.ends, ...), custom_call_target="tpu_custom_call", output_to_operand_aliasing={{0}: (3, {}), {1}: (4, {}), {2}: (5, {})} | custom-call | flops 3000000 | bytes 3000000 | tf_op jit(solution)/shard_map/join/pallas_call | solution.py:839
  20.0 9.6 %all_to_all.5 = f32[32,1,128]{2,1,0:T(1,128)S(1)} all-to-all(f32[32,1,128]{2,1,0:T(1,128)S(1)} %broadcast_in_dim.9), channel_id=1, replica_groups=mesh['gx'=4,'gy'=4,'gz'=2] {'gx','gy','gz'}, dimensions={0} | all-to-all | bytes 32768 | tf_op jit(solution)/shard_map/all_to_all | solution.py:953
  29.6 1.6 %finish.1 = (f32[3,16,32,128]{3,2,1,0:T(8,128)}, f32[16,32,128]{2,1,0:T(8,128)}) custom-call(f32[32,128]{1,0:T(8,128)S(1)} %bitcast.2, f32[3,16,32,128]{3,2,1,0:T(8,128)S(1)} %get-tuple-element.32.vel, f32[3,24,40,128]{3,2,1,0:T(8,128)S(1)} %get-tuple-element.52.basis, f32[3,6,40,128]{3,2,1,0:T(8,128)S(1)} %get-tuple-element.53.basis_z, ...), custom_call_target="tpu_custom_call" | custom-call | flops 3000000 | bytes 3000000 | tf_op jit(solution)/shard_map/finish/pallas_call | solution.py:839
  (3 shorter events, 0.0 us)
Async XLA Ops:
  2.2 10.6 %collective-permute-start.1 = (f32[304,128]{1,0:T(8,128)S(1)}, f32[304,128]{1,0:T(8,128)S(1)}, u32[]{:S(2)}, u32[]{:S(2)}) collective-permute-start(f32[304,128]{1,0:T(8,128)S(1)} %get-tuple-element.33), channel_id=1, source_target_pairs={{0,2},{1,3},{2,0},{3,1},{4,6},{5,7},{6,4},{7,5},{8,16},{9,17},{10,... | collective-permute-start | bytes 466952 | tf_op jit(solution)/shard_map/ppermute | solution.py:45
  2.7 10.1 %collective-permute-start = (f32[304,128]{1,0:T(8,128)S(1)}, f32[304,128]{1,0:T(8,128)S(1)}, u32[]{:S(2)}, u32[]{:S(2)}) collective-permute-start(f32[304,128]{1,0:T(8,128)S(1)} %get-tuple-element.30.after), channel_id=1, source_target_pairs={{0,8},{1,9},{2,10},{3,11},{4,12},{5,13},{6,14},{7,15},{8,0},{9,1},... | collective-permute-start | bytes 466952 | tf_op jit(solution)/shard_map/ppermute | solution.py:45
  6.9 5.9 %collective-permute-start.2 = (f32[20,8,128]{2,1,0:T(8,128)S(1)}, f32[20,8,128]{2,1,0:T(8,128)S(1)}, u32[]{:S(2)}, u32[]{:S(2)}) collective-permute-start(f32[20,8,128]{2,1,0:T(8,128)S(1)} %get-tuple-element.36), channel_id=1, source_target_pairs={{0,1},{1,0},{2,4},{3,5},{4,2},{5,3},{6,7},{7,6},{8,9},{9,8},{10,12... | collective-permute-start | bytes 245768 | tf_op jit(solution)/shard_map/ppermute | solution.py:45
  8.4 3.8 %collective-permute-start.3 = (f32[6,8,128]{2,1,0:T(8,128)S(1)}, f32[6,8,128]{2,1,0:T(8,128)S(1)}, u32[]{:S(2)}, u32[]{:S(2)}) collective-permute-start(f32[6,8,128]{2,1,0:T(8,128)S(1)} %get-tuple-element.37), channel_id=1, source_target_pairs={{0,1},{1,0},{2,3},{3,2},{4,5},{5,4},{6,7},{7,6},{8,9},{9,8},{10,20... | collective-permute-start | bytes 73736 | tf_op jit(solution)/shard_map/ppermute | solution.py:45
  8.9 3.8 %collective-permute-start.4 = (f32[6,8,128]{2,1,0:T(8,128)S(1)}, f32[6,8,128]{2,1,0:T(8,128)S(1)}, u32[]{:S(2)}, u32[]{:S(2)}) collective-permute-start(f32[6,8,128]{2,1,0:T(8,128)S(1)} %get-tuple-element.38), channel_id=1, source_target_pairs={{0,1},{1,0},{2,12},{3,13},{4,10},{5,11},{6,7},{7,6},{8,9},{9,8},{1... | collective-permute-start | bytes 73736 | tf_op jit(solution)/shard_map/ppermute | solution.py:45
  12.9 2.2 %collective-permute-start.5 = (f32[27,8,128]{2,1,0:T(8,128)S(1)}, f32[27,8,128]{2,1,0:T(8,128)S(1)}, u32[]{:S(2)}, u32[]{:S(2)}) collective-permute-start(f32[27,8,128]{2,1,0:T(8,128)S(1)} %pack_y.1), channel_id=1, source_target_pairs={{0,2},{1,3},{2,0},{3,1},{4,6},{5,7},{6,4},{7,5},{8,10},{9,11},{10,... | collective-permute-start | bytes 331784 | tf_op jit(solution)/shard_map/ppermute | solution.py:45
  15.3 4.1 %collective-permute-start.6 = (f32[2,40,128]{2,1,0:T(8,128)S(1)}, f32[2,40,128]{2,1,0:T(8,128)S(1)}, u32[]{:S(2)}, u32[]{:S(2)}) collective-permute-start(f32[2,40,128]{2,1,0:T(8,128)S(1)} %get-tuple-element.46), channel_id=1, source_target_pairs={{0,1},{1,0},{2,3},{3,2},{4,5},{5,4},{6,7},{7,6},{8,9},{9,8},{10,11... | collective-permute-start | bytes 122888 | tf_op jit(solution)/shard_map/ppermute | solution.py:45

commit v12 on v11

--- a/solution.py
+++ b/solution.py
@@ -879,11 +879,12 @@
         [pltpu.VMEM(phase.shape, jnp.int32), pltpu.SemaphoreType.DMA((3,))],
     )
     rows_y = f32(total + nx // ROWS + 1, ROWS, nz)
-    got_y, odd_rows = [], []
+    got_y, odd_rows, from_odd = [], [], []
     if odd:
+        from_odd = [got_odd, *corners[::-1]]
         odd_rows = call(
             functools.partial(merge_odd, nx),
-            [got_odd, *corners[::-1]],
+            from_odd,
             [VMEM] * (1 + n_x),
             [rows_y],
             "merge_odd",
@@ -891,8 +892,8 @@
     if n_y:
         to_y = call(
             functools.partial(pack_y, nx, ny, n_x),
-            [coef, press, vel, rhs, *got_x, *odd_rows],
-            [VMEM] * (4 + n_x) + [ANY] * len(odd_rows),
+            [coef, press, vel, rhs, *got_x, *from_odd],
+            [VMEM] * (4 + n_x) + [ANY] * len(from_odd),
             [rows_y],
             "pack_y",
         )

time: 31.4 us -> 31.3 us (level)
  no operation moved by 1% of the time
where the time goes in v12:
time: 31.3 us; the launch traced here: 31.1 us
  starting transfers between devices  10.2 us (33%)
  blocking collectives  9.57 us (31%)
  Pallas kernels  9.18 us (29%)
  waiting for transfers between devices  1.44 us (5%)
  between operations  0.69 us (2%)
    ppermute x7, starting transfers between devices, exchange(): return lax.ppermute(send, AXES, swaps(moves))  10.2 us
    all_to_all x1, blocking collectives, on_device(): gathered = lax.all_to_all(spread, AXES, 0, 0).reshape(devices, LANES)  9.57 us
    pallas_call x11, Pallas kernels, call(): pl.pallas_call(kernel, out_shape=shapes, in_specs=in_specs, out_specs=[ou...  9.18 us
    ppermute x7, waiting for transfers between devices, exchange(): return lax.ppermute(send, AXES, swaps(moves))  1.44 us
  transfers between devices with their start and end apart: 7, of which 4 were waited for; matrix products, arithmetic and copies ran while one was open for 0% of the time, Pallas kernels for 16%

profile of v12, /device:TPU:0, one launch (start us, length us, event | category | flops | bytes accessed | tf_op | source)
XLA Modules:
  0.0 31.1 jit_solution(1578169610652850991)
XLA Ops:
  0.6 1.6 %pack_first.1 = (f32[304,128]{1,0:T(8,128)S(1)}, f32[304,128]{1,0:T(8,128)S(1)}, f32[20,8,128]{2,1,0:T(8,128)S(1)}, f32[6,8,128]{2,1,0:T(8,128)S(1)}, f32[6,8,128]{2,1,0:T(8,128)S(1)}) custom-call(s32[16,32,128]{2,1,0:T(8,128)} %phase.3, f32[16,32,128]{2,1,0:T(8,128)} %press.3, f32[3,16,32,128]{3,2,1,0:T(8,128)} %vel.3), custom_call_target="tpu_custom_call" | custom-call | flops 3000000 | bytes 3000000 | tf_op jit(solution)/shard_map/pack_first/pallas_call | solution.py:839
  2.2 0.5 %collective-permute-start.1 = (f32[304,128]{1,0:T(8,128)S(1)}, f32[304,128]{1,0:T(8,128)S(1)}, u32[]{:S(2)}, u32[]{:S(2)}) collective-permute-start(f32[304,128]{1,0:T(8,128)S(1)} %get-tuple-element.33), channel_id=1, source_target_pairs={{0,2},{1,3},{2,0},{3,1},{4,6},{5,7},{6,4},{7,5},{8,16},{9,17},{10,... | collective-permute-start | bytes 466952 | tf_op jit(solution)/shard_map/ppermute | solution.py:45
  2.7 4.2 %collective-permute-start = (f32[304,128]{1,0:T(8,128)S(1)}, f32[304,128]{1,0:T(8,128)S(1)}, u32[]{:S(2)}, u32[]{:S(2)}) collective-permute-start(f32[304,128]{1,0:T(8,128)S(1)} %get-tuple-element.30.after), channel_id=1, source_target_pairs={{0,8},{1,9},{2,10},{3,11},{4,12},{5,13},{6,14},{7,15},{8,0},{9,1},... | collective-permute-start | bytes 466952 | tf_op jit(solution)/shard_map/ppermute | solution.py:45
  6.9 1.5 %collective-permute-start.2 = (f32[20,8,128]{2,1,0:T(8,128)S(1)}, f32[20,8,128]{2,1,0:T(8,128)S(1)}, u32[]{:S(2)}, u32[]{:S(2)}) collective-permute-start(f32[20,8,128]{2,1,0:T(8,128)S(1)} %get-tuple-element.36), channel_id=1, source_target_pairs={{0,1},{1,0},{2,4},{3,5},{4,2},{5,3},{6,7},{7,6},{8,9},{9,8},{10,12... | collective-permute-start | bytes 245768 | tf_op jit(solution)/shard_map/ppermute | solution.py:45
  8.4 0.5 %collective-permute-start.3 = (f32[6,8,128]{2,1,0:T(8,128)S(1)}, f32[6,8,128]{2,1,0:T(8,128)S(1)}, u32[]{:S(2)}, u32[]{:S(2)}) collective-permute-start(f32[6,8,128]{2,1,0:T(8,128)S(1)} %get-tuple-element.37), channel_id=1, source_target_pairs={{0,1},{1,0},{2,3},{3,2},{4,5},{5,4},{6,7},{7,6},{8,9},{9,8},{10,20... | collective-permute-start | bytes 73736 | tf_op jit(solution)/shard_map/ppermute | solution.py:45
  8.9 1.5 %collective-permute-start.4 = (f32[6,8,128]{2,1,0:T(8,128)S(1)}, f32[6,8,128]{2,1,0:T(8,128)S(1)}, u32[]{:S(2)}, u32[]{:S(2)}) collective-permute-start(f32[6,8,128]{2,1,0:T(8,128)S(1)} %get-tuple-element.38), channel_id=1, source_target_pairs={{0,1},{1,0},{2,12},{3,13},{4,10},{5,11},{6,7},{7,6},{8,9},{9,8},{1... | collective-permute-start | bytes 73736 | tf_op jit(solution)/shard_map/ppermute | solution.py:45
  10.4 1.6 %load.1 = (f32[16,32,128]{2,1,0:T(8,128)S(1)}, f32[16,32,128]{2,1,0:T(8,128)S(1)}, f32[3,16,32,128]{3,2,1,0:T(8,128)S(1)}, f32[16,32,128]{2,1,0:T(8,128)S(1)}) custom-call(s32[16,32,128]{2,1,0:T(8,128)} %phase.3, f32[16,32,128]{2,1,0:T(8,128)} %press.3, f32[3,16,32,128]{3,2,1,0:T(8,128)} %vel.3, f32[304,128]{1,0:T(8,128)S(1)} %get-tuple-element.30.after), custom_call_target="tpu_custom_call" | custom-call | flops 3000000 | bytes 3000000 | tf_op jit(solution)/shard_map/load/pallas_call | solution.py:839
  12.0 0.2 collective-permute-done.3.refs_3_.refs_0_
  12.2 0.5 %collective-permute-done.4.refs_4_.refs_1_ = f32[6,8,128]{2,1,0:T(8,128)S(1)} collective-permute-done((f32[6,8,128]{2,1,0:T(8,128)S(1)}, f32[6,8,128]{2,1,0:T(8,128)S(1)}, u32[]{:S(2)}, u32[]{:S(2)}) %collective-permute-start.4) | collective-permute-done | bytes 24608 | tf_op jit(solution)/shard_map/ppermute | solution.py:45
  12.7 0.0 collective-permute-done.2.refs_2_.got
  12.7 0.1 pack_y.1
  12.9 1.2 %collective-permute-start.5 = (f32[27,8,128]{2,1,0:T(8,128)S(1)}, f32[27,8,128]{2,1,0:T(8,128)S(1)}, u32[]{:S(2)}, u32[]{:S(2)}) collective-permute-start(f32[27,8,128]{2,1,0:T(8,128)S(1)} %pack_y.1), channel_id=1, source_target_pairs={{0,2},{1,3},{2,0},{3,1},{4,6},{5,7},{6,4},{7,5},{8,10},{9,11},{10,... | collective-permute-start | bytes 331784 | tf_op jit(solution)/shard_map/ppermute | solution.py:45
  14.1 0.1 merge_odd.1.refs_3_.refs_2_
  14.1 0.6 %stage_z.1 = (f32[24,40,128]{2,1,0:T(8,128)S(1)}, f32[24,40,128]{2,1,0:T(8,128)S(1)}, f32[2,40,128]{2,1,0:T(8,128)S(1)}) custom-call(f32[16,32,128]{2,1,0:T(8,128)S(1)} %get-tuple-element.34.coef, f32[16,32,128]{2,1,0:T(8,128)S(1)} %get-tuple-element.31.press, f32[3,16,32,128]{3,2,1,0:T(8,128)S(1)} %get-tuple-element.32.vel, ...), custom_call_target="tpu_custom_call" | custom-call | flops 3000000 | bytes 3000000 | tf_op jit(solution)/shard_map/stage_z/pallas_call | solution.py:839
  14.7 0.3 %collective-permute-done.5.refs_2_ = f32[27,8,128]{2,1,0:T(8,128)S(1)} collective-permute-done((f32[27,8,128]{2,1,0:T(8,128)S(1)}, f32[27,8,128]{2,1,0:T(8,128)S(1)}, u32[]{:S(2)}, u32[]{:S(2)}) %collective-permute-start.5) | collective-permute-done | bytes 110624 | tf_op jit(solution)/shard_map/ppermute | solution.py:45
  15.0 0.2 pack_z.1
  15.2 0.8 %collective-permute-start.6 = (f32[2,40,128]{2,1,0:T(8,128)S(1)}, f32[2,40,128]{2,1,0:T(8,128)S(1)}, u32[]{:S(2)}, u32[]{:S(2)}) collective-permute-start(f32[2,40,128]{2,1,0:T(8,128)S(1)} %get-tuple-element.46), channel_id=1, source_target_pairs={{0,1},{1,0},{2,3},{3,2},{4,5},{5,4},{6,7},{7,6},{8,9},{9,8},{10,11... | collective-permute-start | bytes 122888 | tf_op jit(solution)/shard_map/ppermute | solution.py:45
  16.1 2.1 %prepare.1 = (f32[3,24,40,128]{3,2,1,0:T(8,128)S(1)}, f32[5,3,40,128]{3,2,1,0:T(8,128)S(1)}, f32[6,8,128]{2,1,0:T(8,128)S(1)}) custom-call(f32[16,32,128]{2,1,0:T(8,128)S(1)} %get-tuple-element.34.coef, f32[3,16,32,128]{3,2,1,0:T(8,128)S(1)} %get-tuple-element.32.vel, f32[16,32,128]{2,1,0:T(8,128)S(1)} %get-tuple-element.35.rhs, ...), custom_call_target="tpu_custom_call" | custom-call | flops 3000000 | bytes 3000000 | tf_op jit(solution)/shard_map/prepare/pallas_call | solution.py:839
  18.1 0.5 %outer_ends.1 = (f32[3,6,40,128]{3,2,1,0:T(8,128)S(1)}, f32[3,40,128]{2,1,0:T(8,128)S(1)}, f32[6,8,128]{2,1,0:T(8,128)S(1)}) custom-call(f32[5,3,40,128]{3,2,1,0:T(8,128)S(1)} %get-tuple-element.45.ends, f32[6,8,128]{2,1,0:T(8,128)S(1)} %get-tuple-element.47.shares_in), custom_call_target="tpu_custom_call" | custom-call | flops 3000000 | bytes 3000000 | tf_op jit(solution)/shard_map/outer_ends/pallas_call | solution.py:839
  18.6 0.3 slopes.1
  18.9 0.4 %collective-permute-done.6.refs_0_ = f32[2,40,128]{2,1,0:T(8,128)S(1)} collective-permute-done((f32[2,40,128]{2,1,0:T(8,128)S(1)}, f32[2,40,128]{2,1,0:T(8,128)S(1)}, u32[]{:S(2)}, u32[]{:S(2)}) %collective-permute-start.6) | collective-permute-done | bytes 40992 | tf_op jit(solution)/shard_map/ppermute | solution.py:45
  19.3 0.6 %join.1 = (f32[3,6,40,128]{3,2,1,0:T(8,128)S(1)}, f32[3,40,128]{2,1,0:T(8,128)S(1)}, f32[6,8,128]{2,1,0:T(8,128)S(1)}, f32[1,128]{1,0:T(1,128)S(1)}) custom-call(f32[16,32,128]{2,1,0:T(8,128)S(1)} %get-tuple-element.39.after.base, f32[5,3,40,128]{3,2,1,0:T(8,128)S(1)} %get-tuple-element.45.ends, ...), custom_call_target="tpu_custom_call", output_to_operand_aliasing={{0}: (3, {}), {1}: (4, {}), {2}: (5, {})} | custom-call | flops 3000000 | bytes 3000000 | tf_op jit(solution)/shard_map/join/pallas_call | solution.py:839
  19.9 9.6 %all_to_all.5 = f32[32,1,128]{2,1,0:T(1,128)S(1)} all-to-all(f32[32,1,128]{2,1,0:T(1,128)S(1)} %broadcast_in_dim.9), channel_id=1, replica_groups=mesh['gx'=4,'gy'=4,'gz'=2] {'gx','gy','gz'}, dimensions={0} | all-to-all | bytes 32768 | tf_op jit(solution)/shard_map/all_to_all | solution.py:954
  29.5 1.6 %finish.1 = (f32[3,16,32,128]{3,2,1,0:T(8,128)}, f32[16,32,128]{2,1,0:T(8,128)}) custom-call(f32[32,128]{1,0:T(8,128)S(1)} %bitcast.2, f32[3,16,32,128]{3,2,1,0:T(8,128)S(1)} %get-tuple-element.32.vel, f32[3,24,40,128]{3,2,1,0:T(8,128)S(1)} %get-tuple-element.52.basis, f32[3,6,40,128]{3,2,1,0:T(8,128)S(1)} %get-tuple-element.53.basis_z, ...), custom_call_target="tpu_custom_call" | custom-call | flops 3000000 | bytes 3000000 | tf_op jit(solution)/shard_map/finish/pallas_call | solution.py:839
  (3 shorter events, 0.0 us)
Async XLA Ops:
  2.2 10.5 %collective-permute-start.1 = (f32[304,128]{1,0:T(8,128)S(1)}, f32[304,128]{1,0:T(8,128)S(1)}, u32[]{:S(2)}, u32[]{:S(2)}) collective-permute-start(f32[304,128]{1,0:T(8,128)S(1)} %get-tuple-element.33), channel_id=1, source_target_pairs={{0,2},{1,3},{2,0},{3,1},{4,6},{5,7},{6,4},{7,5},{8,16},{9,17},{10,... | collective-permute-start | bytes 466952 | tf_op jit(solution)/shard_map/ppermute | solution.py:45
  2.7 10.0 %collective-permute-start = (f32[304,128]{1,0:T(8,128)S(1)}, f32[304,128]{1,0:T(8,128)S(1)}, u32[]{:S(2)}, u32[]{:S(2)}) collective-permute-start(f32[304,128]{1,0:T(8,128)S(1)} %get-tuple-element.30.after), channel_id=1, source_target_pairs={{0,8},{1,9},{2,10},{3,11},{4,12},{5,13},{6,14},{7,15},{8,0},{9,1},... | collective-permute-start | bytes 466952 | tf_op jit(solution)/shard_map/ppermute | solution.py:45
  6.9 5.9 %collective-permute-start.2 = (f32[20,8,128]{2,1,0:T(8,128)S(1)}, f32[20,8,128]{2,1,0:T(8,128)S(1)}, u32[]{:S(2)}, u32[]{:S(2)}) collective-permute-start(f32[20,8,128]{2,1,0:T(8,128)S(1)} %get-tuple-element.36), channel_id=1, source_target_pairs={{0,1},{1,0},{2,4},{3,5},{4,2},{5,3},{6,7},{7,6},{8,9},{9,8},{10,12... | collective-permute-start | bytes 245768 | tf_op jit(solution)/shard_map/ppermute | solution.py:45
  8.4 3.8 %collective-permute-start.3 = (f32[6,8,128]{2,1,0:T(8,128)S(1)}, f32[6,8,128]{2,1,0:T(8,128)S(1)}, u32[]{:S(2)}, u32[]{:S(2)}) collective-permute-start(f32[6,8,128]{2,1,0:T(8,128)S(1)} %get-tuple-element.37), channel_id=1, source_target_pairs={{0,1},{1,0},{2,3},{3,2},{4,5},{5,4},{6,7},{7,6},{8,9},{9,8},{10,20... | collective-permute-start | bytes 73736 | tf_op jit(solution)/shard_map/ppermute | solution.py:45
  8.9 3.8 %collective-permute-start.4 = (f32[6,8,128]{2,1,0:T(8,128)S(1)}, f32[6,8,128]{2,1,0:T(8,128)S(1)}, u32[]{:S(2)}, u32[]{:S(2)}) collective-permute-start(f32[6,8,128]{2,1,0:T(8,128)S(1)} %get-tuple-element.38), channel_id=1, source_target_pairs={{0,1},{1,0},{2,12},{3,13},{4,10},{5,11},{6,7},{7,6},{8,9},{9,8},{1... | collective-permute-start | bytes 73736 | tf_op jit(solution)/shard_map/ppermute | solution.py:45
  12.9 2.2 %collective-permute-start.5 = (f32[27,8,128]{2,1,0:T(8,128)S(1)}, f32[27,8,128]{2,1,0:T(8,128)S(1)}, u32[]{:S(2)}, u32[]{:S(2)}) collective-permute-start(f32[27,8,128]{2,1,0:T(8,128)S(1)} %pack_y.1), channel_id=1, source_target_pairs={{0,2},{1,3},{2,0},{3,1},{4,6},{5,7},{6,4},{7,5},{8,10},{9,11},{10,... | collective-permute-start | bytes 331784 | tf_op jit(solution)/shard_map/ppermute | solution.py:45
  15.2 4.1 %collective-permute-start.6 = (f32[2,40,128]{2,1,0:T(8,128)S(1)}, f32[2,40,128]{2,1,0:T(8,128)S(1)}, u32[]{:S(2)}, u32[]{:S(2)}) collective-permute-start(f32[2,40,128]{2,1,0:T(8,128)S(1)} %get-tuple-element.46), channel_id=1, source_target_pairs={{0,1},{1,0},{2,3},{3,2},{4,5},{5,4},{6,7},{7,6},{8,9},{9,8},{10,11... | collective-permute-start | bytes 122888 | tf_op jit(solution)/shard_map/ppermute | solution.py:45

commit v13 on v12

--- a/solution.py
+++ b/solution.py
@@ -474,6 +474,8 @@
     row = pl.ds(pl.multiple_of(jnp.where(below, 0, ny - ROWS), ROWS), ROWS)
     added = [[[jnp.zeros((ROWS, LANES), jnp.float32) for _ in range(2)] for _ in range(groups // 2 + 1)] for _ in sends]
     for plane in range(total):
+        if plane in (nx + DEPTH - 1, nx + DEPTH):
+            continue
         tile = got[plane]
         c_tile, r_tile = half_tile(tile, below)
         low, high = full_coef[plane, :1, :], full_coef[plane, ny - 1 : ny, :]
@@ -703,12 +705,12 @@
             received = lambda i: sides(even("gz"), got_z, lambda ref: ref[i])[side]
             solve_end(nx, ny, side, received, ends, basis_z, vz_z, shares, *scratch)
 
-    lane = lane_index((1, LANES))
-    row = jnp.zeros((1, LANES), jnp.float32)
+    rows, lanes = row_index((ROWS, LANES)), lane_index((ROWS, LANES))
+    table = jnp.zeros((ROWS, LANES), jnp.float32)
     for which in range(6):
-        value = jnp.sum(jnp.sum(shares[which], 0, keepdims=True), 1, keepdims=True)
-        row = jnp.where(lane == which, value, row)
-    sums[...] = row
+        table = jnp.where(rows == which, jnp.sum(shares[which], 0, keepdims=True), table)
+    table = jnp.where(rows == lanes, jnp.sum(table, 1, keepdims=True), 0.0)
+    sums[...] = jnp.sum(table, 0, keepdims=True)
 
 
 def slopes(nx, ny, n_x, n_y, press, vel, *refs):

time: 31.3 us -> 31.3 us (level)
  no operation moved by 1% of the time
where the time goes in v13:
time: 31.3 us; the launch traced here: 31.1 us
  starting transfers between devices  10.2 us (33%)
  blocking collectives  9.57 us (31%)
  Pallas kernels  9.16 us (29%)
  waiting for transfers between devices  1.44 us (5%)
  between operations  0.69 us (2%)
    ppermute x7, starting transfers between devices, exchange(): return lax.ppermute(send, AXES, swaps(moves))  10.2 us
    all_to_all x1, blocking collectives, on_device(): gathered = lax.all_to_all(spread, AXES, 0, 0).reshape(devices, LANES)  9.57 us
    pallas_call x11, Pallas kernels, call(): pl.pallas_call(kernel, out_shape=shapes, in_specs=in_specs, out_specs=[ou...  9.16 us
    ppermute x7, waiting for transfers between devices, exchange(): return lax.ppermute(send, AXES, swaps(moves))  1.44 us
  transfers between devices with their start and end apart: 7, of which 4 were waited for; matrix products, arithmetic and copies ran while one was open for 0% of the time, Pallas kernels for 16%

profile of v13, /device:TPU:0, one launch (start us, length us, event | category | flops | bytes accessed | tf_op | source)
XLA Modules:
  0.0 31.1 jit_solution(7255713206201528010)
XLA Ops:
  0.6 1.6 %pack_first.1 = (f32[304,128]{1,0:T(8,128)S(1)}, f32[304,128]{1,0:T(8,128)S(1)}, f32[20,8,128]{2,1,0:T(8,128)S(1)}, f32[6,8,128]{2,1,0:T(8,128)S(1)}, f32[6,8,128]{2,1,0:T(8,128)S(1)}) custom-call(s32[16,32,128]{2,1,0:T(8,128)} %phase.3, f32[16,32,128]{2,1,0:T(8,128)} %press.3, f32[3,16,32,128]{3,2,1,0:T(8,128)} %vel.3), custom_call_target="tpu_custom_call" | custom-call | flops 3000000 | bytes 3000000 | tf_op jit(solution)/shard_map/pack_first/pallas_call | solution.py:841
  2.2 0.5 %collective-permute-start.1 = (f32[304,128]{1,0:T(8,128)S(1)}, f32[304,128]{1,0:T(8,128)S(1)}, u32[]{:S(2)}, u32[]{:S(2)}) collective-permute-start(f32[304,128]{1,0:T(8,128)S(1)} %get-tuple-element.33), channel_id=1, source_target_pairs={{0,2},{1,3},{2,0},{3,1},{4,6},{5,7},{6,4},{7,5},{8,16},{9,17},{10,... | collective-permute-start | bytes 466952 | tf_op jit(solution)/shard_map/ppermute | solution.py:45
  2.7 4.2 %collective-permute-start = (f32[304,128]{1,0:T(8,128)S(1)}, f32[304,128]{1,0:T(8,128)S(1)}, u32[]{:S(2)}, u32[]{:S(2)}) collective-permute-start(f32[304,128]{1,0:T(8,128)S(1)} %get-tuple-element.30.after), channel_id=1, source_target_pairs={{0,8},{1,9},{2,10},{3,11},{4,12},{5,13},{6,14},{7,15},{8,0},{9,1},... | collective-permute-start | bytes 466952 | tf_op jit(solution)/shard_map/ppermute | solution.py:45
  6.9 1.5 %collective-permute-start.2 = (f32[20,8,128]{2,1,0:T(8,128)S(1)}, f32[20,8,128]{2,1,0:T(8,128)S(1)}, u32[]{:S(2)}, u32[]{:S(2)}) collective-permute-start(f32[20,8,128]{2,1,0:T(8,128)S(1)} %get-tuple-element.36), channel_id=1, source_target_pairs={{0,1},{1,0},{2,4},{3,5},{4,2},{5,3},{6,7},{7,6},{8,9},{9,8},{10,12... | collective-permute-start | bytes 245768 | tf_op jit(solution)/shard_map/ppermute | solution.py:45
  8.4 0.5 %collective-permute-start.3 = (f32[6,8,128]{2,1,0:T(8,128)S(1)}, f32[6,8,128]{2,1,0:T(8,128)S(1)}, u32[]{:S(2)}, u32[]{:S(2)}) collective-permute-start(f32[6,8,128]{2,1,0:T(8,128)S(1)} %get-tuple-element.37), channel_id=1, source_target_pairs={{0,1},{1,0},{2,3},{3,2},{4,5},{5,4},{6,7},{7,6},{8,9},{9,8},{10,20... | collective-permute-start | bytes 73736 | tf_op jit(solution)/shard_map/ppermute | solution.py:45
  8.9 1.5 %collective-permute-start.4 = (f32[6,8,128]{2,1,0:T(8,128)S(1)}, f32[6,8,128]{2,1,0:T(8,128)S(1)}, u32[]{:S(2)}, u32[]{:S(2)}) collective-permute-start(f32[6,8,128]{2,1,0:T(8,128)S(1)} %get-tuple-element.38), channel_id=1, source_target_pairs={{0,1},{1,0},{2,12},{3,13},{4,10},{5,11},{6,7},{7,6},{8,9},{9,8},{1... | collective-permute-start | bytes 73736 | tf_op jit(solution)/shard_map/ppermute | solution.py:45
  10.4 1.6 %load.1 = (f32[16,32,128]{2,1,0:T(8,128)S(1)}, f32[16,32,128]{2,1,0:T(8,128)S(1)}, f32[3,16,32,128]{3,2,1,0:T(8,128)S(1)}, f32[16,32,128]{2,1,0:T(8,128)S(1)}) custom-call(s32[16,32,128]{2,1,0:T(8,128)} %phase.3, f32[16,32,128]{2,1,0:T(8,128)} %press.3, f32[3,16,32,128]{3,2,1,0:T(8,128)} %vel.3, f32[304,128]{1,0:T(8,128)S(1)} %get-tuple-element.30.after), custom_call_target="tpu_custom_call" | custom-call | flops 3000000 | bytes 3000000 | tf_op jit(solution)/shard_map/load/pallas_call | solution.py:841
  12.0 0.2 collective-permute-done.3.refs_3_.refs_0_
  12.2 0.5 %collective-permute-done.4.refs_4_.refs_1_ = f32[6,8,128]{2,1,0:T(8,128)S(1)} collective-permute-done((f32[6,8,128]{2,1,0:T(8,128)S(1)}, f32[6,8,128]{2,1,0:T(8,128)S(1)}, u32[]{:S(2)}, u32[]{:S(2)}) %collective-permute-start.4) | collective-permute-done | bytes 24608 | tf_op jit(solution)/shard_map/ppermute | solution.py:45
  12.7 0.0 collective-permute-done.2.refs_2_.got
  12.7 0.1 pack_y.1
  12.9 1.2 %collective-permute-start.5 = (f32[27,8,128]{2,1,0:T(8,128)S(1)}, f32[27,8,128]{2,1,0:T(8,128)S(1)}, u32[]{:S(2)}, u32[]{:S(2)}) collective-permute-start(f32[27,8,128]{2,1,0:T(8,128)S(1)} %pack_y.1), channel_id=1, source_target_pairs={{0,2},{1,3},{2,0},{3,1},{4,6},{5,7},{6,4},{7,5},{8,10},{9,11},{10,... | collective-permute-start | bytes 331784 | tf_op jit(solution)/shard_map/ppermute | solution.py:45
  14.1 0.1 merge_odd.1.refs_3_.refs_2_
  14.1 0.6 %stage_z.1 = (f32[24,40,128]{2,1,0:T(8,128)S(1)}, f32[24,40,128]{2,1,0:T(8,128)S(1)}, f32[2,40,128]{2,1,0:T(8,128)S(1)}) custom-call(f32[16,32,128]{2,1,0:T(8,128)S(1)} %get-tuple-element.34.coef, f32[16,32,128]{2,1,0:T(8,128)S(1)} %get-tuple-element.31.press, f32[3,16,32,128]{3,2,1,0:T(8,128)S(1)} %get-tuple-element.32.vel, ...), custom_call_target="tpu_custom_call" | custom-call | flops 3000000 | bytes 3000000 | tf_op jit(solution)/shard_map/stage_z/pallas_call | solution.py:841
  14.7 0.3 %collective-permute-done.5.refs_2_ = f32[27,8,128]{2,1,0:T(8,128)S(1)} collective-permute-done((f32[27,8,128]{2,1,0:T(8,128)S(1)}, f32[27,8,128]{2,1,0:T(8,128)S(1)}, u32[]{:S(2)}, u32[]{:S(2)}) %collective-permute-start.5) | collective-permute-done | bytes 110624 | tf_op jit(solution)/shard_map/ppermute | solution.py:45
  15.0 0.2 pack_z.1
  15.2 0.8 %collective-permute-start.6 = (f32[2,40,128]{2,1,0:T(8,128)S(1)}, f32[2,40,128]{2,1,0:T(8,128)S(1)}, u32[]{:S(2)}, u32[]{:S(2)}) collective-permute-start(f32[2,40,128]{2,1,0:T(8,128)S(1)} %get-tuple-element.46), channel_id=1, source_target_pairs={{0,1},{1,0},{2,3},{3,2},{4,5},{5,4},{6,7},{7,6},{8,9},{9,8},{10,11... | collective-permute-start | bytes 122888 | tf_op jit(solution)/shard_map/ppermute | solution.py:45
  16.0 2.1 %prepare.1 = (f32[3,24,40,128]{3,2,1,0:T(8,128)S(1)}, f32[5,3,40,128]{3,2,1,0:T(8,128)S(1)}, f32[6,8,128]{2,1,0:T(8,128)S(1)}) custom-call(f32[16,32,128]{2,1,0:T(8,128)S(1)} %get-tuple-element.34.coef, f32[3,16,32,128]{3,2,1,0:T(8,128)S(1)} %get-tuple-element.32.vel, f32[16,32,128]{2,1,0:T(8,128)S(1)} %get-tuple-element.35.rhs, ...), custom_call_target="tpu_custom_call" | custom-call | flops 3000000 | bytes 3000000 | tf_op jit(solution)/shard_map/prepare/pallas_call | solution.py:841
  18.1 0.5 %outer_ends.1 = (f32[3,6,40,128]{3,2,1,0:T(8,128)S(1)}, f32[3,40,128]{2,1,0:T(8,128)S(1)}, f32[6,8,128]{2,1,0:T(8,128)S(1)}) custom-call(f32[5,3,40,128]{3,2,1,0:T(8,128)S(1)} %get-tuple-element.45.ends, f32[6,8,128]{2,1,0:T(8,128)S(1)} %get-tuple-element.47.shares_in), custom_call_target="tpu_custom_call" | custom-call | flops 3000000 | bytes 3000000 | tf_op jit(solution)/shard_map/outer_ends/pallas_call | solution.py:841
  18.6 0.3 slopes.1
  18.9 0.4 %collective-permute-done.6.refs_0_ = f32[2,40,128]{2,1,0:T(8,128)S(1)} collective-permute-done((f32[2,40,128]{2,1,0:T(8,128)S(1)}, f32[2,40,128]{2,1,0:T(8,128)S(1)}, u32[]{:S(2)}, u32[]{:S(2)}) %collective-permute-start.6) | collective-permute-done | bytes 40992 | tf_op jit(solution)/shard_map/ppermute | solution.py:45
  19.3 0.6 %join.1 = (f32[3,6,40,128]{3,2,1,0:T(8,128)S(1)}, f32[3,40,128]{2,1,0:T(8,128)S(1)}, f32[6,8,128]{2,1,0:T(8,128)S(1)}, f32[1,128]{1,0:T(1,128)S(1)}) custom-call(f32[16,32,128]{2,1,0:T(8,128)S(1)} %get-tuple-element.39.after.base, f32[5,3,40,128]{3,2,1,0:T(8,128)S(1)} %get-tuple-element.45.ends, ...), custom_call_target="tpu_custom_call", output_to_operand_aliasing={{0}: (3, {}), {1}: (4, {}), {2}: (5, {})} | custom-call | flops 3000000 | bytes 3000000 | tf_op jit(solution)/shard_map/join/pallas_call | solution.py:841
  19.9 9.6 %all_to_all.5 = f32[32,1,128]{2,1,0:T(1,128)S(1)} all-to-all(f32[32,1,128]{2,1,0:T(1,128)S(1)} %broadcast_in_dim.9), channel_id=1, replica_groups=mesh['gx'=4,'gy'=4,'gz'=2] {'gx','gy','gz'}, dimensions={0} | all-to-all | bytes 32768 | tf_op jit(solution)/shard_map/all_to_all | solution.py:956
  29.5 1.6 %finish.1 = (f32[3,16,32,128]{3,2,1,0:T(8,128)}, f32[16,32,128]{2,1,0:T(8,128)}) custom-call(f32[32,128]{1,0:T(8,128)S(1)} %bitcast.2, f32[3,16,32,128]{3,2,1,0:T(8,128)S(1)} %get-tuple-element.32.vel, f32[3,24,40,128]{3,2,1,0:T(8,128)S(1)} %get-tuple-element.52.basis, f32[3,6,40,128]{3,2,1,0:T(8,128)S(1)} %get-tuple-element.53.basis_z, ...), custom_call_target="tpu_custom_call" | custom-call | flops 3000000 | bytes 3000000 | tf_op jit(solution)/shard_map/finish/pallas_call | solution.py:841
  (3 shorter events, 0.0 us)
Async XLA Ops:
  2.2 10.5 %collective-permute-start.1 = (f32[304,128]{1,0:T(8,128)S(1)}, f32[304,128]{1,0:T(8,128)S(1)}, u32[]{:S(2)}, u32[]{:S(2)}) collective-permute-start(f32[304,128]{1,0:T(8,128)S(1)} %get-tuple-element.33), channel_id=1, source_target_pairs={{0,2},{1,3},{2,0},{3,1},{4,6},{5,7},{6,4},{7,5},{8,16},{9,17},{10,... | collective-permute-start | bytes 466952 | tf_op jit(solution)/shard_map/ppermute | solution.py:45
  2.7 10.0 %collective-permute-start = (f32[304,128]{1,0:T(8,128)S(1)}, f32[304,128]{1,0:T(8,128)S(1)}, u32[]{:S(2)}, u32[]{:S(2)}) collective-permute-start(f32[304,128]{1,0:T(8,128)S(1)} %get-tuple-element.30.after), channel_id=1, source_target_pairs={{0,8},{1,9},{2,10},{3,11},{4,12},{5,13},{6,14},{7,15},{8,0},{9,1},... | collective-permute-start | bytes 466952 | tf_op jit(solution)/shard_map/ppermute | solution.py:45
  6.9 5.9 %collective-permute-start.2 = (f32[20,8,128]{2,1,0:T(8,128)S(1)}, f32[20,8,128]{2,1,0:T(8,128)S(1)}, u32[]{:S(2)}, u32[]{:S(2)}) collective-permute-start(f32[20,8,128]{2,1,0:T(8,128)S(1)} %get-tuple-element.36), channel_id=1, source_target_pairs={{0,1},{1,0},{2,4},{3,5},{4,2},{5,3},{6,7},{7,6},{8,9},{9,8},{10,12... | collective-permute-start | bytes 245768 | tf_op jit(solution)/shard_map/ppermute | solution.py:45
  8.4 3.8 %collective-permute-start.3 = (f32[6,8,128]{2,1,0:T(8,128)S(1)}, f32[6,8,128]{2,1,0:T(8,128)S(1)}, u32[]{:S(2)}, u32[]{:S(2)}) collective-permute-start(f32[6,8,128]{2,1,0:T(8,128)S(1)} %get-tuple-element.37), channel_id=1, source_target_pairs={{0,1},{1,0},{2,3},{3,2},{4,5},{5,4},{6,7},{7,6},{8,9},{9,8},{10,20... | collective-permute-start | bytes 73736 | tf_op jit(solution)/shard_map/ppermute | solution.py:45
  8.9 3.8 %collective-permute-start.4 = (f32[6,8,128]{2,1,0:T(8,128)S(1)}, f32[6,8,128]{2,1,0:T(8,128)S(1)}, u32[]{:S(2)}, u32[]{:S(2)}) collective-permute-start(f32[6,8,128]{2,1,0:T(8,128)S(1)} %get-tuple-element.38), channel_id=1, source_target_pairs={{0,1},{1,0},{2,12},{3,13},{4,10},{5,11},{6,7},{7,6},{8,9},{9,8},{1... | collective-permute-start | bytes 73736 | tf_op jit(solution)/shard_map/ppermute | solution.py:45
  12.9 2.2 %collective-permute-start.5 = (f32[27,8,128]{2,1,0:T(8,128)S(1)}, f32[27,8,128]{2,1,0:T(8,128)S(1)}, u32[]{:S(2)}, u32[]{:S(2)}) collective-permute-start(f32[27,8,128]{2,1,0:T(8,128)S(1)} %pack_y.1), channel_id=1, source_target_pairs={{0,2},{1,3},{2,0},{3,1},{4,6},{5,7},{6,4},{7,5},{8,10},{9,11},{10,... | collective-permute-start | bytes 331784 | tf_op jit(solution)/shard_map/ppermute | solution.py:45
  15.2 4.1 %collective-permute-start.6 = (f32[2,40,128]{2,1,0:T(8,128)S(1)}, f32[2,40,128]{2,1,0:T(8,128)S(1)}, u32[]{:S(2)}, u32[]{:S(2)}) collective-permute-start(f32[2,40,128]{2,1,0:T(8,128)S(1)} %get-tuple-element.46), channel_id=1, source_target_pairs={{0,1},{1,0},{2,3},{3,2},{4,5},{5,4},{6,7},{7,6},{8,9},{9,8},{10,11... | collective-permute-start | bytes 122888 | tf_op jit(solution)/shard_map/ppermute | solution.py:45

commit v14 on v13

--- a/solution.py
+++ b/solution.py
@@ -753,10 +753,9 @@
         half = parts.shape[0] // 2
         parts = parts[:half] + parts[half:]
     sums = jnp.sum(parts, 0, keepdims=True)
-    lane = lane_index((1, LANES))
-    m0, m1, m2, m3, m4, m5 = [
-        jnp.sum(jnp.where(lane == which, sums, 0.0), 1, keepdims=True) for which in range(6)
-    ]
+    shape = (ROWS, LANES)
+    table = jnp.sum(jnp.where(row_index(shape) == lane_index(shape), sums, 0.0), 1, keepdims=True)
+    m0, m1, m2, m3, m4, m5 = [table[which : which + 1] for which in range(6)]
     l1, l2 = m2 / m1, m3 / m1
     d1, cross, d2 = m3 - l1 * m2, m4 - l1 * m3, m5 - l2 * m3
     l21 = cross / d1

time: 31.3 us -> 31.3 us (level)
  no operation moved by 1% of the time
where the time goes in v14:
time: 31.3 us; the launch traced here: 31.1 us
  starting transfers between devices  10.2 us (33%)
  blocking collectives  9.57 us (31%)
  Pallas kernels  9.17 us (29%)
  waiting for transfers between devices  1.44 us (5%)
  between operations  0.69 us (2%)
    ppermute x7, starting transfers between devices, exchange(): return lax.ppermute(send, AXES, swaps(moves))  10.2 us
    all_to_all x1, blocking collectives, on_device(): gathered = lax.all_to_all(spread, AXES, 0, 0).reshape(devices, LANES)  9.57 us
    pallas_call x11, Pallas kernels, call(): pl.pallas_call(kernel, out_shape=shapes, in_specs=in_specs, out_specs=[ou...  9.17 us
    ppermute x7, waiting for transfers between devices, exchange(): return lax.ppermute(send, AXES, swaps(moves))  1.44 us
  transfers between devices with their start and end apart: 7, of which 4 were waited for; matrix products, arithmetic and copies ran while one was open for 0% of the time, Pallas kernels for 16%

profile of v14, /device:TPU:0, one launch (start us, length us, event | category | flops | bytes accessed | tf_op | source)
XLA Modules:
  0.0 31.1 jit_solution(13398373902151875039)
XLA Ops:
  0.6 1.6 %pack_first.1 = (f32[304,128]{1,0:T(8,128)S(1)}, f32[304,128]{1,0:T(8,128)S(1)}, f32[20,8,128]{2,1,0:T(8,128)S(1)}, f32[6,8,128]{2,1,0:T(8,128)S(1)}, f32[6,8,128]{2,1,0:T(8,128)S(1)}) custom-call(s32[16,32,128]{2,1,0:T(8,128)} %phase.3, f32[16,32,128]{2,1,0:T(8,128)} %press.3, f32[3,16,32,128]{3,2,1,0:T(8,128)} %vel.3), custom_call_target="tpu_custom_call" | custom-call | flops 3000000 | bytes 3000000 | tf_op jit(solution)/shard_map/pack_first/pallas_call | solution.py:840
  2.2 0.5 %collective-permute-start.1 = (f32[304,128]{1,0:T(8,128)S(1)}, f32[304,128]{1,0:T(8,128)S(1)}, u32[]{:S(2)}, u32[]{:S(2)}) collective-permute-start(f32[304,128]{1,0:T(8,128)S(1)} %get-tuple-element.33), channel_id=1, source_target_pairs={{0,2},{1,3},{2,0},{3,1},{4,6},{5,7},{6,4},{7,5},{8,16},{9,17},{10,... | collective-permute-start | bytes 466952 | tf_op jit(solution)/shard_map/ppermute | solution.py:45
  2.7 4.2 %collective-permute-start = (f32[304,128]{1,0:T(8,128)S(1)}, f32[304,128]{1,0:T(8,128)S(1)}, u32[]{:S(2)}, u32[]{:S(2)}) collective-permute-start(f32[304,128]{1,0:T(8,128)S(1)} %get-tuple-element.30.after), channel_id=1, source_target_pairs={{0,8},{1,9},{2,10},{3,11},{4,12},{5,13},{6,14},{7,15},{8,0},{9,1},... | collective-permute-start | bytes 466952 | tf_op jit(solution)/shard_map/ppermute | solution.py:45
  6.9 1.5 %collective-permute-start.2 = (f32[20,8,128]{2,1,0:T(8,128)S(1)}, f32[20,8,128]{2,1,0:T(8,128)S(1)}, u32[]{:S(2)}, u32[]{:S(2)}) collective-permute-start(f32[20,8,128]{2,1,0:T(8,128)S(1)} %get-tuple-element.36), channel_id=1, source_target_pairs={{0,1},{1,0},{2,4},{3,5},{4,2},{5,3},{6,7},{7,6},{8,9},{9,8},{10,12... | collective-permute-start | bytes 245768 | tf_op jit(solution)/shard_map/ppermute | solution.py:45
  8.4 0.5 %collective-permute-start.3 = (f32[6,8,128]{2,1,0:T(8,128)S(1)}, f32[6,8,128]{2,1,0:T(8,128)S(1)}, u32[]{:S(2)}, u32[]{:S(2)}) collective-permute-start(f32[6,8,128]{2,1,0:T(8,128)S(1)} %get-tuple-element.37), channel_id=1, source_target_pairs={{0,1},{1,0},{2,3},{3,2},{4,5},{5,4},{6,7},{7,6},{8,9},{9,8},{10,20... | collective-permute-start | bytes 73736 | tf_op jit(solution)/shard_map/ppermute | solution.py:45
  8.9 1.5 %collective-permute-start.4 = (f32[6,8,128]{2,1,0:T(8,128)S(1)}, f32[6,8,128]{2,1,0:T(8,128)S(1)}, u32[]{:S(2)}, u32[]{:S(2)}) collective-permute-start(f32[6,8,128]{2,1,0:T(8,128)S(1)} %get-tuple-element.38), channel_id=1, source_target_pairs={{0,1},{1,0},{2,12},{3,13},{4,10},{5,11},{6,7},{7,6},{8,9},{9,8},{1... | collective-permute-start | bytes 73736 | tf_op jit(solution)/shard_map/ppermute | solution.py:45
  10.4 1.6 %load.1 = (f32[16,32,128]{2,1,0:T(8,128)S(1)}, f32[16,32,128]{2,1,0:T(8,128)S(1)}, f32[3,16,32,128]{3,2,1,0:T(8,128)S(1)}, f32[16,32,128]{2,1,0:T(8,128)S(1)}) custom-call(s32[16,32,128]{2,1,0:T(8,128)} %phase.3, f32[16,32,128]{2,1,0:T(8,128)} %press.3, f32[3,16,32,128]{3,2,1,0:T(8,128)} %vel.3, f32[304,128]{1,0:T(8,128)S(1)} %get-tuple-element.30.after), custom_call_target="tpu_custom_call" | custom-call | flops 3000000 | bytes 3000000 | tf_op jit(solution)/shard_map/load/pallas_call | solution.py:840
  12.0 0.2 collective-permute-done.3.refs_3_.refs_0_
  12.2 0.5 %collective-permute-done.4.refs_4_.refs_1_ = f32[6,8,128]{2,1,0:T(8,128)S(1)} collective-permute-done((f32[6,8,128]{2,1,0:T(8,128)S(1)}, f32[6,8,128]{2,1,0:T(8,128)S(1)}, u32[]{:S(2)}, u32[]{:S(2)}) %collective-permute-start.4) | collective-permute-done | bytes 24608 | tf_op jit(solution)/shard_map/ppermute | solution.py:45
  12.7 0.0 collective-permute-done.2.refs_2_.got
  12.7 0.1 pack_y.1
  12.9 1.2 %collective-permute-start.5 = (f32[27,8,128]{2,1,0:T(8,128)S(1)}, f32[27,8,128]{2,1,0:T(8,128)S(1)}, u32[]{:S(2)}, u32[]{:S(2)}) collective-permute-start(f32[27,8,128]{2,1,0:T(8,128)S(1)} %pack_y.1), channel_id=1, source_target_pairs={{0,2},{1,3},{2,0},{3,1},{4,6},{5,7},{6,4},{7,5},{8,10},{9,11},{10,... | collective-permute-start | bytes 331784 | tf_op jit(solution)/shard_map/ppermute | solution.py:45
  14.1 0.1 merge_odd.1.refs_3_.refs_2_
  14.1 0.6 %stage_z.1 = (f32[24,40,128]{2,1,0:T(8,128)S(1)}, f32[24,40,128]{2,1,0:T(8,128)S(1)}, f32[2,40,128]{2,1,0:T(8,128)S(1)}) custom-call(f32[16,32,128]{2,1,0:T(8,128)S(1)} %get-tuple-element.34.coef, f32[16,32,128]{2,1,0:T(8,128)S(1)} %get-tuple-element.31.press, f32[3,16,32,128]{3,2,1,0:T(8,128)S(1)} %get-tuple-element.32.vel, ...), custom_call_target="tpu_custom_call" | custom-call | flops 3000000 | bytes 3000000 | tf_op jit(solution)/shard_map/stage_z/pallas_call | solution.py:840
  14.7 0.3 %collective-permute-done.5.refs_2_ = f32[27,8,128]{2,1,0:T(8,128)S(1)} collective-permute-done((f32[27,8,128]{2,1,0:T(8,128)S(1)}, f32[27,8,128]{2,1,0:T(8,128)S(1)}, u32[]{:S(2)}, u32[]{:S(2)}) %collective-permute-start.5) | collective-permute-done | bytes 110624 | tf_op jit(solution)/shard_map/ppermute | solution.py:45
  15.0 0.2 pack_z.1
  15.2 0.8 %collective-permute-start.6 = (f32[2,40,128]{2,1,0:T(8,128)S(1)}, f32[2,40,128]{2,1,0:T(8,128)S(1)}, u32[]{:S(2)}, u32[]{:S(2)}) collective-permute-start(f32[2,40,128]{2,1,0:T(8,128)S(1)} %get-tuple-element.46), channel_id=1, source_target_pairs={{0,1},{1,0},{2,3},{3,2},{4,5},{5,4},{6,7},{7,6},{8,9},{9,8},{10,11... | collective-permute-start | bytes 122888 | tf_op jit(solution)/shard_map/ppermute | solution.py:45
  16.0 2.1 %prepare.1 = (f32[3,24,40,128]{3,2,1,0:T(8,128)S(1)}, f32[5,3,40,128]{3,2,1,0:T(8,128)S(1)}, f32[6,8,128]{2,1,0:T(8,128)S(1)}) custom-call(f32[16,32,128]{2,1,0:T(8,128)S(1)} %get-tuple-element.34.coef, f32[3,16,32,128]{3,2,1,0:T(8,128)S(1)} %get-tuple-element.32.vel, f32[16,32,128]{2,1,0:T(8,128)S(1)} %get-tuple-element.35.rhs, ...), custom_call_target="tpu_custom_call" | custom-call | flops 3000000 | bytes 3000000 | tf_op jit(solution)/shard_map/prepare/pallas_call | solution.py:840
  18.1 0.5 %outer_ends.1 = (f32[3,6,40,128]{3,2,1,0:T(8,128)S(1)}, f32[3,40,128]{2,1,0:T(8,128)S(1)}, f32[6,8,128]{2,1,0:T(8,128)S(1)}) custom-call(f32[5,3,40,128]{3,2,1,0:T(8,128)S(1)} %get-tuple-element.45.ends, f32[6,8,128]{2,1,0:T(8,128)S(1)} %get-tuple-element.47.shares_in), custom_call_target="tpu_custom_call" | custom-call | flops 3000000 | bytes 3000000 | tf_op jit(solution)/shard_map/outer_ends/pallas_call | solution.py:840
  18.6 0.3 slopes.1
  18.9 0.4 %collective-permute-done.6.refs_0_ = f32[2,40,128]{2,1,0:T(8,128)S(1)} collective-permute-done((f32[2,40,128]{2,1,0:T(8,128)S(1)}, f32[2,40,128]{2,1,0:T(8,128)S(1)}, u32[]{:S(2)}, u32[]{:S(2)}) %collective-permute-start.6) | collective-permute-done | bytes 40992 | tf_op jit(solution)/shard_map/ppermute | solution.py:45
  19.3 0.6 %join.1 = (f32[3,6,40,128]{3,2,1,0:T(8,128)S(1)}, f32[3,40,128]{2,1,0:T(8,128)S(1)}, f32[6,8,128]{2,1,0:T(8,128)S(1)}, f32[1,128]{1,0:T(1,128)S(1)}) custom-call(f32[16,32,128]{2,1,0:T(8,128)S(1)} %get-tuple-element.39.after.base, f32[5,3,40,128]{3,2,1,0:T(8,128)S(1)} %get-tuple-element.45.ends, ...), custom_call_target="tpu_custom_call", output_to_operand_aliasing={{0}: (3, {}), {1}: (4, {}), {2}: (5, {})} | custom-call | flops 3000000 | bytes 3000000 | tf_op jit(solution)/shard_map/join/pallas_call | solution.py:840
  19.9 9.6 %all_to_all.5 = f32[32,1,128]{2,1,0:T(1,128)S(1)} all-to-all(f32[32,1,128]{2,1,0:T(1,128)S(1)} %broadcast_in_dim.9), channel_id=1, replica_groups=mesh['gx'=4,'gy'=4,'gz'=2] {'gx','gy','gz'}, dimensions={0} | all-to-all | bytes 32768 | tf_op jit(solution)/shard_map/all_to_all | solution.py:955
  29.5 1.6 %finish.1 = (f32[3,16,32,128]{3,2,1,0:T(8,128)}, f32[16,32,128]{2,1,0:T(8,128)}) custom-call(f32[32,128]{1,0:T(8,128)S(1)} %bitcast.2, f32[3,16,32,128]{3,2,1,0:T(8,128)S(1)} %get-tuple-element.32.vel, f32[3,24,40,128]{3,2,1,0:T(8,128)S(1)} %get-tuple-element.52.basis, f32[3,6,40,128]{3,2,1,0:T(8,128)S(1)} %get-tuple-element.53.basis_z, ...), custom_call_target="tpu_custom_call" | custom-call | flops 3000000 | bytes 3000000 | tf_op jit(solution)/shard_map/finish/pallas_call | solution.py:840
  (3 shorter events, 0.0 us)
Async XLA Ops:
  2.2 10.5 %collective-permute-start.1 = (f32[304,128]{1,0:T(8,128)S(1)}, f32[304,128]{1,0:T(8,128)S(1)}, u32[]{:S(2)}, u32[]{:S(2)}) collective-permute-start(f32[304,128]{1,0:T(8,128)S(1)} %get-tuple-element.33), channel_id=1, source_target_pairs={{0,2},{1,3},{2,0},{3,1},{4,6},{5,7},{6,4},{7,5},{8,16},{9,17},{10,... | collective-permute-start | bytes 466952 | tf_op jit(solution)/shard_map/ppermute | solution.py:45
  2.7 10.0 %collective-permute-start = (f32[304,128]{1,0:T(8,128)S(1)}, f32[304,128]{1,0:T(8,128)S(1)}, u32[]{:S(2)}, u32[]{:S(2)}) collective-permute-start(f32[304,128]{1,0:T(8,128)S(1)} %get-tuple-element.30.after), channel_id=1, source_target_pairs={{0,8},{1,9},{2,10},{3,11},{4,12},{5,13},{6,14},{7,15},{8,0},{9,1},... | collective-permute-start | bytes 466952 | tf_op jit(solution)/shard_map/ppermute | solution.py:45
  6.9 5.9 %collective-permute-start.2 = (f32[20,8,128]{2,1,0:T(8,128)S(1)}, f32[20,8,128]{2,1,0:T(8,128)S(1)}, u32[]{:S(2)}, u32[]{:S(2)}) collective-permute-start(f32[20,8,128]{2,1,0:T(8,128)S(1)} %get-tuple-element.36), channel_id=1, source_target_pairs={{0,1},{1,0},{2,4},{3,5},{4,2},{5,3},{6,7},{7,6},{8,9},{9,8},{10,12... | collective-permute-start | bytes 245768 | tf_op jit(solution)/shard_map/ppermute | solution.py:45
  8.4 3.8 %collective-permute-start.3 = (f32[6,8,128]{2,1,0:T(8,128)S(1)}, f32[6,8,128]{2,1,0:T(8,128)S(1)}, u32[]{:S(2)}, u32[]{:S(2)}) collective-permute-start(f32[6,8,128]{2,1,0:T(8,128)S(1)} %get-tuple-element.37), channel_id=1, source_target_pairs={{0,1},{1,0},{2,3},{3,2},{4,5},{5,4},{6,7},{7,6},{8,9},{9,8},{10,20... | collective-permute-start | bytes 73736 | tf_op jit(solution)/shard_map/ppermute | solution.py:45
  8.9 3.8 %collective-permute-start.4 = (f32[6,8,128]{2,1,0:T(8,128)S(1)}, f32[6,8,128]{2,1,0:T(8,128)S(1)}, u32[]{:S(2)}, u32[]{:S(2)}) collective-permute-start(f32[6,8,128]{2,1,0:T(8,128)S(1)} %get-tuple-element.38), channel_id=1, source_target_pairs={{0,1},{1,0},{2,12},{3,13},{4,10},{5,11},{6,7},{7,6},{8,9},{9,8},{1... | collective-permute-start | bytes 73736 | tf_op jit(solution)/shard_map/ppermute | solution.py:45
  12.9 2.2 %collective-permute-start.5 = (f32[27,8,128]{2,1,0:T(8,128)S(1)}, f32[27,8,128]{2,1,0:T(8,128)S(1)}, u32[]{:S(2)}, u32[]{:S(2)}) collective-permute-start(f32[27,8,128]{2,1,0:T(8,128)S(1)} %pack_y.1), channel_id=1, source_target_pairs={{0,2},{1,3},{2,0},{3,1},{4,6},{5,7},{6,4},{7,5},{8,10},{9,11},{10,... | collective-permute-start | bytes 331784 | tf_op jit(solution)/shard_map/ppermute | solution.py:45
  15.2 4.1 %collective-permute-start.6 = (f32[2,40,128]{2,1,0:T(8,128)S(1)}, f32[2,40,128]{2,1,0:T(8,128)S(1)}, u32[]{:S(2)}, u32[]{:S(2)}) collective-permute-start(f32[2,40,128]{2,1,0:T(8,128)S(1)} %get-tuple-element.46), channel_id=1, source_target_pairs={{0,1},{1,0},{2,3},{3,2},{4,5},{5,4},{6,7},{7,6},{8,9},{9,8},{10,11... | collective-permute-start | bytes 122888 | tf_op jit(solution)/shard_map/ppermute | solution.py:45
